TPU v7x, 128 devices: a whole 4x4x4 slice. The times are simulated.
128 devices in a mesh: section: 2 (over y_lo), dp: 2 (over core), shard: 32 (over x, z, y_hi).
Axes of the slice: x: 4, y: 4 (y_hi: 2, y_lo: 2; y = y_hi * 2 + y_lo), z: 4, core: 2. Of those that a mesh axis runs over, the one named last changes fastest.
Arguments:
- inputs: bfloat16 [2, 2, 2048, 1536], P('dp', None, 'shard'), may hold values from -6 to 6
- cotangent: bfloat16 [2, 2, 2048, 1536], P('dp', None, 'shard'), may hold values from -6 to 6
- routes: int32 [2, 2, 2, 2048, 6], P('section', 'dp', None, 'shard'), may hold values from 0 to 63, all different within a row; in each aligned block of 64 rows (0 to 63, 64 to 127, ..., all dimensions but the last counted through in order) at most 8 rows name the same one
- norm_attn: bfloat16 [2, 1536], P('section', 'shard'), may hold values from 0.5 to 1.5
- w_query: bfloat16 [2, 1536, 1536], P('section', 'shard'), may hold values from -0.15625 to 0.15625
- w_key: bfloat16 [2, 1536, 512], P('section', 'shard'), may hold values from -0.15625 to 0.15625
- w_value: bfloat16 [2, 1536, 512], P('section', 'shard'), may hold values from -0.15625 to 0.15625
- w_output: bfloat16 [2, 1536, 1536], P('section', 'shard'), may hold values from -3.5 to 3.5
- norm_ffn: bfloat16 [2, 1536], P('section', 'shard'), may hold values from 0.5 to 1.5
- w_router: bfloat16 [2, 1536, 64], P('section', 'shard'), may hold values from -0.078125 to 0.078125
- shared_gate: bfloat16 [2, 1536, 1024], P('section', 'shard'), may hold values from -0.15625 to 0.15625
- shared_up: bfloat16 [2, 1536, 1024], P('section', 'shard'), may hold values from -0.15625 to 0.15625
- shared_down: bfloat16 [2, 1024, 1536], P('section', 'shard'), may hold values from -0.1875 to 0.1875
- expert_gate: bfloat16 [2, 64, 1536, 512], P('section', 'shard'), may hold values from -0.15625 to 0.15625
- expert_up: bfloat16 [2, 64, 1536, 512], P('section', 'shard'), may hold values from -0.15625 to 0.15625
- expert_down: bfloat16 [2, 64, 512, 1536], P('section', 'shard'), may hold values from -0.5 to 0.5
Outputs:
- section_out: bfloat16 [2, 2, 2, 2048, 1536], P('section', 'dp', None, 'shard')
- section_in_grad: bfloat16 [2, 2, 2, 2048, 1536], P('section', 'dp', None, 'shard')
- grad_norm_attn: float32 [2, 1536], P('section', 'shard')
- grad_query: float32 [2, 1536, 1536], P('section', 'shard')
- grad_key: float32 [2, 1536, 512], P('section', 'shard')
- grad_value: float32 [2, 1536, 512], P('section', 'shard')
- grad_output: float32 [2, 1536, 1536], P('section', 'shard')
- grad_norm_ffn: float32 [2, 1536], P('section', 'shard')
- grad_router: float32 [2, 1536, 64], P('section', 'shard')
- grad_shared_gate: float32 [2, 1536, 1024], P('section', 'shard')
- grad_shared_up: float32 [2, 1536, 1024], P('section', 'shard')
- grad_shared_down: float32 [2, 1024, 1536], P('section', 'shard')
- grad_expert_gate: float32 [2, 64, 1536, 512], P('section', 'shard')
- grad_expert_up: float32 [2, 64, 1536, 512], P('section', 'shard')
- grad_expert_down: float32 [2, 64, 512, 1536], P('section', 'shard')
Inputs may be any that keep to these rules, and one draw needn't show every extreme that they name: `routes`: each row names 6 different experts. In each aligned block of 64 rows (one index of shard in one micro-batch) no expert is named by more than 8 rows.
All inputs are finite; a program needn't handle non-finite values.
Results may differ from a plain program's by a relative error of at most 0.035.
Values may be sent and summed in bfloat16 or wider, within the bound.
No kernel may reach another device: no remote copies, remote signals or barrier semaphores. Data moves between devices by JAX's collectives and lax.ppermute only.
A program may use at most 320 MiB of HBM per device.

v0:
```python
import jax
import jax.numpy as jnp
from jax import lax
from jax.sharding import PartitionSpec as P

H = 12
KVH = 4
HD = 128
TOPK = 6


epsilon = 1e-05
masked_score = -1e30


def passed_along(value, axis, steps):
    count = lax.axis_size(axis)
    leading, last = (max(0, -steps), min(count, count - steps))
    return lax.ppermute(value, axis, [(source, source + steps) for source in range(leading, last)])


def normed(layer_in):
    return layer_in * lax.rsqrt(jnp.mean(layer_in * layer_in, axis=-1, keepdims=True) + epsilon)


def norm_back(layer_in, gain, upstream):
    inverse = lax.rsqrt(jnp.mean(layer_in * layer_in, axis=-1, keepdims=True) + epsilon)
    unit_rows = layer_in * inverse
    gain_grad = jnp.sum(upstream * unit_rows, axis=0)
    scaled = upstream * gain
    in_grad = inverse * (scaled - unit_rows * jnp.mean(scaled * unit_rows, axis=-1, keepdims=True))
    return (in_grad, gain_grad)


def silu_of(argument):
    return argument * jax.nn.sigmoid(argument)


def silu_slope(argument):
    sigmoid = jax.nn.sigmoid(argument)
    return sigmoid * (1.0 + argument * (1.0 - sigmoid))


def wide_dot(left_side, right_side):
    return jnp.dot(left_side, right_side, preferred_element_type=jnp.float32)


def wide_einsum(formula, left_side, right_side):
    return jnp.einsum(formula, left_side, right_side, preferred_element_type=jnp.float32)


def route_tables(route_rows, experts, capacity):
    flat_routes = route_rows.reshape(-1)
    one_hot = (flat_routes[:, None] == jnp.arange(experts, dtype=jnp.int32)[None, :]).astype(
        jnp.int32
    )
    before = jnp.cumsum(one_hot, axis=0) - one_hot
    slot_ids = jnp.sum(before * one_hot, axis=1)
    target = flat_routes * capacity + slot_ids
    pick_table = (
        target[:, None] == jnp.arange(experts * capacity, dtype=jnp.int32)[None, :]
    ).astype(jnp.bfloat16)
    chosen = (route_rows[:, :, None] == jnp.arange(experts, dtype=jnp.int32)[None, None, :]).astype(
        jnp.float32
    )
    return (
        pick_table.reshape(route_rows.shape[0], route_rows.shape[1], experts * capacity),
        chosen,
    )


def gate_values(normed_two, router_w, chosen):
    logits = wide_dot(normed_two, router_w)
    picked = jnp.sum(chosen * logits[:, None, :], axis=2)
    return jax.nn.softmax(picked, axis=-1)


def body(
    inputs,
    cotangent,
    routes,
    norm_attn,
    w_query,
    w_key,
    w_value,
    w_output,
    norm_ffn,
    w_router,
    shared_gate,
    shared_up,
    shared_down,
    expert_gate,
    expert_up,
    expert_down,
):
    micro_count = inputs.shape[1]
    block_rows = inputs.shape[2]
    model_width = inputs.shape[3]
    shards = lax.axis_size("shard")
    section_index = lax.axis_index("section")
    position = lax.axis_index("shard")
    batch_tokens = block_rows * shards
    seq_len = micro_count * batch_tokens
    local_experts = expert_gate.shape[1]
    experts = local_experts * shards
    capacity = max(2, (4 * block_rows * TOPK + 3 * experts - 1) // (3 * experts))
    group_size = H // KVH
    head_width = H * HD
    key_width = KVH * HD
    scaling = HD ** (-0.5)
    row_index = jnp.arange(block_rows, dtype=jnp.int32)
    forward_weights = (
        lax.all_gather(norm_attn[0], "shard", axis=0, tiled=True),
        lax.all_gather(w_query[0], "shard", axis=0, tiled=True),
        lax.all_gather(w_key[0], "shard", axis=0, tiled=True),
        lax.all_gather(w_value[0], "shard", axis=0, tiled=True),
        lax.all_gather(w_output[0], "shard", axis=0, tiled=True),
        lax.all_gather(norm_ffn[0], "shard", axis=0, tiled=True),
        lax.all_gather(w_router[0], "shard", axis=0, tiled=True),
        lax.all_gather(shared_gate[0], "shard", axis=0, tiled=True),
        lax.all_gather(shared_up[0], "shard", axis=0, tiled=True),
        lax.all_gather(shared_down[0], "shard", axis=0, tiled=True),
    )
    expert_g = expert_gate[0]
    expert_u = expert_up[0]
    expert_d = expert_down[0]
    local_in = inputs[0]
    local_cot = cotangent[0]
    local_routes = routes[0, 0]
    expert_width = expert_g.shape[2]
    shared_width = forward_weights[7].shape[1]
    expert_rows = shards * capacity

    def attention_scores(queries, cache_keys, micro_index, key_span):
        query_heads = queries.reshape(block_rows, KVH, group_size, HD)
        key_heads = cache_keys[:key_span].reshape(key_span, KVH, HD)
        scores = wide_einsum("cghd,lgd->ghcl", query_heads, key_heads) * scaling
        query_pos = micro_index * batch_tokens + position * block_rows + row_index
        allowed = jnp.arange(key_span, dtype=jnp.int32)[None, :] <= query_pos[:, None]
        return jnp.where(allowed, scores, masked_score)

    (
        gain_one,
        query_w,
        key_w,
        value_w,
        output_w,
        gain_two,
        router_w,
        shared_g,
        shared_u,
        shared_d,
    ) = forward_weights
    gain_one_f = gain_one.astype(jnp.float32)
    gain_two_f = gain_two.astype(jnp.float32)
    cache_keys = jnp.zeros((seq_len, key_width), jnp.bfloat16)
    cache_values = jnp.zeros((seq_len, key_width), jnp.bfloat16)
    store_in = jnp.zeros((micro_count, block_rows, model_width), jnp.bfloat16)
    store_queries = jnp.zeros((micro_count, block_rows, head_width), jnp.bfloat16)
    store_attended = jnp.zeros((micro_count, block_rows, head_width), jnp.bfloat16)
    store_log = jnp.zeros((micro_count, KVH, group_size, block_rows, 1), jnp.float32)
    store_hidden = jnp.zeros((micro_count, block_rows, model_width), jnp.float32)
    store_expert_in = jnp.zeros(
        (micro_count, local_experts, expert_rows, model_width), jnp.bfloat16
    )
    store_gate_pre = jnp.zeros((micro_count, local_experts, expert_rows, expert_width), jnp.float32)
    store_up_pre = jnp.zeros((micro_count, local_experts, expert_rows, expert_width), jnp.float32)
    store_selected = jnp.zeros((micro_count, block_rows, TOPK, model_width), jnp.bfloat16)
    store_shared_gate = jnp.zeros((micro_count, block_rows, shared_width), jnp.float32)
    store_shared_up = jnp.zeros((micro_count, block_rows, shared_width), jnp.float32)
    out_store = jnp.zeros((micro_count, block_rows, model_width), jnp.bfloat16)
    received = jnp.zeros((block_rows, model_width), jnp.bfloat16)
    for moment in range(micro_count + 1):
        micro_index = jnp.clip(moment - section_index, 0, micro_count - 1)
        key_span = min(moment + 1, micro_count) * batch_tokens
        layer_b = jnp.where(section_index == 0, local_in[micro_index], received)
        layer_in = layer_b.astype(jnp.float32)
        normed_one = (normed(layer_in) * gain_one_f).astype(jnp.bfloat16)
        queries = wide_dot(normed_one, query_w).astype(jnp.bfloat16)
        keys_b = wide_dot(normed_one, key_w).astype(jnp.bfloat16)
        values_b = wide_dot(normed_one, value_w).astype(jnp.bfloat16)
        all_keys, all_values = (
            lax.all_gather(keys_b, "shard", axis=0, tiled=True),
            lax.all_gather(values_b, "shard", axis=0, tiled=True),
        )
        cache_keys = lax.dynamic_update_slice_in_dim(
            cache_keys, all_keys, micro_index * batch_tokens, 0
        )
        cache_values = lax.dynamic_update_slice_in_dim(
            cache_values, all_values, micro_index * batch_tokens, 0
        )
        scores = attention_scores(queries, cache_keys, micro_index, key_span)
        peak = jnp.max(scores, axis=-1, keepdims=True)
        log_total = peak + jnp.log(jnp.sum(jnp.exp(scores - peak), axis=-1, keepdims=True))
        probs_rounded = jnp.exp(scores - log_total).astype(jnp.bfloat16)
        value_heads = cache_values[:key_span].reshape(key_span, KVH, HD)
        attended = wide_einsum("ghcl,lgd->cghd", probs_rounded, value_heads)
        attended = attended.reshape(block_rows, head_width).astype(jnp.bfloat16)
        hidden = layer_in + wide_dot(attended, output_w)
        normed_two = (normed(hidden) * gain_two_f).astype(jnp.bfloat16)
        pick_table, chosen = route_tables(local_routes[micro_index], experts, capacity)
        gate_weights = gate_values(normed_two, router_w, chosen)
        outgoing = wide_einsum("cks,cd->sd", pick_table, normed_two).astype(jnp.bfloat16)
        outgoing = outgoing.reshape(shards, local_experts, capacity, model_width)
        expert_in = lax.all_to_all(outgoing, "shard", split_axis=0, concat_axis=2, tiled=True)[0]
        gate_pre = wide_einsum("erd,edf->erf", expert_in, expert_g)
        up_pre = wide_einsum("erd,edf->erf", expert_in, expert_u)
        activated = (silu_of(gate_pre) * up_pre).astype(jnp.bfloat16)
        expert_out = wide_einsum("erf,efd->erd", activated, expert_d).astype(jnp.bfloat16)
        returned = lax.all_to_all(
            expert_out, "shard", split_axis=1, concat_axis=0, tiled=True
        ).reshape(experts * capacity, model_width)
        selected = wide_einsum("cks,sd->ckd", pick_table, returned).astype(jnp.bfloat16)
        routed = jnp.sum(gate_weights[:, :, None] * selected.astype(jnp.float32), axis=1)
        shared_gate_pre = wide_dot(normed_two, shared_g)
        shared_up_pre = wide_dot(normed_two, shared_u)
        shared_act = (silu_of(shared_gate_pre) * shared_up_pre).astype(jnp.bfloat16)
        output_b = (hidden + routed + wide_dot(shared_act, shared_d)).astype(jnp.bfloat16)
        store_in = store_in.at[micro_index].set(layer_b)
        store_queries = store_queries.at[micro_index].set(queries)
        store_attended = store_attended.at[micro_index].set(attended)
        store_log = store_log.at[micro_index].set(log_total)
        store_hidden = store_hidden.at[micro_index].set(hidden)
        store_expert_in = store_expert_in.at[micro_index].set(expert_in)
        store_gate_pre = store_gate_pre.at[micro_index].set(gate_pre)
        store_up_pre = store_up_pre.at[micro_index].set(up_pre)
        store_selected = store_selected.at[micro_index].set(selected)
        store_shared_gate = store_shared_gate.at[micro_index].set(shared_gate_pre)
        store_shared_up = store_shared_up.at[micro_index].set(shared_up_pre)
        out_store = out_store.at[micro_index].set(output_b)
        if moment < micro_count:
            received = passed_along(output_b, "section", 1)
    backward_weights = (
        lax.all_gather(norm_attn[0], "shard", axis=0, tiled=True),
        lax.all_gather(w_query[0], "shard", axis=0, tiled=True),
        lax.all_gather(w_key[0], "shard", axis=0, tiled=True),
        lax.all_gather(w_value[0], "shard", axis=0, tiled=True),
        lax.all_gather(w_output[0], "shard", axis=0, tiled=True),
        lax.all_gather(norm_ffn[0], "shard", axis=0, tiled=True),
        lax.all_gather(w_router[0], "shard", axis=0, tiled=True),
        lax.all_gather(shared_gate[0], "shard", axis=0, tiled=True),
        lax.all_gather(shared_up[0], "shard", axis=0, tiled=True),
        lax.all_gather(shared_down[0], "shard", axis=0, tiled=True),
    )
    (
        gain_one,
        query_w,
        key_w,
        value_w,
        output_w,
        gain_two,
        router_w,
        shared_g,
        shared_u,
        shared_d,
    ) = backward_weights
    gain_one_f = gain_one.astype(jnp.float32)
    gain_two_f = gain_two.astype(jnp.float32)
    grad_gain_one = jnp.zeros(gain_one.shape, jnp.float32)
    grad_gain_two = jnp.zeros(gain_two.shape, jnp.float32)
    partial_keys = jnp.zeros((seq_len, key_width), jnp.float32)
    partial_values = jnp.zeros((seq_len, key_width), jnp.float32)
    grad_store = jnp.zeros((micro_count, block_rows, model_width), jnp.bfloat16)
    keep_normed_one = jnp.zeros((micro_count, block_rows, model_width), jnp.bfloat16)
    keep_normed_two = jnp.zeros((micro_count, block_rows, model_width), jnp.bfloat16)
    keep_shared_act = jnp.zeros((micro_count, block_rows, shared_width), jnp.bfloat16)
    keep_activated = jnp.zeros(
        (micro_count, local_experts, expert_rows, expert_width), jnp.bfloat16
    )
    keep_upstream = jnp.zeros((micro_count, block_rows, model_width), jnp.bfloat16)
    keep_shared_gate_grad = jnp.zeros((micro_count, block_rows, shared_width), jnp.bfloat16)
    keep_shared_up_grad = jnp.zeros((micro_count, block_rows, shared_width), jnp.bfloat16)
    keep_expert_grad = jnp.zeros(
        (micro_count, local_experts, expert_rows, model_width), jnp.bfloat16
    )
    keep_gate_pre_grad = jnp.zeros(
        (micro_count, local_experts, expert_rows, expert_width), jnp.bfloat16
    )
    keep_up_pre_grad = jnp.zeros(
        (micro_count, local_experts, expert_rows, expert_width), jnp.bfloat16
    )
    keep_logit_grad = jnp.zeros((micro_count, block_rows, experts), jnp.bfloat16)
    keep_hidden_grad = jnp.zeros((micro_count, block_rows, model_width), jnp.bfloat16)
    keep_query_grad = jnp.zeros((micro_count, block_rows, head_width), jnp.bfloat16)
    keep_key_grad = jnp.zeros((micro_count, block_rows, key_width), jnp.bfloat16)
    keep_value_grad = jnp.zeros((micro_count, block_rows, key_width), jnp.bfloat16)
    received = jnp.zeros((block_rows, model_width), jnp.bfloat16)
    for moment in range(micro_count + 1):
        raw_index = micro_count - moment - section_index
        live_mask = ((raw_index >= 0) & (raw_index < micro_count)).astype(jnp.float32)
        micro_index = jnp.clip(raw_index, 0, micro_count - 1)
        key_span = min(micro_count, micro_count - moment + 1) * batch_tokens
        upstream = (
            jnp.where(section_index == 1, local_cot[micro_index], received).astype(jnp.float32)
            * live_mask
        )
        layer_in = store_in[micro_index].astype(jnp.float32)
        hidden = store_hidden[micro_index]
        normed_one = (normed(layer_in) * gain_one_f).astype(jnp.bfloat16)
        normed_two = (normed(hidden) * gain_two_f).astype(jnp.bfloat16)
        pick_table, chosen = route_tables(local_routes[micro_index], experts, capacity)
        gate_weights = gate_values(normed_two, router_w, chosen)
        shared_gate_pre = store_shared_gate[micro_index]
        shared_up_pre = store_shared_up[micro_index]
        shared_act = (silu_of(shared_gate_pre) * shared_up_pre).astype(jnp.bfloat16)
        upstream_b = upstream.astype(jnp.bfloat16)
        shared_act_grad = wide_einsum("cd,fd->cf", upstream_b, shared_d)
        shared_gate_grad = (shared_act_grad * shared_up_pre * silu_slope(shared_gate_pre)).astype(
            jnp.bfloat16
        )
        shared_up_grad = (shared_act_grad * silu_of(shared_gate_pre)).astype(jnp.bfloat16)
        normed_two_grad = wide_einsum("cf,df->cd", shared_gate_grad, shared_g) + wide_einsum(
            "cf,df->cd", shared_up_grad, shared_u
        )
        selected = store_selected[micro_index].astype(jnp.float32)
        gate_grad = jnp.sum(upstream[:, None, :] * selected, axis=2)
        selected_grad = (gate_weights[:, :, None] * upstream[:, None, :]).astype(jnp.bfloat16)
        outgoing = wide_einsum("cks,ckd->sd", pick_table, selected_grad).astype(jnp.bfloat16)
        outgoing = outgoing.reshape(shards, local_experts, capacity, model_width)
        expert_grad = lax.all_to_all(outgoing, "shard", split_axis=0, concat_axis=2, tiled=True)[0]
        gate_pre = store_gate_pre[micro_index]
        up_pre = store_up_pre[micro_index]
        activated = (silu_of(gate_pre) * up_pre).astype(jnp.bfloat16)
        act_grad = wide_einsum("erd,efd->erf", expert_grad, expert_d)
        gate_pre_grad = (act_grad * up_pre * silu_slope(gate_pre)).astype(jnp.bfloat16)
        up_pre_grad = (act_grad * silu_of(gate_pre)).astype(jnp.bfloat16)
        expert_in_grad = (
            wide_einsum("erf,edf->erd", gate_pre_grad, expert_g)
            + wide_einsum("erf,edf->erd", up_pre_grad, expert_u)
        ).astype(jnp.bfloat16)
        returned_grad = lax.all_to_all(
            expert_in_grad, "shard", split_axis=1, concat_axis=0, tiled=True
        )
        returned_grad = returned_grad.reshape(experts * capacity, model_width)
        normed_two_grad = normed_two_grad + wide_einsum("cks,sd->cd", pick_table, returned_grad)
        picked_grad = gate_weights * (
            gate_grad - jnp.sum(gate_weights * gate_grad, axis=1, keepdims=True)
        )
        logit_grad = jnp.sum(chosen * picked_grad[:, :, None], axis=1).astype(jnp.bfloat16)
        normed_two_grad = normed_two_grad + wide_einsum("ce,de->cd", logit_grad, router_w)
        hidden_norm_grad, gain_two_grad = norm_back(hidden, gain_two_f, normed_two_grad)
        grad_gain_two = grad_gain_two + gain_two_grad
        hidden_grad = upstream + hidden_norm_grad
        hidden_grad_b = hidden_grad.astype(jnp.bfloat16)
        attended_grad = wide_einsum("cd,hd->ch", hidden_grad_b, output_w).astype(jnp.bfloat16)
        queries = store_queries[micro_index]
        scores = attention_scores(queries, cache_keys, micro_index, key_span)
        probs = jnp.exp(scores - store_log[micro_index])
        probs_rounded = probs.astype(jnp.bfloat16)
        key_heads = cache_keys[:key_span].reshape(key_span, KVH, HD)
        value_heads = cache_values[:key_span].reshape(key_span, KVH, HD)
        attended_heads = attended_grad.reshape(block_rows, KVH, group_size, HD)
        query_heads = queries.reshape(block_rows, KVH, group_size, HD)
        probs_grad = wide_einsum("cghd,lgd->ghcl", attended_heads, value_heads)
        score_grad = (
            probs * (probs_grad - jnp.sum(probs * probs_grad, axis=-1, keepdims=True))
        ).astype(jnp.bfloat16)
        query_grad = wide_einsum("ghcl,lgd->cghd", score_grad, key_heads) * scaling
        query_grad = query_grad.reshape(block_rows, head_width).astype(jnp.bfloat16)
        key_part = (wide_einsum("ghcl,cghd->lgd", score_grad, query_heads) * scaling).reshape(
            key_span, key_width
        )
        value_part = wide_einsum("ghcl,cghd->lgd", probs_rounded, attended_heads).reshape(
            key_span, key_width
        )
        partial_keys = partial_keys.at[:key_span].add(key_part)
        partial_values = partial_values.at[:key_span].add(value_part)
        key_rows = lax.dynamic_slice_in_dim(
            partial_keys, micro_index * batch_tokens, batch_tokens, 0
        )
        value_rows = lax.dynamic_slice_in_dim(
            partial_values, micro_index * batch_tokens, batch_tokens, 0
        )
        own_keys, own_values = (
            lax.psum_scatter(
                key_rows.astype(jnp.bfloat16), "shard", scatter_dimension=0, tiled=True
            ).astype(jnp.float32),
            lax.psum_scatter(
                value_rows.astype(jnp.bfloat16), "shard", scatter_dimension=0, tiled=True
            ).astype(jnp.float32),
        )
        key_grad = (own_keys * live_mask).astype(jnp.bfloat16)
        value_grad = (own_values * live_mask).astype(jnp.bfloat16)
        normed_one_grad = (
            wide_einsum("ch,dh->cd", query_grad, query_w)
            + wide_einsum("ch,dh->cd", key_grad, key_w)
            + wide_einsum("ch,dh->cd", value_grad, value_w)
        )
        in_norm_grad, gain_one_grad = norm_back(layer_in, gain_one_f, normed_one_grad)
        grad_gain_one = grad_gain_one + gain_one_grad
        layer_grad = (hidden_grad + in_norm_grad).astype(jnp.bfloat16)
        kept_grad = jnp.where(live_mask > 0, layer_grad, grad_store[micro_index])
        grad_store = grad_store.at[micro_index].set(kept_grad)
        keep_normed_one = keep_normed_one.at[micro_index].set(normed_one)
        keep_normed_two = keep_normed_two.at[micro_index].set(normed_two)
        keep_shared_act = keep_shared_act.at[micro_index].set(shared_act)
        keep_activated = keep_activated.at[micro_index].set(activated)
        keep_upstream = keep_upstream.at[micro_index].add(upstream_b)
        keep_shared_gate_grad = keep_shared_gate_grad.at[micro_index].add(shared_gate_grad)
        keep_shared_up_grad = keep_shared_up_grad.at[micro_index].add(shared_up_grad)
        keep_expert_grad = keep_expert_grad.at[micro_index].add(expert_grad)
        keep_gate_pre_grad = keep_gate_pre_grad.at[micro_index].add(gate_pre_grad)
        keep_up_pre_grad = keep_up_pre_grad.at[micro_index].add(up_pre_grad)
        keep_logit_grad = keep_logit_grad.at[micro_index].add(logit_grad)
        keep_hidden_grad = keep_hidden_grad.at[micro_index].add(hidden_grad_b)
        keep_query_grad = keep_query_grad.at[micro_index].add(query_grad)
        keep_key_grad = keep_key_grad.at[micro_index].add(key_grad)
        keep_value_grad = keep_value_grad.at[micro_index].add(value_grad)
        if moment < micro_count:
            received = passed_along(layer_grad, "section", -1)
    grad_shared_d = wide_einsum("mcf,mcd->fd", keep_shared_act, keep_upstream)
    grad_shared_g = wide_einsum("mcd,mcf->df", keep_normed_two, keep_shared_gate_grad)
    grad_shared_u = wide_einsum("mcd,mcf->df", keep_normed_two, keep_shared_up_grad)
    grad_router_w = wide_einsum("mcd,mce->de", keep_normed_two, keep_logit_grad)
    grad_output_w = wide_einsum("mch,mcd->hd", store_attended, keep_hidden_grad)
    grad_query_w = wide_einsum("mcd,mch->dh", keep_normed_one, keep_query_grad)
    grad_key_w = wide_einsum("mcd,mch->dh", keep_normed_one, keep_key_grad)
    grad_value_w = wide_einsum("mcd,mch->dh", keep_normed_one, keep_value_grad)
    grad_expert_d = wide_einsum("merf,merd->efd", keep_activated, keep_expert_grad)
    grad_expert_g = wide_einsum("merd,merf->edf", store_expert_in, keep_gate_pre_grad)
    grad_expert_u = wide_einsum("merd,merf->edf", store_expert_in, keep_up_pre_grad)
    (
        share_gain_one,
        share_query,
        share_key,
        share_value,
        share_output,
        share_gain_two,
        share_router,
        share_shared_g,
        share_shared_u,
        share_shared_d,
    ) = (
        lax.psum_scatter(
            grad_gain_one.astype(jnp.bfloat16), "shard", scatter_dimension=0, tiled=True
        ).astype(jnp.float32),
        lax.psum_scatter(
            grad_query_w.astype(jnp.bfloat16), "shard", scatter_dimension=0, tiled=True
        ).astype(jnp.float32),
        lax.psum_scatter(
            grad_key_w.astype(jnp.bfloat16), "shard", scatter_dimension=0, tiled=True
        ).astype(jnp.float32),
        lax.psum_scatter(
            grad_value_w.astype(jnp.bfloat16), "shard", scatter_dimension=0, tiled=True
        ).astype(jnp.float32),
        lax.psum_scatter(
            grad_output_w.astype(jnp.bfloat16), "shard", scatter_dimension=0, tiled=True
        ).astype(jnp.float32),
        lax.psum_scatter(
            grad_gain_two.astype(jnp.bfloat16), "shard", scatter_dimension=0, tiled=True
        ).astype(jnp.float32),
        lax.psum_scatter(
            grad_router_w.astype(jnp.bfloat16), "shard", scatter_dimension=0, tiled=True
        ).astype(jnp.float32),
        lax.psum_scatter(
            grad_shared_g.astype(jnp.bfloat16), "shard", scatter_dimension=0, tiled=True
        ).astype(jnp.float32),
        lax.psum_scatter(
            grad_shared_u.astype(jnp.bfloat16), "shard", scatter_dimension=0, tiled=True
        ).astype(jnp.float32),
        lax.psum_scatter(
            grad_shared_d.astype(jnp.bfloat16), "shard", scatter_dimension=0, tiled=True
        ).astype(jnp.float32),
    )
    summed = (
        lax.psum(share_gain_one.astype(jnp.bfloat16), "dp").astype(jnp.float32),
        lax.psum(share_query.astype(jnp.bfloat16), "dp").astype(jnp.float32),
        lax.psum(share_key.astype(jnp.bfloat16), "dp").astype(jnp.float32),
        lax.psum(share_value.astype(jnp.bfloat16), "dp").astype(jnp.float32),
        lax.psum(share_output.astype(jnp.bfloat16), "dp").astype(jnp.float32),
        lax.psum(share_gain_two.astype(jnp.bfloat16), "dp").astype(jnp.float32),
        lax.psum(share_router.astype(jnp.bfloat16), "dp").astype(jnp.float32),
        lax.psum(share_shared_g.astype(jnp.bfloat16), "dp").astype(jnp.float32),
        lax.psum(share_shared_u.astype(jnp.bfloat16), "dp").astype(jnp.float32),
        lax.psum(share_shared_d.astype(jnp.bfloat16), "dp").astype(jnp.float32),
        lax.psum(grad_expert_g.astype(jnp.bfloat16), "dp").astype(jnp.float32),
        lax.psum(grad_expert_u.astype(jnp.bfloat16), "dp").astype(jnp.float32),
        lax.psum(grad_expert_d.astype(jnp.bfloat16), "dp").astype(jnp.float32),
    )
    return (
        out_store[None, None],
        grad_store[None, None],
        summed[0][None],
        summed[1][None],
        summed[2][None],
        summed[3][None],
        summed[4][None],
        summed[5][None],
        summed[6][None],
        summed[7][None],
        summed[8][None],
        summed[9][None],
        summed[10][None],
        summed[11][None],
        summed[12][None],
    )


def solution(mesh):
    return jax.shard_map(
        body,
        mesh=mesh,
        in_specs=(
            P("dp", None, "shard", None),
            P("dp", None, "shard", None),
            P("section", "dp", None, "shard", None),
            P("section", "shard"),
            P("section", "shard", None),
            P("section", "shard", None),
            P("section", "shard", None),
            P("section", "shard", None),
            P("section", "shard"),
            P("section", "shard", None),
            P("section", "shard", None),
            P("section", "shard", None),
            P("section", "shard", None),
            P("section", "shard", None, None),
            P("section", "shard", None, None),
            P("section", "shard", None, None),
        ),
        out_specs=(
            P("section", "dp", None, "shard", None),
            P("section", "dp", None, "shard", None),
            P("section", "shard"),
            P("section", "shard", None),
            P("section", "shard", None),
            P("section", "shard", None),
            P("section", "shard", None),
            P("section", "shard"),
            P("section", "shard", None),
            P("section", "shard", None),
            P("section", "shard", None),
            P("section", "shard", None),
            P("section", "shard", None, None),
            P("section", "shard", None, None),
            P("section", "shard", None, None),
        ),
        check_vma=False,
    )
```

profile of v0, /device:TPU:1, one launch (start us, length us, event | category | flops | bytes accessed | tf_op | source)
XLA Modules:
  0.0 4725.2 jit_solution(9112021300502306055)
XLA Ops:
  12.5 85.7 %all-reduce.5 = (bf16[1536]{0:T(1024)(128)(2,1)S(1)}, bf16[1536]{0:T(1024)(128)(2,1)S(1)}) all-reduce(bf16[1536]{0:T(1024)(128)(2,1)S(1)} %dynamic-update-slice.268, bf16[1536]{0:T(1024)(128)(2,1)S(1)} %dynamic-update-slice.269), channel_id=2, replica_groups=mesh['section'=2,'dp'=2,'shard'=32] {'shard'}, use_global_device_ids=true, to_apply=%add | all-reduce | flops 3072 | bytes 12288
  162.3 59.7 %all-gather.24.cloned.1.call-done = bf16[2048,512]{1,0:T(8,128)(2,1)} async-done(((bf16[64,512]{1,0:T(8,128)(2,1)}), bf16[2048,512]{1,0:T(8,128)(2,1)}) %all-gather.24.cloned.1.call-update) | async-done | bytes 2097168 | tf_op jit(solution)/shard_map/all_gather | solution.py:184
  231.3 61.9 %all-gather.26.cloned.1.call-done = bf16[2048,512]{1,0:T(8,128)(2,1)} async-done(((bf16[64,512]{1,0:T(8,128)(2,1)}), bf16[2048,512]{1,0:T(8,128)(2,1)}) %all-gather.26.cloned.1.call-update) | async-done | bytes 2097168 | tf_op jit(solution)/shard_map/all_gather | solution.py:183
  302.4 74.7 %all-gather.40.cloned.1.call-done = bf16[1,1536,1536]{2,1,0:T(8,128)(2,1)} async-done(((bf16[1,48,1536]{2,1,0:T(8,128)(2,1)}), bf16[1,1536,1536]{2,1,0:T(8,128)(2,1)}) %all-gather.40.cloned.1.call-update) | async-done | bytes 4718608 | tf_op jit(solution)/shard_map/all_gather | solution.py:114
  395.2 65.7 %all-gather.42.cloned.1.call-done = bf16[1,1536,1536]{2,1,0:T(8,128)(2,1)} async-done(((bf16[1,48,1536]{2,1,0:T(8,128)(2,1)}), bf16[1,1536,1536]{2,1,0:T(8,128)(2,1)}) %all-gather.42.cloned.1.call-update) | async-done | bytes 4718608 | tf_op jit(solution)/shard_map/all_gather | solution.py:117
  519.2 92.8 %all-gather.6 = bf16[1,1536,64]{2,1,0:T(8,128)(2,1)S(1)} all-gather(bf16[1,48,64]{2,1,0:T(8,128)(2,1)} %param.213), channel_id=8, replica_groups=mesh['section'=2,'dp'=2,'shard'=32] {'shard'}, dimensions={1}, use_global_device_ids=true | all-gather | bytes 202752 | tf_op jit(solution)/shard_map/all_gather | solution.py:119
  647.2 65.8 %all-gather.48.cloned.1.call-done = bf16[1,1024,1536]{2,1,0:T(8,128)(2,1)} async-done(((bf16[1,32,1536]{2,1,0:T(8,128)(2,1)}), bf16[1,1024,1536]{2,1,0:T(8,128)(2,1)}) %all-gather.48.cloned.1.call-update) | async-done | bytes 3145744 | tf_op jit(solution)/shard_map/all_gather | solution.py:122
  804.3 64.2 %all-gather.28.cloned.1.call-done = bf16[2048,512]{1,0:T(8,128)(2,1)} async-done(((bf16[64,512]{1,0:T(8,128)(2,1)}), bf16[2048,512]{1,0:T(8,128)(2,1)}) %all-gather.28.cloned.1.call-update) | async-done | bytes 2097168 | tf_op jit(solution)/shard_map/all_gather | solution.py:184
  1072.2 64.2 %all-gather.32.cloned.1.call-done = bf16[2048,512]{1,0:T(8,128)(2,1)} async-done(((bf16[64,512]{1,0:T(8,128)(2,1)}), bf16[2048,512]{1,0:T(8,128)(2,1)}) %all-gather.32.cloned.1.call-update) | async-done | bytes 2097168 | tf_op jit(solution)/shard_map/all_gather | solution.py:184
  1433.6 122.3 %reduce-scatter.15.cloned.1.call-done = bf16[64,512]{1,0:T(8,128)(2,1)} async-done(((bf16[2048,512]{1,0:T(8,128)(2,1)}), bf16[64,512]{1,0:T(8,128)(2,1)}) %reduce-scatter.15.cloned.1.call-update) | async-done | bytes 65552 | tf_op jit(solution)/shard_map/reduce_scatter | solution.py:375
  1562.6 178.0 %reduce-scatter.17.cloned.1.call-done = bf16[64,512]{1,0:T(8,128)(2,1)} async-done(((bf16[2048,512]{1,0:T(8,128)(2,1)}), bf16[64,512]{1,0:T(8,128)(2,1)}) %reduce-scatter.17.cloned.1.call-update) | async-done | bytes 65552 | tf_op jit(solution)/shard_map/reduce_scatter | solution.py:378
  1941.6 144.6 %reduce-scatter.19.cloned.1.call-done = bf16[64,512]{1,0:T(8,128)(2,1)} async-done(((bf16[2048,512]{1,0:T(8,128)(2,1)}), bf16[64,512]{1,0:T(8,128)(2,1)}) %reduce-scatter.19.cloned.1.call-update) | async-done | bytes 65552 | tf_op jit(solution)/shard_map/reduce_scatter | solution.py:375
  2093.0 176.7 %reduce-scatter.21.cloned.1.call-done = bf16[64,512]{1,0:T(8,128)(2,1)} async-done(((bf16[2048,512]{1,0:T(8,128)(2,1)}), bf16[64,512]{1,0:T(8,128)(2,1)}) %reduce-scatter.21.cloned.1.call-update) | async-done | bytes 65552 | tf_op jit(solution)/shard_map/reduce_scatter | solution.py:378
  2420.3 167.6 %reduce-scatter.23.cloned.1.call-done = bf16[64,512]{1,0:T(8,128)(2,1)} async-done(((bf16[2048,512]{1,0:T(8,128)(2,1)}), bf16[64,512]{1,0:T(8,128)(2,1)}) %reduce-scatter.23.cloned.1.call-update) | async-done | bytes 65552 | tf_op jit(solution)/shard_map/reduce_scatter | solution.py:375
  2593.6 178.7 %reduce-scatter.25.cloned.1.call-done = bf16[64,512]{1,0:T(8,128)(2,1)} async-done(((bf16[2048,512]{1,0:T(8,128)(2,1)}), bf16[64,512]{1,0:T(8,128)(2,1)}) %reduce-scatter.25.cloned.1.call-update) | async-done | bytes 65552 | tf_op jit(solution)/shard_map/reduce_scatter | solution.py:378
  2860.4 76.7 %all-reduce.4 = (bf16[1536]{0:T(1024)(128)(2,1)S(1)}, bf16[1536]{0:T(1024)(128)(2,1)S(1)}) all-reduce(bf16[1536]{0:T(1024)(128)(2,1)S(1)} %add_convert_fusion.3, bf16[1536]{0:T(1024)(128)(2,1)S(1)} %add_convert_fusion.2), channel_id=18, replica_groups=mesh['section'=2,'dp'=2,'shard'=32] {'shard'}, use_global_device_ids=true, to_apply=%region_87.88.clone | all-reduce | flops 3072 | bytes 12288
  2938.2 75.8 %reduce-scatter.35.cloned.1.call-done = bf16[48,64]{1,0:T(8,128)(2,1)} async-done(((bf16[1536,64]{1,0:T(8,128)(2,1)}), bf16[48,64]{1,0:T(8,128)(2,1)}) %reduce-scatter.35.cloned.1.call-update) | async-done | bytes 6160 | tf_op jit(solution)/shard_map/reduce_scatter | solution.py:452
  3014.1 224.9 %reduce-scatter.29.cloned.1.call-done = bf16[48,512]{1,0:T(8,128)(2,1)} async-done(((bf16[1536,512]{1,0:T(8,128)(2,1)}), bf16[48,512]{1,0:T(8,128)(2,1)}) %reduce-scatter.29.cloned.1.call-update) | async-done | bytes 49168 | tf_op jit(solution)/shard_map/reduce_scatter | solution.py:440
  3238.9 225.7 %reduce-scatter.31.cloned.1.call-done = bf16[48,512]{1,0:T(8,128)(2,1)} async-done(((bf16[1536,512]{1,0:T(8,128)(2,1)}), bf16[48,512]{1,0:T(8,128)(2,1)}) %reduce-scatter.31.cloned.1.call-update) | async-done | bytes 49168 | tf_op jit(solution)/shard_map/reduce_scatter | solution.py:443
  3470.8 222.0 %reduce-scatter.41.cloned.1.call-done = bf16[32,1536]{1,0:T(8,128)(2,1)} async-done(((bf16[1024,1536]{1,0:T(8,128)(2,1)}), bf16[32,1536]{1,0:T(8,128)(2,1)}) %reduce-scatter.41.cloned.1.call-update) | async-done | bytes 98320 | tf_op jit(solution)/shard_map/reduce_scatter | solution.py:461
  3692.7 228.0 %reduce-scatter.39.cloned.1.call-done = bf16[48,1024]{1,0:T(8,128)(2,1)} async-done(((bf16[1536,1024]{1,0:T(8,128)(2,1)}), bf16[48,1024]{1,0:T(8,128)(2,1)}) %reduce-scatter.39.cloned.1.call-update) | async-done | bytes 98320 | tf_op jit(solution)/shard_map/reduce_scatter | solution.py:458
  3920.7 228.6 %reduce-scatter.37.cloned.1.call-done = bf16[48,1024]{1,0:T(8,128)(2,1)} async-done(((bf16[1536,1024]{1,0:T(8,128)(2,1)}), bf16[48,1024]{1,0:T(8,128)(2,1)}) %reduce-scatter.37.cloned.1.call-update) | async-done | bytes 98320 | tf_op jit(solution)/shard_map/reduce_scatter | solution.py:455
  4149.3 233.4 %reduce-scatter.33.cloned.1.call-done = bf16[48,1536]{1,0:T(8,128)(2,1)} async-done(((bf16[1536,1536]{1,0:T(8,128)(2,1)}), bf16[48,1536]{1,0:T(8,128)(2,1)}) %reduce-scatter.33.cloned.1.call-update) | async-done | bytes 147472 | tf_op jit(solution)/shard_map/reduce_scatter | solution.py:446
  4382.7 234.2 %reduce-scatter.27.cloned.1.call-done = bf16[48,1536]{1,0:T(8,128)(2,1)} async-done(((bf16[1536,1536]{1,0:T(8,128)(2,1)}), bf16[48,1536]{1,0:T(8,128)(2,1)}) %reduce-scatter.27.cloned.1.call-update) | async-done | bytes 147472 | tf_op jit(solution)/shard_map/reduce_scatter | solution.py:437
  (937 shorter events, 1354.8 us)
Async XLA Ops:
  8.7 213.3 %all-gather.24.cloned.1.call-start = ((), (), s32[]{:S(2)}) async-start(), calls=%async_computation.26 | async-start | bytes 2162688 | tf_op jit(solution)/shard_map/all_gather | solution.py:184
  102.0 191.1 %all-gather.26.cloned.1.call-start = ((), (), s32[]{:S(2)}) async-start(), calls=%async_computation.27 | async-start | bytes 2162688 | tf_op jit(solution)/shard_map/all_gather | solution.py:183
  153.0 224.1 %all-gather.40.cloned.1.call-start = ((), (), s32[]{:S(2)}) async-start(), calls=%async_computation.48 | async-start | bytes 4866048 | tf_op jit(solution)/shard_map/all_gather | solution.py:114
  153.6 307.4 %all-gather.42.cloned.1.call-start = ((), (), s32[]{:S(2)}) async-start(), calls=%async_computation.49 | async-start | bytes 4866048 | tf_op jit(solution)/shard_map/all_gather | solution.py:117
  154.2 463.0 %all-gather.46.cloned.1.call-start = ((), (), s32[]{:S(2)}) async-start(), calls=%async_computation.51 | async-start | bytes 3244032 | tf_op jit(solution)/shard_map/all_gather | solution.py:121
  154.9 483.1 %all-gather.44.cloned.1.call-start = ((), (), s32[]{:S(2)}) async-start(), calls=%async_computation.50 | async-start | bytes 3244032 | tf_op jit(solution)/shard_map/all_gather | solution.py:120
  155.7 557.4 %all-gather.48.cloned.1.call-start = ((), (), s32[]{:S(2)}) async-start(), calls=%async_computation.52 | async-start | bytes 3244032 | tf_op jit(solution)/shard_map/all_gather | solution.py:122
  519.1 278.1 %all-gather.30.cloned.1.call-start = ((), (), s32[]{:S(2)}) async-start(), calls=%async_computation.29 | async-start | bytes 2162688 | tf_op jit(solution)/shard_map/all_gather | solution.py:183
  1308.6 247.3 %reduce-scatter.15.cloned.1.call-start = ((), (), s32[]{:S(2)}) async-start(), calls=%async_computation.32 | async-start | bytes 2162688 | tf_op jit(solution)/shard_map/reduce_scatter | solution.py:375
  1394.1 346.5 %reduce-scatter.17.cloned.1.call-start = ((), (), s32[]{:S(2)}) async-start(), calls=%async_computation.33 | async-start | bytes 2162688 | tf_op jit(solution)/shard_map/reduce_scatter | solution.py:378
  1799.1 287.1 %reduce-scatter.19.cloned.1.call-start = ((), (), s32[]{:S(2)}) async-start(), calls=%async_computation.34 | async-start | bytes 2162688 | tf_op jit(solution)/shard_map/reduce_scatter | solution.py:375
  1890.3 379.4 %reduce-scatter.21.cloned.1.call-start = ((), (), s32[]{:S(2)}) async-start(), calls=%async_computation.35 | async-start | bytes 2162688 | tf_op jit(solution)/shard_map/reduce_scatter | solution.py:378
  2326.6 261.4 %reduce-scatter.23.cloned.1.call-start = ((), (), s32[]{:S(2)}) async-start(), calls=%async_computation.36 | async-start | bytes 2162688 | tf_op jit(solution)/shard_map/reduce_scatter | solution.py:375
  2390.8 381.5 %reduce-scatter.25.cloned.1.call-start = ((), (), s32[]{:S(2)}) async-start(), calls=%async_computation.37 | async-start | bytes 2162688 | tf_op jit(solution)/shard_map/reduce_scatter | solution.py:378
  2412.4 601.7 %reduce-scatter.35.cloned.1.call-start = ((), (), s32[]{:S(2)}) async-start(), calls=%async_computation.42 | async-start | bytes 405504 | tf_op jit(solution)/shard_map/reduce_scatter | solution.py:452
  2420.3 818.7 %reduce-scatter.29.cloned.1.call-start = ((), (), s32[]{:S(2)}) async-start(), calls=%async_computation.39 | async-start | bytes 1622016 | tf_op jit(solution)/shard_map/reduce_scatter | solution.py:440
  2592.2 872.4 %reduce-scatter.31.cloned.1.call-start = ((), (), s32[]{:S(2)}) async-start(), calls=%async_computation.40 | async-start | bytes 1622016 | tf_op jit(solution)/shard_map/reduce_scatter | solution.py:443
  2776.6 916.2 %reduce-scatter.41.cloned.1.call-start = ((), (), s32[]{:S(2)}) async-start(), calls=%async_computation.45 | async-start | bytes 3244032 | tf_op jit(solution)/shard_map/reduce_scatter | solution.py:461
  2780.3 1140.3 %reduce-scatter.39.cloned.1.call-start = ((), (), s32[]{:S(2)}) async-start(), calls=%async_computation.44 | async-start | bytes 3244032 | tf_op jit(solution)/shard_map/reduce_scatter | solution.py:458
  2784.3 1365.1 %reduce-scatter.37.cloned.1.call-start = ((), (), s32[]{:S(2)}) async-start(), calls=%async_computation.43 | async-start | bytes 3244032 | tf_op jit(solution)/shard_map/reduce_scatter | solution.py:455
  2788.0 1594.7 %reduce-scatter.33.cloned.1.call-start = ((), (), s32[]{:S(2)}) async-start(), calls=%async_computation.41 | async-start | bytes 4866048 | tf_op jit(solution)/shard_map/reduce_scatter | solution.py:446
  2803.0 1814.0 %reduce-scatter.27.cloned.1.call-start = ((), (), s32[]{:S(2)}) async-start(), calls=%async_computation.38 | async-start | bytes 4866048 | tf_op jit(solution)/shard_map/reduce_scatter | solution.py:437
  2822.3 1821.8 %all-reduce.11.cloned.1.call-start = ((), (), s32[]{:S(2)}) async-start(), calls=%async_computation.53 | async-start | bytes 223232 | tf_op jit(solution)/shard_map/psum | solution.py:466
  3464.6 1232.7 %all-reduce.13.cloned.1.call-start = ((), (), s32[]{:S(2)}) async-start(), calls=%async_computation.54 | async-start | bytes 20054016 | tf_op jit(solution)/shard_map/psum | solution.py:467
  (230 other events, 3763.2 us)
Sparse Core Ops, SparseCore 0:
  11.1 70.4 all-gather.35
  153.9 68.0 all-gather.23
  225.4 67.6 all-gather.25
  295.9 81.0 all-gather.39
  379.9 81.0 all-gather.41
  464.0 95.9 all-gather.45
  563.1 74.8 all-gather.43
  641.1 71.9 all-gather.47
  726.2 70.9 all-gather.29
  993.1 72.0 all-gather.33
  1394.2 161.5 reduce-scatter.14
  1558.2 182.3 reduce-scatter.16
  1890.4 195.7 reduce-scatter.18
  2088.5 181.1 reduce-scatter.20
  2391.0 196.9 reduce-scatter.22
  2591.0 181.2 reduce-scatter.24
  2777.0 236.9 reduce-scatter.34
  3019.0 219.9 reduce-scatter.28
  3244.6 219.9 reduce-scatter.30
  3469.7 223.0 reduce-scatter.40
  3697.6 223.0 reduce-scatter.38
  3926.3 222.9 reduce-scatter.36
  4154.9 227.7 reduce-scatter.32
  4389.1 227.7 reduce-scatter.26
  (5 shorter events, 273.7 us)
where the time goes:
time: 4740 us; the launch traced here: 4730 us
  waiting for transfers between devices  3430 us (72%)
  matrix products  381 us (8%)
  blocking collectives  295 us (6%)
  local copies, waits for them, and re-layouts  269 us (6%)
  other arithmetic  264 us (6%)
  starting transfers between devices  72.5 us (2%)
    reduce_scatter x3, waiting for transfers between devices, body(): lax.psum_scatter(value_rows.astype(jnp.bfloat16), 'shard', scatter_dimens...  533 us
    reduce_scatter x3, waiting for transfers between devices, body(): lax.psum_scatter(key_rows.astype(jnp.bfloat16), 'shard', scatter_dimensio...  435 us
    dot_general x86, matrix products, wide_einsum(): jnp.einsum(formula, left_side, right_side, preferred_element_type=jnp.flo...  304 us
    reduce_scatter x1, waiting for transfers between devices, body(): lax.psum_scatter(grad_query_w.astype(jnp.bfloat16), 'shard', scatter_dime...  234 us
    reduce_scatter x1, waiting for transfers between devices, body(): lax.psum_scatter(grad_output_w.astype(jnp.bfloat16), 'shard', scatter_dim...  233 us
    reduce_scatter x1, waiting for transfers between devices, body(): lax.psum_scatter(grad_shared_g.astype(jnp.bfloat16), 'shard', scatter_dim...  229 us
    reduce_scatter x1, waiting for transfers between devices, body(): lax.psum_scatter(grad_shared_u.astype(jnp.bfloat16), 'shard', scatter_dim...  228 us
    reduce_scatter x1, waiting for transfers between devices, body(): lax.psum_scatter(grad_value_w.astype(jnp.bfloat16), 'shard', scatter_dime...  226 us
  transfers between devices with their start and end apart: 43, of which 40 were waited for; matrix products, arithmetic and copies ran while one was open for 11% of the time, Pallas kernels for 0%

commit v1 on v0

v1 whole, which is shorter than its diff:
```python
import functools

import jax
import jax.numpy as jnp
from jax import lax
from jax.experimental import pallas as pl
from jax.experimental.pallas import tpu as pltpu
from jax.sharding import PartitionSpec as P

H = 12
KVH = 4
HD = 128
GROUP = H // KVH
TOPK = 6
CAP = 8

epsilon = 1e-05
masked_score = -1e30
scaling = HD ** (-0.5)
log2_scale = scaling * 1.4426950408889634
bf = jnp.bfloat16
f32 = jnp.float32


def inverse_rms(rows):
    return lax.rsqrt(jnp.mean(rows * rows, axis=-1, keepdims=True) + epsilon)


def norm_back(layer_in, gain, upstream):
    inverse = inverse_rms(layer_in)
    unit_rows = layer_in * inverse
    gain_grad = jnp.sum(upstream * unit_rows, axis=0)
    scaled = upstream * gain
    in_grad = inverse * (scaled - unit_rows * jnp.mean(scaled * unit_rows, axis=-1, keepdims=True))
    return (in_grad, gain_grad)


def silu_parts(argument):
    sigmoid = jax.nn.sigmoid(argument)
    return argument * sigmoid, sigmoid * (1.0 + argument * (1.0 - sigmoid))


def dot(left_side, right_side):
    return jnp.dot(left_side, right_side, preferred_element_type=f32)


def dot_nt(left_side, right_side):
    return lax.dot_general(
        left_side, right_side, (((1,), (1,)), ((), ())), preferred_element_type=f32
    )


def dot_tn(left_side, right_side):
    return lax.dot_general(
        left_side, right_side, (((0,), (0,)), ((), ())), preferred_element_type=f32
    )


def wide_einsum(formula, left_side, right_side):
    return jnp.einsum(formula, left_side, right_side, preferred_element_type=f32)


def stacked_heads(ref, part):
    return jnp.concatenate(
        [ref[part, :, g * HD : (g + 1) * HD] for g in range(GROUP)], axis=0
    )


def diagonal_mask(rows, chunk, block, zy):
    key_at = lax.broadcasted_iota(jnp.int32, (rows, chunk), 1)
    row_at = lax.broadcasted_iota(jnp.int32, (rows, chunk), 0)
    return key_at <= zy * block + lax.rem(row_at, block)


def attention_forward_kernel(chunk, has_prev, info_ref, q_ref, *refs):
    if has_prev:
        prev_ref, cur_ref, o_ref, log_ref = refs
    else:
        cur_ref, o_ref, log_ref = refs
    parts, block, _ = q_ref.shape
    zy = info_ref[0]
    mask = diagonal_mask(GROUP * block, chunk, block, zy)
    for part in range(parts):
        queries = stacked_heads(q_ref, part)
        pieces = []
        if has_prev:
            bias = jnp.where(info_ref[1] > 0, 0.0, masked_score).astype(f32)
            pieces.append((dot_nt(queries, prev_ref[:, :HD]) + bias, prev_ref, 0, prev_ref.shape[0]))
        if part > 0:
            pieces.append((dot_nt(queries, cur_ref[: part * chunk, :HD]), cur_ref, 0, part * chunk))
        last = dot_nt(queries, cur_ref[part * chunk : (part + 1) * chunk, :HD])
        pieces.append(
            (jnp.where(mask, last, masked_score), cur_ref, part * chunk, (part + 1) * chunk)
        )
        peak = functools.reduce(
            jnp.maximum, [jnp.max(s, axis=-1, keepdims=True) for s, _, _, _ in pieces]
        )
        peak = peak * log2_scale
        total = jnp.zeros((GROUP * block, 1), f32)
        mixed = jnp.zeros((GROUP * block, HD), f32)
        for s, ref, start, stop in pieces:
            probs = jnp.exp2(s * log2_scale - peak)
            total = total + jnp.sum(probs, axis=-1, keepdims=True)
            mixed = mixed + dot(probs.astype(bf), ref[start:stop, HD:])
        out = (mixed / total).astype(bf)
        for g in range(GROUP):
            o_ref[part, :, g * HD : (g + 1) * HD] = out[g * block : (g + 1) * block]
        log_ref[part] = jnp.broadcast_to(peak + jnp.log2(total), (GROUP * block, HD))


def attention_backward_kernel(chunk, has_prev, info_ref, q_ref, do_ref, o_ref, log_ref, *refs):
    if has_prev:
        prev_ref, cur_ref, dq_ref, dcur_ref, dprev_ref = refs
        dprev_ref[...] = jnp.zeros(dprev_ref.shape, f32)
    else:
        cur_ref, dq_ref, dcur_ref = refs
    dcur_ref[...] = jnp.zeros(dcur_ref.shape, f32)
    parts, block, _ = q_ref.shape
    zy = info_ref[0]
    mask = diagonal_mask(GROUP * block, chunk, block, zy)
    for part in range(parts):
        queries = stacked_heads(q_ref, part)
        out_grad = stacked_heads(do_ref, part)
        out = stacked_heads(o_ref, part)
        inner = jnp.sum(out_grad.astype(f32) * out.astype(f32), axis=-1, keepdims=True)
        log_total = log_ref[part][:, :1]
        query_grad = jnp.zeros((GROUP * block, HD), f32)
        pieces = []
        if has_prev:
            log_prev = log_total + jnp.where(info_ref[1] > 0, 0.0, -masked_score).astype(f32)
            for start in range(0, prev_ref.shape[0], chunk):
                pieces.append((prev_ref, dprev_ref, start, log_prev, False))
        for start in range(0, (part + 1) * chunk, chunk):
            pieces.append((cur_ref, dcur_ref, start, log_total, start == part * chunk))
        for ref, grad_ref, start, log_row, on_diagonal in pieces:
            keys = ref[start : start + chunk, :HD]
            scores = dot_nt(queries, keys)
            probs = jnp.exp2(scores * log2_scale - log_row)
            if on_diagonal:
                probs = jnp.where(mask, probs, 0.0)
            probs_grad = dot_nt(out_grad, ref[start : start + chunk, HD:])
            score_grad = (probs * (probs_grad - inner)).astype(bf)
            query_grad = query_grad + dot(score_grad, keys)
            grad_ref[start : start + chunk, :HD] += dot_tn(score_grad, queries) * scaling
            grad_ref[start : start + chunk, HD:] += dot_tn(probs.astype(bf), out_grad)
        out_rows = (query_grad * scaling).astype(bf)
        for g in range(GROUP):
            dq_ref[part, :, g * HD : (g + 1) * HD] = out_rows[g * block : (g + 1) * block]


def vmem_specs(count):
    return [pl.BlockSpec(memory_space=pltpu.VMEM)] * count


def kernel_params():
    return pltpu.CompilerParams(vmem_limit_bytes=50 * 1024 * 1024)


def attention_forward(info, queries, prev, cur):
    parts, block, _ = queries.shape
    chunk = cur.shape[0] // parts
    kvs = (cur,) if prev is None else (prev, cur)
    keys = sum(kv.shape[0] for kv in kvs)
    rows = parts * GROUP * block
    return pl.pallas_call(
        functools.partial(attention_forward_kernel, chunk, prev is not None),
        out_shape=(
            jax.ShapeDtypeStruct(queries.shape, bf),
            jax.ShapeDtypeStruct((parts, GROUP * block, HD), f32),
        ),
        in_specs=[pl.BlockSpec(memory_space=pltpu.SMEM)] + vmem_specs(1 + len(kvs)),
        out_specs=tuple(vmem_specs(2)),
        compiler_params=kernel_params(),
        cost_estimate=pl.CostEstimate(
            flops=4 * rows * keys * HD,
            bytes_accessed=keys * 512 + rows * 1024,
            transcendentals=rows * keys,
        ),
    )(info, queries, *kvs)


def attention_backward(info, queries, out_grad, out, logs, prev, cur):
    parts, block, _ = queries.shape
    chunk = cur.shape[0] // parts
    kvs = (cur,) if prev is None else (prev, cur)
    keys = sum(kv.shape[0] for kv in kvs)
    rows = parts * GROUP * block
    return pl.pallas_call(
        functools.partial(attention_backward_kernel, chunk, prev is not None),
        out_shape=(jax.ShapeDtypeStruct(queries.shape, bf),)
        + tuple(jax.ShapeDtypeStruct(kv.shape, f32) for kv in reversed(kvs)),
        in_specs=[pl.BlockSpec(memory_space=pltpu.SMEM)] + vmem_specs(4 + len(kvs)),
        out_specs=tuple(vmem_specs(1 + len(kvs))),
        compiler_params=kernel_params(),
        cost_estimate=pl.CostEstimate(
            flops=10 * rows * keys * HD,
            bytes_accessed=keys * 1536 + rows * 1536,
            transcendentals=rows * keys,
        ),
    )(info, queries, out_grad, out, logs, *kvs)


def body(
    inputs,
    cotangent,
    routes,
    norm_attn,
    w_query,
    w_key,
    w_value,
    w_output,
    norm_ffn,
    w_router,
    shared_gate,
    shared_up,
    shared_down,
    expert_gate,
    expert_up,
    expert_down,
):
    micro_count, block, width = inputs.shape[1:]
    shards = lax.axis_size("shard")
    section = lax.axis_index("section")
    core = lax.axis_index("dp")
    position = lax.axis_index("shard")
    ring = shards // KVH
    local_experts = expert_gate.shape[1]
    experts = local_experts * shards
    slots = experts * CAP
    rows_per = w_query.shape[1]
    head_width = H * HD
    key_width = KVH * HD
    qkv_width = head_width + 2 * key_width
    shared_width = shared_gate.shape[2]
    down_rows = shared_down.shape[1]
    is_first = section == 0
    low_core = core == 0
    rings = [[x * ring + zy for x in range(KVH)] for zy in range(ring)]

    def exchange(value):
        return lax.all_to_all(value, "shard", split_axis=0, concat_axis=0, tiled=True)

    def exchange_x(value):
        return lax.all_to_all(
            value, "shard", split_axis=0, concat_axis=0, tiled=True, axis_index_groups=rings
        )

    def twin(value):
        return lax.ppermute(value, "dp", [(0, 1), (1, 0)])

    def mine_of(low_half, high_half):
        return jnp.where(low_core, low_half, high_half)

    def halves(value):
        half = value.shape[-1] // 2
        return value[..., :half], value[..., half:]

    down_flat = (rows_per, down_rows * width // 2 // rows_per)
    tail = jnp.concatenate(
        [
            w_router[0],
            norm_attn[0][:, None],
            norm_ffn[0][:, None],
            jnp.zeros((rows_per, 128 - experts - 2), bf),
        ],
        axis=1,
    )
    qkv_rows = jnp.concatenate([w_query[0], w_key[0], w_value[0]], axis=1)
    packed = jnp.concatenate(
        [
            mine_of(*halves(qkv_rows)),
            mine_of(*halves(w_output[0])),
            mine_of(shared_gate[0], shared_up[0]),
            mine_of(*halves(shared_down[0])).reshape(down_flat),
        ],
        axis=1,
    )
    sizes = [qkv_width // 2, width // 2, shared_width, down_flat[1]]
    gathered = lax.all_gather(
        jnp.concatenate([packed, tail], axis=1), "shard", axis=0, tiled=True
    )
    own_half, tail = gathered[:, : sum(sizes)], gathered[:, sum(sizes) :]
    other_half = twin(own_half)

    def cut(value):
        starts = [sum(sizes[:i]) for i in range(len(sizes))]
        qkv, out, gate_up, down = [
            value[:, start : start + size] for start, size in zip(starts, sizes)
        ]
        return qkv, out, gate_up, down.reshape(down_rows * shards, width // 2)

    qkv_w, output_w, gate_up_w, down_w = zip(cut(own_half), cut(other_half))
    router_w = tail[:, :experts]
    gains = tail[:, experts : experts + 2].T.astype(f32)
    gain_one, gain_two = gains[0][None], gains[1][None]

    def project(rows, pair):
        own, other = dot(rows, pair[0]), dot(rows, pair[1])
        return jnp.concatenate(
            [jnp.where(low_core, own, other), jnp.where(low_core, other, own)], axis=1
        )

    def project_back(low_half, high_half, pair):
        own = jnp.where(low_core, low_half, high_half)
        other = jnp.where(low_core, high_half, low_half)
        return dot_nt(own, pair[0]) + dot_nt(other, pair[1])

    expert_g, expert_u, expert_d = expert_gate[0], expert_up[0], expert_down[0]
    local_routes = routes[0, 0]
    slot_of = jnp.arange(slots, dtype=jnp.int32)
    spread = (jnp.arange(experts, dtype=jnp.int32)[:, None] == slot_of[None, :] // CAP).astype(bf)
    router_slots = dot(router_w, spread).astype(bf)
    row_index = jnp.arange(block, dtype=jnp.int32)
    earlier = (row_index[:, None] > row_index[None, :]).astype(bf)

    def slot_table(route_rows):
        named = jnp.any(
            route_rows[:, :, None] == jnp.arange(experts, dtype=jnp.int32)[None, None, :], axis=1
        ).astype(bf)
        slot_ids = dot(earlier, named).astype(bf)
        return (dot(named, spread) > 0.5) & (
            dot(slot_ids, spread).astype(jnp.int32) == (slot_of % CAP)[None, :]
        )

    tables = [slot_table(local_routes[m]) for m in range(micro_count)]
    info = jnp.stack([position % ring, (section == 0).astype(jnp.int32)]).astype(jnp.int32)
    info_all = jnp.stack([position % ring, jnp.ones_like(position)]).astype(jnp.int32)

    def gate_values(normed_two, table):
        logits = jnp.where(table, dot(normed_two, router_slots), masked_score)
        weights = jnp.exp(logits - jnp.max(logits, axis=-1, keepdims=True))
        weights = jnp.where(table, weights, 0.0)
        return weights / jnp.sum(weights, axis=-1, keepdims=True)

    def high_low(value):
        high = value.astype(bf)
        return high, (value - high.astype(f32)).astype(bf)

    def to_experts(rows):
        return (
            exchange(rows.reshape(shards, local_experts, CAP, width))
            .transpose(1, 0, 2, 3)
            .reshape(local_experts, shards * CAP, width)
        )

    def from_experts(rows):
        return exchange(
            rows.reshape(local_experts, shards, CAP, width).transpose(1, 0, 2, 3)
        ).reshape(slots, width)

    def forward(moment, received, previous):
        first_micro = min(moment, micro_count - 1)
        second_micro = max(moment - 1, 0)
        layer_b = jnp.where(is_first, inputs[0, first_micro], received)
        table = jnp.where(is_first, tables[first_micro], tables[second_micro])
        layer_in = layer_b.astype(f32)
        normed_one = (layer_in * inverse_rms(layer_in) * gain_one).astype(bf)
        qkv = project(normed_one, qkv_w).astype(bf)
        queries = qkv[:, :head_width].reshape(block, KVH, GROUP * HD).transpose(1, 0, 2)
        pairs = jnp.concatenate(
            [
                qkv[:, head_width : head_width + key_width].reshape(block, KVH, HD),
                qkv[:, head_width + key_width :].reshape(block, KVH, HD),
            ],
            axis=2,
        ).transpose(1, 0, 2)
        pairs = jnp.broadcast_to(pairs[:, None], (KVH, ring, block, 2 * HD))
        cache = exchange(pairs.reshape(shards, block, 2 * HD)).reshape(shards * block, 2 * HD)
        queries = exchange_x(queries)
        attn_info = info if moment == 1 else info_all
        out_rows, logs = attention_forward(attn_info, queries, previous, cache)
        attended = exchange_x(out_rows).transpose(1, 0, 2).reshape(block, head_width)
        hidden = layer_in + project(attended, output_w)
        normed_two = (hidden * inverse_rms(hidden) * gain_two).astype(bf)
        gates = gate_values(normed_two, table)
        pick = table.astype(bf)
        expert_in = to_experts(dot_tn(pick, normed_two).astype(bf))
        gate_pre = wide_einsum("erd,edf->erf", expert_in, expert_g)
        up_pre = wide_einsum("erd,edf->erf", expert_in, expert_u)
        activated = (silu_parts(gate_pre)[0] * up_pre).astype(bf)
        returned = from_experts(wide_einsum("erf,efd->erd", activated, expert_d).astype(bf))
        high, low = high_low(gates)
        routed = dot(high, returned) + dot(low, returned)
        shared_pre = project(normed_two, gate_up_w)
        shared_gate_pre, shared_up_pre = halves(shared_pre)
        shared_act = (silu_parts(shared_gate_pre)[0] * shared_up_pre).astype(bf)
        output_b = (hidden + routed + project(shared_act, down_w)).astype(bf)
        kept = dict(
            layer_b=layer_b,
            pick=pick,
            table=table,
            normed_one=normed_one,
            queries=queries,
            cache=cache,
            previous=previous,
            info=attn_info,
            out_rows=out_rows,
            logs=logs,
            attended=attended,
            hidden=hidden,
            normed_two=normed_two,
            gates=gates,
            expert_in=expert_in,
            gate_pre=gate_pre,
            up_pre=up_pre,
            activated=activated,
            returned=returned,
            shared_gate_pre=shared_gate_pre,
            shared_up_pre=shared_up_pre,
            shared_act=shared_act,
            output_b=output_b,
        )
        return output_b, kept

    saved = []
    received = jnp.zeros((block, width), bf)
    previous = None
    for moment in range(micro_count + 1):
        output_b, kept = forward(moment, received, previous)
        saved.append(kept)
        previous = kept["cache"]
        if moment < micro_count:
            received = lax.ppermute(output_b, "section", [(0, 1)])

    def ffn_backward(kept, upstream_b):
        upstream = upstream_b.astype(f32)
        gates, hidden = kept["gates"], kept["hidden"]
        high, low = high_low(gates)
        outgoing = dot_tn(high, upstream_b) + dot_tn(low, upstream_b)
        expert_grad = to_experts(outgoing.astype(bf))
        act_silu, act_slope = silu_parts(kept["gate_pre"])
        act_grad = wide_einsum("erd,efd->erf", expert_grad, expert_d)
        gate_pre_grad = (act_grad * kept["up_pre"] * act_slope).astype(bf)
        up_pre_grad = (act_grad * act_silu).astype(bf)
        expert_in_grad = (
            wide_einsum("erf,edf->erd", gate_pre_grad, expert_g)
            + wide_einsum("erf,edf->erd", up_pre_grad, expert_u)
        ).astype(bf)
        returned_grad = from_experts(expert_in_grad)
        shared_act_grad = project_back(*halves(upstream_b), down_w)
        shared_silu, shared_slope = silu_parts(kept["shared_gate_pre"])
        shared_gate_grad = (shared_act_grad * kept["shared_up_pre"] * shared_slope).astype(bf)
        shared_up_grad = (shared_act_grad * shared_silu).astype(bf)
        normed_two_grad = project_back(shared_gate_grad, shared_up_grad, gate_up_w)
        gate_grad = dot_nt(upstream_b, kept["returned"])
        picked_grad = gates * (gate_grad - jnp.sum(gates * gate_grad, axis=1, keepdims=True))
        picked_b = picked_grad.astype(bf)
        normed_two_grad = normed_two_grad + dot_nt(picked_b, router_slots)
        normed_two_grad = normed_two_grad + dot(kept["pick"], returned_grad)
        logit_grad = dot_nt(picked_b, spread).astype(bf)
        hidden_norm_grad, gain_two_grad = norm_back(hidden, gain_two, normed_two_grad)
        hidden_grad = upstream + hidden_norm_grad
        return dict(
            hidden_grad=hidden_grad,
            hidden_grad_b=hidden_grad.astype(bf),
            upstream_b=upstream_b,
            expert_grad=expert_grad,
            gate_pre_grad=gate_pre_grad,
            up_pre_grad=up_pre_grad,
            shared_gate_grad=shared_gate_grad,
            shared_up_grad=shared_up_grad,
            logit_grad=logit_grad,
            gain_two_grad=gain_two_grad,
        )

    def attention_back(kept, grads, carried):
        attended_grad = output_back(grads["hidden_grad_b"]).astype(bf)
        out_grad = exchange_x(
            attended_grad.reshape(block, KVH, GROUP * HD).transpose(1, 0, 2)
        )
        results = attention_backward(
            kept["info"],
            kept["queries"],
            out_grad,
            kept["out_rows"],
            kept["logs"],
            kept["previous"],
            kept["cache"],
        )
        cache_grad = results[1] if carried is None else results[1] + carried
        carried = results[2] if len(results) > 2 else None
        query_grad = exchange_x(results[0]).transpose(1, 0, 2).reshape(block, head_width)
        parts = exchange(cache_grad.astype(bf).reshape(shards, block, 2 * HD))
        own = jnp.sum(parts.reshape(KVH, ring, block, 2 * HD).astype(f32), axis=1).astype(bf)
        own = own.transpose(1, 0, 2)
        qkv_grad = jnp.concatenate(
            [
                query_grad,
                own[:, :, :HD].reshape(block, key_width),
                own[:, :, HD:].reshape(block, key_width),
            ],
            axis=1,
        )
        normed_one_grad = project_back(*halves(qkv_grad), qkv_w)
        in_norm_grad, gain_one_grad = norm_back(
            kept["layer_b"].astype(f32), gain_one, normed_one_grad
        )
        layer_grad = (grads["hidden_grad"] + in_norm_grad).astype(bf)
        grads = dict(grads, qkv_grad=qkv_grad, gain_one_grad=gain_one_grad, layer_grad=layer_grad)
        return grads, carried

    def output_back(rows):
        return project_back(*halves(rows), output_w)

    backs = [None] * (micro_count + 1)
    received = jnp.zeros((block, width), bf)
    carried = None
    for moment in range(micro_count + 1):
        source = micro_count - moment
        raw_second = source - 1
        if raw_second >= 0:
            second = cotangent[0, raw_second]
        else:
            second = jnp.zeros((block, width), bf)
        first = received if moment > 0 else jnp.zeros((block, width), bf)
        upstream_b = jnp.where(is_first, first, second)
        grads = ffn_backward(saved[source], upstream_b)
        grads, carried = attention_back(saved[source], grads, carried)
        backs[source] = grads
        if moment < micro_count:
            received = lax.ppermute(grads["layer_grad"], "section", [(1, 0)])

    def live(name, store, axis):
        ends = jnp.where(is_first, store[0][name], store[micro_count][name])
        return jnp.concatenate([ends, store[1][name]], axis=axis)

    def kept_rows(name, axis=0):
        return live(name, saved, axis)

    def back_rows(name, axis=0):
        return live(name, backs, axis)

    expert_parts = [
        wide_einsum("erd,erf->edf", kept_rows("expert_in", 1), back_rows("gate_pre_grad", 1)),
        wide_einsum("erd,erf->edf", kept_rows("expert_in", 1), back_rows("up_pre_grad", 1)),
        wide_einsum("erf,erd->efd", kept_rows("activated", 1), back_rows("expert_grad", 1)),
    ]
    expert_parts = [part.astype(bf) for part in expert_parts]
    expert_grads = [part.astype(f32) + twin(part).astype(f32) for part in expert_parts]

    def both(value):
        return jnp.concatenate([value, twin(value)], axis=0)

    def both_halves(low_half, high_half):
        own = jnp.where(low_core, low_half, high_half)
        other = jnp.where(low_core, high_half, low_half)
        return jnp.concatenate([own, twin(other)], axis=0)

    normed_one, normed_two = kept_rows("normed_one"), kept_rows("normed_two")
    grad_gate_up = dot_tn(
        both(normed_two), both_halves(back_rows("shared_gate_grad"), back_rows("shared_up_grad"))
    )
    grad_out = dot_tn(
        both(kept_rows("attended")), both_halves(*halves(back_rows("hidden_grad_b")))
    )
    grad_down = dot_tn(
        both(kept_rows("shared_act")), both_halves(*halves(back_rows("upstream_b")))
    )
    grad_qkv = dot_tn(both(normed_one), both_halves(*halves(back_rows("qkv_grad"))))
    grad_router = dot_tn(normed_two, back_rows("logit_grad"))
    gain_sums = jnp.stack(
        [
            sum(grads["gain_one_grad"] for grads in backs),
            sum(grads["gain_two_grad"] for grads in backs),
        ]
    )
    grad_tail = jnp.concatenate(
        [grad_router, gain_sums.T, jnp.zeros((width, 128 - experts - 2), f32)], axis=1
    )

    def scattered(value):
        pieces = value.astype(bf).reshape(shards, value.shape[0] // shards, value.shape[1])
        return jnp.sum(exchange(pieces).astype(f32), axis=0)

    share_rows = scattered(jnp.concatenate([grad_gate_up, grad_out], axis=1))
    share_down = scattered(grad_down)
    share_last = scattered(jnp.concatenate([grad_qkv, grad_tail], axis=1))

    def joined(own):
        other = twin(own)
        return jnp.where(low_core, own, other), jnp.where(low_core, other, own)

    low_rows, high_rows = joined(share_rows)
    low_down, high_down = joined(share_down)
    low_last, high_last = joined(share_last)
    half_qkv = qkv_width // 2
    qkv_out = jnp.concatenate([low_last[:, :half_qkv], high_last[:, :half_qkv]], axis=1)
    tail_out = low_last[:, half_qkv:] + high_last[:, half_qkv:]
    output_out = jnp.concatenate([low_rows[:, shared_width:], high_rows[:, shared_width:]], axis=1)
    down_out = jnp.concatenate([low_down, high_down], axis=1)

    out_store = jnp.stack(
        [
            jnp.where(is_first, saved[m]["output_b"], saved[m + 1]["output_b"])
            for m in range(micro_count)
        ]
    )
    grad_store = jnp.stack(
        [
            jnp.where(is_first, backs[m]["layer_grad"], backs[m + 1]["layer_grad"])
            for m in range(micro_count)
        ]
    )
    return (
        out_store[None, None],
        grad_store[None, None],
        tail_out[:, experts][None],
        qkv_out[:, :head_width][None],
        qkv_out[:, head_width : head_width + key_width][None],
        qkv_out[:, head_width + key_width :][None],
        output_out[None],
        tail_out[:, experts + 1][None],
        tail_out[:, :experts][None],
        low_rows[:, :shared_width][None],
        high_rows[:, :shared_width][None],
        down_out[None],
        expert_grads[0][None],
        expert_grads[1][None],
        expert_grads[2][None],
    )


def solution(mesh):
    rows = P("section", "shard", None)
    vector = P("section", "shard")
    expert = P("section", "shard", None, None)
    tokens = P("dp", None, "shard", None)
    section_tokens = P("section", "dp", None, "shard", None)
    weights = (vector, rows, rows, rows, rows, vector, rows, rows, rows, rows) + (expert,) * 3
    return jax.shard_map(
        body,
        mesh=mesh,
        in_specs=(tokens, tokens, section_tokens) + weights,
        out_specs=(section_tokens, section_tokens) + weights,
        check_vma=False,
    )
```

time: 4740 us -> 1180 us (0.25)
  waiting for transfers between devices: 3430 us -> 387 us
  blocking collectives: 295 us -> 63.9 us
  other arithmetic: 264 us -> 85.5 us
  local copies, waits for them, and re-layouts: 269 us -> 105 us
  matrix products: 381 us -> 249 us
  starting transfers between devices: 72.5 us -> 202 us
  Pallas kernels: 0 us -> 53.2 us
    reduce_scatter x14 -> x0, waiting for transfers between devices: 2640 us -> none  [the longest x3 533 us: body(): lax.psum_scatter(value_rows.astype(jnp.bfloat16), 'shard', scatter_dimens...]
    all_gather x13 -> x1, waiting for transfers between devices: 607 us -> 125 us  [body(): lax.all_gather(jnp.concatenate([packed, tail], axis=1), 'shard', axis=0,...]
    unnamed x2 -> x0, blocking collectives: 162 us -> none
    dot_general x113 -> x109, matrix products: 381 us -> 249 us  [the longest x41 89.7 us: dot(): return jnp.dot(left_side, right_side, preferred_element_type=f32)]
    all_to_all x10 -> x29, waiting for transfers between devices: 103 us -> 223 us  [the longest x19 203 us: exchange(): lax.all_to_all(value, 'shard', split_axis=0, concat_axis=0, tiled=True)]
    all_to_all x10 -> x29, starting transfers between devices: 60.8 us -> 156 us  [the longest x19 117 us: exchange(): lax.all_to_all(value, 'shard', split_axis=0, concat_axis=0, tiled=True)]
    all_gather x1 -> x0, blocking collectives: 92.8 us -> none  [body(): lax.all_gather(w_router[0], 'shard', axis=0, tiled=True)]
    convert_element_type x28 -> x0, local copies, waits for them, and re-layouts: 61.7 us -> none  [the longest x8 11.6 us: body(): attended = attended.reshape(block_rows, head_width).astype(jnp.bfloat16)]
  transfers between devices with their start and end apart: 43 -> 49, of which waited for: 40 -> 34; matrix products, arithmetic and copies ran while one was open for 11% -> 27% of each run, Pallas kernels for 0% -> 2%
where the time goes in v1:
time: 1180 us; the launch traced here: 1160 us
  waiting for transfers between devices  387 us (33%)
  matrix products  249 us (21%)
  starting transfers between devices  202 us (17%)
  local copies, waits for them, and re-layouts  105 us (9%)
  other arithmetic  85.5 us (7%)
  blocking collectives  63.9 us (5%)
  Pallas kernels  53.2 us (5%)
  between operations  17.9 us (2%)
    all_to_all x19, waiting for transfers between devices, exchange(): lax.all_to_all(value, 'shard', split_axis=0, concat_axis=0, tiled=True)  203 us
    all_gather x1, waiting for transfers between devices, body(): lax.all_gather(jnp.concatenate([packed, tail], axis=1), 'shard', axis=0,...  125 us
    all_to_all x19, starting transfers between devices, exchange(): lax.all_to_all(value, 'shard', split_axis=0, concat_axis=0, tiled=True)  117 us
    dot_general x41, matrix products, dot(): return jnp.dot(left_side, right_side, preferred_element_type=f32)  89.7 us
    dot_general x33, matrix products, dot_nt(): lax.dot_general(left_side, right_side, (((1,), (1,)), ((), ())), preferre...  85.1 us
    dot_general x21, matrix products, wide_einsum(): jnp.einsum(formula, left_side, right_side, preferred_element_type=f32)  49.9 us
    all_to_all x2, blocking collectives, exchange(): lax.all_to_all(value, 'shard', split_axis=0, concat_axis=0, tiled=True)  48.4 us
    all_to_all x10, starting transfers between devices, exchange_x(): lax.all_to_all(value, 'shard', split_axis=0, concat_axis=0, tiled=True, a...  39.4 us
  transfers between devices with their start and end apart: 49, of which 34 were waited for; matrix products, arithmetic and copies ran while one was open for 27% of the time, Pallas kernels for 2%

profile of v1, /device:TPU:1, one launch (start us, length us, event | category | flops | bytes accessed | tf_op | source)
XLA Modules:
  0.0 1164.0 jit_solution(17384155013615601739)
XLA Ops:
  14.2 124.8 %all-gather.2.cloned.1.call-done = bf16[1536,3712]{1,0:T(8,128)(2,1)} async-done(((bf16[48,3712]{1,0:T(8,128)(2,1)}), bf16[1536,3712]{1,0:T(8,128)(2,1)}) %all-gather.2.cloned.1.call-update) | async-done | bytes 11403280 | tf_op jit(solution)/shard_map/all_gather | solution.py:279
  139.1 9.6 slice.338
  155.8 10.8 collective-permute-done
  186.5 15.6 %all-to-all-done.1 = bf16[32,64,256]{2,1,0:T(8,128)(2,1)} async-done(((bf16[32,64,256]{2,1,0:T(8,128)(2,1)}), bf16[32,64,256]{2,1,0:T(8,128)(2,1)}, u32[]{:S(2)}, u32[]{:S(2)}) %all-to-all-start.1) | async-done | bytes 1048608 | tf_op jit(solution)/shard_map/all_to_all | solution.py:241
  276.8 11.5 all-to-all-done.4
  320.2 9.9 all-to-all-start.6
  333.2 13.7 %all-to-all-done.6 = bf16[32,64,256]{2,1,0:T(8,128)(2,1)} async-done(((bf16[32,64,256]{2,1,0:T(8,128)(2,1)}), bf16[32,64,256]{2,1,0:T(8,128)(2,1)}, u32[]{:S(2)}, u32[]{:S(2)}) %all-to-all-start.6) | async-done | bytes 1048608 | tf_op jit(solution)/shard_map/all_to_all | solution.py:241
  370.6 23.8 %all_to_all.165 = bf16[32,2,8,1536]{3,2,1,0:T(8,128)(2,1)S(1)} all-to-all(bf16[32,2,8,1536]{3,2,1,0:T(8,128)(2,1)S(1)} %bitcast.501), channel_id=1, replica_groups=mesh['section'=2,'dp'=2,'shard'=32] {'shard'}, dimensions={0} | all-to-all | bytes 3145728 | tf_op jit(solution)/shard_map/all_to_all | solution.py:241
  418.5 9.3 all-to-all-done.9
  459.1 24.6 %all_to_all.166 = bf16[32,64,256]{2,1,0:T(8,128)(2,1)S(1)} all-to-all(bf16[32,64,256]{2,1,0:T(8,128)(2,1)S(1)} %bitcast.510), channel_id=1, replica_groups=mesh['section'=2,'dp'=2,'shard'=32] {'shard'}, dimensions={0} | all-to-all | bytes 2097152 | tf_op jit(solution)/shard_map/all_to_all | solution.py:241
  517.5 13.9 %all-to-all-done.13 = bf16[32,2,8,1536]{3,2,1,0:T(8,128)(2,1)} async-done(((bf16[32,2,8,1536]{3,2,1,0:T(8,128)(2,1)}), bf16[32,2,8,1536]{3,2,1,0:T(8,128)(2,1)}, u32[]{:S(2)}, u32[]{:S(2)}) %all-to-all-start.13) | async-done | bytes 1572896 | tf_op jit(solution)/shard_map/all_to_all | solution.py:241
  549.5 9.3 all-to-all-done.15
  575.9 10.4 all-to-all-done.14
  605.2 8.9 all-to-all-done.16
  631.7 14.8 %shard_map.274 = (bf16[4,64,384]{2,1,0:T(8,128)(2,1)S(1)}, f32[2048,256]{1,0:T(8,128)}, f32[2048,256]{1,0:T(8,128)}) custom-call(s32[2]{0:T(128)S(1)} %pad_add_fusion.info_ref, bf16[4,64,384]{2,1,0:T(8,128)(2,1)} %all-to-all-done.10.q_ref, bf16[4,64,384]{2,1,0:T(8,128)(2,1)S(1)} %all_to_all.168.do_ref, bf16[4,64,384]{2,1,0:T(8,128)(2,1)S(1)} %copy-done.6, ...), custom_call_target="tpu_custom_call" | custom-call | flops 4026531840 | bytes 7471104 | tf_op jit(solution)/shard_map/pallas_call | solution.py:188
  664.5 12.1 %all-to-all-done.19 = bf16[32,64,256]{2,1,0:T(8,128)(2,1)} async-done(((bf16[32,64,256]{2,1,0:T(8,128)(2,1)}), bf16[32,64,256]{2,1,0:T(8,128)(2,1)}, u32[]{:S(2)}, u32[]{:S(2)}) %all-to-all-start.19) | async-done | bytes 1048608 | tf_op jit(solution)/shard_map/all_to_all | solution.py:241
  688.9 15.9 %collective-permute-done.3 = bf16[64,1536]{1,0:T(8,128)(2,1)S(1)} collective-permute-done((bf16[64,1536]{1,0:T(8,128)(2,1)S(1)}, bf16[64,1536]{1,0:T(8,128)(2,1)S(1)}, u32[]{:S(2)}, u32[]{:S(2)}) %collective-permute-start.3) | collective-permute-done | bytes 196640 | tf_op jit(solution)/shard_map/ppermute | solution.py:521
  724.0 11.3 all-to-all-done.20
  763.0 9.1 all-to-all-done.21
  793.4 15.1 %shard_map.275 = (bf16[4,64,384]{2,1,0:T(8,128)(2,1)S(1)}, f32[2048,256]{1,0:T(8,128)}, f32[2048,256]{1,0:T(8,128)}) custom-call(s32[2]{0:T(128)S(1)} %pad_add_fusion.1.info_ref, bf16[4,64,384]{2,1,0:T(8,128)(2,1)S(1)} %all-to-all-done.5.q_ref, bf16[4,64,384]{2,1,0:T(8,128)(2,1)} %all-to-all-done.22.do_ref, bf16[4,64,384]{2,1,0:T(8,128)(2,1)S(1)} %copy-done.4, ...), custom_call_target="tpu_custom_call" | custom-call | flops 4026531840 | bytes 7471104 | tf_op jit(solution)/shard_map/pallas_call | solution.py:188
  916.1 8.2 all-to-all-done.26
  1050.1 30.2 %all-to-all-done.31 = bf16[32,48,1792]{2,1,0:T(8,128)(2,1)} async-done(((bf16[32,48,1792]{2,1,0:T(8,128)(2,1)}), bf16[32,48,1792]{2,1,0:T(8,128)(2,1)}, u32[]{:S(2)}, u32[]{:S(2)}) %all-to-all-start.31) | async-done | bytes 5505056 | tf_op jit(solution)/shard_map/all_to_all | solution.py:241
  1080.3 10.3 all-to-all-start.30
  1124.3 21.4 %all-to-all-done.30 = bf16[32,48,1408]{2,1,0:T(8,128)(2,1)} async-done(((bf16[32,48,1408]{2,1,0:T(8,128)(2,1)}), bf16[32,48,1408]{2,1,0:T(8,128)(2,1)}, u32[]{:S(2)}, u32[]{:S(2)}) %all-to-all-start.30) | async-done | bytes 4325408 | tf_op jit(solution)/shard_map/all_to_all | solution.py:241
  (831 shorter events, 701.6 us)
Async XLA Ops:
  7.2 131.9 %all-gather.2.cloned.1.call-start = ((), (), s32[]{:S(2)}) async-start(), calls=%async_computation.33 | async-start | bytes 11759616 | tf_op jit(solution)/shard_map/all_gather | solution.py:279
  225.1 26.9 %all-to-all-start.3 = ((bf16[32,2,8,1536]{3,2,1,0:T(8,128)(2,1)}), bf16[32,2,8,1536]{3,2,1,0:T(8,128)(2,1)}, u32[]{:S(2)}, u32[]{:S(2)}) async-start(bf16[32,2,8,1536]{3,2,1,0:T(8,128)(2,1)} %bitcast.500), calls=%async_computation.3 | async-start | bytes 3145728 | tf_op jit(solution)/shard_map/all_to_all | solution.py:241
  261.7 26.6 %all-to-all-start.4 = ((bf16[32,2,8,1536]{3,2,1,0:T(8,128)(2,1)}), bf16[32,2,8,1536]{3,2,1,0:T(8,128)(2,1)}, u32[]{:S(2)}, u32[]{:S(2)}) async-start(bf16[32,2,8,1536]{3,2,1,0:T(8,128)(2,1)} %bitcast.497), calls=%async_computation.4 | async-start | bytes 3145728 | tf_op jit(solution)/shard_map/all_to_all | solution.py:241
  320.2 26.7 %all-to-all-start.6 = ((bf16[32,64,256]{2,1,0:T(8,128)(2,1)}), bf16[32,64,256]{2,1,0:T(8,128)(2,1)}, u32[]{:S(2)}, u32[]{:S(2)}) async-start(bf16[32,64,256]{2,1,0:T(8,128)(2,1)} %bitcast.509), calls=%async_computation.6 | async-start | bytes 2097152 | tf_op jit(solution)/shard_map/all_to_all | solution.py:241
  401.2 26.6 %all-to-all-start.9 = ((bf16[32,2,8,1536]{3,2,1,0:T(8,128)(2,1)}), bf16[32,2,8,1536]{3,2,1,0:T(8,128)(2,1)}, u32[]{:S(2)}, u32[]{:S(2)}) async-start(bf16[32,2,8,1536]{3,2,1,0:T(8,128)(2,1)} %bitcast.498), calls=%async_computation.9 | async-start | bytes 3145728 | tf_op jit(solution)/shard_map/all_to_all | solution.py:241
  504.9 26.5 %all-to-all-start.13 = ((bf16[32,2,8,1536]{3,2,1,0:T(8,128)(2,1)}), bf16[32,2,8,1536]{3,2,1,0:T(8,128)(2,1)}, u32[]{:S(2)}, u32[]{:S(2)}) async-start(bf16[32,2,8,1536]{3,2,1,0:T(8,128)(2,1)} %bitcast.499), calls=%async_computation.13 | async-start | bytes 3145728 | tf_op jit(solution)/shard_map/all_to_all | solution.py:241
  531.4 27.5 %all-to-all-start.15 = ((bf16[32,2,8,1536]{3,2,1,0:T(8,128)(2,1)}), bf16[32,2,8,1536]{3,2,1,0:T(8,128)(2,1)}, u32[]{:S(2)}, u32[]{:S(2)}) async-start(bf16[32,2,8,1536]{3,2,1,0:T(8,128)(2,1)} %bitcast.503), calls=%async_computation.15 | async-start | bytes 3145728 | tf_op jit(solution)/shard_map/all_to_all | solution.py:241
  558.9 27.4 %all-to-all-start.14 = ((bf16[32,2,8,1536]{3,2,1,0:T(8,128)(2,1)}), bf16[32,2,8,1536]{3,2,1,0:T(8,128)(2,1)}, u32[]{:S(2)}, u32[]{:S(2)}) async-start(bf16[32,2,8,1536]{3,2,1,0:T(8,128)(2,1)} %bitcast.495), calls=%async_computation.14 | async-start | bytes 3145728 | tf_op jit(solution)/shard_map/all_to_all | solution.py:241
  586.3 27.8 %all-to-all-start.16 = ((bf16[32,2,8,1536]{3,2,1,0:T(8,128)(2,1)}), bf16[32,2,8,1536]{3,2,1,0:T(8,128)(2,1)}, u32[]{:S(2)}, u32[]{:S(2)}) async-start(bf16[32,2,8,1536]{3,2,1,0:T(8,128)(2,1)} %bitcast.494), calls=%async_computation.16 | async-start | bytes 3145728 | tf_op jit(solution)/shard_map/all_to_all | solution.py:241
  707.3 28.0 %all-to-all-start.20 = ((bf16[32,2,8,1536]{3,2,1,0:T(8,128)(2,1)}), bf16[32,2,8,1536]{3,2,1,0:T(8,128)(2,1)}, u32[]{:S(2)}, u32[]{:S(2)}) async-start(bf16[32,2,8,1536]{3,2,1,0:T(8,128)(2,1)} %bitcast.504), calls=%async_computation.20 | async-start | bytes 3145728 | tf_op jit(solution)/shard_map/all_to_all | solution.py:241
  718.0 219.0 %collective-permute-start.13 = (bf16[128,1024]{1,0:T(8,128)(2,1)}, bf16[128,1024]{1,0:T(8,128)(2,1)}, u32[]{:S(2)}, u32[]{:S(2)}) collective-permute-start(bf16[128,1024]{1,0:T(8,128)(2,1)} %pad_maximum_fusion.11), channel_id=1, source_target_pairs={{0,32},{32,0},{1,33},{33,1},{2,34},{34,2},{3,35},{35,3},{4,36},{36... | collective-permute-start | bytes 786440 | tf_op jit(solution)/shard_map/ppermute | solution.py:249
  743.4 28.7 %all-to-all-start.21 = ((bf16[32,2,8,1536]{3,2,1,0:T(8,128)(2,1)}), bf16[32,2,8,1536]{3,2,1,0:T(8,128)(2,1)}, u32[]{:S(2)}, u32[]{:S(2)}) async-start(bf16[32,2,8,1536]{3,2,1,0:T(8,128)(2,1)} %bitcast.496), calls=%async_computation.21 | async-start | bytes 3145728 | tf_op jit(solution)/shard_map/all_to_all | solution.py:241
  788.0 199.7 %collective-permute-start.8 = (bf16[128,1536]{1,0:T(8,128)(2,1)}, bf16[128,1536]{1,0:T(8,128)(2,1)}, u32[]{:S(2)}, u32[]{:S(2)}) collective-permute-start(bf16[128,1536]{1,0:T(8,128)(2,1)} %pad_maximum_fusion.5), channel_id=1, source_target_pairs={{0,32},{32,0},{1,33},{33,1},{2,34},{34,2},{3,35},{35,3},{4,36},{36... | collective-permute-start | bytes 1179656 | tf_op jit(solution)/shard_map/ppermute | solution.py:249
  825.3 170.4 %collective-permute-start.10 = (bf16[128,1536]{1,0:T(8,128)(2,1)}, bf16[128,1536]{1,0:T(8,128)(2,1)}, u32[]{:S(2)}, u32[]{:S(2)}) collective-permute-start(bf16[128,1536]{1,0:T(8,128)(2,1)} %pad_maximum_fusion.6), channel_id=1, source_target_pairs={{0,32},{32,0},{1,33},{33,1},{2,34},{34,2},{3,35},{35,3},{4,36},{36... | collective-permute-start | bytes 1179656 | tf_op jit(solution)/shard_map/ppermute | solution.py:249
  859.5 27.7 %all-to-all-start.25 = ((bf16[32,2,8,1536]{3,2,1,0:T(8,128)(2,1)}), bf16[32,2,8,1536]{3,2,1,0:T(8,128)(2,1)}, u32[]{:S(2)}, u32[]{:S(2)}) async-start(bf16[32,2,8,1536]{3,2,1,0:T(8,128)(2,1)} %bitcast.502), calls=%async_computation.25 | async-start | bytes 3145728 | tf_op jit(solution)/shard_map/all_to_all | solution.py:241
  875.1 61.9 %collective-permute-start.14 = (bf16[128,768]{1,0:T(8,128)(2,1)}, bf16[128,768]{1,0:T(8,128)(2,1)}, u32[]{:S(2)}, u32[]{:S(2)}) collective-permute-start(bf16[128,768]{1,0:T(8,128)(2,1)} %get-tuple-element.112), channel_id=1, source_target_pairs={{0,32},{32,0},{1,33},{33,1},{2,34},{34,2},{3,35},{35,3},{4,36},{36... | collective-permute-start | bytes 589832 | tf_op jit(solution)/shard_map/ppermute | solution.py:249
  896.1 28.2 %all-to-all-start.26 = ((bf16[32,2,8,1536]{3,2,1,0:T(8,128)(2,1)}), bf16[32,2,8,1536]{3,2,1,0:T(8,128)(2,1)}, u32[]{:S(2)}, u32[]{:S(2)}) async-start(bf16[32,2,8,1536]{3,2,1,0:T(8,128)(2,1)} %bitcast.493), calls=%async_computation.26 | async-start | bytes 3145728 | tf_op jit(solution)/shard_map/all_to_all | solution.py:241
  942.1 28.2 %all-to-all-start.32 = ((bf16[32,32,768]{2,1,0:T(8,128)(2,1)}), bf16[32,32,768]{2,1,0:T(8,128)(2,1)}, u32[]{:S(2)}, u32[]{:S(2)}) async-start(bf16[32,32,768]{2,1,0:T(8,128)(2,1)} %bitcast.526), calls=%async_computation.32 | async-start | bytes 3145728 | tf_op jit(solution)/shard_map/all_to_all | solution.py:241
  956.7 31.0 %collective-permute-start.9 = (bf16[128,1024]{1,0:T(8,128)(2,1)}, bf16[128,1024]{1,0:T(8,128)(2,1)}, u32[]{:S(2)}, u32[]{:S(2)}) collective-permute-start(bf16[128,1024]{1,0:T(8,128)(2,1)} %get-tuple-element.108), channel_id=1, source_target_pairs={{0,32},{32,0},{1,33},{33,1},{2,34},{34,2},{3,35},{35,3},{4,36},{36... | collective-permute-start | bytes 786440 | tf_op jit(solution)/shard_map/ppermute | solution.py:249
  1004.4 75.9 %all-to-all-start.31 = ((bf16[32,48,1792]{2,1,0:T(8,128)(2,1)}), bf16[32,48,1792]{2,1,0:T(8,128)(2,1)}, u32[]{:S(2)}, u32[]{:S(2)}) async-start(bf16[32,48,1792]{2,1,0:T(8,128)(2,1)} %pad_maximum_fusion), calls=%async_computation.31 | async-start | bytes 11010048 | tf_op jit(solution)/shard_map/all_to_all | solution.py:241
  1015.7 87.3 %collective-permute-start.16 = (bf16[2,1536,512]{2,1,0:T(8,128)(2,1)}, bf16[2,1536,512]{2,1,0:T(8,128)(2,1)}, u32[]{:S(2)}, u32[]{:S(2)}) collective-permute-start(bf16[2,1536,512]{2,1,0:T(8,128)(2,1)} %convolution_convert_fusion.4), channel_id=1, source_target_pairs={{0,32},{32,0},{1,33},{33,1},{2,34},{34,2},{3,35},{35,3},{4,36},{36... | collective-permute-start | bytes 9437192 | tf_op jit(solution)/shard_map/ppermute | solution.py:249
  1018.3 91.3 %collective-permute-start.17 = (bf16[2,1536,512]{2,1,0:T(8,128)(2,1)}, bf16[2,1536,512]{2,1,0:T(8,128)(2,1)}, u32[]{:S(2)}, u32[]{:S(2)}) collective-permute-start(bf16[2,1536,512]{2,1,0:T(8,128)(2,1)} %convolution_convert_fusion.3), channel_id=1, source_target_pairs={{0,32},{32,0},{1,33},{33,1},{2,34},{34,2},{3,35},{35,3},{4,36},{36... | collective-permute-start | bytes 9437192 | tf_op jit(solution)/shard_map/ppermute | solution.py:249
  1080.3 65.5 %all-to-all-start.30 = ((bf16[32,48,1408]{2,1,0:T(8,128)(2,1)}), bf16[32,48,1408]{2,1,0:T(8,128)(2,1)}, u32[]{:S(2)}, u32[]{:S(2)}) async-start(bf16[32,48,1408]{2,1,0:T(8,128)(2,1)} %concatenate.183), calls=%async_computation.30 | async-start | bytes 8650752 | tf_op jit(solution)/shard_map/all_to_all | solution.py:241
  1120.3 30.3 %collective-permute-start.12 = (f32[48,1792]{1,0:T(8,128)}, f32[48,1792]{1,0:T(8,128)}, u32[]{:S(2)}, u32[]{:S(2)}) collective-permute-start(f32[48,1792]{1,0:T(8,128)} %convert_reduce_fusion), channel_id=1, source_target_pairs={{0,32},{32,0},{1,33},{33,1},{2,34},{34,2},{3,35},{35,3},{4,36},{36... | collective-permute-start | bytes 1032200 | tf_op jit(solution)/shard_map/ppermute | solution.py:249
  (260 other events, 2000.3 us)
Sparse Core Ops, SparseCore 0:
  14.4 124.6 all-gather.1

commit v2 on v1

v2 whole, which is shorter than its diff:
```python
import functools

import jax
import jax.numpy as jnp
from jax import lax
from jax.experimental import pallas as pl
from jax.experimental.pallas import tpu as pltpu
from jax.sharding import PartitionSpec as P

H = 12
KVH = 4
HD = 128
GROUP = H // KVH
TOPK = 6
CAP = 8

epsilon = 1e-05
masked_score = -1e30
scaling = HD ** (-0.5)
log2_scale = scaling * 1.4426950408889634
bf = jnp.bfloat16
f32 = jnp.float32
VMEM_LIMIT = 32 * 1024 * 1024
KEPT = ("ring_one", "attended", "normed_two", "shared_act", "expert_in", "activated")
BACK = (
    "qkv_grad",
    "ring_hidden",
    "gain_one_grad",
    "gain_two_grad",
    "logit_grad",
    "upstream_b",
    "shared_gate_grad",
    "shared_up_grad",
    "expert_grad",
    "gate_pre_grad",
    "up_pre_grad",
)


def inverse_rms(rows):
    return lax.rsqrt(jnp.mean(rows * rows, axis=-1, keepdims=True) + epsilon)


def norm_back(layer_in, gain, upstream):
    inverse = inverse_rms(layer_in)
    unit_rows = layer_in * inverse
    gain_grad = jnp.sum(upstream * unit_rows, axis=0)
    scaled = upstream * gain
    in_grad = inverse * (scaled - unit_rows * jnp.mean(scaled * unit_rows, axis=-1, keepdims=True))
    return (in_grad, gain_grad)


def silu_parts(argument):
    sigmoid = jax.nn.sigmoid(argument)
    return argument * sigmoid, sigmoid * (1.0 + argument * (1.0 - sigmoid))


def dot(left_side, right_side):
    return jnp.dot(left_side, right_side, preferred_element_type=f32)


def dot_nt(left_side, right_side):
    return lax.dot_general(
        left_side, right_side, (((1,), (1,)), ((), ())), preferred_element_type=f32
    )


def dot_tn(left_side, right_side):
    return lax.dot_general(
        left_side, right_side, (((0,), (0,)), ((), ())), preferred_element_type=f32
    )


def wide_einsum(formula, left_side, right_side):
    return jnp.einsum(formula, left_side, right_side, preferred_element_type=f32)


def stacked_heads(ref, part, micro):
    return jnp.concatenate(
        [ref[part, micro, :, g * HD : (g + 1) * HD] for g in range(GROUP)], axis=0
    )


def store_heads(ref, part, micro, rows):
    block = ref.shape[2]
    for g in range(GROUP):
        ref[part, micro, :, g * HD : (g + 1) * HD] = rows[g * block : (g + 1) * block]


def diagonal_mask(rows, chunk, block, zy):
    key_at = lax.broadcasted_iota(jnp.int32, (rows, chunk), 1)
    row_at = lax.broadcasted_iota(jnp.int32, (rows, chunk), 0)
    return key_at <= zy * block + lax.rem(row_at, block)


def attention_forward_kernel(info_ref, q_ref, kv_ref, o_ref, log_ref):
    parts, micros, block, _ = q_ref.shape
    span = kv_ref.shape[1]
    chunk = span // parts
    rows = GROUP * block
    mask = diagonal_mask(rows, chunk, block, info_ref[0])
    for part in range(parts):
        for micro in range(micros):
            queries = stacked_heads(q_ref, part, micro)
            pieces = [(m, 0, span) for m in range(micro)]
            if part > 0:
                pieces.append((micro, 0, part * chunk))
            pieces.append((micro, part * chunk, (part + 1) * chunk))
            scores = [dot_nt(queries, kv_ref[m, start:stop, :HD]) for m, start, stop in pieces]
            scores[-1] = jnp.where(mask, scores[-1], masked_score)
            peak = functools.reduce(
                jnp.maximum, [jnp.max(s, axis=-1, keepdims=True) for s in scores]
            )
            peak = peak * log2_scale
            total = jnp.zeros((rows, 1), f32)
            mixed = jnp.zeros((rows, HD), f32)
            for s, (m, start, stop) in zip(scores, pieces):
                probs = jnp.exp2(s * log2_scale - peak)
                total = total + jnp.sum(probs, axis=-1, keepdims=True)
                mixed = mixed + dot(probs.astype(bf), kv_ref[m, start:stop, HD:])
            store_heads(o_ref, part, micro, (mixed / total).astype(bf))
            log_ref[part, micro] = jnp.broadcast_to(peak + jnp.log2(total), (rows, HD))


def attention_backward_kernel(
    info_ref, q_ref, do_ref, o_ref, log_ref, kv_ref, dq_ref, dkv_ref
):
    parts, micros, block, _ = q_ref.shape
    span = kv_ref.shape[1]
    chunk = span // parts
    rows = GROUP * block
    mask = diagonal_mask(rows, chunk, block, info_ref[0])
    dkv_ref[...] = jnp.zeros(dkv_ref.shape, f32)
    for part in range(parts):
        for micro in range(micros):
            queries = stacked_heads(q_ref, part, micro)
            out_grad = stacked_heads(do_ref, part, micro)
            out = stacked_heads(o_ref, part, micro)
            inner = jnp.sum(out_grad.astype(f32) * out.astype(f32), axis=-1, keepdims=True)
            log_total = log_ref[part, micro][:, :1]
            query_grad = jnp.zeros((rows, HD), f32)
            pieces = [(m, start) for m in range(micro) for start in range(0, span, chunk)]
            pieces += [(micro, start) for start in range(0, (part + 1) * chunk, chunk)]
            for m, start in pieces:
                keys = kv_ref[m, start : start + chunk, :HD]
                probs = jnp.exp2(dot_nt(queries, keys) * log2_scale - log_total)
                if (m, start) == (micro, part * chunk):
                    probs = jnp.where(mask, probs, 0.0)
                probs_grad = dot_nt(out_grad, kv_ref[m, start : start + chunk, HD:])
                score_grad = (probs * (probs_grad - inner)).astype(bf)
                query_grad = query_grad + dot(score_grad, keys)
                dkv_ref[m, start : start + chunk, :HD] += dot_tn(score_grad, queries) * scaling
                dkv_ref[m, start : start + chunk, HD:] += dot_tn(probs.astype(bf), out_grad)
            store_heads(dq_ref, part, micro, (query_grad * scaling).astype(bf))


def in_vmem(count):
    return [pl.BlockSpec(memory_space=pltpu.VMEM)] * count


def attention_call(kernel, factor, out_shape, info, queries, *rest):
    parts, micros, block, _ = queries.shape
    rows = parts * micros * GROUP * block
    keys = rest[-1].shape[0] * rest[-1].shape[1]
    return pl.pallas_call(
        kernel,
        out_shape=out_shape,
        in_specs=[pl.BlockSpec(memory_space=pltpu.SMEM)] + in_vmem(1 + len(rest)),
        out_specs=tuple(in_vmem(len(out_shape))),
        compiler_params=pltpu.CompilerParams(vmem_limit_bytes=VMEM_LIMIT),
        cost_estimate=pl.CostEstimate(
            flops=factor * rows * keys * HD,
            bytes_accessed=factor * (keys + rows) * HD,
            transcendentals=rows * keys // 2,
        ),
    )(info, queries, *rest)


def attention_forward(info, queries, kv):
    parts, micros, block, _ = queries.shape
    logs = jax.ShapeDtypeStruct((parts, micros, GROUP * block, HD), f32)
    out = jax.ShapeDtypeStruct(queries.shape, bf)
    return attention_call(attention_forward_kernel, 2, (out, logs), info, queries, kv)


def attention_backward(info, queries, out_grad, out, logs, kv):
    shapes = (jax.ShapeDtypeStruct(queries.shape, bf), jax.ShapeDtypeStruct(kv.shape, f32))
    return attention_call(
        attention_backward_kernel, 5, shapes, info, queries, out_grad, out, logs, kv
    )


def body(
    inputs,
    cotangent,
    routes,
    norm_attn,
    w_query,
    w_key,
    w_value,
    w_output,
    norm_ffn,
    w_router,
    shared_gate,
    shared_up,
    shared_down,
    expert_gate,
    expert_up,
    expert_down,
):
    micros, block, width = inputs.shape[1:]
    tokens = micros * block
    shards = lax.axis_size("shard")
    section = lax.axis_index("section")
    core = lax.axis_index("dp")
    position = lax.axis_index("shard")
    heads = KVH
    ring = shards // heads
    local_experts = expert_gate.shape[1]
    experts = local_experts * shards
    room = micros * CAP
    slots = experts * room
    rows_per = w_query.shape[1]
    half_rows = rows_per // 2
    group_width = GROUP * HD
    head_width = H * HD
    key_width = KVH * HD
    part_width = group_width + 2 * HD
    shared_width = shared_gate.shape[2]
    down_rows = shared_down.shape[1]
    is_first = section == 0
    low_core = core == 0
    x_groups = [[x * ring + zy for x in range(heads)] for zy in range(ring)]
    zy_groups = [[x * ring + zy for zy in range(ring)] for x in range(heads)]

    def exchange(value, groups=None):
        return lax.all_to_all(
            value, "shard", split_axis=0, concat_axis=0, tiled=True, axis_index_groups=groups
        )

    def copies(value, count):
        return jnp.broadcast_to(value[None], (count,) + value.shape)

    def twin(value):
        return lax.ppermute(value, "dp", [(0, 1), (1, 0)])

    def mine_of(low_half, high_half):
        return jnp.where(low_core, low_half, high_half)

    def ordered(own, other, axis):
        low_half, high_half = mine_of(own, other), mine_of(other, own)
        return jnp.concatenate([low_half, high_half], axis=axis)

    def halves(value):
        half = value.shape[-1] // 2
        return value[..., :half], value[..., half:]

    def my_rows(value):
        return mine_of(value[..., :half_rows, :], value[..., half_rows:, :])

    tail = jnp.concatenate(
        [
            w_router[0],
            norm_attn[0][:, None],
            norm_ffn[0][:, None],
            jnp.zeros((rows_per, 128 - experts - 2), bf),
        ],
        axis=1,
    )
    by_head = jnp.concatenate(
        [
            w_query[0].reshape(rows_per, heads, group_width),
            w_key[0].reshape(rows_per, heads, HD),
            w_value[0].reshape(rows_per, heads, HD),
            jnp.broadcast_to(tail[:, None], (rows_per, heads, 128)),
        ],
        axis=2,
    ).transpose(1, 0, 2)
    by_head = my_rows(by_head)
    by_head = jnp.broadcast_to(
        by_head[:, None], (heads, ring, half_rows, part_width + 128)
    ).reshape(shards, half_rows, part_width + 128)
    own_part = exchange(by_head)
    fetched = ordered(own_part, twin(own_part), 1).reshape(width, part_width + 128)
    qkv_w, tail = fetched[:, :part_width], fetched[:, part_width:]
    own_out = lax.all_gather(my_rows(w_output[0]), "shard", axis_index_groups=zy_groups)
    output_w = ordered(own_out, twin(own_out), 1).reshape(group_width, width)
    router_w = tail[:, :experts]
    gains = tail[:, experts : experts + 2].T.astype(f32)
    gain_one, gain_two = gains[0][None], gains[1][None]

    down_flat = (rows_per, down_rows * width // 2 // rows_per)
    shared_rows = jnp.concatenate(
        [
            mine_of(shared_gate[0], shared_up[0]),
            mine_of(*halves(shared_down[0])).reshape(down_flat),
        ],
        axis=1,
    )
    own_shared = lax.all_gather(shared_rows, "shard", axis=0, tiled=True)
    other_shared = twin(own_shared)

    def cut(value):
        down = value[:, shared_width:].reshape(down_rows * shards, width // 2)
        return value[:, :shared_width], down

    gate_up_w, down_w = zip(cut(own_shared), cut(other_shared))

    def project(rows, pair):
        return ordered(dot(rows, pair[0]), dot(rows, pair[1]), 1)

    def project_back(low_half, high_half, pair):
        own, other = mine_of(low_half, high_half), mine_of(high_half, low_half)
        return dot_nt(own, pair[0]) + dot_nt(other, pair[1])

    expert_g, expert_u, expert_d = expert_gate[0], expert_up[0], expert_down[0]
    local_routes = routes[0, 0].reshape(tokens, TOPK)
    slot_of = jnp.arange(slots, dtype=jnp.int32)
    expert_of = jnp.arange(experts, dtype=jnp.int32)
    token_of = jnp.arange(tokens, dtype=jnp.int32)
    spread = (expert_of[:, None] == slot_of[None, :] // room).astype(bf)
    router_slots = dot(router_w, spread).astype(bf)
    named = jnp.any(local_routes[:, :, None] == expert_of[None, None, :], axis=1).astype(bf)
    earlier = (token_of[:, None] > token_of[None, :]) & (
        token_of[:, None] // block == token_of[None, :] // block
    )
    slot_ids = dot(earlier.astype(bf), named).astype(jnp.int32) + CAP * (token_of // block)[:, None]
    table = (dot(named, spread) > 0.5) & (
        dot(slot_ids.astype(bf), spread).astype(jnp.int32) == (slot_of % room)[None, :]
    )
    pick = table.astype(bf)
    info = jnp.stack([position % ring]).astype(jnp.int32)

    def gate_values(normed_two):
        logits = jnp.where(table, dot(normed_two, router_slots), masked_score)
        weights = jnp.exp(logits - jnp.max(logits, axis=-1, keepdims=True))
        weights = jnp.where(table, weights, 0.0)
        return weights / jnp.sum(weights, axis=-1, keepdims=True)

    def high_low(value):
        high = value.astype(bf)
        return high, (value - high.astype(f32)).astype(bf)

    def to_experts(rows):
        return (
            exchange(rows.reshape(shards, local_experts, room, width))
            .transpose(1, 0, 2, 3)
            .reshape(local_experts, shards * room, width)
        )

    def from_experts(rows):
        return exchange(
            rows.reshape(local_experts, shards, room, width).transpose(1, 0, 2, 3)
        ).reshape(slots, width)

    def sum_over_x(rows):
        parts = exchange(rows.astype(bf).reshape(heads, tokens, width), x_groups)
        return jnp.sum(parts.astype(f32), axis=0)

    def ring_rows(rows):
        return exchange(copies(rows, heads), x_groups).reshape(heads * tokens, width)

    def forward(layer_b):
        layer_in = layer_b.astype(f32)
        normed_one = (layer_in * inverse_rms(layer_in) * gain_one).astype(bf)
        ring_one = ring_rows(normed_one)
        qkv = dot(ring_one, qkv_w).astype(bf)
        queries = qkv[:, :group_width].reshape(heads, micros, block, group_width)
        pairs = exchange(copies(qkv[:, group_width:], ring), zy_groups)
        pairs = pairs.reshape(ring, heads, micros, block, 2 * HD).transpose(2, 1, 0, 3, 4)
        cache = pairs.reshape(micros, shards * block, 2 * HD)
        attended, logs = attention_forward(info, queries, cache)
        hidden = layer_in + sum_over_x(
            dot(attended.reshape(heads * tokens, group_width), output_w)
        )
        normed_two = (hidden * inverse_rms(hidden) * gain_two).astype(bf)
        gates = gate_values(normed_two)
        expert_in = to_experts(dot_tn(pick, normed_two).astype(bf))
        gate_pre = wide_einsum("erd,edf->erf", expert_in, expert_g)
        up_pre = wide_einsum("erd,edf->erf", expert_in, expert_u)
        activated = (silu_parts(gate_pre)[0] * up_pre).astype(bf)
        returned = from_experts(wide_einsum("erf,efd->erd", activated, expert_d).astype(bf))
        high, low = high_low(gates)
        routed = dot(high, returned) + dot(low, returned)
        shared_gate_pre, shared_up_pre = halves(project(normed_two, gate_up_w))
        shared_act = (silu_parts(shared_gate_pre)[0] * shared_up_pre).astype(bf)
        output_b = (hidden + routed + project(shared_act, down_w)).astype(bf)
        return dict(
            layer_b=layer_b,
            ring_one=ring_one,
            queries=queries,
            cache=cache,
            attended=attended,
            logs=logs,
            hidden=hidden,
            normed_two=normed_two,
            gates=gates,
            expert_in=expert_in,
            gate_pre=gate_pre,
            up_pre=up_pre,
            activated=activated,
            returned=returned,
            shared_gate_pre=shared_gate_pre,
            shared_up_pre=shared_up_pre,
            shared_act=shared_act,
            output_b=output_b,
        )

    def ffn_backward(kept, upstream_b):
        upstream = upstream_b.astype(f32)
        gates, hidden = kept["gates"], kept["hidden"]
        high, low = high_low(gates)
        outgoing = dot_tn(high, upstream_b) + dot_tn(low, upstream_b)
        expert_grad = to_experts(outgoing.astype(bf))
        act_silu, act_slope = silu_parts(kept["gate_pre"])
        act_grad = wide_einsum("erd,efd->erf", expert_grad, expert_d)
        gate_pre_grad = (act_grad * kept["up_pre"] * act_slope).astype(bf)
        up_pre_grad = (act_grad * act_silu).astype(bf)
        expert_in_grad = (
            wide_einsum("erf,edf->erd", gate_pre_grad, expert_g)
            + wide_einsum("erf,edf->erd", up_pre_grad, expert_u)
        ).astype(bf)
        returned_grad = from_experts(expert_in_grad)
        shared_act_grad = project_back(*halves(upstream_b), down_w)
        shared_silu, shared_slope = silu_parts(kept["shared_gate_pre"])
        shared_gate_grad = (shared_act_grad * kept["shared_up_pre"] * shared_slope).astype(bf)
        shared_up_grad = (shared_act_grad * shared_silu).astype(bf)
        normed_two_grad = project_back(shared_gate_grad, shared_up_grad, gate_up_w)
        gate_grad = dot_nt(upstream_b, kept["returned"])
        picked_grad = gates * (gate_grad - jnp.sum(gates * gate_grad, axis=1, keepdims=True))
        picked_b = picked_grad.astype(bf)
        normed_two_grad = normed_two_grad + dot_nt(picked_b, router_slots)
        normed_two_grad = normed_two_grad + dot(pick, returned_grad)
        logit_grad = dot_nt(picked_b, spread).astype(bf)
        hidden_norm_grad, gain_two_grad = norm_back(hidden, gain_two, normed_two_grad)
        return dict(
            hidden_grad=upstream + hidden_norm_grad,
            upstream_b=upstream_b,
            expert_grad=expert_grad,
            gate_pre_grad=gate_pre_grad,
            up_pre_grad=up_pre_grad,
            shared_gate_grad=shared_gate_grad,
            shared_up_grad=shared_up_grad,
            logit_grad=logit_grad,
            gain_two_grad=gain_two_grad,
        )

    def attention_back(kept, grads):
        ring_hidden = ring_rows(grads["hidden_grad"].astype(bf))
        out_grad = dot_nt(ring_hidden, output_w).astype(bf)
        out_grad = out_grad.reshape(heads, micros, block, group_width)
        query_grad, cache_grad = attention_backward(
            info, kept["queries"], out_grad, kept["attended"], kept["logs"], kept["cache"]
        )
        parts = cache_grad.astype(bf).reshape(micros, heads, ring, block, 2 * HD)
        parts = parts.transpose(2, 1, 0, 3, 4).reshape(ring, heads * tokens, 2 * HD)
        pair_grad = jnp.sum(exchange(parts, zy_groups).astype(f32), axis=0).astype(bf)
        qkv_grad = jnp.concatenate(
            [query_grad.reshape(heads * tokens, group_width), pair_grad], axis=1
        )
        normed_one_grad = sum_over_x(dot_nt(qkv_grad, qkv_w))
        in_norm_grad, gain_one_grad = norm_back(
            kept["layer_b"].astype(f32), gain_one, normed_one_grad
        )
        return dict(
            grads,
            ring_hidden=ring_hidden,
            qkv_grad=qkv_grad,
            gain_one_grad=gain_one_grad,
            layer_grad=(grads["hidden_grad"] + in_norm_grad).astype(bf),
        )

    first = forward(inputs[0].reshape(tokens, width))
    second = forward(lax.ppermute(first["output_b"], "section", [(0, 1)]))
    second_back = ffn_backward(second, cotangent[0].reshape(tokens, width))
    second_back = attention_back(second, second_back)
    received = lax.ppermute(second_back["layer_grad"], "section", [(1, 0)])
    first_back = attention_back(first, ffn_backward(first, received))

    kept = {name: jnp.where(is_first, first[name], second[name]) for name in KEPT}
    back = {name: jnp.where(is_first, first_back[name], second_back[name]) for name in BACK}

    expert_parts = [
        wide_einsum("erd,erf->edf", kept["expert_in"], back["gate_pre_grad"]),
        wide_einsum("erd,erf->edf", kept["expert_in"], back["up_pre_grad"]),
        wide_einsum("erf,erd->efd", kept["activated"], back["expert_grad"]),
    ]
    expert_parts = [part.astype(bf) for part in expert_parts]
    expert_grads = [part.astype(f32) + twin(part).astype(f32) for part in expert_parts]

    def both(value):
        return jnp.concatenate([value, twin(value)], axis=0)

    def both_halves(low_half, high_half):
        own, other = mine_of(low_half, high_half), mine_of(high_half, low_half)
        return jnp.concatenate([own, twin(other)], axis=0)

    grad_gate_up = dot_tn(
        both(kept["normed_two"]), both_halves(back["shared_gate_grad"], back["shared_up_grad"])
    )
    grad_down = dot_tn(both(kept["shared_act"]), both_halves(*halves(back["upstream_b"])))
    shared_flat = (shards, down_rows * width // 2 // shared_width, shared_width)
    shared_pieces = jnp.concatenate(
        [
            grad_gate_up.astype(bf).reshape(shards, rows_per, shared_width),
            grad_down.astype(bf).reshape(shared_flat),
        ],
        axis=1,
    )
    share_shared = jnp.sum(exchange(shared_pieces).astype(f32), axis=0)
    other_shared = twin(share_shared)

    grad_out = dot_tn(
        kept["attended"].reshape(heads * tokens, group_width), back["ring_hidden"]
    )
    share_out = jnp.sum(
        exchange(grad_out.astype(bf).reshape(ring, rows_per, width), zy_groups).astype(f32), axis=0
    )
    grad_qkv = dot_tn(kept["ring_one"], back["qkv_grad"])
    grad_router = dot_tn(kept["normed_two"], back["logit_grad"])
    gain_sums = jnp.stack([back["gain_one_grad"], back["gain_two_grad"]])
    grad_tail = jnp.concatenate(
        [grad_router, gain_sums.T, jnp.zeros((width, 128 - experts - 2), f32)], axis=1
    )
    pieces = exchange(
        jnp.concatenate([grad_qkv, grad_tail], axis=1)
        .astype(bf)
        .reshape(shards, rows_per, part_width + 128)
    ).astype(f32)
    share_qkv = jnp.sum(
        pieces[:, :, :part_width].reshape(heads, ring, rows_per, part_width), axis=1
    )
    share_qkv = share_qkv.transpose(1, 0, 2)
    share_tail = jnp.sum(pieces[:, :, part_width:], axis=0)

    def total(share):
        return share + twin(share)

    out_total, qkv_total, tail_total = total(share_out), total(share_qkv), total(share_tail)
    low_shared, high_shared = (
        mine_of(share_shared, other_shared),
        mine_of(other_shared, share_shared),
    )
    down_shape = (down_rows, width // 2)
    down_total = jnp.concatenate(
        [low_shared[rows_per:].reshape(down_shape), high_shared[rows_per:].reshape(down_shape)],
        axis=1,
    )
    token_shape = (1, 1, micros, block, width)
    return (
        jnp.where(is_first, first["output_b"], second["output_b"]).reshape(token_shape),
        jnp.where(is_first, first_back["layer_grad"], second_back["layer_grad"]).reshape(
            token_shape
        ),
        tail_total[:, experts][None],
        qkv_total[:, :, :group_width].reshape(1, rows_per, head_width),
        qkv_total[:, :, group_width : group_width + HD].reshape(1, rows_per, key_width),
        qkv_total[:, :, group_width + HD :].reshape(1, rows_per, key_width),
        out_total[None],
        tail_total[:, experts + 1][None],
        tail_total[:, :experts][None],
        low_shared[:rows_per][None],
        high_shared[:rows_per][None],
        down_total[None],
        expert_grads[0][None],
        expert_grads[1][None],
        expert_grads[2][None],
    )


def solution(mesh):
    rows = P("section", "shard", None)
    vector = P("section", "shard")
    expert = P("section", "shard", None, None)
    tokens = P("dp", None, "shard", None)
    section_tokens = P("section", "dp", None, "shard", None)
    weights = (vector, rows, rows, rows, rows, vector, rows, rows, rows, rows) + (expert,) * 3
    return jax.shard_map(
        body,
        mesh=mesh,
        in_specs=(tokens, tokens, section_tokens) + weights,
        out_specs=(section_tokens, section_tokens) + weights,
        check_vma=False,
    )
```

time: 1180 us -> 1180 us (level)
  blocking collectives: 63.9 us -> 229 us
  matrix products: 249 us -> 164 us
  starting transfers between devices: 202 us -> 157 us
  waiting for transfers between devices: 387 us -> 360 us
    all_gather x1, waiting for transfers between devices: 125 us -> 0.02 us  [body(): own_shared = lax.all_gather(shared_rows, 'shard', axis=0, tiled=True)]
    all_to_all x29 -> x18, waiting for transfers between devices: 223 us -> 339 us  [exchange(): lax.all_to_all(value, 'shard', split_axis=0, concat_axis=0, tiled=True, a...]
    all_to_all x4 -> x6, blocking collectives: 63.9 us -> 170 us  [exchange(): lax.all_to_all(value, 'shard', split_axis=0, concat_axis=0, tiled=True, a...]
    all_gather x0 -> x1, blocking collectives: none -> 58.9 us  [body(): lax.all_gather(my_rows(w_output[0]), 'shard', axis_index_groups=zy_groups)]
    dot_general x33 -> x17, matrix products: 85.1 us -> 38.8 us  [dot_nt(): lax.dot_general(left_side, right_side, (((1,), (1,)), ((), ())), preferre...]
    dot_general x41 -> x23, matrix products: 89.7 us -> 54.8 us  [dot(): return jnp.dot(left_side, right_side, preferred_element_type=f32)]
    all_to_all x29 -> x18, starting transfers between devices: 156 us -> 128 us  [exchange(): lax.all_to_all(value, 'shard', split_axis=0, concat_axis=0, tiled=True, a...]
    reshape x28 -> x14, local copies, waits for them, and re-layouts: 37.1 us -> 23.7 us  [the longest x4 7.63 us: from_experts(): rows.reshape(local_experts, shards, room, width).transpose(1, 0, 2, 3)]
  transfers between devices with their start and end apart: 49 -> 35, of which waited for: 34 -> 20; matrix products, arithmetic and copies ran while one was open for 27% -> 20% of each run, Pallas kernels for 2% -> 2%
where the time goes in v2:
time: 1180 us; the launch traced here: 1160 us
  waiting for transfers between devices  360 us (31%)
  blocking collectives  229 us (19%)
  matrix products  164 us (14%)
  starting transfers between devices  157 us (13%)
  local copies, waits for them, and re-layouts  103 us (9%)
  other arithmetic  83.4 us (7%)
  Pallas kernels  45.6 us (4%)
  between operations  16.5 us (1%)
    all_to_all x18, waiting for transfers between devices, exchange(): lax.all_to_all(value, 'shard', split_axis=0, concat_axis=0, tiled=True, a...  339 us
    all_to_all x6, blocking collectives, exchange(): lax.all_to_all(value, 'shard', split_axis=0, concat_axis=0, tiled=True, a...  170 us
    all_to_all x18, starting transfers between devices, exchange(): lax.all_to_all(value, 'shard', split_axis=0, concat_axis=0, tiled=True, a...  128 us
    all_gather x1, blocking collectives, body(): lax.all_gather(my_rows(w_output[0]), 'shard', axis_index_groups=zy_groups)  58.9 us
    dot_general x23, matrix products, dot(): return jnp.dot(left_side, right_side, preferred_element_type=f32)  54.8 us
    dot_general x15, matrix products, wide_einsum(): jnp.einsum(formula, left_side, right_side, preferred_element_type=f32)  45.8 us
    pallas_call x4, Pallas kernels, attention_call(): pl.pallas_call(kernel, out_shape=out_shape, in_specs=[pl.BlockSpec(memory...  45.6 us
    dot_general x17, matrix products, dot_nt(): lax.dot_general(left_side, right_side, (((1,), (1,)), ((), ())), preferre...  38.8 us
  transfers between devices with their start and end apart: 35, of which 20 were waited for; matrix products, arithmetic and copies ran while one was open for 20% of the time, Pallas kernels for 2%

profile of v2, /device:TPU:1, one launch (start us, length us, event | category | flops | bytes accessed | tf_op | source)
XLA Modules:
  0.0 1158.5 jit_solution(1680794423045164451)
XLA Ops:
  16.8 30.7 %all_to_all.120 = bf16[32,24,768]{2,1,0:T(8,128)(2,1)} all-to-all(bf16[32,24,768]{2,1,0:T(8,128)(2,1)S(1)} %bitcast.306), channel_id=1, replica_groups=mesh['section'=2,'dp'=2,'shard'=32] {'shard'}, dimensions={0} | all-to-all | bytes 2359296 | tf_op jit(solution)/shard_map/all_to_all | solution.py:237
  64.6 20.3 %all-to-all-done.1 = bf16[4,128,1536]{1,2,0:T(8,128)(2,1)} async-done(((bf16[4,128,1536]{1,2,0:T(8,128)(2,1)}), bf16[4,128,1536]{1,2,0:T(8,128)(2,1)}, u32[]{:S(2)}, u32[]{:S(2)}) %all-to-all-start.1) | async-done | bytes 1572896 | tf_op jit(solution)/shard_map/all_to_all | solution.py:237
  97.6 58.9 %all_gather.7 = bf16[8,24,1536]{2,1,0:T(8,128)(2,1)} all-gather(bf16[1,24,1536]{2,1,0:T(8,128)(2,1)S(1)} %slice_select_fusion.1), channel_id=1, replica_groups={{0,1,2,3,4,5,6,7},{8,9,10,11,12,13,14,15},{16,17,18,19,20,21,22,23},{24..., dimensions={0}, use_global_device_ids=true | all-gather | bytes 663552 | tf_op jit(solution)/shard_map/all_gather | solution.py:286
  184.5 19.5 %all-to-all-done.3 = bf16[4,128,1536]{2,1,0:T(8,128)(2,1)} async-done(((bf16[4,128,1536]{2,1,0:T(8,128)(2,1)}), bf16[4,128,1536]{2,1,0:T(8,128)(2,1)}, u32[]{:S(2)}, u32[]{:S(2)}) %all-to-all-start.3) | async-done | bytes 1572896 | tf_op jit(solution)/shard_map/all_to_all | solution.py:237
  220.3 38.4 %all-to-all-done.4 = bf16[32,2,16,1536]{3,2,1,0:T(8,128)(2,1)} async-done(((bf16[32,2,16,1536]{3,2,1,0:T(8,128)(2,1)}), bf16[32,2,16,1536]{3,2,1,0:T(8,128)(2,1)}, u32[]{:S(2)}, u32[]{:S(2)}) %all-to-all-start.4) | async-done | bytes 3145760 | tf_op jit(solution)/shard_map/all_to_all | solution.py:237
  295.8 25.3 %all-to-all-done.5 = bf16[32,2,16,1536]{3,2,1,0:T(8,128)(2,1)} async-done(((bf16[32,2,16,1536]{3,2,1,0:T(8,128)(2,1)}), bf16[32,2,16,1536]{3,2,1,0:T(8,128)(2,1)}, u32[]{:S(2)}, u32[]{:S(2)}) %all-to-all-start.5) | async-done | bytes 3145760 | tf_op jit(solution)/shard_map/all_to_all | solution.py:237
  352.1 23.2 %all_to_all.121 = bf16[4,128,1536]{1,2,0:T(8,128)(2,1)} all-to-all(bf16[4,128,1536]{1,2,0:T(8,128)(2,1)S(1)} %broadcast_in_dim.52), channel_id=1, replica_groups={{0,8,16,24},{1,9,17,25},{2,10,18,26},{3,11,19,27},{4,12,20,28},{5,13,21..., dimensions={0} | all-to-all | bytes 3145728 | tf_op jit(solution)/shard_map/all_to_all | solution.py:237
  393.1 23.0 %all-to-all-done.7 = bf16[8,512,256]{2,1,0:T(8,128)(2,1)} async-done(((bf16[8,512,256]{2,1,0:T(8,128)(2,1)}), bf16[8,512,256]{2,1,0:T(8,128)(2,1)}, u32[]{:S(2)}, u32[]{:S(2)}) %all-to-all-start.7) | async-done | bytes 2097184 | tf_op jit(solution)/shard_map/all_to_all | solution.py:237
  431.7 15.8 %all-to-all-done.8 = bf16[4,128,1536]{2,1,0:T(8,128)(2,1)} async-done(((bf16[4,128,1536]{2,1,0:T(8,128)(2,1)}), bf16[4,128,1536]{2,1,0:T(8,128)(2,1)}, u32[]{:S(2)}, u32[]{:S(2)}) %all-to-all-start.8) | async-done | bytes 1572896 | tf_op jit(solution)/shard_map/all_to_all | solution.py:237
  455.1 10.3 all-to-all-start.9
  472.3 34.2 %all-to-all-done.9 = bf16[32,2,16,1536]{3,2,1,0:T(8,128)(2,1)} async-done(((bf16[32,2,16,1536]{3,2,1,0:T(8,128)(2,1)}), bf16[32,2,16,1536]{3,2,1,0:T(8,128)(2,1)}, u32[]{:S(2)}, u32[]{:S(2)}) %all-to-all-start.9) | async-done | bytes 3145760 | tf_op jit(solution)/shard_map/all_to_all | solution.py:237
  525.0 31.2 %all-to-all-done.11 = bf16[32,2,16,1536]{3,2,1,0:T(8,128)(2,1)} async-done(((bf16[32,2,16,1536]{3,2,1,0:T(8,128)(2,1)}), bf16[32,2,16,1536]{3,2,1,0:T(8,128)(2,1)}, u32[]{:S(2)}, u32[]{:S(2)}) %all-to-all-start.11) | async-done | bytes 3145760 | tf_op jit(solution)/shard_map/all_to_all | solution.py:237
  585.0 32.7 %all-to-all-done.10 = bf16[32,2,16,1536]{3,2,1,0:T(8,128)(2,1)} async-done(((bf16[32,2,16,1536]{3,2,1,0:T(8,128)(2,1)}), bf16[32,2,16,1536]{3,2,1,0:T(8,128)(2,1)}, u32[]{:S(2)}, u32[]{:S(2)}) %all-to-all-start.10) | async-done | bytes 3145760 | tf_op jit(solution)/shard_map/all_to_all | solution.py:237
  646.3 20.1 %all-to-all-done.12 = bf16[32,2,16,1536]{3,2,1,0:T(8,128)(2,1)} async-done(((bf16[32,2,16,1536]{3,2,1,0:T(8,128)(2,1)}), bf16[32,2,16,1536]{3,2,1,0:T(8,128)(2,1)}, u32[]{:S(2)}, u32[]{:S(2)}) %all-to-all-start.12) | async-done | bytes 3145760 | tf_op jit(solution)/shard_map/all_to_all | solution.py:237
  671.3 20.9 %all_to_all.122 = bf16[4,128,1536]{2,1,0:T(8,128)(2,1)S(1)} all-to-all(bf16[4,128,1536]{2,1,0:T(8,128)(2,1)S(1)} %broadcast_in_dim.54), channel_id=1, replica_groups={{0,8,16,24},{1,9,17,25},{2,10,18,26},{3,11,19,27},{4,12,20,28},{5,13,21..., dimensions={0} | all-to-all | bytes 3145728 | tf_op jit(solution)/shard_map/all_to_all | solution.py:237
  693.4 16.5 %shard_map.273 = (bf16[4,2,64,384]{3,2,1,0:T(8,128)(2,1)S(1)}, f32[2,2048,256]{2,1,0:T(8,128)S(1)}) custom-call(s32[1]{0:T(128)} %bitcast.1.info_ref, bf16[4,2,64,384]{3,2,1,0:T(8,128)(2,1)S(1)} %bitcast.268, bf16[4,2,64,384]{3,2,1,0:T(8,128)(2,1)S(1)} %bitcast.274, bf16[4,2,64,384]{3,2,1,0:T(8,128)(2,1)S(1)} %get-tuple-element.24.o_ref, ...), custom_call_target="tpu_custom_call" | custom-call | flops 4026531840 | bytes 3604480 | tf_op jit(solution)/shard_map/pallas_call | solution.py:165
  710.9 35.0 %all_to_all.123 = bf16[8,512,256]{2,1,0:T(8,128)(2,1)} all-to-all(bf16[8,512,256]{2,1,0:T(8,128)(2,1)S(1)} %bitcast.299), channel_id=1, replica_groups={{0,1,2,3,4,5,6,7},{8,9,10,11,12,13,14,15},{16,17,18,19,20,21,22,23},{24..., dimensions={0} | all-to-all | bytes 4194304 | tf_op jit(solution)/shard_map/all_to_all | solution.py:237
  751.7 19.7 %all_to_all.124 = bf16[4,128,1536]{2,1,0:T(8,128)(2,1)S(1)} all-to-all(bf16[4,128,1536]{2,1,0:T(8,128)(2,1)S(1)} %bitcast.331), channel_id=1, replica_groups={{0,8,16,24},{1,9,17,25},{2,10,18,26},{3,11,19,27},{4,12,20,28},{5,13,21..., dimensions={0} | all-to-all | bytes 3145728 | tf_op jit(solution)/shard_map/all_to_all | solution.py:237
  774.4 10.1 collective-permute-done.4
  786.7 40.6 %all_to_all.125 = bf16[32,2,16,1536]{3,2,1,0:T(8,128)(2,1)S(1)} all-to-all(bf16[32,2,16,1536]{3,2,1,0:T(8,128)(2,1)S(1)} %bitcast.284), channel_id=1, replica_groups=mesh['section'=2,'dp'=2,'shard'=32] {'shard'}, dimensions={0} | all-to-all | bytes 6291456 | tf_op jit(solution)/shard_map/all_to_all | solution.py:237
  839.6 10.0 all-to-all-start.17
  871.7 19.1 %all-to-all-done.17 = bf16[32,2,16,1536]{3,2,1,0:T(8,128)(2,1)} async-done(((bf16[32,2,16,1536]{3,2,1,0:T(8,128)(2,1)}), bf16[32,2,16,1536]{3,2,1,0:T(8,128)(2,1)}, u32[]{:S(2)}, u32[]{:S(2)}) %all-to-all-start.17) | async-done | bytes 3145760 | tf_op jit(solution)/shard_map/all_to_all | solution.py:237
  921.5 16.5 %shard_map.274 = (bf16[4,2,64,384]{3,2,1,0:T(8,128)(2,1)S(1)}, f32[2,2048,256]{2,1,0:T(8,128)S(1)}) custom-call(s32[1]{0:T(128)} %bitcast.1.info_ref, bf16[4,2,64,384]{3,2,1,0:T(8,128)(2,1)S(1)} %bitcast.266, bf16[4,2,64,384]{3,2,1,0:T(8,128)(2,1)S(1)} %bitcast.273, bf16[4,2,64,384]{3,2,1,0:T(8,128)(2,1)S(1)} %copy-done.6, ...), custom_call_target="tpu_custom_call" | custom-call | flops 4026531840 | bytes 3604480 | tf_op jit(solution)/shard_map/pallas_call | solution.py:165
  1105.5 29.0 %all-to-all-done.23 = bf16[32,72,1024]{2,1,0:T(8,128)(2,1)} async-done(((bf16[32,72,1024]{2,1,0:T(8,128)(2,1)}), bf16[32,72,1024]{2,1,0:T(8,128)(2,1)}, u32[]{:S(2)}, u32[]{:S(2)}) %all-to-all-start.23) | async-done | bytes 4718624 | tf_op jit(solution)/shard_map/all_to_all | solution.py:237
  (611 shorter events, 540.7 us)
Async XLA Ops:
  59.2 25.7 %all-to-all-start.1 = ((bf16[4,128,1536]{1,2,0:T(8,128)(2,1)}), bf16[4,128,1536]{1,2,0:T(8,128)(2,1)}, u32[]{:S(2)}, u32[]{:S(2)}) async-start(bf16[4,128,1536]{1,2,0:T(8,128)(2,1)} %broadcast_in_dim.48), calls=%async_computation.1 | async-start | bytes 3145728 | tf_op jit(solution)/shard_map/all_to_all | solution.py:237
  63.7 154.8 %all-gather.2.cloned.1.call-start = ((), (), s32[]{:S(2)}) async-start(), calls=%async_computation.24 | async-start | bytes 4866048 | tf_op jit(solution)/shard_map/all_gather | solution.py:300
  93.2 74.8 %all-to-all-start.2 = ((bf16[8,512,256]{2,1,0:T(8,128)(2,1)}), bf16[8,512,256]{2,1,0:T(8,128)(2,1)}, u32[]{:S(2)}, u32[]{:S(2)}) async-start(bf16[8,512,256]{2,1,0:T(8,128)(2,1)} %broadcast_in_dim.49), calls=%async_computation.2 | async-start | bytes 4194304 | tf_op jit(solution)/shard_map/all_to_all | solution.py:237
  179.2 24.9 %all-to-all-start.3 = ((bf16[4,128,1536]{2,1,0:T(8,128)(2,1)}), bf16[4,128,1536]{2,1,0:T(8,128)(2,1)}, u32[]{:S(2)}, u32[]{:S(2)}) async-start(bf16[4,128,1536]{2,1,0:T(8,128)(2,1)} %bitcast.304), calls=%async_computation.3 | async-start | bytes 3145728 | tf_op jit(solution)/shard_map/all_to_all | solution.py:237
  213.6 45.1 %all-to-all-start.4 = ((bf16[32,2,16,1536]{3,2,1,0:T(8,128)(2,1)}), bf16[32,2,16,1536]{3,2,1,0:T(8,128)(2,1)}, u32[]{:S(2)}, u32[]{:S(2)}) async-start(bf16[32,2,16,1536]{3,2,1,0:T(8,128)(2,1)} %bitcast.278), calls=%async_computation.4 | async-start | bytes 6291456 | tf_op jit(solution)/shard_map/all_to_all | solution.py:237
  218.5 106.2 %collective-permute-start.2 = (bf16[1536,1536]{1,0:T(8,128)(2,1)}, bf16[1536,1536]{1,0:T(8,128)(2,1)}, u32[]{:S(2)}, u32[]{:S(2)}) collective-permute-start(bf16[1536,1536]{1,0:T(8,128)(2,1)} %all-gather.2.cloned.1.call-done), channel_id=1, source_target_pairs={{0,32},{32,0},{1,33},{33,1},{2,34},{34,2},{3,35},{35,3},{4,36},{36... | collective-permute-start | bytes 14155784 | tf_op jit(solution)/shard_map/ppermute | solution.py:245
  271.0 50.1 %all-to-all-start.5 = ((bf16[32,2,16,1536]{3,2,1,0:T(8,128)(2,1)}), bf16[32,2,16,1536]{3,2,1,0:T(8,128)(2,1)}, u32[]{:S(2)}, u32[]{:S(2)}) async-start(bf16[32,2,16,1536]{3,2,1,0:T(8,128)(2,1)} %bitcast.277), calls=%async_computation.5 | async-start | bytes 6291456 | tf_op jit(solution)/shard_map/all_to_all | solution.py:237
  383.5 32.6 %all-to-all-start.7 = ((bf16[8,512,256]{2,1,0:T(8,128)(2,1)}), bf16[8,512,256]{2,1,0:T(8,128)(2,1)}, u32[]{:S(2)}, u32[]{:S(2)}) async-start(bf16[8,512,256]{2,1,0:T(8,128)(2,1)} %broadcast_in_dim.53), calls=%async_computation.7 | async-start | bytes 4194304 | tf_op jit(solution)/shard_map/all_to_all | solution.py:237
  455.1 51.4 %all-to-all-start.9 = ((bf16[32,2,16,1536]{3,2,1,0:T(8,128)(2,1)}), bf16[32,2,16,1536]{3,2,1,0:T(8,128)(2,1)}, u32[]{:S(2)}, u32[]{:S(2)}) async-start(bf16[32,2,16,1536]{3,2,1,0:T(8,128)(2,1)} %bitcast.279), calls=%async_computation.9 | async-start | bytes 6291456 | tf_op jit(solution)/shard_map/all_to_all | solution.py:237
  506.5 49.7 %all-to-all-start.11 = ((bf16[32,2,16,1536]{3,2,1,0:T(8,128)(2,1)}), bf16[32,2,16,1536]{3,2,1,0:T(8,128)(2,1)}, u32[]{:S(2)}, u32[]{:S(2)}) async-start(bf16[32,2,16,1536]{3,2,1,0:T(8,128)(2,1)} %bitcast.283), calls=%async_computation.11 | async-start | bytes 6291456 | tf_op jit(solution)/shard_map/all_to_all | solution.py:237
  567.1 50.7 %all-to-all-start.10 = ((bf16[32,2,16,1536]{3,2,1,0:T(8,128)(2,1)}), bf16[32,2,16,1536]{3,2,1,0:T(8,128)(2,1)}, u32[]{:S(2)}, u32[]{:S(2)}) async-start(bf16[32,2,16,1536]{3,2,1,0:T(8,128)(2,1)} %bitcast.280), calls=%async_computation.10 | async-start | bytes 6291456 | tf_op jit(solution)/shard_map/all_to_all | solution.py:237
  617.8 48.7 %all-to-all-start.12 = ((bf16[32,2,16,1536]{3,2,1,0:T(8,128)(2,1)}), bf16[32,2,16,1536]{3,2,1,0:T(8,128)(2,1)}, u32[]{:S(2)}, u32[]{:S(2)}) async-start(bf16[32,2,16,1536]{3,2,1,0:T(8,128)(2,1)} %bitcast.276), calls=%async_computation.12 | async-start | bytes 6291456 | tf_op jit(solution)/shard_map/all_to_all | solution.py:237
  839.6 51.2 %all-to-all-start.17 = ((bf16[32,2,16,1536]{3,2,1,0:T(8,128)(2,1)}), bf16[32,2,16,1536]{3,2,1,0:T(8,128)(2,1)}, u32[]{:S(2)}, u32[]{:S(2)}) async-start(bf16[32,2,16,1536]{3,2,1,0:T(8,128)(2,1)} %bitcast.275), calls=%async_computation.17 | async-start | bytes 6291456 | tf_op jit(solution)/shard_map/all_to_all | solution.py:237
  902.0 134.7 %collective-permute-start.8 = (bf16[128,1536]{1,0:T(8,128)(2,1)}, bf16[128,1536]{1,0:T(8,128)(2,1)}, u32[]{:S(2)}, u32[]{:S(2)}) collective-permute-start(bf16[128,1536]{1,0:T(8,128)(2,1)} %get-tuple-element.48), channel_id=1, source_target_pairs={{0,32},{32,0},{1,33},{33,1},{2,34},{34,2},{3,35},{35,3},{4,36},{36... | collective-permute-start | bytes 1179656 | tf_op jit(solution)/shard_map/ppermute | solution.py:245
  905.3 143.8 %collective-permute-start.10 = (bf16[128,1024]{1,0:T(8,128)(2,1)}, bf16[128,1024]{1,0:T(8,128)(2,1)}, u32[]{:S(2)}, u32[]{:S(2)}) collective-permute-start(bf16[128,1024]{1,0:T(8,128)(2,1)} %get-tuple-element.46), channel_id=1, source_target_pairs={{0,32},{32,0},{1,33},{33,1},{2,34},{34,2},{3,35},{35,3},{4,36},{36... | collective-permute-start | bytes 786440 | tf_op jit(solution)/shard_map/ppermute | solution.py:245
  940.2 32.3 %all-to-all-start.19 = ((bf16[8,512,256]{2,1,0:T(8,128)(2,1)}), bf16[8,512,256]{2,1,0:T(8,128)(2,1)}, u32[]{:S(2)}, u32[]{:S(2)}) async-start(bf16[8,512,256]{2,1,0:T(8,128)(2,1)} %bitcast.298), calls=%async_computation.19 | async-start | bytes 4194304 | tf_op jit(solution)/shard_map/all_to_all | solution.py:237
  949.2 96.0 %collective-permute-start.9 = (bf16[128,1024]{1,0:T(8,128)(2,1)}, bf16[128,1024]{1,0:T(8,128)(2,1)}, u32[]{:S(2)}, u32[]{:S(2)}) collective-permute-start(bf16[128,1024]{1,0:T(8,128)(2,1)} %broadcast_select_fusion.14), channel_id=1, source_target_pairs={{0,32},{32,0},{1,33},{33,1},{2,34},{34,2},{3,35},{35,3},{4,36},{36... | collective-permute-start | bytes 786440 | tf_op jit(solution)/shard_map/ppermute | solution.py:245
  958.2 119.1 %collective-permute-start.13 = (bf16[2,1536,512]{2,1,0:T(8,128)(2,1)}, bf16[2,1536,512]{2,1,0:T(8,128)(2,1)}, u32[]{:S(2)}, u32[]{:S(2)}) collective-permute-start(bf16[2,1536,512]{2,1,0:T(8,128)(2,1)} %convolution_convert_fusion.3), channel_id=1, source_target_pairs={{0,32},{32,0},{1,33},{33,1},{2,34},{34,2},{3,35},{35,3},{4,36},{36... | collective-permute-start | bytes 9437192 | tf_op jit(solution)/shard_map/ppermute | solution.py:245
  962.0 121.9 %collective-permute-start.14 = (bf16[2,1536,512]{2,1,0:T(8,128)(2,1)}, bf16[2,1536,512]{2,1,0:T(8,128)(2,1)}, u32[]{:S(2)}, u32[]{:S(2)}) collective-permute-start(bf16[2,1536,512]{2,1,0:T(8,128)(2,1)} %convolution_convert_fusion.2), channel_id=1, source_target_pairs={{0,32},{32,0},{1,33},{33,1},{2,34},{34,2},{3,35},{35,3},{4,36},{36... | collective-permute-start | bytes 9437192 | tf_op jit(solution)/shard_map/ppermute | solution.py:245
  1000.3 25.2 %all-to-all-start.22 = ((bf16[8,48,1536]{2,1,0:T(8,128)(2,1)}), bf16[8,48,1536]{2,1,0:T(8,128)(2,1)}, u32[]{:S(2)}, u32[]{:S(2)}) async-start(bf16[8,48,1536]{2,1,0:T(8,128)(2,1)} %bitcast.334), calls=%async_computation.22 | async-start | bytes 2359296 | tf_op jit(solution)/shard_map/all_to_all | solution.py:237
  1025.4 35.6 %all-to-all-start.21 = ((bf16[32,48,768]{2,1,0:T(8,128)(2,1)}), bf16[32,48,768]{2,1,0:T(8,128)(2,1)}, u32[]{:S(2)}, u32[]{:S(2)}) async-start(bf16[32,48,768]{2,1,0:T(8,128)(2,1)} %maximum_maximum_fusion), calls=%async_computation.21 | async-start | bytes 4718592 | tf_op jit(solution)/shard_map/all_to_all | solution.py:237
  1045.3 47.7 %collective-permute-start.15 = (bf16[2,512,1536]{2,1,0:T(8,128)(2,1)}, bf16[2,512,1536]{2,1,0:T(8,128)(2,1)}, u32[]{:S(2)}, u32[]{:S(2)}) collective-permute-start(bf16[2,512,1536]{2,1,0:T(8,128)(2,1)} %convolution_convert_fusion.1), channel_id=1, source_target_pairs={{0,32},{32,0},{1,33},{33,1},{2,34},{34,2},{3,35},{35,3},{4,36},{36... | collective-permute-start | bytes 9437192 | tf_op jit(solution)/shard_map/ppermute | solution.py:245
  1061.1 73.5 %all-to-all-start.23 = ((bf16[32,72,1024]{2,1,0:T(8,128)(2,1)}), bf16[32,72,1024]{2,1,0:T(8,128)(2,1)}, u32[]{:S(2)}, u32[]{:S(2)}) async-start(bf16[32,72,1024]{2,1,0:T(8,128)(2,1)} %pad_maximum_fusion), calls=%async_computation.23 | async-start | bytes 9437184 | tf_op jit(solution)/shard_map/all_to_all | solution.py:237
  1103.7 36.0 %collective-permute-start.6 = (f32[48,4,640]{2,0,1:T(8,128)}, f32[48,4,640]{2,0,1:T(8,128)}, u32[]{:S(2)}, u32[]{:S(2)}) collective-permute-start(f32[48,4,640]{2,0,1:T(8,128)} %bitcast.80), channel_id=1, source_target_pairs={{0,32},{32,0},{1,33},{33,1},{2,34},{34,2},{3,35},{35,3},{4,36},{36... | collective-permute-start | bytes 1474568 | tf_op jit(solution)/shard_map/ppermute | solution.py:245
  (183 other events, 2016.2 us)
Sparse Core Ops, SparseCore 0:
  68.1 101.7 all-gather.1

commit v3 on v2

--- a/solution.py
+++ b/solution.py
@@ -283,8 +283,6 @@
     own_part = exchange(by_head)
     fetched = ordered(own_part, twin(own_part), 1).reshape(width, part_width + 128)
     qkv_w, tail = fetched[:, :part_width], fetched[:, part_width:]
-    own_out = lax.all_gather(my_rows(w_output[0]), "shard", axis_index_groups=zy_groups)
-    output_w = ordered(own_out, twin(own_out), 1).reshape(group_width, width)
     router_w = tail[:, :experts]
     gains = tail[:, experts : experts + 2].T.astype(f32)
     gain_one, gain_two = gains[0][None], gains[1][None]
@@ -297,8 +295,15 @@
         ],
         axis=1,
     )
-    own_shared = lax.all_gather(shared_rows, "shard", axis=0, tiled=True)
+    gathered = lax.all_gather(
+        jnp.concatenate([shared_rows, my_rows(w_output[0])], axis=0), "shard"
+    )
+    own_shared = gathered[:, :rows_per].reshape(width, width)
+    own_out = lax.dynamic_slice_in_dim(
+        gathered[:, rows_per:], (position // ring) * ring, ring, axis=0
+    )
     other_shared = twin(own_shared)
+    output_w = ordered(own_out, twin(own_out), 1).reshape(group_width, width)
 
     def cut(value):
         down = value[:, shared_width:].reshape(down_rows * shards, width // 2)
@@ -360,7 +365,7 @@
     def ring_rows(rows):
         return exchange(copies(rows, heads), x_groups).reshape(heads * tokens, width)
 
-    def forward(layer_b):
+    def attend(layer_b):
         layer_in = layer_b.astype(f32)
         normed_one = (layer_in * inverse_rms(layer_in) * gain_one).astype(bf)
         ring_one = ring_rows(normed_one)
@@ -370,9 +375,18 @@
         pairs = pairs.reshape(ring, heads, micros, block, 2 * HD).transpose(2, 1, 0, 3, 4)
         cache = pairs.reshape(micros, shards * block, 2 * HD)
         attended, logs = attention_forward(info, queries, cache)
-        hidden = layer_in + sum_over_x(
-            dot(attended.reshape(heads * tokens, group_width), output_w)
-        )
+        return dict(
+            layer_b=layer_b,
+            ring_one=ring_one,
+            queries=queries,
+            cache=cache,
+            attended=attended,
+            logs=logs,
+        )
+
+    def feed(kept):
+        attended = kept["attended"].reshape(heads * tokens, group_width)
+        hidden = kept["layer_b"].astype(f32) + sum_over_x(dot(attended, output_w))
         normed_two = (hidden * inverse_rms(hidden) * gain_two).astype(bf)
         gates = gate_values(normed_two)
         expert_in = to_experts(dot_tn(pick, normed_two).astype(bf))
@@ -386,12 +400,6 @@
         shared_act = (silu_parts(shared_gate_pre)[0] * shared_up_pre).astype(bf)
         output_b = (hidden + routed + project(shared_act, down_w)).astype(bf)
         return dict(
-            layer_b=layer_b,
-            ring_one=ring_one,
-            queries=queries,
-            cache=cache,
-            attended=attended,
-            logs=logs,
             hidden=hidden,
             normed_two=normed_two,
             gates=gates,
@@ -470,101 +478,122 @@
             layer_grad=(grads["hidden_grad"] + in_norm_grad).astype(bf),
         )
 
-    first = forward(inputs[0].reshape(tokens, width))
-    second = forward(lax.ppermute(first["output_b"], "section", [(0, 1)]))
-    second_back = ffn_backward(second, cotangent[0].reshape(tokens, width))
-    second_back = attention_back(second, second_back)
-    received = lax.ppermute(second_back["layer_grad"], "section", [(1, 0)])
-    first_back = attention_back(first, ffn_backward(first, received))
-
-    kept = {name: jnp.where(is_first, first[name], second[name]) for name in KEPT}
-    back = {name: jnp.where(is_first, first_back[name], second_back[name]) for name in BACK}
-
-    expert_parts = [
-        wide_einsum("erd,erf->edf", kept["expert_in"], back["gate_pre_grad"]),
-        wide_einsum("erd,erf->edf", kept["expert_in"], back["up_pre_grad"]),
-        wide_einsum("erf,erd->efd", kept["activated"], back["expert_grad"]),
-    ]
-    expert_parts = [part.astype(bf) for part in expert_parts]
-    expert_grads = [part.astype(f32) + twin(part).astype(f32) for part in expert_parts]
-
-    def both(value):
-        return jnp.concatenate([value, twin(value)], axis=0)
-
-    def both_halves(low_half, high_half):
-        own, other = mine_of(low_half, high_half), mine_of(high_half, low_half)
-        return jnp.concatenate([own, twin(other)], axis=0)
-
-    grad_gate_up = dot_tn(
-        both(kept["normed_two"]), both_halves(back["shared_gate_grad"], back["shared_up_grad"])
-    )
-    grad_down = dot_tn(both(kept["shared_act"]), both_halves(*halves(back["upstream_b"])))
-    shared_flat = (shards, down_rows * width // 2 // shared_width, shared_width)
-    shared_pieces = jnp.concatenate(
-        [
-            grad_gate_up.astype(bf).reshape(shards, rows_per, shared_width),
-            grad_down.astype(bf).reshape(shared_flat),
-        ],
-        axis=1,
-    )
-    share_shared = jnp.sum(exchange(shared_pieces).astype(f32), axis=0)
-    other_shared = twin(share_shared)
-
-    grad_out = dot_tn(
-        kept["attended"].reshape(heads * tokens, group_width), back["ring_hidden"]
-    )
-    share_out = jnp.sum(
-        exchange(grad_out.astype(bf).reshape(ring, rows_per, width), zy_groups).astype(f32), axis=0
-    )
-    grad_qkv = dot_tn(kept["ring_one"], back["qkv_grad"])
-    grad_router = dot_tn(kept["normed_two"], back["logit_grad"])
-    gain_sums = jnp.stack([back["gain_one_grad"], back["gain_two_grad"]])
-    grad_tail = jnp.concatenate(
-        [grad_router, gain_sums.T, jnp.zeros((width, 128 - experts - 2), f32)], axis=1
-    )
-    pieces = exchange(
-        jnp.concatenate([grad_qkv, grad_tail], axis=1)
-        .astype(bf)
-        .reshape(shards, rows_per, part_width + 128)
-    ).astype(f32)
-    share_qkv = jnp.sum(
-        pieces[:, :, :part_width].reshape(heads, ring, rows_per, part_width), axis=1
-    )
-    share_qkv = share_qkv.transpose(1, 0, 2)
-    share_tail = jnp.sum(pieces[:, :, part_width:], axis=0)
-
-    def total(share):
-        return share + twin(share)
-
-    out_total, qkv_total, tail_total = total(share_out), total(share_qkv), total(share_tail)
-    low_shared, high_shared = (
-        mine_of(share_shared, other_shared),
-        mine_of(other_shared, share_shared),
-    )
-    down_shape = (down_rows, width // 2)
-    down_total = jnp.concatenate(
-        [low_shared[rows_per:].reshape(down_shape), high_shared[rows_per:].reshape(down_shape)],
-        axis=1,
+    def only(wanted, live):
+        def dead():
+            return jax.tree.map(lambda leaf: jnp.zeros(leaf.shape, leaf.dtype), jax.eval_shape(live))
+
+        return lax.cond(wanted, live, dead)
+
+    def weight_grads(kept, back):
+        expert_parts = [
+            wide_einsum("erd,erf->edf", kept["expert_in"], back["gate_pre_grad"]),
+            wide_einsum("erd,erf->edf", kept["expert_in"], back["up_pre_grad"]),
+            wide_einsum("erf,erd->efd", kept["activated"], back["expert_grad"]),
+        ]
+        expert_parts = [part.astype(bf) for part in expert_parts]
+        expert_grads = [part.astype(f32) + twin(part).astype(f32) for part in expert_parts]
+
+        def both(value):
+            return jnp.concatenate([value, twin(value)], axis=0)
+
+        def both_halves(low_half, high_half):
+            own, other = mine_of(low_half, high_half), mine_of(high_half, low_half)
+            return jnp.concatenate([own, twin(other)], axis=0)
+
+        grad_gate_up = dot_tn(
+            both(kept["normed_two"]), both_halves(back["shared_gate_grad"], back["shared_up_grad"])
+        )
+        grad_down = dot_tn(both(kept["shared_act"]), both_halves(*halves(back["upstream_b"])))
+        shared_flat = (shards, down_rows * width // 2 // shared_width, shared_width)
+        shared_pieces = jnp.concatenate(
+            [
+                grad_gate_up.astype(bf).reshape(shards, rows_per, shared_width),
+                grad_down.astype(bf).reshape(shared_flat),
+            ],
+            axis=1,
+        )
+        share_shared = jnp.sum(exchange(shared_pieces).astype(f32), axis=0)
+        other_shared = twin(share_shared)
+
+        grad_out = dot_tn(
+            kept["attended"].reshape(heads * tokens, group_width), back["ring_hidden"]
+        )
+        share_out = jnp.sum(
+            exchange(grad_out.astype(bf).reshape(ring, rows_per, width), zy_groups).astype(f32), axis=0
+        )
+        grad_qkv = dot_tn(kept["ring_one"], back["qkv_grad"])
+        grad_router = dot_tn(kept["normed_two"], back["logit_grad"])
+        gain_sums = jnp.stack([back["gain_one_grad"], back["gain_two_grad"]])
+        grad_tail = jnp.concatenate(
+            [grad_router, gain_sums.T, jnp.zeros((width, 128 - experts - 2), f32)], axis=1
+        )
+        pieces = exchange(
+            jnp.concatenate([grad_qkv, grad_tail], axis=1)
+            .astype(bf)
+            .reshape(shards, rows_per, part_width + 128)
+        ).astype(f32)
+        share_qkv = jnp.sum(
+            pieces[:, :, :part_width].reshape(heads, ring, rows_per, part_width), axis=1
+        )
+        share_qkv = share_qkv.transpose(1, 0, 2)
+        share_tail = jnp.sum(pieces[:, :, part_width:], axis=0)
+
+        def total(share):
+            return share + twin(share)
+
+        out_total, qkv_total, tail_total = total(share_out), total(share_qkv), total(share_tail)
+        low_shared, high_shared = (
+            mine_of(share_shared, other_shared),
+            mine_of(other_shared, share_shared),
+        )
+        down_shape = (down_rows, width // 2)
+        down_total = jnp.concatenate(
+            [low_shared[rows_per:].reshape(down_shape), high_shared[rows_per:].reshape(down_shape)],
+            axis=1,
+        )
+        return (
+            tail_total[:, experts],
+            qkv_total[:, :, :group_width].reshape(rows_per, head_width),
+            qkv_total[:, :, group_width : group_width + HD].reshape(rows_per, key_width),
+            qkv_total[:, :, group_width + HD :].reshape(rows_per, key_width),
+            out_total,
+            tail_total[:, experts + 1],
+            tail_total[:, :experts],
+            low_shared[:rows_per],
+            high_shared[:rows_per],
+            down_total,
+        ) + tuple(expert_grads)
+
+    def second_phase(layer_b):
+        kept = attend(layer_b)
+        kept = dict(kept, **feed(kept))
+        back = ffn_backward(kept, cotangent[0].reshape(tokens, width))
+        back = attention_back(kept, back)
+        return (
+            {name: kept[name] for name in KEPT + ("output_b",)},
+            {name: back[name] for name in BACK + ("layer_grad",)},
+        )
+
+    def first_last(kept, received):
+        back = attention_back(kept, ffn_backward(kept, received))
+        return (back["layer_grad"], kept["output_b"]) + weight_grads(kept, back)
+
+    def second_last(kept, back):
+        return (back["layer_grad"], kept["output_b"]) + weight_grads(kept, back)
+
+    first = attend(inputs[0].reshape(tokens, width))
+    first = dict(first, **only(is_first, lambda: feed(first)))
+    received = lax.ppermute(first["output_b"], "section", [(0, 1)])
+    second, second_back = only(jnp.logical_not(is_first), lambda: second_phase(received))
+    received_back = lax.ppermute(second_back["layer_grad"], "section", [(1, 0)])
+    layer_grad, output_b, *weight_totals = lax.cond(
+        is_first,
+        lambda: first_last(first, received_back),
+        lambda: second_last(second, second_back),
     )
     token_shape = (1, 1, micros, block, width)
-    return (
-        jnp.where(is_first, first["output_b"], second["output_b"]).reshape(token_shape),
-        jnp.where(is_first, first_back["layer_grad"], second_back["layer_grad"]).reshape(
-            token_shape
-        ),
-        tail_total[:, experts][None],
-        qkv_total[:, :, :group_width].reshape(1, rows_per, head_width),
-        qkv_total[:, :, group_width : group_width + HD].reshape(1, rows_per, key_width),
-        qkv_total[:, :, group_width + HD :].reshape(1, rows_per, key_width),
-        out_total[None],
-        tail_total[:, experts + 1][None],
-        tail_total[:, :experts][None],
-        low_shared[:rows_per][None],
-        high_shared[:rows_per][None],
-        down_total[None],
-        expert_grads[0][None],
-        expert_grads[1][None],
-        expert_grads[2][None],
+    return (output_b.reshape(token_shape), layer_grad.reshape(token_shape)) + tuple(
+        value[None] for value in weight_totals
     )
 
 

time: 1180 us -> 1210 us (1.025)
  waiting for transfers between devices: 360 us -> 632 us
  starting transfers between devices: 157 us -> 74.9 us
  blocking collectives: 229 us -> 154 us
  matrix products: 164 us -> 103 us
  loops' own time: 0 us -> 22.5 us
  Pallas kernels: 45.6 us -> 23.8 us
  other arithmetic: 83.4 us -> 63.9 us
    ppermute x2, waiting for transfers between devices: 16.4 us -> 428 us  [the longest x1 426 us: body(): received_back = lax.ppermute(second_back['layer_grad'], 'section', [(1, 0)])]
    all_to_all x18 -> x10, waiting for transfers between devices: 339 us -> 136 us  [exchange(): lax.all_to_all(value, 'shard', split_axis=0, concat_axis=0, tiled=True, a...]
    all_to_all x18 -> x10, starting transfers between devices: 128 us -> 56.3 us  [exchange(): lax.all_to_all(value, 'shard', split_axis=0, concat_axis=0, tiled=True, a...]
    all_gather x1, waiting for transfers between devices: 0.02 us -> 64.4 us  [body(): lax.all_gather(jnp.concatenate([shared_rows, my_rows(w_output[0])], axis=...]
    all_gather x1 -> x0, blocking collectives: 58.9 us -> none  [body(): lax.all_gather(my_rows(w_output[0]), 'shard', axis_index_groups=zy_groups)]
    cond x0 -> x120, local copies, waits for them, and re-layouts: none -> 30.4 us
    dot_general x23 -> x13, matrix products: 54.8 us -> 26 us  [dot(): return jnp.dot(left_side, right_side, preferred_element_type=f32)]
    another operation x0 -> x3, loops' own time: none -> 22.5 us  [the longest x2 15.6 us: only(): return lax.cond(wanted, live, dead)]
  transfers between devices with their start and end apart: 35 -> 27, of which waited for: 20 -> 13; matrix products, arithmetic and copies ran while one was open for 20% -> 15% of each run, Pallas kernels for 2% -> 2%
where the time goes in v3:
time: 1210 us; the launch traced here: 1200 us
  waiting for transfers between devices  632 us (52%)
  blocking collectives  154 us (13%)
  local copies, waits for them, and re-layouts  110 us (9%)
  matrix products  103 us (9%)
  starting transfers between devices  74.9 us (6%)
  other arithmetic  63.9 us (5%)
  Pallas kernels  23.8 us (2%)
  loops' own time  22.5 us (2%)
  between operations  14.9 us (1%)
    ppermute x1, waiting for transfers between devices, body(): received_back = lax.ppermute(second_back['layer_grad'], 'section', [(1, 0)])  426 us
    all_to_all x4, blocking collectives, exchange(): lax.all_to_all(value, 'shard', split_axis=0, concat_axis=0, tiled=True, a...  154 us
    all_to_all x10, waiting for transfers between devices, exchange(): lax.all_to_all(value, 'shard', split_axis=0, concat_axis=0, tiled=True, a...  136 us
    all_gather x1, waiting for transfers between devices, body(): lax.all_gather(jnp.concatenate([shared_rows, my_rows(w_output[0])], axis=...  64.4 us
    all_to_all x10, starting transfers between devices, exchange(): lax.all_to_all(value, 'shard', split_axis=0, concat_axis=0, tiled=True, a...  56.3 us
    dot_general x9, matrix products, wide_einsum(): jnp.einsum(formula, left_side, right_side, preferred_element_type=f32)  39.2 us
    cond x120, local copies, waits for them, and re-layouts  30.4 us
    dot_general x13, matrix products, dot(): return jnp.dot(left_side, right_side, preferred_element_type=f32)  26 us
  transfers between devices with their start and end apart: 27, of which 13 were waited for; matrix products, arithmetic and copies ran while one was open for 15% of the time, Pallas kernels for 2%

profile of v3, /device:TPU:1, one launch (start us, length us, event | category | flops | bytes accessed | tf_op | source)
XLA Modules:
  0.0 1199.0 jit_solution(13991054958407703740)
XLA Ops:
  17.9 32.8 %all_to_all.115 = bf16[32,24,768]{2,1,0:T(8,128)(2,1)S(1)} all-to-all(bf16[32,24,768]{2,1,0:T(8,128)(2,1)S(1)} %bitcast.344), channel_id=1, replica_groups=mesh['section'=2,'dp'=2,'shard'=32] {'shard'}, dimensions={0} | all-to-all | bytes 2359296 | tf_op jit(solution)/shard_map/all_to_all | solution.py:237
  56.9 64.4 %all-gather.3.cloned.1.call-done = bf16[2304,1536]{1,0:T(8,128)(2,1)} async-done(((bf16[72,1536]{1,0:T(8,128)(2,1)}), bf16[2304,1536]{1,0:T(8,128)(2,1)}) %all-gather.3.cloned.1.call-update) | async-done | bytes 7077904 | tf_op jit(solution)/shard_map/all_gather | solution.py:298
  127.5 24.3 %all_to_all.116 = bf16[4,128,1536]{2,1,0:T(8,128)(2,1)S(1)} all-to-all(bf16[4,128,1536]{2,1,0:T(8,128)(2,1)S(1)} %broadcast_in_dim.185), channel_id=1, replica_groups={{0,8,16,24},{1,9,17,25},{2,10,18,26},{3,11,19,27},{4,12,20,28},{5,13,21..., dimensions={0} | all-to-all | bytes 3145728 | tf_op jit(solution)/shard_map/all_to_all | solution.py:237
  167.9 18.7 %all-to-all-done.26 = bf16[8,512,256]{2,1,0:T(8,128)(2,1)} async-done(((bf16[8,512,256]{2,1,0:T(8,128)(2,1)}), bf16[8,512,256]{2,1,0:T(8,128)(2,1)}, u32[]{:S(2)}, u32[]{:S(2)}) %all-to-all-start.26) | async-done | bytes 2097184 | tf_op jit(solution)/shard_map/all_to_all | solution.py:237
  188.5 7.2 shard_map.272
  218.7 157.9 %conditional.3 = (bf16[2,512,512]{2,1,0:T(8,128)(2,1)}, bf16[2,512,1536]{2,1,0:T(8,128)(2,1)}, f32[2,512,512]{2,1,0:T(8,128)}, f32[128,1024]{1,0:T(8,128)}, f32[...) conditional(s32[]{:T(128)} %convert_element_type.356, () %tuple.59, ...), branch_computations={%region_2.3_spmd, %region_3.8_spmd} | conditional | flops 8268152832 | bytes 183000032 | solution.py:485
  226.6 17.3 %all-to-all-done = bf16[4,128,1536]{2,1,0:T(8,128)(2,1)} async-done(((bf16[4,128,1536]{2,1,0:T(8,128)(2,1)}), bf16[4,128,1536]{2,1,0:T(8,128)(2,1)}, u32[]{:S(2)}, u32[]{:S(2)}) %all-to-all-start) | async-done | bytes 1572896 | tf_op jit(solution)/shard_map/cond/branch_1_fun/all_to_all | solution.py:237
  250.7 45.6 %all_to_all.111 = bf16[32,2,16,1536]{3,2,1,0:T(8,128)(2,1)S(1)} all-to-all(bf16[32,2,16,1536]{3,2,1,0:T(8,128)(2,1)S(1)} %bitcast.308), channel_id=1, replica_groups=mesh['section'=2,'dp'=2,'shard'=32] {'shard'}, dimensions={0} | all-to-all | bytes 6291456 | tf_op jit(solution)/shard_map/cond/branch_1_fun/all_to_all | solution.py:237
  332.3 30.1 %all-to-all-done.2 = bf16[32,2,16,1536]{3,2,1,0:T(8,128)(2,1)} async-done(((bf16[32,2,16,1536]{3,2,1,0:T(8,128)(2,1)}), bf16[32,2,16,1536]{3,2,1,0:T(8,128)(2,1)}, u32[]{:S(2)}, u32[]{:S(2)}) %all-to-all-start.2) | async-done | bytes 3145760 | tf_op jit(solution)/shard_map/cond/branch_1_fun/all_to_all | solution.py:237
  383.5 21.8 %conditional.4 = (bf16[2,512,512]{2,1,0:T(8,128)(2,1)S(1)}, bf16[4,2,64,384]{3,2,1,0:T(8,128)(2,1)S(1)}, bf16[2,512,1536]{2,1,0:T(8,128)(2,1)}, bf16[128,1536]{1...) conditional(s32[]{:T(128)} %convert_element_type.357, () %tuple.58, ...), branch_computations={%region_8.9_spmd, %region_9.22_spmd} | conditional | flops 24623452160 | bytes 554140224 | solution.py:485
  406.6 426.2 %collective-permute-done.26 = bf16[128,1536]{1,0:T(8,128)(2,1)S(1)} collective-permute-done((bf16[128,1536]{1,0:T(8,128)(2,1)S(1)}, bf16[128,1536]{1,0:T(8,128)(2,1)S(1)}, u32[]{:S(2)}, u32[]{:S(2)}) %collective-permute-start.26) | collective-permute-done | bytes 393248 | tf_op jit(solution)/shard_map/ppermute | solution.py:588
  832.7 358.2 %conditional.5 = (bf16[128,1536]{1,0:T(8,128)(2,1)}, bf16[128,1536]{1,0:T(8,128)(2,1)}, f32[1,48]{1,0:T(1,128)S(1)}, f32[1,48,1536]{2,1,0:T(8,128)S(1)}, f32[1,4...) conditional(s32[]{:T(128)} %convert_element_type.356, ...), branch_computations={%region_22.27_spmd, %region_27.41_spmd} | conditional | flops 21469503488 | bytes 597697664 | solution.py:589
  842.9 51.3 %all_to_all.114 = bf16[32,2,16,1536]{3,2,1,0:T(8,128)(2,1)S(1)} all-to-all(bf16[32,2,16,1536]{3,2,1,0:T(8,128)(2,1)S(1)} %bitcast.318), channel_id=1, replica_groups=mesh['section'=2,'dp'=2,'shard'=32] {'shard'}, dimensions={0} | all-to-all | bytes 6291456 | tf_op jit(solution)/shard_map/cond/branch_1_fun/all_to_all | solution.py:237
  929.7 23.6 %all-to-all-done.17 = bf16[32,2,16,1536]{3,2,1,0:T(8,128)(2,1)} async-done(((bf16[32,2,16,1536]{3,2,1,0:T(8,128)(2,1)}), bf16[32,2,16,1536]{3,2,1,0:T(8,128)(2,1)}, u32[]{:S(2)}, u32[]{:S(2)}) %all-to-all-start.17) | async-done | bytes 3145760 | tf_op jit(solution)/shard_map/cond/branch_1_fun/all_to_all | solution.py:237
  988.7 7.8 all-to-all-start.23
  1007.4 16.5 %branch_1_fun.5 = (bf16[4,2,64,384]{3,2,1,0:T(8,128)(2,1)S(1)}, f32[2,2048,256]{2,1,0:T(8,128)S(1)}) custom-call(s32[1]{0:T(128)} %get-tuple-element.269.info_ref, bf16[4,2,64,384]{3,2,1,0:T(8,128)(2,1)S(1)} %copy-done.105, bf16[4,2,64,384]{3,2,1,0:T(8,128)(2,1)S(1)} %bitcast.306, bf16[4,2,64,384]{3,2,1,0:T(8,128)(2,1)S(1)} %copy-done.102, ...), custom_call_target="tpu_custom_call" | custom-call | flops 4026531840 | bytes 3604480 | tf_op jit(solution)/shard_map/cond/branch_1_fun/pallas_call | solution.py:165
  1025.6 30.3 %all-to-all-done.23 = bf16[32,72,1024]{2,1,0:T(8,128)(2,1)} async-done(((bf16[32,72,1024]{2,1,0:T(8,128)(2,1)}), bf16[32,72,1024]{2,1,0:T(8,128)(2,1)}, u32[]{:S(2)}, u32[]{:S(2)}) %all-to-all-start.23) | async-done | bytes 4718624 | tf_op jit(solution)/shard_map/cond/branch_1_fun/all_to_all | solution.py:237
  1100.1 6.6 add_bitcast_fusion.6
  1108.6 9.1 all-to-all-done.20
  1117.6 7.0 all-to-all-start.22
  1157.0 6.5 add_bitcast_fusion.4
  1163.6 6.6 copy.290
  1170.1 6.6 copy.292
  1176.7 6.6 copy.294
  (376 shorter events, 316.4 us)
Async XLA Ops:
  7.2 114.1 %all-gather.3.cloned.1.call-start = ((), (), s32[]{:S(2)}) async-start(), calls=%async_computation.27 | async-start | bytes 7299072 | tf_op jit(solution)/shard_map/all_gather | solution.py:298
  50.7 4.0 collective-permute-start.22
  126.1 82.2 %collective-permute-start.24 = (bf16[1536,1536]{1,0:T(8,128)(2,1)}, bf16[1536,1536]{1,0:T(8,128)(2,1)}, u32[]{:S(2)}, u32[]{:S(2)}) collective-permute-start(bf16[1536,1536]{1,0:T(8,128)(2,1)} %bitcast.115), channel_id=1, source_target_pairs={{0,32},{32,0},{1,33},{33,1},{2,34},{34,2},{3,35},{35,3},{4,36},{36... | collective-permute-start | bytes 14155784 | tf_op jit(solution)/shard_map/ppermute | solution.py:245
  154.8 31.8 %all-to-all-start.26 = ((bf16[8,512,256]{2,1,0:T(8,128)(2,1)}), bf16[8,512,256]{2,1,0:T(8,128)(2,1)}, u32[]{:S(2)}, u32[]{:S(2)}) async-start(bf16[8,512,256]{2,1,0:T(8,128)(2,1)} %broadcast_in_dim.186), calls=%async_computation.26 | async-start | bytes 4194304 | tf_op jit(solution)/shard_map/all_to_all | solution.py:237
  162.6 43.3 %collective-permute-start.23 = (bf16[8,24,1536]{2,1,0:T(8,128)(2,1)}, bf16[8,24,1536]{2,1,0:T(8,128)(2,1)}, u32[]{:S(2)}, u32[]{:S(2)}) collective-permute-start(bf16[8,24,1536]{2,1,0:T(8,128)(2,1)} %constant_dynamic-slice_fusion), channel_id=1, source_target_pairs={{0,32},{32,0},{1,33},{33,1},{2,34},{34,2},{3,35},{35,3},{4,36},{36... | collective-permute-start | bytes 1769480 | tf_op jit(solution)/shard_map/ppermute | solution.py:245
  220.8 23.1 %all-to-all-start = ((bf16[4,128,1536]{2,1,0:T(8,128)(2,1)}), bf16[4,128,1536]{2,1,0:T(8,128)(2,1)}, u32[]{:S(2)}, u32[]{:S(2)}) async-start(bf16[4,128,1536]{2,1,0:T(8,128)(2,1)} %bitcast.342), calls=%async_computation | async-start | bytes 3145728 | tf_op jit(solution)/shard_map/cond/branch_1_fun/all_to_all | solution.py:237
  315.7 46.7 %all-to-all-start.2 = ((bf16[32,2,16,1536]{3,2,1,0:T(8,128)(2,1)}), bf16[32,2,16,1536]{3,2,1,0:T(8,128)(2,1)}, u32[]{:S(2)}, u32[]{:S(2)}) async-start(bf16[32,2,16,1536]{3,2,1,0:T(8,128)(2,1)} %bitcast.313), calls=%async_computation.2 | async-start | bytes 6291456 | tf_op jit(solution)/shard_map/cond/branch_1_fun/all_to_all | solution.py:237
  376.6 6.8 collective-permute-start.25
  405.3 427.5 %collective-permute-start.26 = (bf16[128,1536]{1,0:T(8,128)(2,1)S(1)}, bf16[128,1536]{1,0:T(8,128)(2,1)S(1)}, u32[]{:S(2)}, u32[]{:S(2)}) collective-permute-start(bf16[128,1536]{1,0:T(8,128)(2,1)S(1)} %get-tuple-element.368), channel_id=1, source_target_pairs={{64,0},{65,1},{66,2},{67,3},{68,4},{69,5},{70,6},{71,7},{72,8},{73... | collective-permute-start | bytes 1179656 | tf_op jit(solution)/shard_map/ppermute | solution.py:588
  908.4 44.9 %all-to-all-start.17 = ((bf16[32,2,16,1536]{3,2,1,0:T(8,128)(2,1)}), bf16[32,2,16,1536]{3,2,1,0:T(8,128)(2,1)}, u32[]{:S(2)}, u32[]{:S(2)}) async-start(bf16[32,2,16,1536]{3,2,1,0:T(8,128)(2,1)} %bitcast.311), calls=%async_computation.17 | async-start | bytes 6291456 | tf_op jit(solution)/shard_map/cond/branch_1_fun/all_to_all | solution.py:237
  962.7 24.8 %all-to-all-start.18 = ((bf16[4,128,1536]{2,1,0:T(8,128)(2,1)}), bf16[4,128,1536]{2,1,0:T(8,128)(2,1)S(1)}, u32[]{:S(2)}, u32[]{:S(2)}) async-start(bf16[4,128,1536]{2,1,0:T(8,128)(2,1)} %broadcast_in_dim.163), calls=%async_computation.18 | async-start | bytes 3145728 | tf_op jit(solution)/shard_map/cond/branch_1_fun/all_to_all | solution.py:237
  968.4 4.1 collective-permute-start.16
  970.2 8.0 collective-permute-start.14
  970.7 7.4 collective-permute-start.15
  988.7 67.2 %all-to-all-start.23 = ((bf16[32,72,1024]{2,1,0:T(8,128)(2,1)}), bf16[32,72,1024]{2,1,0:T(8,128)(2,1)}, u32[]{:S(2)}, u32[]{:S(2)}) async-start(bf16[32,72,1024]{2,1,0:T(8,128)(2,1)} %pad_maximum_fusion.2), calls=%async_computation.23 | async-start | bytes 9437184 | tf_op jit(solution)/shard_map/cond/branch_1_fun/all_to_all | solution.py:237
  1004.0 96.0 %collective-permute-start.19 = (bf16[2,1536,512]{1,2,0:T(8,128)(2,1)}, bf16[2,1536,512]{1,2,0:T(8,128)(2,1)}, u32[]{:S(2)}, u32[]{:S(2)}) collective-permute-start(bf16[2,1536,512]{1,2,0:T(8,128)(2,1)} %fusion.65), channel_id=1, source_target_pairs={{0,32},{32,0},{1,33},{33,1},{2,34},{34,2},{3,35},{35,3},{4,36},{36... | collective-permute-start | bytes 9437192 | tf_op jit(solution)/shard_map/cond/branch_1_fun/ppermute | solution.py:245
  1055.9 32.1 %all-to-all-start.19 = ((bf16[8,512,256]{2,1,0:T(8,128)(2,1)}), bf16[8,512,256]{2,1,0:T(8,128)(2,1)S(1)}, u32[]{:S(2)}, u32[]{:S(2)}) async-start(bf16[8,512,256]{2,1,0:T(8,128)(2,1)} %bitcast.336), calls=%async_computation.19 | async-start | bytes 4194304 | tf_op jit(solution)/shard_map/cond/branch_1_fun/all_to_all | solution.py:237
  1070.8 76.6 %collective-permute-start.20 = (bf16[2,1536,512]{1,2,0:T(8,128)(2,1)}, bf16[2,1536,512]{1,2,0:T(8,128)(2,1)}, u32[]{:S(2)}, u32[]{:S(2)}) collective-permute-start(bf16[2,1536,512]{1,2,0:T(8,128)(2,1)} %fusion.66), channel_id=1, source_target_pairs={{0,32},{32,0},{1,33},{33,1},{2,34},{34,2},{3,35},{35,3},{4,36},{36... | collective-permute-start | bytes 9437192 | tf_op jit(solution)/shard_map/cond/branch_1_fun/ppermute | solution.py:245
  1077.7 5.4 collective-permute-start.18
  1082.7 74.3 %collective-permute-start.21 = (bf16[2,512,1536]{1,2,0:T(8,128)(2,1)}, bf16[2,512,1536]{1,2,0:T(8,128)(2,1)}, u32[]{:S(2)}, u32[]{:S(2)}) collective-permute-start(bf16[2,512,1536]{1,2,0:T(8,128)(2,1)} %fusion.67), channel_id=1, source_target_pairs={{0,32},{32,0},{1,33},{33,1},{2,34},{34,2},{3,35},{35,3},{4,36},{36... | collective-permute-start | bytes 9437192 | tf_op jit(solution)/shard_map/cond/branch_1_fun/ppermute | solution.py:245
  1093.2 24.4 %all-to-all-start.20 = ((bf16[4,128,1536]{2,1,0:T(8,128)(2,1)}), bf16[4,128,1536]{2,1,0:T(8,128)(2,1)S(1)}, u32[]{:S(2)}, u32[]{:S(2)}) async-start(bf16[4,128,1536]{2,1,0:T(8,128)(2,1)} %bitcast.370), calls=%async_computation.20 | async-start | bytes 3145728 | tf_op jit(solution)/shard_map/cond/branch_1_fun/all_to_all | solution.py:237
  1117.6 23.9 %all-to-all-start.22 = ((bf16[8,48,1536]{2,1,0:T(8,128)(2,1)}), bf16[8,48,1536]{2,1,0:T(8,128)(2,1)}, u32[]{:S(2)}, u32[]{:S(2)}) async-start(bf16[8,48,1536]{2,1,0:T(8,128)(2,1)} %bitcast.377), calls=%async_computation.22 | async-start | bytes 2359296 | tf_op jit(solution)/shard_map/cond/branch_1_fun/all_to_all | solution.py:237
  1141.5 43.4 %all-to-all-start.21 = ((bf16[32,48,768]{2,1,0:T(8,128)(2,1)}), bf16[32,48,768]{2,1,0:T(8,128)(2,1)S(1)}, u32[]{:S(2)}, u32[]{:S(2)}) async-start(bf16[32,48,768]{2,1,0:T(8,128)(2,1)} %maximum_maximum_fusion.1), calls=%async_computation.21 | async-start | bytes 4718592 | tf_op jit(solution)/shard_map/cond/branch_1_fun/all_to_all | solution.py:237
  1155.3 28.0 %collective-permute-start.13 = (f32[48,1536]{1,0:T(8,128)S(1)}, f32[48,1536]{1,0:T(8,128)}, u32[]{:S(2)}, u32[]{:S(2)}) collective-permute-start(f32[48,1536]{1,0:T(8,128)S(1)} %convert_reduce_fusion.7), channel_id=1, source_target_pairs={{0,32},{32,0},{1,33},{33,1},{2,34},{34,2},{3,35},{35,3},{4,36},{36... | collective-permute-start | bytes 884744 | tf_op jit(solution)/shard_map/cond/branch_1_fun/ppermute | solution.py:245
  (81 other events, 1261.7 us)
Sparse Core Ops, SparseCore 0:
  12.6 108.6 all-gather.2

commit v4 on v2

v4 whole, which is shorter than its diff:
```python
import functools

import jax
import jax.numpy as jnp
from jax import lax
from jax.experimental import pallas as pl
from jax.experimental.pallas import tpu as pltpu
from jax.sharding import PartitionSpec as P

H = 12
KVH = 4
HD = 128
GROUP = H // KVH
TOPK = 6
CAP = 8

epsilon = 1e-05
masked_score = -1e30
scaling = HD ** (-0.5)
log2_scale = scaling * 1.4426950408889634
bf = jnp.bfloat16
f32 = jnp.float32
VMEM_LIMIT = 32 * 1024 * 1024


def inverse_rms(rows):
    return lax.rsqrt(jnp.mean(rows * rows, axis=-1, keepdims=True) + epsilon)


def norm_back(layer_in, gain, upstream):
    inverse = inverse_rms(layer_in)
    unit_rows = layer_in * inverse
    gain_grad = jnp.sum(upstream * unit_rows, axis=0)
    scaled = upstream * gain
    in_grad = inverse * (scaled - unit_rows * jnp.mean(scaled * unit_rows, axis=-1, keepdims=True))
    return (in_grad, gain_grad)


def silu_parts(argument):
    sigmoid = jax.nn.sigmoid(argument)
    return argument * sigmoid, sigmoid * (1.0 + argument * (1.0 - sigmoid))


def dot(left_side, right_side):
    return jnp.dot(left_side, right_side, preferred_element_type=f32)


def dot_nt(left_side, right_side):
    return lax.dot_general(
        left_side, right_side, (((1,), (1,)), ((), ())), preferred_element_type=f32
    )


def dot_tn(left_side, right_side):
    return lax.dot_general(
        left_side, right_side, (((0,), (0,)), ((), ())), preferred_element_type=f32
    )


def wide_einsum(formula, left_side, right_side):
    return jnp.einsum(formula, left_side, right_side, preferred_element_type=f32)


def stacked_heads(ref, part):
    return jnp.concatenate(
        [ref[part, :, g * HD : (g + 1) * HD] for g in range(GROUP)], axis=0
    )


def store_heads(ref, part, rows):
    block = ref.shape[1]
    for g in range(GROUP):
        ref[part, :, g * HD : (g + 1) * HD] = rows[g * block : (g + 1) * block]


def cached(ref, start, stop, column):
    rows = ref[:, start:stop, column : column + HD]
    return rows.reshape(rows.shape[0] * rows.shape[1], HD)


def diagonal_mask(rows, chunk, block, zy):
    key_at = lax.broadcasted_iota(jnp.int32, (rows, chunk), 1)
    row_at = lax.broadcasted_iota(jnp.int32, (rows, chunk), 0)
    return key_at <= zy * block + lax.rem(row_at, block)


def attention_forward_kernel(has_prev, info_ref, q_ref, *refs):
    prev_ref = refs[0] if has_prev else None
    cur_ref, o_ref, log_ref = refs[-3:]
    parts, block, _ = q_ref.shape
    rows = GROUP * block
    mask = diagonal_mask(rows, cur_ref.shape[0] * block, block, info_ref[0])
    for part in range(parts):
        queries = stacked_heads(q_ref, part)
        pieces = [(prev_ref, 0, parts * block)] if has_prev else []
        if part > 0:
            pieces.append((cur_ref, 0, part * block))
        pieces.append((cur_ref, part * block, (part + 1) * block))
        scores = [dot_nt(queries, cached(ref, start, stop, 0)) for ref, start, stop in pieces]
        if has_prev:
            scores[0] = scores[0] + jnp.where(info_ref[1] > 0, 0.0, masked_score).astype(f32)
        scores[-1] = jnp.where(mask, scores[-1], masked_score)
        peak = functools.reduce(
            jnp.maximum, [jnp.max(s, axis=-1, keepdims=True) for s in scores]
        )
        peak = peak * log2_scale
        total = jnp.zeros((rows, 1), f32)
        mixed = jnp.zeros((rows, HD), f32)
        for s, (ref, start, stop) in zip(scores, pieces):
            probs = jnp.exp2(s * log2_scale - peak)
            total = total + jnp.sum(probs, axis=-1, keepdims=True)
            mixed = mixed + dot(probs.astype(bf), cached(ref, start, stop, HD))
        store_heads(o_ref, part, (mixed / total).astype(bf))
        log_ref[part] = jnp.broadcast_to(peak + jnp.log2(total), (rows, HD))


def attention_backward_kernel(has_prev, has_carry, info_ref, q_ref, do_ref, o_ref, log_ref, *refs):
    refs = list(refs)
    sum_ref = refs.pop()
    carry_ref = refs.pop(0) if has_carry else None
    prev_ref = refs.pop(0) if has_prev else None
    cur_ref, dq_ref, dcur_ref = refs[:3]
    dprev_ref = refs[3] if has_prev else None
    sum_ref[...] = carry_ref[...] if has_carry else jnp.zeros(sum_ref.shape, f32)
    if has_prev:
        dprev_ref[...] = jnp.zeros(dprev_ref.shape, f32)
    parts, block, _ = q_ref.shape
    ring = cur_ref.shape[0]
    rows = GROUP * block
    mask = diagonal_mask(rows, ring * block, block, info_ref[0])
    for part in range(parts):
        queries = stacked_heads(q_ref, part)
        out_grad = stacked_heads(do_ref, part)
        out = stacked_heads(o_ref, part)
        inner = jnp.sum(out_grad.astype(f32) * out.astype(f32), axis=-1, keepdims=True)
        log_total = log_ref[part][:, :1]
        query_grad = jnp.zeros((rows, HD), f32)
        pieces = []
        if has_prev:
            log_prev = log_total + jnp.where(info_ref[1] > 0, 0.0, -masked_score).astype(f32)
            pieces = [(prev_ref, dprev_ref, p, log_prev) for p in range(parts)]
        pieces += [(cur_ref, sum_ref, p, log_total) for p in range(part + 1)]
        for ref, grad_ref, at, log_row in pieces:
            start, stop = at * block, (at + 1) * block
            keys = cached(ref, start, stop, 0)
            probs = jnp.exp2(dot_nt(queries, keys) * log2_scale - log_row)
            if ref is cur_ref and at == part:
                probs = jnp.where(mask, probs, 0.0)
            probs_grad = dot_nt(out_grad, cached(ref, start, stop, HD))
            score_grad = (probs * (probs_grad - inner)).astype(bf)
            query_grad = query_grad + dot(score_grad, keys)
            key_grad = dot_tn(score_grad, queries) * scaling
            value_grad = dot_tn(probs.astype(bf), out_grad)
            grad_ref[:, start:stop, :HD] += key_grad.reshape(ring, block, HD)
            grad_ref[:, start:stop, HD:] += value_grad.reshape(ring, block, HD)
        store_heads(dq_ref, part, (query_grad * scaling).astype(bf))
    dcur_ref[...] = sum_ref[...].astype(bf)


def attention_call(kernel, factor, out_shape, scratch, info, queries, *rest):
    parts, block, _ = queries.shape
    rows = parts * GROUP * block
    keys = sum(ref.shape[0] * ref.shape[1] for ref in rest if ref.shape == rest[-1].shape)
    in_vmem = pl.BlockSpec(memory_space=pltpu.VMEM)
    return pl.pallas_call(
        kernel,
        out_shape=out_shape,
        in_specs=[pl.BlockSpec(memory_space=pltpu.SMEM)] + [in_vmem] * (1 + len(rest)),
        out_specs=(in_vmem,) * len(out_shape),
        scratch_shapes=scratch,
        compiler_params=pltpu.CompilerParams(vmem_limit_bytes=VMEM_LIMIT),
        cost_estimate=pl.CostEstimate(
            flops=factor * rows * keys * HD,
            bytes_accessed=factor * (keys + rows) * HD,
            transcendentals=rows * keys // 2,
        ),
    )(info, queries, *rest)


def attention_forward(info, qkv, prev, cur):
    parts, block, _ = qkv.shape
    shapes = (
        jax.ShapeDtypeStruct((parts, block, GROUP * HD), bf),
        jax.ShapeDtypeStruct((parts, GROUP * block, HD), f32),
    )
    caches = (cur,) if prev is None else (prev, cur)
    kernel = functools.partial(attention_forward_kernel, prev is not None)
    return attention_call(kernel, 2, shapes, [], info, qkv, *caches)


def attention_backward(info, qkv, out_grad, out, logs, carry, prev, cur):
    shapes = (jax.ShapeDtypeStruct(out.shape, bf), jax.ShapeDtypeStruct(cur.shape, bf))
    if prev is not None:
        shapes += (jax.ShapeDtypeStruct(cur.shape, f32),)
    extra = tuple(value for value in (carry, prev) if value is not None)
    kernel = functools.partial(attention_backward_kernel, prev is not None, carry is not None)
    scratch = [pltpu.VMEM(cur.shape, f32)]
    return attention_call(
        kernel, 5, shapes, scratch, info, qkv, out_grad, out, logs, *extra, cur
    )


def body(
    inputs,
    cotangent,
    routes,
    norm_attn,
    w_query,
    w_key,
    w_value,
    w_output,
    norm_ffn,
    w_router,
    shared_gate,
    shared_up,
    shared_down,
    expert_gate,
    expert_up,
    expert_down,
):
    micros, block, width = inputs.shape[1:]
    shards = lax.axis_size("shard")
    section = lax.axis_index("section")
    core = lax.axis_index("dp")
    position = lax.axis_index("shard")
    heads = KVH
    ring = shards // heads
    local_experts = expert_gate.shape[1]
    experts = local_experts * shards
    slots = experts * CAP
    rows_per = w_query.shape[1]
    half_rows = rows_per // 2
    group_width = GROUP * HD
    head_width = H * HD
    key_width = KVH * HD
    part_width = group_width + 2 * HD
    shared_width = shared_gate.shape[2]
    down_rows = shared_down.shape[1]
    is_first = section == 0
    low_core = core == 0
    x_groups = [[x * ring + zy for x in range(heads)] for zy in range(ring)]
    zy_groups = [[x * ring + zy for zy in range(ring)] for x in range(heads)]

    def exchange(value, groups=None):
        return lax.all_to_all(
            value, "shard", split_axis=0, concat_axis=0, tiled=True, axis_index_groups=groups
        )

    def copies(value, count):
        return jnp.broadcast_to(value[None], (count,) + value.shape)

    def twin(value):
        return lax.ppermute(value, "dp", [(0, 1), (1, 0)])

    def mine_of(low_half, high_half):
        return jnp.where(low_core, low_half, high_half)

    def ordered(own, other, axis):
        low_half, high_half = mine_of(own, other), mine_of(other, own)
        return jnp.concatenate([low_half, high_half], axis=axis)

    def halves(value):
        half = value.shape[-1] // 2
        return value[..., :half], value[..., half:]

    def my_rows(value):
        return mine_of(value[..., :half_rows, :], value[..., half_rows:, :])

    tail = jnp.concatenate(
        [
            w_router[0],
            norm_attn[0][:, None],
            norm_ffn[0][:, None],
            jnp.zeros((rows_per, 128 - experts - 2), bf),
        ],
        axis=1,
    )
    by_head = jnp.concatenate(
        [
            w_query[0].reshape(rows_per, heads, group_width),
            w_key[0].reshape(rows_per, heads, HD),
            w_value[0].reshape(rows_per, heads, HD),
            jnp.broadcast_to(tail[:, None], (rows_per, heads, 128)),
        ],
        axis=2,
    ).transpose(1, 0, 2)
    by_head = my_rows(by_head)
    by_head = jnp.broadcast_to(
        by_head[:, None], (heads, ring, half_rows, part_width + 128)
    ).reshape(shards, half_rows, part_width + 128)
    own_part = exchange(by_head)
    fetched = ordered(own_part, twin(own_part), 1).reshape(width, part_width + 128)
    qkv_w, tail = fetched[:, :part_width], fetched[:, part_width:]
    router_w = tail[:, :experts]
    gains = tail[:, experts : experts + 2].T.astype(f32)
    gain_one, gain_two = gains[0][None], gains[1][None]

    down_half = down_rows // 2
    down_flat = (half_rows, down_half * width // half_rows)
    packed = jnp.concatenate(
        [
            my_rows(jnp.concatenate([shared_gate[0], shared_up[0], w_output[0]], axis=1)),
            mine_of(shared_down[0][:down_half], shared_down[0][down_half:]).reshape(down_flat),
        ],
        axis=1,
    )
    gathered = lax.all_gather(packed, "shard")
    ends = (2 * shared_width, 2 * shared_width + width)
    own_gate_up = gathered[:, :, : ends[0]]
    own_down = gathered[:, :, ends[1] :].reshape(shards, down_half, width)
    own_out = lax.dynamic_slice_in_dim(
        gathered[:, :, ends[0] : ends[1]], (position // ring) * ring, ring, axis=0
    )
    output_w = ordered(own_out, twin(own_out), 1).reshape(group_width, width)
    gate_up_w = ordered(own_gate_up, twin(own_gate_up), 1).reshape(width, 2 * shared_width)
    down_w = ordered(own_down, twin(own_down), 1).reshape(shards * down_rows, width)

    expert_g, expert_u, expert_d = expert_gate[0], expert_up[0], expert_down[0]
    slot_of = jnp.arange(slots, dtype=jnp.int32)
    expert_of = jnp.arange(experts, dtype=jnp.int32)
    row_of = jnp.arange(block, dtype=jnp.int32)
    spread = (expert_of[:, None] == slot_of[None, :] // CAP).astype(bf)
    router_slots = dot(router_w, spread).astype(bf)
    earlier = (row_of[:, None] > row_of[None, :]).astype(bf)

    def slot_table(route_rows):
        named = jnp.any(route_rows[:, :, None] == expert_of[None, None, :], axis=1).astype(bf)
        slot_ids = dot(earlier, named).astype(bf)
        return (dot(named, spread) > 0.5) & (
            dot(slot_ids, spread).astype(jnp.int32) == (slot_of % CAP)[None, :]
        )

    info = jnp.stack([position % ring, is_first.astype(jnp.int32)]).astype(jnp.int32)
    info_all = jnp.stack([position % ring, jnp.ones_like(position)]).astype(jnp.int32)

    def gate_values(normed_two, table):
        logits = jnp.where(table, dot(normed_two, router_slots), masked_score)
        weights = jnp.exp(logits - jnp.max(logits, axis=-1, keepdims=True))
        weights = jnp.where(table, weights, 0.0)
        return weights / jnp.sum(weights, axis=-1, keepdims=True)

    def high_low(value):
        high = value.astype(bf)
        return high, (value - high.astype(f32)).astype(bf)

    def to_experts(rows):
        return (
            exchange(rows.reshape(shards, local_experts, CAP, width))
            .transpose(1, 0, 2, 3)
            .reshape(local_experts, shards * CAP, width)
        )

    def from_experts(rows):
        return exchange(
            rows.reshape(local_experts, shards, CAP, width).transpose(1, 0, 2, 3)
        ).reshape(slots, width)

    def sum_over_x(rows):
        parts = exchange(rows.astype(bf).reshape(heads, block, width), x_groups)
        return jnp.sum(parts.astype(f32), axis=0)

    def ring_rows(rows):
        return exchange(copies(rows, heads), x_groups).reshape(heads * block, width)

    def forward(moment, received, previous):
        first_micro = min(moment, micros - 1)
        second_micro = max(moment - 1, 0)
        layer_b = jnp.where(is_first, inputs[0, first_micro], received)
        table = slot_table(
            jnp.where(is_first, routes[0, 0, first_micro], routes[0, 0, second_micro])
        )
        pick = table.astype(bf)
        layer_in = layer_b.astype(f32)
        normed_one = (layer_in * inverse_rms(layer_in) * gain_one).astype(bf)
        ring_one = ring_rows(normed_one)
        qkv = dot(ring_one, qkv_w).astype(bf)
        cache = exchange(copies(qkv[:, group_width:], ring), zy_groups)
        qkv = qkv.reshape(heads, block, part_width)
        attn_info = info if moment == 1 else info_all
        attended, logs = attention_forward(attn_info, qkv, previous, cache)
        attended_rows = attended.reshape(heads * block, group_width)
        hidden = layer_in + sum_over_x(dot(attended_rows, output_w))
        normed_two = (hidden * inverse_rms(hidden) * gain_two).astype(bf)
        gates = gate_values(normed_two, table)
        expert_in = to_experts(dot_tn(pick, normed_two).astype(bf))
        gate_pre = wide_einsum("erd,edf->erf", expert_in, expert_g)
        up_pre = wide_einsum("erd,edf->erf", expert_in, expert_u)
        activated = (silu_parts(gate_pre)[0] * up_pre).astype(bf)
        returned = from_experts(wide_einsum("erf,efd->erd", activated, expert_d).astype(bf))
        high, low = high_low(gates)
        routed = dot(high, returned) + dot(low, returned)
        shared_gate_pre, shared_up_pre = halves(dot(normed_two, gate_up_w))
        shared_act = (silu_parts(shared_gate_pre)[0] * shared_up_pre).astype(bf)
        output_b = (hidden + routed + dot(shared_act, down_w)).astype(bf)
        return dict(
            layer_b=layer_b,
            pick=pick,
            ring_one=ring_one,
            qkv=qkv,
            cache=cache,
            previous=previous,
            info=attn_info,
            attended=attended,
            logs=logs,
            hidden=hidden,
            normed_two=normed_two,
            gates=gates,
            expert_in=expert_in,
            gate_pre=gate_pre,
            up_pre=up_pre,
            activated=activated,
            returned=returned,
            shared_gate_pre=shared_gate_pre,
            shared_up_pre=shared_up_pre,
            shared_act=shared_act,
            output_b=output_b,
        )

    def ffn_backward(kept, upstream_b):
        upstream = upstream_b.astype(f32)
        gates, hidden = kept["gates"], kept["hidden"]
        high, low = high_low(gates)
        outgoing = dot_tn(high, upstream_b) + dot_tn(low, upstream_b)
        expert_grad = to_experts(outgoing.astype(bf))
        act_silu, act_slope = silu_parts(kept["gate_pre"])
        act_grad = wide_einsum("erd,efd->erf", expert_grad, expert_d)
        gate_pre_grad = (act_grad * kept["up_pre"] * act_slope).astype(bf)
        up_pre_grad = (act_grad * act_silu).astype(bf)
        expert_in_grad = (
            wide_einsum("erf,edf->erd", gate_pre_grad, expert_g)
            + wide_einsum("erf,edf->erd", up_pre_grad, expert_u)
        ).astype(bf)
        returned_grad = from_experts(expert_in_grad)
        shared_act_grad = dot_nt(upstream_b, down_w)
        shared_silu, shared_slope = silu_parts(kept["shared_gate_pre"])
        shared_gate_grad = (shared_act_grad * kept["shared_up_pre"] * shared_slope).astype(bf)
        shared_up_grad = (shared_act_grad * shared_silu).astype(bf)
        normed_two_grad = dot_nt(
            jnp.concatenate([shared_gate_grad, shared_up_grad], axis=1), gate_up_w
        )
        gate_grad = dot_nt(upstream_b, kept["returned"])
        picked_grad = gates * (gate_grad - jnp.sum(gates * gate_grad, axis=1, keepdims=True))
        picked_b = picked_grad.astype(bf)
        normed_two_grad = normed_two_grad + dot_nt(picked_b, router_slots)
        normed_two_grad = normed_two_grad + dot(kept["pick"], returned_grad)
        logit_grad = dot_nt(picked_b, spread).astype(bf)
        hidden_norm_grad, gain_two_grad = norm_back(hidden, gain_two, normed_two_grad)
        return dict(
            hidden_grad=upstream + hidden_norm_grad,
            upstream_b=upstream_b,
            expert_grad=expert_grad,
            gate_pre_grad=gate_pre_grad,
            up_pre_grad=up_pre_grad,
            shared_gate_grad=shared_gate_grad,
            shared_up_grad=shared_up_grad,
            logit_grad=logit_grad,
            gain_two_grad=gain_two_grad,
        )

    def attention_back(kept, grads, carried):
        ring_hidden = ring_rows(grads["hidden_grad"].astype(bf))
        out_grad = dot_nt(ring_hidden, output_w).astype(bf)
        results = attention_backward(
            kept["info"],
            kept["qkv"],
            out_grad.reshape(heads, block, group_width),
            kept["attended"],
            kept["logs"],
            carried,
            kept["previous"],
            kept["cache"],
        )
        carried = results[2] if len(results) > 2 else None
        pair_grad = jnp.sum(exchange(results[1], zy_groups).astype(f32), axis=0).astype(bf)
        qkv_grad = jnp.concatenate(
            [results[0].reshape(heads * block, group_width), pair_grad], axis=1
        )
        normed_one_grad = sum_over_x(dot_nt(qkv_grad, qkv_w))
        in_norm_grad, gain_one_grad = norm_back(
            kept["layer_b"].astype(f32), gain_one, normed_one_grad
        )
        grads = dict(
            grads,
            ring_hidden=ring_hidden,
            qkv_grad=qkv_grad,
            gain_one_grad=gain_one_grad,
            layer_grad=(grads["hidden_grad"] + in_norm_grad).astype(bf),
        )
        return grads, carried

    nothing = jnp.zeros((block, width), bf)
    saved = []
    received, previous = nothing, None
    for moment in range(micros + 1):
        kept = forward(moment, received, previous)
        saved.append(kept)
        previous = kept["cache"]
        if moment < micros:
            received = lax.ppermute(kept["output_b"], "section", [(0, 1)])
    backs = [None] * (micros + 1)
    received, carried = nothing, None
    for source in range(micros, -1, -1):
        own = cotangent[0, source - 1] if source > 0 else nothing
        upstream_b = jnp.where(is_first, received, own)
        grads = ffn_backward(saved[source], upstream_b)
        backs[source], carried = attention_back(saved[source], grads, carried)
        if source > 0:
            received = lax.ppermute(backs[source]["layer_grad"], "section", [(1, 0)])

    def live(name, store, axis):
        ends = jnp.where(is_first, store[0][name], store[micros][name])
        return jnp.concatenate([ends, store[1][name]], axis=axis)

    def kept_rows(name, axis=0):
        return live(name, saved, axis)

    def back_rows(name, axis=0):
        return live(name, backs, axis)

    expert_parts = [
        wide_einsum("erd,erf->edf", kept_rows("expert_in", 1), back_rows("gate_pre_grad", 1)),
        wide_einsum("erd,erf->edf", kept_rows("expert_in", 1), back_rows("up_pre_grad", 1)),
        wide_einsum("erf,erd->efd", kept_rows("activated", 1), back_rows("expert_grad", 1)),
    ]
    expert_parts = [part.astype(bf) for part in expert_parts]
    expert_grads = [part.astype(f32) + twin(part).astype(f32) for part in expert_parts]

    def both(value):
        return jnp.concatenate([value, twin(value)], axis=0)

    def both_halves(low_half, high_half):
        own, other = mine_of(low_half, high_half), mine_of(high_half, low_half)
        return jnp.concatenate([own, twin(other)], axis=0)

    normed_two = kept_rows("normed_two")
    grad_gate_up = dot_tn(
        both(normed_two), both_halves(back_rows("shared_gate_grad"), back_rows("shared_up_grad"))
    )
    grad_down = dot_tn(both(kept_rows("shared_act")), both_halves(*halves(back_rows("upstream_b"))))
    shared_flat = (shards, down_rows * width // 2 // shared_width, shared_width)
    shared_pieces = jnp.concatenate(
        [
            grad_gate_up.astype(bf).reshape(shards, rows_per, shared_width),
            grad_down.astype(bf).reshape(shared_flat),
        ],
        axis=1,
    )
    share_shared = jnp.sum(exchange(shared_pieces).astype(f32), axis=0)
    other_shared = twin(share_shared)

    grad_out = dot_tn(
        kept_rows("attended").reshape(micros * heads * block, group_width),
        back_rows("ring_hidden"),
    )
    share_out = jnp.sum(
        exchange(grad_out.astype(bf).reshape(ring, rows_per, width), zy_groups).astype(f32), axis=0
    )
    grad_qkv = dot_tn(kept_rows("ring_one"), back_rows("qkv_grad"))
    grad_router = dot_tn(normed_two, back_rows("logit_grad"))
    gain_sums = jnp.stack(
        [sum(grads[name] for grads in backs) for name in ("gain_one_grad", "gain_two_grad")]
    )
    grad_tail = jnp.concatenate(
        [grad_router, gain_sums.T, jnp.zeros((width, 128 - experts - 2), f32)], axis=1
    )
    pieces = exchange(
        jnp.concatenate([grad_qkv, grad_tail], axis=1)
        .astype(bf)
        .reshape(shards, rows_per, part_width + 128)
    ).astype(f32)
    share_qkv = jnp.sum(
        pieces[:, :, :part_width].reshape(heads, ring, rows_per, part_width), axis=1
    )
    share_qkv = share_qkv.transpose(1, 0, 2)
    share_tail = jnp.sum(pieces[:, :, part_width:], axis=0)

    def total(share):
        return share + twin(share)

    out_total, qkv_total, tail_total = total(share_out), total(share_qkv), total(share_tail)
    low_shared, high_shared = (
        mine_of(share_shared, other_shared),
        mine_of(other_shared, share_shared),
    )
    down_shape = (down_rows, width // 2)
    down_total = jnp.concatenate(
        [low_shared[rows_per:].reshape(down_shape), high_shared[rows_per:].reshape(down_shape)],
        axis=1,
    )
    def by_micro(store, name):
        return jnp.stack(
            [jnp.where(is_first, store[m][name], store[m + 1][name]) for m in range(micros)]
        )[None, None]

    return (
        by_micro(saved, "output_b"),
        by_micro(backs, "layer_grad"),
        tail_total[:, experts][None],
        qkv_total[:, :, :group_width].reshape(1, rows_per, head_width),
        qkv_total[:, :, group_width : group_width + HD].reshape(1, rows_per, key_width),
        qkv_total[:, :, group_width + HD :].reshape(1, rows_per, key_width),
        out_total[None],
        tail_total[:, experts + 1][None],
        tail_total[:, :experts][None],
        low_shared[:rows_per][None],
        high_shared[:rows_per][None],
        down_total[None],
        expert_grads[0][None],
        expert_grads[1][None],
        expert_grads[2][None],
    )


def solution(mesh):
    rows = P("section", "shard", None)
    vector = P("section", "shard")
    expert = P("section", "shard", None, None)
    tokens = P("dp", None, "shard", None)
    section_tokens = P("section", "dp", None, "shard", None)
    weights = (vector, rows, rows, rows, rows, vector, rows, rows, rows, rows) + (expert,) * 3
    return jax.shard_map(
        body,
        mesh=mesh,
        in_specs=(tokens, tokens, section_tokens) + weights,
        out_specs=(section_tokens, section_tokens) + weights,
        check_vma=False,
    )
```

time: 1180 us -> 1120 us (0.949)
  waiting for transfers between devices: 360 us -> 288 us
  other arithmetic: 83.4 us -> 114 us
  blocking collectives: 229 us -> 200 us
  matrix products: 164 us -> 183 us
  local copies, waits for them, and re-layouts: 103 us -> 89.4 us
    all_to_all x18 -> x24, waiting for transfers between devices: 339 us -> 209 us  [exchange(): lax.all_to_all(value, 'shard', split_axis=0, concat_axis=0, tiled=True, a...]
    all_gather x1 -> x0, blocking collectives: 58.9 us -> none  [body(): lax.all_gather(my_rows(w_output[0]), 'shard', axis_index_groups=zy_groups)]
    all_gather x1, waiting for transfers between devices: 0.02 us -> 51.5 us  [body(): gathered = lax.all_gather(packed, 'shard')]
    all_to_all x6 -> x10, blocking collectives: 170 us -> 200 us  [exchange(): lax.all_to_all(value, 'shard', split_axis=0, concat_axis=0, tiled=True, a...]
    unnamed x344 -> x494, local copies, waits for them, and re-layouts: 23.8 us -> 37.2 us
    dot_general x17 -> x21, matrix products: 38.8 us -> 51.4 us  [dot_nt(): lax.dot_general(left_side, right_side, (((1,), (1,)), ((), ())), preferre...]
    transpose x7 -> x0, local copies, waits for them, and re-layouts: 12.5 us -> none  [the longest x4 7.03 us: to_experts(): return exchange(rows.reshape(shards, local_experts, room, width)).transpo...]
    ppermute x2 -> x4, waiting for transfers between devices: 16.4 us -> 24.3 us  [the longest x2 19.2 us: body(): received = lax.ppermute(backs[source]['layer_grad'], 'section', [(1, 0)])]
  transfers between devices with their start and end apart: 35 -> 44, of which waited for: 20 -> 27; matrix products, arithmetic and copies ran while one was open for 20% -> 24% of each run, Pallas kernels for 2% -> 1%
where the time goes in v4:
time: 1120 us; the launch traced here: 1100 us
  waiting for transfers between devices  288 us (26%)
  blocking collectives  200 us (18%)
  matrix products  183 us (16%)
  starting transfers between devices  163 us (15%)
  other arithmetic  114 us (10%)
  local copies, waits for them, and re-layouts  89.4 us (8%)
  Pallas kernels  47.3 us (4%)
  between operations  17.8 us (2%)
    all_to_all x24, waiting for transfers between devices, exchange(): lax.all_to_all(value, 'shard', split_axis=0, concat_axis=0, tiled=True, a...  209 us
    all_to_all x10, blocking collectives, exchange(): lax.all_to_all(value, 'shard', split_axis=0, concat_axis=0, tiled=True, a...  200 us
    all_to_all x24, starting transfers between devices, exchange(): lax.all_to_all(value, 'shard', split_axis=0, concat_axis=0, tiled=True, a...  131 us
    dot_general x31, matrix products, dot(): return jnp.dot(left_side, right_side, preferred_element_type=f32)  54.9 us
    all_gather x1, waiting for transfers between devices, body(): gathered = lax.all_gather(packed, 'shard')  51.5 us
    dot_general x21, matrix products, dot_nt(): lax.dot_general(left_side, right_side, (((1,), (1,)), ((), ())), preferre...  51.4 us
    dot_general x21, matrix products, wide_einsum(): jnp.einsum(formula, left_side, right_side, preferred_element_type=f32)  50.9 us
    pallas_call x6, Pallas kernels, attention_call(): pl.pallas_call(kernel, out_shape=out_shape, in_specs=[pl.BlockSpec(memory...  47.3 us
  transfers between devices with their start and end apart: 44, of which 27 were waited for; matrix products, arithmetic and copies ran while one was open for 24% of the time, Pallas kernels for 1%

profile of v4, /device:TPU:1, one launch (start us, length us, event | category | flops | bytes accessed | tf_op | source)
XLA Modules:
  0.0 1101.6 jit_solution(4185820234706490027)
XLA Ops:
  12.8 32.3 %all_to_all.170 = bf16[32,24,768]{2,1,0:T(8,128)(2,1)} all-to-all(bf16[32,24,768]{2,1,0:T(8,128)(2,1)S(1)} %bitcast.508), channel_id=1, replica_groups=mesh['section'=2,'dp'=2,'shard'=32] {'shard'}, dimensions={0} | all-to-all | bytes 2359296 | tf_op jit(solution)/shard_map/all_to_all | solution.py:245
  52.9 21.4 %all_to_all.171 = bf16[4,64,1536]{2,1,0:T(8,128)(2,1)S(1)} all-to-all(bf16[4,64,1536]{2,1,0:T(8,128)(2,1)S(1)} %broadcast_in_dim.65), channel_id=1, replica_groups={{0,8,16,24},{1,9,17,25},{2,10,18,26},{3,11,19,27},{4,12,20,28},{5,13,21..., dimensions={0} | all-to-all | bytes 1572864 | tf_op jit(solution)/shard_map/all_to_all | solution.py:245
  80.7 51.5 %all-gather.3.cloned.1.call-done = bf16[768,4608]{1,0:T(8,128)(2,1)} async-done(((bf16[24,4608]{1,0:T(8,128)(2,1)}), bf16[768,4608]{1,0:T(8,128)(2,1)}) %all-gather.3.cloned.1.call-update) | async-done | bytes 7077904 | tf_op jit(solution)/shard_map/all_gather | solution.py:307
  180.5 16.6 %all-to-all-done.4 = bf16[32,2,8,1536]{3,2,1,0:T(8,128)(2,1)} async-done(((bf16[32,2,8,1536]{3,2,1,0:T(8,128)(2,1)}), bf16[32,2,8,1536]{3,2,1,0:T(8,128)(2,1)}, u32[]{:S(2)}, u32[]{:S(2)}) %all-to-all-start.4) | async-done | bytes 1572896 | tf_op jit(solution)/shard_map/all_to_all | solution.py:245
  247.4 12.8 %all_to_all.172 = bf16[4,64,1536]{2,1,0:T(8,128)(2,1)S(1)} all-to-all(bf16[4,64,1536]{2,1,0:T(8,128)(2,1)S(1)} %broadcast_in_dim.69), channel_id=1, replica_groups={{0,8,16,24},{1,9,17,25},{2,10,18,26},{3,11,19,27},{4,12,20,28},{5,13,21..., dimensions={0} | all-to-all | bytes 1572864 | tf_op jit(solution)/shard_map/all_to_all | solution.py:245
  271.0 14.2 %all-to-all-done.7.refs_1_.refs_0_.refs_2_ = bf16[8,256,256]{2,1,0:T(8,128)(2,1)} async-done(((bf16[8,256,256]{2,1,0:T(8,128)(2,1)}), bf16[8,256,256]{2,1,0:T(8,128)(2,1)}, u32[]{:S(2)}, u32[]{:S(2)}) %all-to-all-start.7) | async-done | bytes 1048608 | tf_op jit(solution)/shard_map/all_to_all | solution.py:245
  311.2 27.8 %all_to_all.173 = bf16[32,2,8,1536]{3,2,1,0:T(8,128)(2,1)S(1)} all-to-all(bf16[32,2,8,1536]{3,2,1,0:T(8,128)(2,1)S(1)} %bitcast.504), channel_id=1, replica_groups=mesh['section'=2,'dp'=2,'shard'=32] {'shard'}, dimensions={0} | all-to-all | bytes 3145728 | tf_op jit(solution)/shard_map/all_to_all | solution.py:245
  362.4 10.7 all-to-all-done.10
  387.4 10.9 all_to_all.174
  399.3 21.9 %all_to_all.175.refs_1_ = bf16[8,256,256]{2,1,0:T(8,128)(2,1)S(1)} all-to-all(bf16[8,256,256]{2,1,0:T(8,128)(2,1)S(1)} %broadcast_in_dim.72), channel_id=1, replica_groups={{0,1,2,3,4,5,6,7},{8,9,10,11,12,13,14,15},{16,17,18,19,20,21,22,23},{24..., dimensions={0} | all-to-all | bytes 2097152 | tf_op jit(solution)/shard_map/all_to_all | solution.py:245
  458.8 15.6 %all-to-all-done.14 = bf16[32,2,8,1536]{3,2,1,0:T(8,128)(2,1)} async-done(((bf16[32,2,8,1536]{3,2,1,0:T(8,128)(2,1)}), bf16[32,2,8,1536]{3,2,1,0:T(8,128)(2,1)}, u32[]{:S(2)}, u32[]{:S(2)}) %all-to-all-start.14) | async-done | bytes 1572896 | tf_op jit(solution)/shard_map/all_to_all | solution.py:245
  490.4 11.8 %all-to-all-done.16 = bf16[32,2,8,1536]{3,2,1,0:T(8,128)(2,1)} async-done(((bf16[32,2,8,1536]{3,2,1,0:T(8,128)(2,1)}), bf16[32,2,8,1536]{3,2,1,0:T(8,128)(2,1)}, u32[]{:S(2)}, u32[]{:S(2)}) %all-to-all-start.16) | async-done | bytes 1572896 | tf_op jit(solution)/shard_map/all_to_all | solution.py:245
  516.9 13.9 %all-to-all-done.15 = bf16[32,2,8,1536]{3,2,1,0:T(8,128)(2,1)} async-done(((bf16[32,2,8,1536]{3,2,1,0:T(8,128)(2,1)}), bf16[32,2,8,1536]{3,2,1,0:T(8,128)(2,1)}, u32[]{:S(2)}, u32[]{:S(2)}) %all-to-all-start.15) | async-done | bytes 1572896 | tf_op jit(solution)/shard_map/all_to_all | solution.py:245
  548.2 11.8 %all-to-all-done.17 = bf16[32,2,8,1536]{3,2,1,0:T(8,128)(2,1)} async-done(((bf16[32,2,8,1536]{3,2,1,0:T(8,128)(2,1)}), bf16[32,2,8,1536]{3,2,1,0:T(8,128)(2,1)}, u32[]{:S(2)}, u32[]{:S(2)}) %all-to-all-start.17) | async-done | bytes 1572896 | tf_op jit(solution)/shard_map/all_to_all | solution.py:245
  568.1 12.2 %all_to_all.176 = bf16[4,64,1536]{2,1,0:T(8,128)(2,1)S(1)} all-to-all(bf16[4,64,1536]{2,1,0:T(8,128)(2,1)S(1)} %broadcast_in_dim.74), channel_id=1, replica_groups={{0,8,16,24},{1,9,17,25},{2,10,18,26},{3,11,19,27},{4,12,20,28},{5,13,21..., dimensions={0} | all-to-all | bytes 1572864 | tf_op jit(solution)/shard_map/all_to_all | solution.py:245
  581.2 12.8 %shard_map.274 = (bf16[4,64,384]{2,1,0:T(8,128)(2,1)S(1)}, bf16[8,256,256]{2,1,0:T(8,128)(2,1)S(1)}, f32[8,256,256]{2,1,0:T(8,128)S(1)}) custom-call(s32[2]{0:T(128)S(1)} %pad_add_fusion.info_ref, bf16[4,64,640]{2,1,0:T(8,128)(2,1)S(1)} %bitcast.468, bf16[4,64,384]{2,1,0:T(8,128)(2,1)S(1)} %bitcast.473, bf16[4,64,384]{2,1,0:T(8,128)(2,1)S(1)} %copy-done.6, ...), custom_call_target="tpu_custom_call" | custom-call | flops 2013265920 | bytes 3112960 | tf_op jit(solution)/shard_map/pallas_call | solution.py:165
  596.0 22.8 %all_to_all.177 = bf16[8,256,256]{2,1,0:T(8,128)(2,1)} all-to-all(bf16[8,256,256]{2,1,0:T(8,128)(2,1)S(1)} %get-tuple-element.34), channel_id=1, replica_groups={{0,1,2,3,4,5,6,7},{8,9,10,11,12,13,14,15},{16,17,18,19,20,21,22,23},{24..., dimensions={0} | all-to-all | bytes 2097152 | tf_op jit(solution)/shard_map/all_to_all | solution.py:245
  623.5 11.7 %all_to_all.178 = bf16[4,64,1536]{2,1,0:T(8,128)(2,1)S(1)} all-to-all(bf16[4,64,1536]{2,1,0:T(8,128)(2,1)S(1)} %bitcast.532), channel_id=1, replica_groups={{0,8,16,24},{1,9,17,25},{2,10,18,26},{3,11,19,27},{4,12,20,28},{5,13,21..., dimensions={0} | all-to-all | bytes 1572864 | tf_op jit(solution)/shard_map/all_to_all | solution.py:245
  637.8 10.6 collective-permute-done.6
  650.0 25.8 %all_to_all.179 = bf16[32,2,8,1536]{3,2,1,0:T(8,128)(2,1)S(1)} all-to-all(bf16[32,2,8,1536]{3,2,1,0:T(8,128)(2,1)S(1)} %bitcast.507), channel_id=1, replica_groups=mesh['section'=2,'dp'=2,'shard'=32] {'shard'}, dimensions={0} | all-to-all | bytes 3145728 | tf_op jit(solution)/shard_map/all_to_all | solution.py:245
  696.8 12.4 %all-to-all-done.22 = bf16[32,2,8,1536]{3,2,1,0:T(8,128)(2,1)} async-done(((bf16[32,2,8,1536]{3,2,1,0:T(8,128)(2,1)}), bf16[32,2,8,1536]{3,2,1,0:T(8,128)(2,1)}, u32[]{:S(2)}, u32[]{:S(2)}) %all-to-all-start.22) | async-done | bytes 1572896 | tf_op jit(solution)/shard_map/all_to_all | solution.py:245
  735.0 13.1 %shard_map.275 = (bf16[4,64,384]{2,1,0:T(8,128)(2,1)S(1)}, bf16[8,256,256]{2,1,0:T(8,128)(2,1)S(1)}, f32[8,256,256]{2,1,0:T(8,128)S(1)}) custom-call(s32[2]{0:T(128)S(1)} %pad_add_fusion.1.info_ref, bf16[4,64,640]{2,1,0:T(8,128)(2,1)S(1)} %bitcast.466, bf16[4,64,384]{2,1,0:T(8,128)(2,1)S(1)} %bitcast.472, bf16[4,64,384]{2,1,0:T(8,128)(2,1)S(1)} %get-tuple-element.30.o_ref, ...), custom_call_target="tpu_custom_call" | custom-call | flops 3019898880 | bytes 4423680 | tf_op jit(solution)/shard_map/pallas_call | solution.py:165
  857.7 12.4 %all-to-all-done.27 = bf16[32,2,8,1536]{3,2,1,0:T(8,128)(2,1)} async-done(((bf16[32,2,8,1536]{3,2,1,0:T(8,128)(2,1)}), bf16[32,2,8,1536]{3,2,1,0:T(8,128)(2,1)}, u32[]{:S(2)}, u32[]{:S(2)}) %all-to-all-start.27) | async-done | bytes 1572896 | tf_op jit(solution)/shard_map/all_to_all | solution.py:245
  1048.4 28.3 %all-to-all-done.33 = bf16[32,72,1024]{2,1,0:T(8,128)(2,1)} async-done(((bf16[32,72,1024]{2,1,0:T(8,128)(2,1)}), bf16[32,72,1024]{2,1,0:T(8,128)(2,1)}, u32[]{:S(2)}, u32[]{:S(2)}) %all-to-all-start.33) | async-done | bytes 4718624 | tf_op jit(solution)/shard_map/all_to_all | solution.py:245
  (828 shorter events, 648.0 us)
Async XLA Ops:
  7.2 125.0 %all-gather.3.cloned.1.call-start = ((), (), s32[]{:S(2)}) async-start(), calls=%async_computation.34 | async-start | bytes 7299072 | tf_op jit(solution)/shard_map/all_gather | solution.py:307
  76.3 60.8 %all-to-all-start.2 = ((bf16[8,256,256]{2,1,0:T(8,128)(2,1)}), bf16[8,256,256]{2,1,0:T(8,128)(2,1)}, u32[]{:S(2)}, u32[]{:S(2)}) async-start(bf16[8,256,256]{2,1,0:T(8,128)(2,1)} %broadcast_in_dim.66), calls=%async_computation.2 | async-start | bytes 2097152 | tf_op jit(solution)/shard_map/all_to_all | solution.py:245
  161.4 51.8 %collective-permute-start.2 = (bf16[32,24,2048]{2,1,0:T(8,128)(2,1)}, bf16[32,24,2048]{2,1,0:T(8,128)(2,1)}, u32[]{:S(2)}, u32[]{:S(2)}) collective-permute-start(bf16[32,24,2048]{2,1,0:T(8,128)(2,1)} %slice.196), channel_id=1, source_target_pairs={{0,32},{32,0},{1,33},{33,1},{2,34},{34,2},{3,35},{35,3},{4,36},{36... | collective-permute-start | bytes 9437192 | tf_op jit(solution)/shard_map/ppermute | solution.py:253
  167.2 30.0 %all-to-all-start.4 = ((bf16[32,2,8,1536]{3,2,1,0:T(8,128)(2,1)}), bf16[32,2,8,1536]{3,2,1,0:T(8,128)(2,1)}, u32[]{:S(2)}, u32[]{:S(2)}) async-start(bf16[32,2,8,1536]{3,2,1,0:T(8,128)(2,1)} %bitcast.498), calls=%async_computation.4 | async-start | bytes 3145728 | tf_op jit(solution)/shard_map/all_to_all | solution.py:245
  206.9 29.4 %all-to-all-start.5 = ((bf16[32,2,8,1536]{3,2,1,0:T(8,128)(2,1)}), bf16[32,2,8,1536]{3,2,1,0:T(8,128)(2,1)}, u32[]{:S(2)}, u32[]{:S(2)}) async-start(bf16[32,2,8,1536]{3,2,1,0:T(8,128)(2,1)} %bitcast.501), calls=%async_computation.5 | async-start | bytes 3145728 | tf_op jit(solution)/shard_map/all_to_all | solution.py:245
  263.0 22.3 %all-to-all-start.7 = ((bf16[8,256,256]{2,1,0:T(8,128)(2,1)}), bf16[8,256,256]{2,1,0:T(8,128)(2,1)}, u32[]{:S(2)}, u32[]{:S(2)}) async-start(bf16[8,256,256]{2,1,0:T(8,128)(2,1)} %broadcast_in_dim.70), calls=%async_computation.7 | async-start | bytes 2097152 | tf_op jit(solution)/shard_map/all_to_all | solution.py:245
  345.8 27.3 %all-to-all-start.10 = ((bf16[32,2,8,1536]{3,2,1,0:T(8,128)(2,1)}), bf16[32,2,8,1536]{3,2,1,0:T(8,128)(2,1)}, u32[]{:S(2)}, u32[]{:S(2)}) async-start(bf16[32,2,8,1536]{3,2,1,0:T(8,128)(2,1)} %bitcast.502), calls=%async_computation.10 | async-start | bytes 3145728 | tf_op jit(solution)/shard_map/all_to_all | solution.py:245
  448.5 25.9 %all-to-all-start.14 = ((bf16[32,2,8,1536]{3,2,1,0:T(8,128)(2,1)}), bf16[32,2,8,1536]{3,2,1,0:T(8,128)(2,1)}, u32[]{:S(2)}, u32[]{:S(2)}) async-start(bf16[32,2,8,1536]{3,2,1,0:T(8,128)(2,1)} %bitcast.503), calls=%async_computation.14 | async-start | bytes 3145728 | tf_op jit(solution)/shard_map/all_to_all | solution.py:245
  474.4 27.8 %all-to-all-start.16 = ((bf16[32,2,8,1536]{3,2,1,0:T(8,128)(2,1)}), bf16[32,2,8,1536]{3,2,1,0:T(8,128)(2,1)}, u32[]{:S(2)}, u32[]{:S(2)}) async-start(bf16[32,2,8,1536]{3,2,1,0:T(8,128)(2,1)} %bitcast.506), calls=%async_computation.16 | async-start | bytes 3145728 | tf_op jit(solution)/shard_map/all_to_all | solution.py:245
  502.2 28.6 %all-to-all-start.15 = ((bf16[32,2,8,1536]{3,2,1,0:T(8,128)(2,1)}), bf16[32,2,8,1536]{3,2,1,0:T(8,128)(2,1)}, u32[]{:S(2)}, u32[]{:S(2)}) async-start(bf16[32,2,8,1536]{3,2,1,0:T(8,128)(2,1)} %bitcast.499), calls=%async_computation.15 | async-start | bytes 3145728 | tf_op jit(solution)/shard_map/all_to_all | solution.py:245
  530.8 29.2 %all-to-all-start.17 = ((bf16[32,2,8,1536]{3,2,1,0:T(8,128)(2,1)}), bf16[32,2,8,1536]{3,2,1,0:T(8,128)(2,1)}, u32[]{:S(2)}, u32[]{:S(2)}) async-start(bf16[32,2,8,1536]{3,2,1,0:T(8,128)(2,1)} %bitcast.497), calls=%async_computation.17 | async-start | bytes 3145728 | tf_op jit(solution)/shard_map/all_to_all | solution.py:245
  682.8 26.4 %all-to-all-start.22 = ((bf16[32,2,8,1536]{3,2,1,0:T(8,128)(2,1)}), bf16[32,2,8,1536]{3,2,1,0:T(8,128)(2,1)}, u32[]{:S(2)}, u32[]{:S(2)}) async-start(bf16[32,2,8,1536]{3,2,1,0:T(8,128)(2,1)} %bitcast.500), calls=%async_computation.22 | async-start | bytes 3145728 | tf_op jit(solution)/shard_map/all_to_all | solution.py:245
  804.3 29.8 %all-to-all-start.26 = ((bf16[32,2,8,1536]{3,2,1,0:T(8,128)(2,1)}), bf16[32,2,8,1536]{3,2,1,0:T(8,128)(2,1)}, u32[]{:S(2)}, u32[]{:S(2)}) async-start(bf16[32,2,8,1536]{3,2,1,0:T(8,128)(2,1)} %bitcast.505), calls=%async_computation.26 | async-start | bytes 3145728 | tf_op jit(solution)/shard_map/all_to_all | solution.py:245
  813.9 170.3 %collective-permute-start.11 = (bf16[128,1536]{1,0:T(8,128)(2,1)}, bf16[128,1536]{1,0:T(8,128)(2,1)}, u32[]{:S(2)}, u32[]{:S(2)}) collective-permute-start(bf16[128,1536]{1,0:T(8,128)(2,1)} %pad_maximum_fusion.8), channel_id=1, source_target_pairs={{0,32},{32,0},{1,33},{33,1},{2,34},{34,2},{3,35},{35,3},{4,36},{36... | collective-permute-start | bytes 1179656 | tf_op jit(solution)/shard_map/ppermute | solution.py:253
  819.7 174.5 %collective-permute-start.13 = (bf16[128,1024]{1,0:T(8,128)(2,1)}, bf16[128,1024]{1,0:T(8,128)(2,1)}, u32[]{:S(2)}, u32[]{:S(2)}) collective-permute-start(bf16[128,1024]{1,0:T(8,128)(2,1)} %pad_maximum_fusion.15), channel_id=1, source_target_pairs={{0,32},{32,0},{1,33},{33,1},{2,34},{34,2},{3,35},{35,3},{4,36},{36... | collective-permute-start | bytes 786440 | tf_op jit(solution)/shard_map/ppermute | solution.py:253
  843.0 27.0 %all-to-all-start.27 = ((bf16[32,2,8,1536]{3,2,1,0:T(8,128)(2,1)}), bf16[32,2,8,1536]{3,2,1,0:T(8,128)(2,1)}, u32[]{:S(2)}, u32[]{:S(2)}) async-start(bf16[32,2,8,1536]{3,2,1,0:T(8,128)(2,1)} %bitcast.496), calls=%async_computation.27 | async-start | bytes 3145728 | tf_op jit(solution)/shard_map/all_to_all | solution.py:245
  890.4 97.3 %collective-permute-start.12 = (bf16[128,1024]{1,0:T(8,128)(2,1)}, bf16[128,1024]{1,0:T(8,128)(2,1)}, u32[]{:S(2)}, u32[]{:S(2)}) collective-permute-start(bf16[128,1024]{1,0:T(8,128)(2,1)} %get-tuple-element.108), channel_id=1, source_target_pairs={{0,32},{32,0},{1,33},{33,1},{2,34},{34,2},{3,35},{35,3},{4,36},{36... | collective-permute-start | bytes 786440 | tf_op jit(solution)/shard_map/ppermute | solution.py:253
  899.8 122.1 %collective-permute-start.16 = (bf16[2,1536,512]{2,1,0:T(8,128)(2,1)}, bf16[2,1536,512]{2,1,0:T(8,128)(2,1)}, u32[]{:S(2)}, u32[]{:S(2)}) collective-permute-start(bf16[2,1536,512]{2,1,0:T(8,128)(2,1)} %convolution_convert_fusion.3), channel_id=1, source_target_pairs={{0,32},{32,0},{1,33},{33,1},{2,34},{34,2},{3,35},{35,3},{4,36},{36... | collective-permute-start | bytes 9437192 | tf_op jit(solution)/shard_map/ppermute | solution.py:253
  920.4 108.0 %collective-permute-start.17 = (bf16[2,1536,512]{2,1,0:T(8,128)(2,1)}, bf16[2,1536,512]{2,1,0:T(8,128)(2,1)}, u32[]{:S(2)}, u32[]{:S(2)}) collective-permute-start(bf16[2,1536,512]{2,1,0:T(8,128)(2,1)} %convolution_convert_fusion.2), channel_id=1, source_target_pairs={{0,32},{32,0},{1,33},{33,1},{2,34},{34,2},{3,35},{35,3},{4,36},{36... | collective-permute-start | bytes 9437192 | tf_op jit(solution)/shard_map/ppermute | solution.py:253
  971.9 34.2 %all-to-all-start.31 = ((bf16[32,48,768]{2,1,0:T(8,128)(2,1)}), bf16[32,48,768]{2,1,0:T(8,128)(2,1)}, u32[]{:S(2)}, u32[]{:S(2)}) async-start(bf16[32,48,768]{2,1,0:T(8,128)(2,1)} %maximum_maximum_fusion), calls=%async_computation.31 | async-start | bytes 4718592 | tf_op jit(solution)/shard_map/all_to_all | solution.py:245
  984.2 50.8 %collective-permute-start.18 = (bf16[2,512,1536]{2,1,0:T(8,128)(2,1)}, bf16[2,512,1536]{2,1,0:T(8,128)(2,1)}, u32[]{:S(2)}, u32[]{:S(2)}) collective-permute-start(bf16[2,512,1536]{2,1,0:T(8,128)(2,1)} %convolution_convert_fusion.1), channel_id=1, source_target_pairs={{0,32},{32,0},{1,33},{33,1},{2,34},{34,2},{3,35},{35,3},{4,36},{36... | collective-permute-start | bytes 9437192 | tf_op jit(solution)/shard_map/ppermute | solution.py:253
  1006.1 70.6 %all-to-all-start.33 = ((bf16[32,72,1024]{2,1,0:T(8,128)(2,1)}), bf16[32,72,1024]{2,1,0:T(8,128)(2,1)}, u32[]{:S(2)}, u32[]{:S(2)}) async-start(bf16[32,72,1024]{2,1,0:T(8,128)(2,1)} %pad_maximum_fusion.1), calls=%async_computation.33 | async-start | bytes 9437184 | tf_op jit(solution)/shard_map/all_to_all | solution.py:245
  1020.4 21.2 %collective-permute-start.10 = (f32[48,1536]{1,0:T(8,128)S(1)}, f32[48,1536]{1,0:T(8,128)S(1)}, u32[]{:S(2)}, u32[]{:S(2)}) collective-permute-start(f32[48,1536]{1,0:T(8,128)S(1)} %convert_reduce_fusion.1), channel_id=1, source_target_pairs={{0,32},{32,0},{1,33},{33,1},{2,34},{34,2},{3,35},{35,3},{4,36},{36... | collective-permute-start | bytes 884744 | tf_op jit(solution)/shard_map/ppermute | solution.py:253
  1046.6 36.0 %collective-permute-start.9 = (f32[48,4,640]{2,0,1:T(8,128)}, f32[48,4,640]{2,0,1:T(8,128)}, u32[]{:S(2)}, u32[]{:S(2)}) collective-permute-start(f32[48,4,640]{2,0,1:T(8,128)} %bitcast.98), channel_id=1, source_target_pairs={{0,32},{32,0},{1,33},{33,1},{2,34},{34,2},{3,35},{35,3},{4,36},{36... | collective-permute-start | bytes 1474568 | tf_op jit(solution)/shard_map/ppermute | solution.py:253
  (267 other events, 2102.4 us)
Sparse Core Ops, SparseCore 0:
  11.6 120.5 all-gather.2

commit v5 on v4

--- a/solution.py
+++ b/solution.py
@@ -61,21 +61,27 @@
     return jnp.einsum(formula, left_side, right_side, preferred_element_type=f32)
 
 
-def stacked_heads(ref, part):
-    return jnp.concatenate(
-        [ref[part, :, g * HD : (g + 1) * HD] for g in range(GROUP)], axis=0
-    )
-
-
-def store_heads(ref, part, rows):
+def arrival(info_ref, parts, part):
+    return lax.rem(info_ref[2] + parts - part, parts)
+
+
+def stacked_heads(ref, at):
+    return jnp.concatenate([ref[at, :, g * HD : (g + 1) * HD] for g in range(GROUP)], axis=0)
+
+
+def store_heads(ref, at, rows):
     block = ref.shape[1]
     for g in range(GROUP):
-        ref[part, :, g * HD : (g + 1) * HD] = rows[g * block : (g + 1) * block]
-
-
-def cached(ref, start, stop, column):
-    rows = ref[:, start:stop, column : column + HD]
+        ref[at, :, g * HD : (g + 1) * HD] = rows[g * block : (g + 1) * block]
+
+
+def cached(ref, span, column):
+    rows = ref[:, span, column : column + HD]
     return rows.reshape(rows.shape[0] * rows.shape[1], HD)
+
+
+def block_span(at, block):
+    return pl.ds(pl.multiple_of(at * block, block), block)
 
 
 def diagonal_mask(rows, chunk, block, zy):
@@ -90,13 +96,13 @@
     parts, block, _ = q_ref.shape
     rows = GROUP * block
     mask = diagonal_mask(rows, cur_ref.shape[0] * block, block, info_ref[0])
+    spans = [block_span(arrival(info_ref, parts, part), block) for part in range(parts)]
     for part in range(parts):
-        queries = stacked_heads(q_ref, part)
-        pieces = [(prev_ref, 0, parts * block)] if has_prev else []
-        if part > 0:
-            pieces.append((cur_ref, 0, part * block))
-        pieces.append((cur_ref, part * block, (part + 1) * block))
-        scores = [dot_nt(queries, cached(ref, start, stop, 0)) for ref, start, stop in pieces]
+        at = arrival(info_ref, parts, part)
+        queries = stacked_heads(q_ref, at)
+        pieces = [(prev_ref, slice(None))] if has_prev else []
+        pieces += [(cur_ref, spans[p]) for p in range(part + 1)]
+        scores = [dot_nt(queries, cached(ref, span, 0)) for ref, span in pieces]
         if has_prev:
             scores[0] = scores[0] + jnp.where(info_ref[1] > 0, 0.0, masked_score).astype(f32)
         scores[-1] = jnp.where(mask, scores[-1], masked_score)
@@ -106,12 +112,12 @@
         peak = peak * log2_scale
         total = jnp.zeros((rows, 1), f32)
         mixed = jnp.zeros((rows, HD), f32)
-        for s, (ref, start, stop) in zip(scores, pieces):
+        for s, (ref, span) in zip(scores, pieces):
             probs = jnp.exp2(s * log2_scale - peak)
             total = total + jnp.sum(probs, axis=-1, keepdims=True)
-            mixed = mixed + dot(probs.astype(bf), cached(ref, start, stop, HD))
-        store_heads(o_ref, part, (mixed / total).astype(bf))
-        log_ref[part] = jnp.broadcast_to(peak + jnp.log2(total), (rows, HD))
+            mixed = mixed + dot(probs.astype(bf), cached(ref, span, HD))
+        store_heads(o_ref, at, (mixed / total).astype(bf))
+        log_ref[at] = jnp.broadcast_to(peak + jnp.log2(total), (rows, HD))
 
 
 def attention_backward_kernel(has_prev, has_carry, info_ref, q_ref, do_ref, o_ref, log_ref, *refs):
@@ -128,32 +134,36 @@
     ring = cur_ref.shape[0]
     rows = GROUP * block
     mask = diagonal_mask(rows, ring * block, block, info_ref[0])
+    spans = [block_span(arrival(info_ref, parts, part), block) for part in range(parts)]
     for part in range(parts):
-        queries = stacked_heads(q_ref, part)
-        out_grad = stacked_heads(do_ref, part)
-        out = stacked_heads(o_ref, part)
+        at = arrival(info_ref, parts, part)
+        queries = stacked_heads(q_ref, at)
+        out_grad = stacked_heads(do_ref, at)
+        out = stacked_heads(o_ref, at)
         inner = jnp.sum(out_grad.astype(f32) * out.astype(f32), axis=-1, keepdims=True)
-        log_total = log_ref[part][:, :1]
+        log_total = log_ref[at][:, :1]
         query_grad = jnp.zeros((rows, HD), f32)
         pieces = []
         if has_prev:
             log_prev = log_total + jnp.where(info_ref[1] > 0, 0.0, -masked_score).astype(f32)
-            pieces = [(prev_ref, dprev_ref, p, log_prev) for p in range(parts)]
-        pieces += [(cur_ref, sum_ref, p, log_total) for p in range(part + 1)]
-        for ref, grad_ref, at, log_row in pieces:
-            start, stop = at * block, (at + 1) * block
-            keys = cached(ref, start, stop, 0)
+            pieces = [
+                (prev_ref, dprev_ref, slice(p * block, (p + 1) * block), log_prev, False)
+                for p in range(parts)
+            ]
+        pieces += [(cur_ref, sum_ref, spans[p], log_total, p == part) for p in range(part + 1)]
+        for ref, grad_ref, span, log_row, on_diagonal in pieces:
+            keys = cached(ref, span, 0)
             probs = jnp.exp2(dot_nt(queries, keys) * log2_scale - log_row)
-            if ref is cur_ref and at == part:
+            if on_diagonal:
                 probs = jnp.where(mask, probs, 0.0)
-            probs_grad = dot_nt(out_grad, cached(ref, start, stop, HD))
+            probs_grad = dot_nt(out_grad, cached(ref, span, HD))
             score_grad = (probs * (probs_grad - inner)).astype(bf)
             query_grad = query_grad + dot(score_grad, keys)
             key_grad = dot_tn(score_grad, queries) * scaling
             value_grad = dot_tn(probs.astype(bf), out_grad)
-            grad_ref[:, start:stop, :HD] += key_grad.reshape(ring, block, HD)
-            grad_ref[:, start:stop, HD:] += value_grad.reshape(ring, block, HD)
-        store_heads(dq_ref, part, (query_grad * scaling).astype(bf))
+            grad_ref[:, span, :HD] += key_grad.reshape(ring, block, HD)
+            grad_ref[:, span, HD:] += value_grad.reshape(ring, block, HD)
+        store_heads(dq_ref, at, (query_grad * scaling).astype(bf))
     dcur_ref[...] = sum_ref[...].astype(bf)
 
 
@@ -238,7 +248,6 @@
     down_rows = shared_down.shape[1]
     is_first = section == 0
     low_core = core == 0
-    x_groups = [[x * ring + zy for x in range(heads)] for zy in range(ring)]
     zy_groups = [[x * ring + zy for zy in range(ring)] for x in range(heads)]
 
     def exchange(value, groups=None):
@@ -295,23 +304,21 @@
     gains = tail[:, experts : experts + 2].T.astype(f32)
     gain_one, gain_two = gains[0][None], gains[1][None]
 
+    all_out = lax.all_gather(my_rows(w_output[0]), "shard")
+    own_out = lax.dynamic_slice_in_dim(all_out, (position // ring) * ring, ring, axis=0)
+    output_w = ordered(own_out, twin(own_out), 1).reshape(group_width, width)
     down_half = down_rows // 2
     down_flat = (half_rows, down_half * width // half_rows)
     packed = jnp.concatenate(
         [
-            my_rows(jnp.concatenate([shared_gate[0], shared_up[0], w_output[0]], axis=1)),
+            my_rows(jnp.concatenate([shared_gate[0], shared_up[0]], axis=1)),
             mine_of(shared_down[0][:down_half], shared_down[0][down_half:]).reshape(down_flat),
         ],
         axis=1,
     )
     gathered = lax.all_gather(packed, "shard")
-    ends = (2 * shared_width, 2 * shared_width + width)
-    own_gate_up = gathered[:, :, : ends[0]]
-    own_down = gathered[:, :, ends[1] :].reshape(shards, down_half, width)
-    own_out = lax.dynamic_slice_in_dim(
-        gathered[:, :, ends[0] : ends[1]], (position // ring) * ring, ring, axis=0
-    )
-    output_w = ordered(own_out, twin(own_out), 1).reshape(group_width, width)
+    own_gate_up = gathered[:, :, : 2 * shared_width]
+    own_down = gathered[:, :, 2 * shared_width :].reshape(shards, down_half, width)
     gate_up_w = ordered(own_gate_up, twin(own_gate_up), 1).reshape(width, 2 * shared_width)
     down_w = ordered(own_down, twin(own_down), 1).reshape(shards * down_rows, width)
 
@@ -330,8 +337,9 @@
             dot(slot_ids, spread).astype(jnp.int32) == (slot_of % CAP)[None, :]
         )
 
-    info = jnp.stack([position % ring, is_first.astype(jnp.int32)]).astype(jnp.int32)
-    info_all = jnp.stack([position % ring, jnp.ones_like(position)]).astype(jnp.int32)
+    here = [position % ring, jnp.ones_like(position), position // ring]
+    info_all = jnp.stack(here).astype(jnp.int32)
+    info = jnp.stack([here[0], is_first.astype(here[0].dtype), here[2]]).astype(jnp.int32)
 
     def gate_values(normed_two, table):
         logits = jnp.where(table, dot(normed_two, router_slots), masked_score)
@@ -355,12 +363,17 @@
             rows.reshape(local_experts, shards, CAP, width).transpose(1, 0, 2, 3)
         ).reshape(slots, width)
 
+    def shift_x(value, steps):
+        pairs = [(p, (p // ring + steps) % heads * ring + p % ring) for p in range(shards)]
+        return lax.ppermute(value, "shard", pairs)
+
     def sum_over_x(rows):
-        parts = exchange(rows.astype(bf).reshape(heads, block, width), x_groups)
-        return jnp.sum(parts.astype(f32), axis=0)
+        parts = rows.reshape(heads, block, width)
+        away = [shift_x(parts[k].astype(bf), -k).astype(f32) for k in range(1, heads)]
+        return sum(away, parts[0])
 
     def ring_rows(rows):
-        return exchange(copies(rows, heads), x_groups).reshape(heads * block, width)
+        return jnp.concatenate([rows] + [shift_x(rows, k) for k in range(1, heads)], axis=0)
 
     def forward(moment, received, previous):
         first_micro = min(moment, micros - 1)
@@ -537,24 +550,19 @@
         both(normed_two), both_halves(back_rows("shared_gate_grad"), back_rows("shared_up_grad"))
     )
     grad_down = dot_tn(both(kept_rows("shared_act")), both_halves(*halves(back_rows("upstream_b"))))
-    shared_flat = (shards, down_rows * width // 2 // shared_width, shared_width)
-    shared_pieces = jnp.concatenate(
-        [
-            grad_gate_up.astype(bf).reshape(shards, rows_per, shared_width),
-            grad_down.astype(bf).reshape(shared_flat),
-        ],
-        axis=1,
-    )
-    share_shared = jnp.sum(exchange(shared_pieces).astype(f32), axis=0)
-    other_shared = twin(share_shared)
+
+    def scattered(value, groups=None):
+        count = shards if groups is None else len(groups[0])
+        pieces = value.astype(bf).reshape(count, value.shape[0] // count, value.shape[1])
+        return jnp.sum(exchange(pieces, groups).astype(f32), axis=0)
+
+    share_gate_up, share_down = scattered(grad_gate_up), scattered(grad_down)
 
     grad_out = dot_tn(
         kept_rows("attended").reshape(micros * heads * block, group_width),
         back_rows("ring_hidden"),
     )
-    share_out = jnp.sum(
-        exchange(grad_out.astype(bf).reshape(ring, rows_per, width), zy_groups).astype(f32), axis=0
-    )
+    share_out = scattered(grad_out, zy_groups)
     grad_qkv = dot_tn(kept_rows("ring_one"), back_rows("qkv_grad"))
     grad_router = dot_tn(normed_two, back_rows("logit_grad"))
     gain_sums = jnp.stack(
@@ -578,15 +586,9 @@
         return share + twin(share)
 
     out_total, qkv_total, tail_total = total(share_out), total(share_qkv), total(share_tail)
-    low_shared, high_shared = (
-        mine_of(share_shared, other_shared),
-        mine_of(other_shared, share_shared),
-    )
-    down_shape = (down_rows, width // 2)
-    down_total = jnp.concatenate(
-        [low_shared[rows_per:].reshape(down_shape), high_shared[rows_per:].reshape(down_shape)],
-        axis=1,
-    )
+    other_gate_up = twin(share_gate_up)
+    down_total = ordered(share_down, twin(share_down), 1)
+
     def by_micro(store, name):
         return jnp.stack(
             [jnp.where(is_first, store[m][name], store[m + 1][name]) for m in range(micros)]
@@ -602,8 +604,8 @@
         out_total[None],
         tail_total[:, experts + 1][None],
         tail_total[:, :experts][None],
-        low_shared[:rows_per][None],
-        high_shared[:rows_per][None],
+        mine_of(share_gate_up, other_gate_up)[None],
+        mine_of(other_gate_up, share_gate_up)[None],
         down_total[None],
         expert_grads[0][None],
         expert_grads[1][None],

time: 1120 us -> 1110 us (level)
  blocking collectives: 200 us -> 60.3 us
  waiting for transfers between devices: 288 us -> 412 us
  starting transfers between devices: 163 us -> 213 us
  matrix products: 183 us -> 162 us
  other arithmetic: 114 us -> 101 us
    all_to_all x10 -> x2, blocking collectives: 200 us -> 60.3 us  [exchange(): lax.all_to_all(value, 'shard', split_axis=0, concat_axis=0, tiled=True, a...]
    ppermute x0 -> x36, waiting for transfers between devices: none -> 117 us  [shift_x(): return lax.ppermute(value, 'shard', pairs)]
    ppermute x0 -> x36, starting transfers between devices: none -> 38.2 us  [shift_x(): return lax.ppermute(value, 'shard', pairs)]
    all_gather x0 -> x1, waiting for transfers between devices: none -> 28.8 us  [body(): all_out = lax.all_gather(my_rows(w_output[0]), 'shard')]
    all_gather x1, waiting for transfers between devices: 51.5 us -> 39.5 us  [body(): gathered = lax.all_gather(packed, 'shard')]
    all_to_all x24 -> x21, starting transfers between devices: 131 us -> 139 us  [exchange(): lax.all_to_all(value, 'shard', split_axis=0, concat_axis=0, tiled=True, a...]
    all_to_all x24 -> x21, waiting for transfers between devices: 209 us -> 202 us  [exchange(): lax.all_to_all(value, 'shard', split_axis=0, concat_axis=0, tiled=True, a...]
    unnamed x494 -> x577, local copies, waits for them, and re-layouts: 37.2 us -> 31.6 us
  transfers between devices with their start and end apart: 44 -> 79, of which waited for: 27 -> 57; matrix products, arithmetic and copies ran while one was open for 24% -> 22% of each run, Pallas kernels for 1% -> 2%
where the time goes in v5:
time: 1110 us; the launch traced here: 1090 us
  waiting for transfers between devices  412 us (37%)
  starting transfers between devices  213 us (19%)
  matrix products  162 us (15%)
  other arithmetic  101 us (9%)
  local copies, waits for them, and re-layouts  79.3 us (7%)
  blocking collectives  60.3 us (5%)
  Pallas kernels  48.8 us (4%)
  between operations  18 us (2%)
    all_to_all x21, waiting for transfers between devices, exchange(): lax.all_to_all(value, 'shard', split_axis=0, concat_axis=0, tiled=True, a...  202 us
    all_to_all x21, starting transfers between devices, exchange(): lax.all_to_all(value, 'shard', split_axis=0, concat_axis=0, tiled=True, a...  139 us
    ppermute x36, waiting for transfers between devices, shift_x(): return lax.ppermute(value, 'shard', pairs)  117 us
    all_to_all x2, blocking collectives, exchange(): lax.all_to_all(value, 'shard', split_axis=0, concat_axis=0, tiled=True, a...  60.3 us
    pallas_call x6, Pallas kernels, attention_call(): pl.pallas_call(kernel, out_shape=out_shape, in_specs=[pl.BlockSpec(memory...  48.8 us
    dot_general x21, matrix products, wide_einsum(): jnp.einsum(formula, left_side, right_side, preferred_element_type=f32)  47.9 us
    dot_general x31, matrix products, dot(): return jnp.dot(left_side, right_side, preferred_element_type=f32)  46.5 us
    dot_general x21, matrix products, dot_nt(): lax.dot_general(left_side, right_side, (((1,), (1,)), ((), ())), preferre...  42.3 us
  transfers between devices with their start and end apart: 79, of which 57 were waited for; matrix products, arithmetic and copies ran while one was open for 22% of the time, Pallas kernels for 2%

profile of v5, /device:TPU:1, one launch (start us, length us, event | category | flops | bytes accessed | tf_op | source)
XLA Modules:
  0.0 1094.9 jit_solution(2385491490707770659)
XLA Ops:
  15.8 11.6 %all-to-all-start = ((bf16[32,24,768]{2,1,0:T(8,128)(2,1)}), bf16[32,24,768]{2,1,0:T(8,128)(2,1)}, u32[]{:S(2)}, u32[]{:S(2)}) async-start(bf16[32,24,768]{2,1,0:T(8,128)(2,1)} %bitcast.465), calls=%async_computation | async-start | bytes 2359296 | tf_op jit(solution)/shard_map/all_to_all | solution.py:254
  31.9 14.9 %all-to-all-done = bf16[32,24,768]{2,1,0:T(8,128)(2,1)} async-done(((bf16[32,24,768]{2,1,0:T(8,128)(2,1)}), bf16[32,24,768]{2,1,0:T(8,128)(2,1)}, u32[]{:S(2)}, u32[]{:S(2)}) %all-to-all-start) | async-done | bytes 1179680 | tf_op jit(solution)/shard_map/all_to_all | solution.py:254
  76.8 28.8 %all-gather.4.cloned.1.call-done = bf16[32,24,1536]{2,1,0:T(8,128)(2,1)} async-done(((bf16[1,24,1536]{2,1,0:T(8,128)(2,1)}), bf16[32,24,1536]{2,1,0:T(8,128)(2,1)}) %all-gather.4.cloned.1.call-update) | async-done | bytes 2359312 | tf_op jit(solution)/shard_map/all_gather | solution.py:307
  131.9 29.7 %all_to_all.115 = bf16[32,2,8,1536]{3,2,1,0:T(8,128)(2,1)S(1)} all-to-all(bf16[32,2,8,1536]{3,2,1,0:T(8,128)(2,1)S(1)} %bitcast.460), channel_id=1, replica_groups=mesh['section'=2,'dp'=2,'shard'=32] {'shard'}, dimensions={0} | all-to-all | bytes 3145728 | tf_op jit(solution)/shard_map/all_to_all | solution.py:254
  164.7 39.5 %all-gather.6.cloned.1.call-done = bf16[768,3072]{1,0:T(8,128)(2,1)} async-done(((bf16[24,3072]{1,0:T(8,128)(2,1)}), bf16[768,3072]{1,0:T(8,128)(2,1)}) %all-gather.6.cloned.1.call-update) | async-done | bytes 4718608 | tf_op jit(solution)/shard_map/all_gather | solution.py:319
  229.6 14.2 %all-to-all-done.3 = bf16[32,2,8,1536]{3,2,1,0:T(8,128)(2,1)} async-done(((bf16[32,2,8,1536]{3,2,1,0:T(8,128)(2,1)}), bf16[32,2,8,1536]{3,2,1,0:T(8,128)(2,1)}, u32[]{:S(2)}, u32[]{:S(2)}) %all-to-all-start.3) | async-done | bytes 1572896 | tf_op jit(solution)/shard_map/all_to_all | solution.py:254
  296.0 12.6 %all-to-all-done.4.refs_1_.refs_0_.refs_2_ = bf16[8,256,256]{2,1,0:T(8,128)(2,1)} async-done(((bf16[8,256,256]{2,1,0:T(8,128)(2,1)}), bf16[8,256,256]{2,1,0:T(8,128)(2,1)}, u32[]{:S(2)}, u32[]{:S(2)}) %all-to-all-start.4) | async-done | bytes 1048608 | tf_op jit(solution)/shard_map/all_to_all | solution.py:254
  327.2 30.6 %all_to_all.116 = bf16[32,2,8,1536]{3,2,1,0:T(8,128)(2,1)S(1)} all-to-all(bf16[32,2,8,1536]{3,2,1,0:T(8,128)(2,1)S(1)} %bitcast.461), channel_id=1, replica_groups=mesh['section'=2,'dp'=2,'shard'=32] {'shard'}, dimensions={0} | all-to-all | bytes 3145728 | tf_op jit(solution)/shard_map/all_to_all | solution.py:254
  379.2 12.3 %all-to-all-done.6 = bf16[32,2,8,1536]{3,2,1,0:T(8,128)(2,1)} async-done(((bf16[32,2,8,1536]{3,2,1,0:T(8,128)(2,1)}), bf16[32,2,8,1536]{3,2,1,0:T(8,128)(2,1)}, u32[]{:S(2)}, u32[]{:S(2)}) %all-to-all-start.6) | async-done | bytes 1572896 | tf_op jit(solution)/shard_map/all_to_all | solution.py:254
  426.0 12.1 %all-to-all-done.7.refs_1_ = bf16[8,256,256]{2,1,0:T(8,128)(2,1)} async-done(((bf16[8,256,256]{2,1,0:T(8,128)(2,1)}), bf16[8,256,256]{2,1,0:T(8,128)(2,1)}, u32[]{:S(2)}, u32[]{:S(2)}) %all-to-all-start.7) | async-done | bytes 1048608 | tf_op jit(solution)/shard_map/all_to_all | solution.py:254
  470.8 16.8 %all-to-all-done.8 = bf16[32,2,8,1536]{3,2,1,0:T(8,128)(2,1)} async-done(((bf16[32,2,8,1536]{3,2,1,0:T(8,128)(2,1)}), bf16[32,2,8,1536]{3,2,1,0:T(8,128)(2,1)}, u32[]{:S(2)}, u32[]{:S(2)}) %all-to-all-start.8) | async-done | bytes 1572896 | tf_op jit(solution)/shard_map/all_to_all | solution.py:254
  503.4 11.6 %all-to-all-done.10 = bf16[32,2,8,1536]{3,2,1,0:T(8,128)(2,1)} async-done(((bf16[32,2,8,1536]{3,2,1,0:T(8,128)(2,1)}), bf16[32,2,8,1536]{3,2,1,0:T(8,128)(2,1)}, u32[]{:S(2)}, u32[]{:S(2)}) %all-to-all-start.10) | async-done | bytes 1572896 | tf_op jit(solution)/shard_map/all_to_all | solution.py:254
  529.7 14.0 %all-to-all-done.9 = bf16[32,2,8,1536]{3,2,1,0:T(8,128)(2,1)} async-done(((bf16[32,2,8,1536]{3,2,1,0:T(8,128)(2,1)}), bf16[32,2,8,1536]{3,2,1,0:T(8,128)(2,1)}, u32[]{:S(2)}, u32[]{:S(2)}) %all-to-all-start.9) | async-done | bytes 1572896 | tf_op jit(solution)/shard_map/all_to_all | solution.py:254
  560.9 11.8 %all-to-all-done.11 = bf16[32,2,8,1536]{3,2,1,0:T(8,128)(2,1)} async-done(((bf16[32,2,8,1536]{3,2,1,0:T(8,128)(2,1)}), bf16[32,2,8,1536]{3,2,1,0:T(8,128)(2,1)}, u32[]{:S(2)}, u32[]{:S(2)}) %all-to-all-start.11) | async-done | bytes 1572896 | tf_op jit(solution)/shard_map/all_to_all | solution.py:254
  594.9 13.5 %shard_map.274 = (bf16[4,64,384]{2,1,0:T(8,128)(2,1)S(1)}, bf16[8,256,256]{2,1,0:T(8,128)(2,1)S(1)}, f32[8,256,256]{2,1,0:T(8,128)S(1)}) custom-call(s32[3]{0:T(128)S(1)} %add_add_fusion.info_ref, bf16[4,64,640]{2,1,0:T(8,128)(2,1)S(1)} %bitcast.416, bf16[4,64,384]{2,1,0:T(8,128)(2,1)S(1)} %bitcast.419, bf16[4,64,384]{2,1,0:T(8,128)(2,1)S(1)} %copy-done.10, ...), custom_call_target="tpu_custom_call" | custom-call | flops 2013265920 | bytes 3112960 | tf_op jit(solution)/shard_map/pallas_call | solution.py:175
  617.5 14.1 %all-to-all-done.12 = bf16[8,256,256]{2,1,0:T(8,128)(2,1)} async-done(((bf16[8,256,256]{2,1,0:T(8,128)(2,1)}), bf16[8,256,256]{2,1,0:T(8,128)(2,1)}, u32[]{:S(2)}, u32[]{:S(2)}) %all-to-all-start.12) | async-done | bytes 1048608 | tf_op jit(solution)/shard_map/all_to_all | solution.py:254
  649.3 12.8 %collective-permute-done.30 = bf16[64,1536]{1,0:T(8,128)(2,1)S(1)} collective-permute-done((bf16[64,1536]{1,0:T(8,128)(2,1)S(1)}, bf16[64,1536]{1,0:T(8,128)(2,1)S(1)}, u32[]{:S(2)}, u32[]{:S(2)}) %collective-permute-start.30) | collective-permute-done | bytes 196640 | tf_op jit(solution)/shard_map/ppermute | solution.py:521
  677.1 17.5 %all-to-all-done.13 = bf16[32,2,8,1536]{3,2,1,0:T(8,128)(2,1)} async-done(((bf16[32,2,8,1536]{3,2,1,0:T(8,128)(2,1)}), bf16[32,2,8,1536]{3,2,1,0:T(8,128)(2,1)}, u32[]{:S(2)}, u32[]{:S(2)}) %all-to-all-start.13) | async-done | bytes 1572896 | tf_op jit(solution)/shard_map/all_to_all | solution.py:254
  722.3 9.5 all-to-all-done.14
  752.3 13.6 %shard_map.275 = (bf16[4,64,384]{2,1,0:T(8,128)(2,1)S(1)}, bf16[8,256,256]{2,1,0:T(8,128)(2,1)S(1)}, f32[8,256,256]{2,1,0:T(8,128)S(1)}) custom-call(s32[3]{0:T(128)S(1)} %add_add_fusion.1.info_ref, bf16[4,64,640]{2,1,0:T(8,128)(2,1)S(1)} %bitcast.414, bf16[4,64,384]{2,1,0:T(8,128)(2,1)S(1)} %bitcast.417, bf16[4,64,384]{2,1,0:T(8,128)(2,1)S(1)} %copy-done.8, ...), custom_call_target="tpu_custom_call" | custom-call | flops 3019898880 | bytes 4423680 | tf_op jit(solution)/shard_map/pallas_call | solution.py:175
  882.1 8.8 all-to-all-start.21
  905.5 32.0 %collective-permute-done.40 = bf16[64,1536]{1,0:T(8,128)(2,1)S(1)} collective-permute-done((bf16[64,1536]{1,0:T(8,128)(2,1)S(1)}, bf16[64,1536]{1,0:T(8,128)(2,1)S(1)}, u32[]{:S(2)}, u32[]{:S(2)}) %collective-permute-start.40) | collective-permute-done | bytes 196640 | tf_op jit(solution)/shard_map/ppermute | solution.py:368
  1027.9 11.2 %all-to-all-done.22 = bf16[32,32,768]{2,1,0:T(8,128)(2,1)} async-done(((bf16[32,32,768]{2,1,0:T(8,128)(2,1)}), bf16[32,32,768]{2,1,0:T(8,128)(2,1)}, u32[]{:S(2)}, u32[]{:S(2)}) %all-to-all-start.22) | async-done | bytes 1572896 | tf_op jit(solution)/shard_map/all_to_all | solution.py:254
  1067.7 10.1 all-to-all-done.19
  (968 shorter events, 673.3 us)
Async XLA Ops:
  7.2 98.4 %all-gather.4.cloned.1.call-start = ((), (), s32[]{:S(2)}) async-start(), calls=%async_computation.23 | async-start | bytes 2433024 | tf_op jit(solution)/shard_map/all_gather | solution.py:307
  15.8 31.0 %all-to-all-start = ((bf16[32,24,768]{2,1,0:T(8,128)(2,1)}), bf16[32,24,768]{2,1,0:T(8,128)(2,1)}, u32[]{:S(2)}, u32[]{:S(2)}) async-start(bf16[32,24,768]{2,1,0:T(8,128)(2,1)} %bitcast.465), calls=%async_computation | async-start | bytes 2359296 | tf_op jit(solution)/shard_map/all_to_all | solution.py:254
  27.4 176.9 %all-gather.6.cloned.1.call-start = ((), (), s32[]{:S(2)}) async-start(), calls=%async_computation.24 | async-start | bytes 4866048 | tf_op jit(solution)/shard_map/all_gather | solution.py:319
  72.4 36.6 %all-to-all-start.1 = ((bf16[8,256,256]{2,1,0:T(8,128)(2,1)}), bf16[8,256,256]{2,1,0:T(8,128)(2,1)}, u32[]{:S(2)}, u32[]{:S(2)}) async-start(bf16[8,256,256]{2,1,0:T(8,128)(2,1)} %broadcast_in_dim.53), calls=%async_computation.1 | async-start | bytes 2097152 | tf_op jit(solution)/shard_map/all_to_all | solution.py:254
  208.4 40.1 %collective-permute-start.8 = (bf16[32,24,2048]{2,1,0:T(8,128)(2,1)}, bf16[32,24,2048]{2,1,0:T(8,128)(2,1)}, u32[]{:S(2)}, u32[]{:S(2)}) collective-permute-start(bf16[32,24,2048]{2,1,0:T(8,128)(2,1)} %slice.324), channel_id=1, source_target_pairs={{0,32},{32,0},{1,33},{33,1},{2,34},{34,2},{3,35},{35,3},{4,36},{36... | collective-permute-start | bytes 9437192 | tf_op jit(solution)/shard_map/ppermute | solution.py:262
  214.1 29.7 %all-to-all-start.3 = ((bf16[32,2,8,1536]{3,2,1,0:T(8,128)(2,1)}), bf16[32,2,8,1536]{3,2,1,0:T(8,128)(2,1)}, u32[]{:S(2)}, u32[]{:S(2)}) async-start(bf16[32,2,8,1536]{3,2,1,0:T(8,128)(2,1)} %bitcast.457), calls=%async_computation.3 | async-start | bytes 3145728 | tf_op jit(solution)/shard_map/all_to_all | solution.py:254
  543.7 29.0 %all-to-all-start.11 = ((bf16[32,2,8,1536]{3,2,1,0:T(8,128)(2,1)}), bf16[32,2,8,1536]{3,2,1,0:T(8,128)(2,1)}, u32[]{:S(2)}, u32[]{:S(2)}) async-start(bf16[32,2,8,1536]{3,2,1,0:T(8,128)(2,1)} %bitcast.455), calls=%async_computation.11 | async-start | bytes 3145728 | tf_op jit(solution)/shard_map/all_to_all | solution.py:254
  664.6 30.0 %all-to-all-start.13 = ((bf16[32,2,8,1536]{3,2,1,0:T(8,128)(2,1)}), bf16[32,2,8,1536]{3,2,1,0:T(8,128)(2,1)}, u32[]{:S(2)}, u32[]{:S(2)}) async-start(bf16[32,2,8,1536]{3,2,1,0:T(8,128)(2,1)} %bitcast.463), calls=%async_computation.13 | async-start | bytes 3145728 | tf_op jit(solution)/shard_map/all_to_all | solution.py:254
  702.8 29.0 %all-to-all-start.14 = ((bf16[32,2,8,1536]{3,2,1,0:T(8,128)(2,1)}), bf16[32,2,8,1536]{3,2,1,0:T(8,128)(2,1)}, u32[]{:S(2)}, u32[]{:S(2)}) async-start(bf16[32,2,8,1536]{3,2,1,0:T(8,128)(2,1)} %bitcast.454), calls=%async_computation.14 | async-start | bytes 3145728 | tf_op jit(solution)/shard_map/all_to_all | solution.py:254
  711.5 153.1 %collective-permute-start.47 = (bf16[128,1536]{1,0:T(8,128)(2,1)}, bf16[128,1536]{1,0:T(8,128)(2,1)}, u32[]{:S(2)}, u32[]{:S(2)}) collective-permute-start(bf16[128,1536]{1,0:T(8,128)(2,1)} %pad_maximum_fusion.11), channel_id=1, source_target_pairs={{0,32},{32,0},{1,33},{33,1},{2,34},{34,2},{3,35},{35,3},{4,36},{36... | collective-permute-start | bytes 1179656 | tf_op jit(solution)/shard_map/ppermute | solution.py:262
  716.0 286.9 %collective-permute-start.50 = (bf16[128,1024]{1,0:T(8,128)(2,1)}, bf16[128,1024]{1,0:T(8,128)(2,1)}, u32[]{:S(2)}, u32[]{:S(2)}) collective-permute-start(bf16[128,1024]{1,0:T(8,128)(2,1)} %pad_maximum_fusion.17), channel_id=1, source_target_pairs={{0,32},{32,0},{1,33},{33,1},{2,34},{34,2},{3,35},{35,3},{4,36},{36... | collective-permute-start | bytes 786440 | tf_op jit(solution)/shard_map/ppermute | solution.py:262
  814.2 29.7 %all-to-all-start.16 = ((bf16[32,2,8,1536]{3,2,1,0:T(8,128)(2,1)}), bf16[32,2,8,1536]{3,2,1,0:T(8,128)(2,1)}, u32[]{:S(2)}, u32[]{:S(2)}) async-start(bf16[32,2,8,1536]{3,2,1,0:T(8,128)(2,1)} %bitcast.462), calls=%async_computation.16 | async-start | bytes 3145728 | tf_op jit(solution)/shard_map/all_to_all | solution.py:254
  829.1 35.5 %collective-permute-start.48 = (bf16[128,1024]{1,0:T(8,128)(2,1)}, bf16[128,1024]{1,0:T(8,128)(2,1)}, u32[]{:S(2)}, u32[]{:S(2)}) collective-permute-start(bf16[128,1024]{1,0:T(8,128)(2,1)} %get-tuple-element.127), channel_id=1, source_target_pairs={{0,32},{32,0},{1,33},{33,1},{2,34},{34,2},{3,35},{35,3},{4,36},{36... | collective-permute-start | bytes 786440 | tf_op jit(solution)/shard_map/ppermute | solution.py:262
  852.8 29.3 %all-to-all-start.17 = ((bf16[32,2,8,1536]{3,2,1,0:T(8,128)(2,1)}), bf16[32,2,8,1536]{3,2,1,0:T(8,128)(2,1)}, u32[]{:S(2)}, u32[]{:S(2)}) async-start(bf16[32,2,8,1536]{3,2,1,0:T(8,128)(2,1)} %bitcast.453), calls=%async_computation.17 | async-start | bytes 3145728 | tf_op jit(solution)/shard_map/all_to_all | solution.py:254
  872.2 173.3 %collective-permute-start.53 = (bf16[2,1536,512]{2,1,0:T(8,128)(2,1)}, bf16[2,1536,512]{2,1,0:T(8,128)(2,1)}, u32[]{:S(2)}, u32[]{:S(2)}) collective-permute-start(bf16[2,1536,512]{2,1,0:T(8,128)(2,1)} %convolution_convert_fusion.3), channel_id=1, source_target_pairs={{0,32},{32,0},{1,33},{33,1},{2,34},{34,2},{3,35},{35,3},{4,36},{36... | collective-permute-start | bytes 9437192 | tf_op jit(solution)/shard_map/ppermute | solution.py:262
  882.1 67.4 %all-to-all-start.21 = ((bf16[32,48,1024]{2,1,0:T(8,128)(2,1)}), bf16[32,48,1024]{2,1,0:T(8,128)(2,1)}, u32[]{:S(2)}, u32[]{:S(2)}) async-start(bf16[32,48,1024]{2,1,0:T(8,128)(2,1)} %bitcast.466), calls=%async_computation.21 | async-start | bytes 6291456 | tf_op jit(solution)/shard_map/all_to_all | solution.py:254
  901.1 36.4 %collective-permute-start.40 = (bf16[64,1536]{1,0:T(8,128)(2,1)S(1)}, bf16[64,1536]{1,0:T(8,128)(2,1)S(1)}, u32[]{:S(2)}, u32[]{:S(2)}) collective-permute-start(bf16[64,1536]{1,0:T(8,128)(2,1)S(1)} %fusion.306), channel_id=1, source_target_pairs={{0,24},{1,25},{2,26},{3,27},{4,28},{5,29},{6,30},{7,31},{8,0},{9,1... | collective-permute-start | bytes 589832 | tf_op jit(solution)/shard_map/ppermute | solution.py:368
  903.6 33.9 %collective-permute-start.39 = (bf16[64,1536]{1,0:T(8,128)(2,1)S(1)}, bf16[64,1536]{1,0:T(8,128)(2,1)S(1)}, u32[]{:S(2)}, u32[]{:S(2)}) collective-permute-start(bf16[64,1536]{1,0:T(8,128)(2,1)S(1)} %fusion.306), channel_id=1, source_target_pairs={{0,16},{1,17},{2,18},{3,19},{4,20},{5,21},{6,22},{7,23},{8,24},{9,... | collective-permute-start | bytes 589832 | tf_op jit(solution)/shard_map/ppermute | solution.py:368
  904.1 34.9 %collective-permute-start.38 = (bf16[64,1536]{1,0:T(8,128)(2,1)S(1)}, bf16[64,1536]{1,0:T(8,128)(2,1)S(1)}, u32[]{:S(2)}, u32[]{:S(2)}) collective-permute-start(bf16[64,1536]{1,0:T(8,128)(2,1)S(1)} %fusion.306), channel_id=1, source_target_pairs={{0,8},{1,9},{2,10},{3,11},{4,12},{5,13},{6,14},{7,15},{8,16},{9,17... | collective-permute-start | bytes 589832 | tf_op jit(solution)/shard_map/ppermute | solution.py:368
  969.3 38.7 %all-to-all-start.20 = ((bf16[8,48,1536]{2,1,0:T(8,128)(2,1)}), bf16[8,48,1536]{2,1,0:T(8,128)(2,1)}, u32[]{:S(2)}, u32[]{:S(2)}) async-start(bf16[8,48,1536]{2,1,0:T(8,128)(2,1)} %bitcast.472), calls=%async_computation.20 | async-start | bytes 2359296 | tf_op jit(solution)/shard_map/all_to_all | solution.py:254
  988.2 63.9 %collective-permute-start.54 = (bf16[2,1536,512]{2,1,0:T(8,128)(2,1)}, bf16[2,1536,512]{2,1,0:T(8,128)(2,1)}, u32[]{:S(2)}, u32[]{:S(2)}) collective-permute-start(bf16[2,1536,512]{2,1,0:T(8,128)(2,1)} %convolution_convert_fusion.2), channel_id=1, source_target_pairs={{0,32},{32,0},{1,33},{33,1},{2,34},{34,2},{3,35},{35,3},{4,36},{36... | collective-permute-start | bytes 9437192 | tf_op jit(solution)/shard_map/ppermute | solution.py:262
  995.2 65.9 %collective-permute-start.55 = (bf16[2,512,1536]{2,1,0:T(8,128)(2,1)}, bf16[2,512,1536]{2,1,0:T(8,128)(2,1)}, u32[]{:S(2)}, u32[]{:S(2)}) collective-permute-start(bf16[2,512,1536]{2,1,0:T(8,128)(2,1)} %convolution_convert_fusion.1), channel_id=1, source_target_pairs={{0,32},{32,0},{1,33},{33,1},{2,34},{34,2},{3,35},{35,3},{4,36},{36... | collective-permute-start | bytes 9437192 | tf_op jit(solution)/shard_map/ppermute | solution.py:262
  1008.0 31.1 %all-to-all-start.22 = ((bf16[32,32,768]{2,1,0:T(8,128)(2,1)}), bf16[32,32,768]{2,1,0:T(8,128)(2,1)}, u32[]{:S(2)}, u32[]{:S(2)}) async-start(bf16[32,32,768]{2,1,0:T(8,128)(2,1)} %bitcast.469), calls=%async_computation.22 | async-start | bytes 3145728 | tf_op jit(solution)/shard_map/all_to_all | solution.py:254
  1039.1 38.7 %all-to-all-start.19 = ((bf16[32,48,768]{2,1,0:T(8,128)(2,1)}), bf16[32,48,768]{2,1,0:T(8,128)(2,1)}, u32[]{:S(2)}, u32[]{:S(2)}) async-start(bf16[32,48,768]{2,1,0:T(8,128)(2,1)} %maximum_maximum_fusion), calls=%async_computation.19 | async-start | bytes 4718592 | tf_op jit(solution)/shard_map/all_to_all | solution.py:254
  (341 other events, 4314.5 us)
Sparse Core Ops, SparseCore 0:
  11.6 93.9 all-gather.3
  109.1 95.1 all-gather.5

commit v6 on v5

--- a/solution.py
+++ b/solution.py
@@ -297,16 +297,6 @@
     by_head = jnp.broadcast_to(
         by_head[:, None], (heads, ring, half_rows, part_width + 128)
     ).reshape(shards, half_rows, part_width + 128)
-    own_part = exchange(by_head)
-    fetched = ordered(own_part, twin(own_part), 1).reshape(width, part_width + 128)
-    qkv_w, tail = fetched[:, :part_width], fetched[:, part_width:]
-    router_w = tail[:, :experts]
-    gains = tail[:, experts : experts + 2].T.astype(f32)
-    gain_one, gain_two = gains[0][None], gains[1][None]
-
-    all_out = lax.all_gather(my_rows(w_output[0]), "shard")
-    own_out = lax.dynamic_slice_in_dim(all_out, (position // ring) * ring, ring, axis=0)
-    output_w = ordered(own_out, twin(own_out), 1).reshape(group_width, width)
     down_half = down_rows // 2
     down_flat = (half_rows, down_half * width // half_rows)
     packed = jnp.concatenate(
@@ -316,11 +306,23 @@
         ],
         axis=1,
     )
+    by_head, packed = lax.optimization_barrier((by_head, packed))
     gathered = lax.all_gather(packed, "shard")
+    own_part = exchange(by_head)
+    own_part, out_rows = lax.optimization_barrier(
+        (own_part, copies(my_rows(w_output[0]), ring))
+    )
+    fetched = ordered(own_part, twin(own_part), 1).reshape(width, part_width + 128)
+    qkv_w, tail = fetched[:, :part_width], fetched[:, part_width:]
+    own_out = exchange(out_rows, zy_groups)
+    output_w = ordered(own_out, twin(own_out), 1).reshape(group_width, width)
     own_gate_up = gathered[:, :, : 2 * shared_width]
     own_down = gathered[:, :, 2 * shared_width :].reshape(shards, down_half, width)
     gate_up_w = ordered(own_gate_up, twin(own_gate_up), 1).reshape(width, 2 * shared_width)
     down_w = ordered(own_down, twin(own_down), 1).reshape(shards * down_rows, width)
+    router_w = tail[:, :experts]
+    gains = tail[:, experts : experts + 2].T.astype(f32)
+    gain_one, gain_two = gains[0][None], gains[1][None]
 
     expert_g, expert_u, expert_d = expert_gate[0], expert_up[0], expert_down[0]
     slot_of = jnp.arange(slots, dtype=jnp.int32)
@@ -363,9 +365,23 @@
             rows.reshape(local_experts, shards, CAP, width).transpose(1, 0, 2, 3)
         ).reshape(slots, width)
 
+    def moved(p, steps):
+        return (p // ring + steps) % heads * ring + p % ring
+
     def shift_x(value, steps):
-        pairs = [(p, (p // ring + steps) % heads * ring + p % ring) for p in range(shards)]
-        return lax.ppermute(value, "shard", pairs)
+        return lax.ppermute(value, "shard", [(p, moved(p, steps)) for p in range(shards)])
+
+    def next_ring(value):
+        return jnp.stack(
+            [
+                lax.ppermute(
+                    value,
+                    ("section", "shard"),
+                    [(p, shards + moved(p, steps)) for p in range(shards)],
+                )
+                for steps in range(heads)
+            ]
+        )
 
     def sum_over_x(rows):
         parts = rows.reshape(heads, block, width)
@@ -375,17 +391,23 @@
     def ring_rows(rows):
         return jnp.concatenate([rows] + [shift_x(rows, k) for k in range(1, heads)], axis=0)
 
+    ring_inputs = [
+        jnp.stack([inputs[0, m]] + [shift_x(inputs[0, m], k) for k in range(1, heads)])
+        for m in range(micros)
+    ]
+
     def forward(moment, received, previous):
         first_micro = min(moment, micros - 1)
         second_micro = max(moment - 1, 0)
-        layer_b = jnp.where(is_first, inputs[0, first_micro], received)
+        ring_b = jnp.where(is_first, ring_inputs[first_micro], received)
+        layer_b = ring_b[0]
         table = slot_table(
             jnp.where(is_first, routes[0, 0, first_micro], routes[0, 0, second_micro])
         )
         pick = table.astype(bf)
         layer_in = layer_b.astype(f32)
-        normed_one = (layer_in * inverse_rms(layer_in) * gain_one).astype(bf)
-        ring_one = ring_rows(normed_one)
+        ring_in = ring_b.reshape(heads * block, width).astype(f32)
+        ring_one = (ring_in * inverse_rms(ring_in) * gain_one).astype(bf)
         qkv = dot(ring_one, qkv_w).astype(bf)
         cache = exchange(copies(qkv[:, group_width:], ring), zy_groups)
         qkv = qkv.reshape(heads, block, part_width)
@@ -404,7 +426,8 @@
         routed = dot(high, returned) + dot(low, returned)
         shared_gate_pre, shared_up_pre = halves(dot(normed_two, gate_up_w))
         shared_act = (silu_parts(shared_gate_pre)[0] * shared_up_pre).astype(bf)
-        output_b = (hidden + routed + dot(shared_act, down_w)).astype(bf)
+        beside = lax.optimization_barrier(hidden + dot(shared_act, down_w))
+        output_b = (beside + routed).astype(bf)
         return dict(
             layer_b=layer_b,
             pick=pick,
@@ -455,6 +478,7 @@
         picked_grad = gates * (gate_grad - jnp.sum(gates * gate_grad, axis=1, keepdims=True))
         picked_b = picked_grad.astype(bf)
         normed_two_grad = normed_two_grad + dot_nt(picked_b, router_slots)
+        normed_two_grad = lax.optimization_barrier(normed_two_grad)
         normed_two_grad = normed_two_grad + dot(kept["pick"], returned_grad)
         logit_grad = dot_nt(picked_b, spread).astype(bf)
         hidden_norm_grad, gain_two_grad = norm_back(hidden, gain_two, normed_two_grad)
@@ -503,13 +527,13 @@
 
     nothing = jnp.zeros((block, width), bf)
     saved = []
-    received, previous = nothing, None
+    received, previous = jnp.zeros((heads, block, width), bf), None
     for moment in range(micros + 1):
         kept = forward(moment, received, previous)
         saved.append(kept)
         previous = kept["cache"]
         if moment < micros:
-            received = lax.ppermute(kept["output_b"], "section", [(0, 1)])
+            received = next_ring(kept["output_b"])
     backs = [None] * (micros + 1)
     received, carried = nothing, None
     for source in range(micros, -1, -1):

time: 1110 us -> 1070 us (0.964)
  waiting for transfers between devices: 412 us -> 358 us
  starting transfers between devices: 213 us -> 231 us
    all_gather x1, waiting for transfers between devices: 39.5 us -> 0.01 us  [body(): gathered = lax.all_gather(packed, 'shard')]
    all_gather x1 -> x0, waiting for transfers between devices: 28.8 us -> none  [body(): all_out = lax.all_gather(my_rows(w_output[0]), 'shard')]
    all_to_all x21 -> x22, waiting for transfers between devices: 202 us -> 230 us  [exchange(): lax.all_to_all(value, 'shard', split_axis=0, concat_axis=0, tiled=True, a...]
    ppermute x38 -> x41, starting transfers between devices: 45.7 us -> 55.5 us  [the longest x33 36.1 us: shift_x(): lax.ppermute(value, 'shard', [(p, moved(p, steps)) for p in range(shards)])]
    ppermute x38 -> x41, waiting for transfers between devices: 122 us -> 113 us  [the longest x33 86.6 us: shift_x(): lax.ppermute(value, 'shard', [(p, moved(p, steps)) for p in range(shards)])]
    all_to_all x21 -> x22, starting transfers between devices: 139 us -> 147 us  [exchange(): lax.all_to_all(value, 'shard', split_axis=0, concat_axis=0, tiled=True, a...]
    unnamed x577 -> x567, local copies, waits for them, and re-layouts: 31.6 us -> 31 us
  transfers between devices with their start and end apart: 79 -> 82, of which waited for: 57 -> 52; matrix products, arithmetic and copies ran while one was open for 22% -> 24% of each run, Pallas kernels for 2% -> 2%
where the time goes in v6:
time: 1070 us; the launch traced here: 1060 us
  waiting for transfers between devices  358 us (33%)
  starting transfers between devices  231 us (22%)
  matrix products  161 us (15%)
  other arithmetic  108 us (10%)
  local copies, waits for them, and re-layouts  80.8 us (8%)
  blocking collectives  54.7 us (5%)
  Pallas kernels  48.9 us (5%)
  between operations  18 us (2%)
    all_to_all x22, waiting for transfers between devices, exchange(): lax.all_to_all(value, 'shard', split_axis=0, concat_axis=0, tiled=True, a...  230 us
    all_to_all x22, starting transfers between devices, exchange(): lax.all_to_all(value, 'shard', split_axis=0, concat_axis=0, tiled=True, a...  147 us
    ppermute x33, waiting for transfers between devices, shift_x(): lax.ppermute(value, 'shard', [(p, moved(p, steps)) for p in range(shards)])  86.6 us
    all_to_all x2, blocking collectives, exchange(): lax.all_to_all(value, 'shard', split_axis=0, concat_axis=0, tiled=True, a...  54.7 us
    pallas_call x6, Pallas kernels, attention_call(): pl.pallas_call(kernel, out_shape=out_shape, in_specs=[pl.BlockSpec(memory...  48.9 us
    dot_general x21, matrix products, dot_nt(): lax.dot_general(left_side, right_side, (((1,), (1,)), ((), ())), preferre...  46.5 us
    dot_general x31, matrix products, dot(): return jnp.dot(left_side, right_side, preferred_element_type=f32)  46.2 us
    dot_general x21, matrix products, wide_einsum(): jnp.einsum(formula, left_side, right_side, preferred_element_type=f32)  44.3 us
  transfers between devices with their start and end apart: 82, of which 52 were waited for; matrix products, arithmetic and copies ran while one was open for 24% of the time, Pallas kernels for 2%

profile of v6, /device:TPU:1, one launch (start us, length us, event | category | flops | bytes accessed | tf_op | source)
XLA Modules:
  0.0 1061.7 jit_solution(2365102774947889971)
XLA Ops:
  17.3 11.6 %all-to-all-start = ((bf16[32,24,768]{2,1,0:T(8,128)(2,1)}), bf16[32,24,768]{2,1,0:T(8,128)(2,1)}, u32[]{:S(2)}, u32[]{:S(2)}) async-start(bf16[32,24,768]{2,1,0:T(8,128)(2,1)} %bitcast.539), calls=%async_computation | async-start | bytes 2359296 | tf_op jit(solution)/shard_map/all_to_all | solution.py:254
  29.7 18.0 %all-to-all-done = bf16[32,24,768]{2,1,0:T(8,128)(2,1)} async-done(((bf16[32,24,768]{2,1,0:T(8,128)(2,1)}), bf16[32,24,768]{2,1,0:T(8,128)(2,1)}, u32[]{:S(2)}, u32[]{:S(2)}) %all-to-all-start) | async-done | bytes 1179680 | tf_op jit(solution)/shard_map/all_to_all | solution.py:254
  86.1 17.6 %all-to-all-done.1.refs_0_.refs_1_ = bf16[8,256,256]{2,1,0:T(8,128)(2,1)} async-done(((bf16[8,256,256]{2,1,0:T(8,128)(2,1)}), bf16[8,256,256]{2,1,0:T(8,128)(2,1)}, u32[]{:S(2)}, u32[]{:S(2)}) %all-to-all-start.1) | async-done | bytes 1048608 | tf_op jit(solution)/shard_map/all_to_all | solution.py:254
  131.0 25.7 %all_to_all.120 = bf16[32,2,8,1536]{3,2,1,0:T(8,128)(2,1)S(1)} all-to-all(bf16[32,2,8,1536]{3,2,1,0:T(8,128)(2,1)S(1)} %bitcast.534), channel_id=1, replica_groups=mesh['section'=2,'dp'=2,'shard'=32] {'shard'}, dimensions={0} | all-to-all | bytes 3145728 | tf_op jit(solution)/shard_map/all_to_all | solution.py:254
  190.3 10.5 all-to-all-done.4
  257.6 15.4 %all-to-all-done.5.refs_1_.refs_0_.refs_2_ = bf16[8,256,256]{2,1,0:T(8,128)(2,1)} async-done(((bf16[8,256,256]{2,1,0:T(8,128)(2,1)}), bf16[8,256,256]{2,1,0:T(8,128)(2,1)}, u32[]{:S(2)}, u32[]{:S(2)}) %all-to-all-start.5) | async-done | bytes 1048608 | tf_op jit(solution)/shard_map/all_to_all | solution.py:254
  296.1 28.9 %all_to_all.121 = bf16[32,2,8,1536]{3,2,1,0:T(8,128)(2,1)S(1)} all-to-all(bf16[32,2,8,1536]{3,2,1,0:T(8,128)(2,1)S(1)} %bitcast.535), channel_id=1, replica_groups=mesh['section'=2,'dp'=2,'shard'=32] {'shard'}, dimensions={0} | all-to-all | bytes 3145728 | tf_op jit(solution)/shard_map/all_to_all | solution.py:254
  344.0 14.7 %all-to-all-done.7 = bf16[32,2,8,1536]{3,2,1,0:T(8,128)(2,1)} async-done(((bf16[32,2,8,1536]{3,2,1,0:T(8,128)(2,1)}), bf16[32,2,8,1536]{3,2,1,0:T(8,128)(2,1)}, u32[]{:S(2)}, u32[]{:S(2)}) %all-to-all-start.7) | async-done | bytes 1572896 | tf_op jit(solution)/shard_map/all_to_all | solution.py:254
  377.1 10.3 collective-permute-done.20
  400.1 16.4 %all-to-all-done.8.refs_1_ = bf16[8,256,256]{2,1,0:T(8,128)(2,1)} async-done(((bf16[8,256,256]{2,1,0:T(8,128)(2,1)}), bf16[8,256,256]{2,1,0:T(8,128)(2,1)}, u32[]{:S(2)}, u32[]{:S(2)}) %all-to-all-start.8) | async-done | bytes 1048608 | tf_op jit(solution)/shard_map/all_to_all | solution.py:254
  452.2 17.4 %all-to-all-done.9 = bf16[32,2,8,1536]{3,2,1,0:T(8,128)(2,1)} async-done(((bf16[32,2,8,1536]{3,2,1,0:T(8,128)(2,1)}), bf16[32,2,8,1536]{3,2,1,0:T(8,128)(2,1)}, u32[]{:S(2)}, u32[]{:S(2)}) %all-to-all-start.9) | async-done | bytes 1572896 | tf_op jit(solution)/shard_map/all_to_all | solution.py:254
  486.1 12.3 %all-to-all-done.11 = bf16[32,2,8,1536]{3,2,1,0:T(8,128)(2,1)} async-done(((bf16[32,2,8,1536]{3,2,1,0:T(8,128)(2,1)}), bf16[32,2,8,1536]{3,2,1,0:T(8,128)(2,1)}, u32[]{:S(2)}, u32[]{:S(2)}) %all-to-all-start.11) | async-done | bytes 1572896 | tf_op jit(solution)/shard_map/all_to_all | solution.py:254
  518.7 10.1 all-to-all-done.10
  547.9 11.3 %all-to-all-done.12 = bf16[32,2,8,1536]{3,2,1,0:T(8,128)(2,1)} async-done(((bf16[32,2,8,1536]{3,2,1,0:T(8,128)(2,1)}), bf16[32,2,8,1536]{3,2,1,0:T(8,128)(2,1)}, u32[]{:S(2)}, u32[]{:S(2)}) %all-to-all-start.12) | async-done | bytes 1572896 | tf_op jit(solution)/shard_map/all_to_all | solution.py:254
  573.2 13.5 %shard_map.274 = (bf16[4,64,384]{2,1,0:T(8,128)(2,1)S(1)}, bf16[8,256,256]{2,1,0:T(8,128)(2,1)S(1)}, f32[8,256,256]{2,1,0:T(8,128)S(1)}) custom-call(s32[3]{0:T(128)S(1)} %add_add_fusion.info_ref, bf16[4,64,640]{2,1,0:T(8,128)(2,1)S(1)} %bitcast.492, bf16[4,64,384]{2,1,0:T(8,128)(2,1)S(1)} %bitcast.495, bf16[4,64,384]{2,1,0:T(8,128)(2,1)S(1)} %copy-done.10, ...), custom_call_target="tpu_custom_call" | custom-call | flops 2013265920 | bytes 3112960 | tf_op jit(solution)/shard_map/pallas_call | solution.py:175
  589.0 9.7 all-to-all-start.13
  601.1 14.0 %all-to-all-done.13 = bf16[8,256,256]{2,1,0:T(8,128)(2,1)} async-done(((bf16[8,256,256]{2,1,0:T(8,128)(2,1)}), bf16[8,256,256]{2,1,0:T(8,128)(2,1)}, u32[]{:S(2)}, u32[]{:S(2)}) %all-to-all-start.13) | async-done | bytes 1048608 | tf_op jit(solution)/shard_map/all_to_all | solution.py:254
  657.2 11.8 %all-to-all-done.14 = bf16[32,2,8,1536]{3,2,1,0:T(8,128)(2,1)} async-done(((bf16[32,2,8,1536]{3,2,1,0:T(8,128)(2,1)}), bf16[32,2,8,1536]{3,2,1,0:T(8,128)(2,1)}, u32[]{:S(2)}, u32[]{:S(2)}) %all-to-all-start.14) | async-done | bytes 1572896 | tf_op jit(solution)/shard_map/all_to_all | solution.py:254
  718.4 13.6 %shard_map.275 = (bf16[4,64,384]{2,1,0:T(8,128)(2,1)S(1)}, bf16[8,256,256]{2,1,0:T(8,128)(2,1)S(1)}, f32[8,256,256]{2,1,0:T(8,128)S(1)}) custom-call(s32[3]{0:T(128)S(1)} %add_add_fusion.1.info_ref, bf16[4,64,640]{2,1,0:T(8,128)(2,1)S(1)} %bitcast.490, bf16[4,64,384]{2,1,0:T(8,128)(2,1)S(1)} %bitcast.493, bf16[4,64,384]{2,1,0:T(8,128)(2,1)S(1)} %copy-done.8, ...), custom_call_target="tpu_custom_call" | custom-call | flops 3019898880 | bytes 4423680 | tf_op jit(solution)/shard_map/pallas_call | solution.py:175
  747.1 10.6 all-to-all-done.16
  802.6 12.2 %all-to-all-done.17 = bf16[32,2,8,1536]{3,2,1,0:T(8,128)(2,1)} async-done(((bf16[32,2,8,1536]{3,2,1,0:T(8,128)(2,1)}), bf16[32,2,8,1536]{3,2,1,0:T(8,128)(2,1)}, u32[]{:S(2)}, u32[]{:S(2)}) %all-to-all-start.17) | async-done | bytes 1572896 | tf_op jit(solution)/shard_map/all_to_all | solution.py:254
  878.3 27.6 %collective-permute-done.43 = bf16[64,1536]{1,0:T(8,128)(2,1)S(1)} collective-permute-done((bf16[64,1536]{1,0:T(8,128)(2,1)S(1)}, bf16[64,1536]{1,0:T(8,128)(2,1)S(1)}, u32[]{:S(2)}, u32[]{:S(2)}) %collective-permute-start.43) | collective-permute-done | bytes 196640 | tf_op jit(solution)/shard_map/ppermute | solution.py:372
  994.6 11.3 %all-to-all-done.23 = bf16[32,32,768]{2,1,0:T(8,128)(2,1)} async-done(((bf16[32,32,768]{2,1,0:T(8,128)(2,1)}), bf16[32,32,768]{2,1,0:T(8,128)(2,1)}, u32[]{:S(2)}, u32[]{:S(2)}) %all-to-all-start.23) | async-done | bytes 1572896 | tf_op jit(solution)/shard_map/all_to_all | solution.py:254
  1034.4 10.1 all-to-all-done.20
  (968 shorter events, 689.1 us)
Async XLA Ops:
  17.3 30.4 %all-to-all-start = ((bf16[32,24,768]{2,1,0:T(8,128)(2,1)}), bf16[32,24,768]{2,1,0:T(8,128)(2,1)}, u32[]{:S(2)}, u32[]{:S(2)}) async-start(bf16[32,24,768]{2,1,0:T(8,128)(2,1)} %bitcast.539), calls=%async_computation | async-start | bytes 2359296 | tf_op jit(solution)/shard_map/all_to_all | solution.py:254
  28.9 132.9 %all-gather.3.cloned.1.call-start = ((), (), s32[]{:S(2)}) async-start(), calls=%async_computation.24 | async-start | bytes 4866048 | tf_op jit(solution)/shard_map/all_gather | solution.py:310
  165.9 41.6 %collective-permute-start.8 = (bf16[32,24,2048]{2,1,0:T(8,128)(2,1)}, bf16[32,24,2048]{2,1,0:T(8,128)(2,1)}, u32[]{:S(2)}, u32[]{:S(2)}) collective-permute-start(bf16[32,24,2048]{2,1,0:T(8,128)(2,1)} %slice.341), channel_id=1, source_target_pairs={{0,32},{32,0},{1,33},{33,1},{2,34},{34,2},{3,35},{35,3},{4,36},{36... | collective-permute-start | bytes 9437192 | tf_op jit(solution)/shard_map/ppermute | solution.py:262
  183.1 45.0 %collective-permute-start.12 = (bf16[64,1536]{1,0:T(8,128)(2,1)}, bf16[64,1536]{1,0:T(8,128)(2,1)}, u32[]{:S(2)}, u32[]{:S(2)}) collective-permute-start(bf16[64,1536]{1,0:T(8,128)(2,1)} %get-tuple-element.153), channel_id=1, source_target_pairs={{0,24},{1,25},{2,26},{3,27},{4,28},{5,29},{6,30},{7,31},{8,0},{9,1... | collective-permute-start | bytes 589832 | tf_op jit(solution)/shard_map/ppermute | solution.py:372
  185.8 43.6 %collective-permute-start.11 = (bf16[64,1536]{1,0:T(8,128)(2,1)}, bf16[64,1536]{1,0:T(8,128)(2,1)}, u32[]{:S(2)}, u32[]{:S(2)}) collective-permute-start(bf16[64,1536]{1,0:T(8,128)(2,1)} %get-tuple-element.153), channel_id=1, source_target_pairs={{0,16},{1,17},{2,18},{3,19},{4,20},{5,21},{6,22},{7,23},{8,24},{9,... | collective-permute-start | bytes 589832 | tf_op jit(solution)/shard_map/ppermute | solution.py:372
  186.3 44.4 %collective-permute-start.10 = (bf16[64,1536]{1,0:T(8,128)(2,1)}, bf16[64,1536]{1,0:T(8,128)(2,1)}, u32[]{:S(2)}, u32[]{:S(2)}) collective-permute-start(bf16[64,1536]{1,0:T(8,128)(2,1)} %get-tuple-element.153), channel_id=1, source_target_pairs={{0,8},{1,9},{2,10},{3,11},{4,12},{5,13},{6,14},{7,15},{8,16},{9,17... | collective-permute-start | bytes 589832 | tf_op jit(solution)/shard_map/ppermute | solution.py:372
  439.9 29.7 %all-to-all-start.9 = ((bf16[32,2,8,1536]{3,2,1,0:T(8,128)(2,1)}), bf16[32,2,8,1536]{3,2,1,0:T(8,128)(2,1)}, u32[]{:S(2)}, u32[]{:S(2)}) async-start(bf16[32,2,8,1536]{3,2,1,0:T(8,128)(2,1)} %bitcast.533), calls=%async_computation.9 | async-start | bytes 3145728 | tf_op jit(solution)/shard_map/all_to_all | solution.py:254
  498.5 30.3 %all-to-all-start.10 = ((bf16[32,2,8,1536]{3,2,1,0:T(8,128)(2,1)}), bf16[32,2,8,1536]{3,2,1,0:T(8,128)(2,1)}, u32[]{:S(2)}, u32[]{:S(2)}) async-start(bf16[32,2,8,1536]{3,2,1,0:T(8,128)(2,1)} %bitcast.531), calls=%async_computation.10 | async-start | bytes 3145728 | tf_op jit(solution)/shard_map/all_to_all | solution.py:254
  528.7 30.4 %all-to-all-start.12 = ((bf16[32,2,8,1536]{3,2,1,0:T(8,128)(2,1)}), bf16[32,2,8,1536]{3,2,1,0:T(8,128)(2,1)}, u32[]{:S(2)}, u32[]{:S(2)}) async-start(bf16[32,2,8,1536]{3,2,1,0:T(8,128)(2,1)} %bitcast.529), calls=%async_computation.12 | async-start | bytes 3145728 | tf_op jit(solution)/shard_map/all_to_all | solution.py:254
  639.4 29.5 %all-to-all-start.14 = ((bf16[32,2,8,1536]{3,2,1,0:T(8,128)(2,1)}), bf16[32,2,8,1536]{3,2,1,0:T(8,128)(2,1)}, u32[]{:S(2)}, u32[]{:S(2)}) async-start(bf16[32,2,8,1536]{3,2,1,0:T(8,128)(2,1)} %bitcast.536), calls=%async_computation.14 | async-start | bytes 3145728 | tf_op jit(solution)/shard_map/all_to_all | solution.py:254
  651.7 192.8 %collective-permute-start.50 = (bf16[128,1536]{1,0:T(8,128)(2,1)}, bf16[128,1536]{1,0:T(8,128)(2,1)}, u32[]{:S(2)}, u32[]{:S(2)}) collective-permute-start(bf16[128,1536]{1,0:T(8,128)(2,1)} %pad_maximum_fusion.10), channel_id=1, source_target_pairs={{0,32},{32,0},{1,33},{33,1},{2,34},{34,2},{3,35},{35,3},{4,36},{36... | collective-permute-start | bytes 1179656 | tf_op jit(solution)/shard_map/ppermute | solution.py:262
  656.9 312.7 %collective-permute-start.53 = (bf16[128,1024]{1,0:T(8,128)(2,1)}, bf16[128,1024]{1,0:T(8,128)(2,1)}, u32[]{:S(2)}, u32[]{:S(2)}) collective-permute-start(bf16[128,1024]{1,0:T(8,128)(2,1)} %pad_maximum_fusion.16), channel_id=1, source_target_pairs={{0,32},{32,0},{1,33},{33,1},{2,34},{34,2},{3,35},{35,3},{4,36},{36... | collective-permute-start | bytes 786440 | tf_op jit(solution)/shard_map/ppermute | solution.py:262
  784.7 30.1 %all-to-all-start.17 = ((bf16[32,2,8,1536]{3,2,1,0:T(8,128)(2,1)}), bf16[32,2,8,1536]{3,2,1,0:T(8,128)(2,1)}, u32[]{:S(2)}, u32[]{:S(2)}) async-start(bf16[32,2,8,1536]{3,2,1,0:T(8,128)(2,1)} %bitcast.537), calls=%async_computation.17 | async-start | bytes 3145728 | tf_op jit(solution)/shard_map/all_to_all | solution.py:254
  823.6 29.1 %all-to-all-start.18 = ((bf16[32,2,8,1536]{3,2,1,0:T(8,128)(2,1)}), bf16[32,2,8,1536]{3,2,1,0:T(8,128)(2,1)}, u32[]{:S(2)}, u32[]{:S(2)}) async-start(bf16[32,2,8,1536]{3,2,1,0:T(8,128)(2,1)} %bitcast.527), calls=%async_computation.18 | async-start | bytes 3145728 | tf_op jit(solution)/shard_map/all_to_all | solution.py:254
  852.1 160.1 %collective-permute-start.56 = (bf16[2,1536,512]{2,1,0:T(8,128)(2,1)}, bf16[2,1536,512]{2,1,0:T(8,128)(2,1)}, u32[]{:S(2)}, u32[]{:S(2)}) collective-permute-start(bf16[2,1536,512]{2,1,0:T(8,128)(2,1)} %convolution_convert_fusion.3), channel_id=1, source_target_pairs={{0,32},{32,0},{1,33},{33,1},{2,34},{34,2},{3,35},{35,3},{4,36},{36... | collective-permute-start | bytes 9437192 | tf_op jit(solution)/shard_map/ppermute | solution.py:262
  852.7 65.5 %all-to-all-start.22 = ((bf16[32,48,1024]{2,1,0:T(8,128)(2,1)}), bf16[32,48,1024]{2,1,0:T(8,128)(2,1)}, u32[]{:S(2)}, u32[]{:S(2)}) async-start(bf16[32,48,1024]{2,1,0:T(8,128)(2,1)} %bitcast.540), calls=%async_computation.22 | async-start | bytes 6291456 | tf_op jit(solution)/shard_map/all_to_all | solution.py:254
  873.9 32.0 %collective-permute-start.43 = (bf16[64,1536]{1,0:T(8,128)(2,1)S(1)}, bf16[64,1536]{1,0:T(8,128)(2,1)S(1)}, u32[]{:S(2)}, u32[]{:S(2)}) collective-permute-start(bf16[64,1536]{1,0:T(8,128)(2,1)S(1)} %fusion.287), channel_id=1, source_target_pairs={{0,24},{1,25},{2,26},{3,27},{4,28},{5,29},{6,30},{7,31},{8,0},{9,1... | collective-permute-start | bytes 589832 | tf_op jit(solution)/shard_map/ppermute | solution.py:372
  876.4 29.5 %collective-permute-start.42 = (bf16[64,1536]{1,0:T(8,128)(2,1)S(1)}, bf16[64,1536]{1,0:T(8,128)(2,1)S(1)}, u32[]{:S(2)}, u32[]{:S(2)}) collective-permute-start(bf16[64,1536]{1,0:T(8,128)(2,1)S(1)} %fusion.287), channel_id=1, source_target_pairs={{0,16},{1,17},{2,18},{3,19},{4,20},{5,21},{6,22},{7,23},{8,24},{9,... | collective-permute-start | bytes 589832 | tf_op jit(solution)/shard_map/ppermute | solution.py:372
  876.9 30.9 %collective-permute-start.41 = (bf16[64,1536]{1,0:T(8,128)(2,1)S(1)}, bf16[64,1536]{1,0:T(8,128)(2,1)S(1)}, u32[]{:S(2)}, u32[]{:S(2)}) collective-permute-start(bf16[64,1536]{1,0:T(8,128)(2,1)S(1)} %fusion.287), channel_id=1, source_target_pairs={{0,8},{1,9},{2,10},{3,11},{4,12},{5,13},{6,14},{7,15},{8,16},{9,17... | collective-permute-start | bytes 589832 | tf_op jit(solution)/shard_map/ppermute | solution.py:372
  940.0 34.7 %all-to-all-start.21 = ((bf16[8,48,1536]{2,1,0:T(8,128)(2,1)}), bf16[8,48,1536]{2,1,0:T(8,128)(2,1)}, u32[]{:S(2)}, u32[]{:S(2)}) async-start(bf16[8,48,1536]{2,1,0:T(8,128)(2,1)} %bitcast.546), calls=%async_computation.21 | async-start | bytes 2359296 | tf_op jit(solution)/shard_map/all_to_all | solution.py:254
  955.5 63.2 %collective-permute-start.57 = (bf16[2,1536,512]{2,1,0:T(8,128)(2,1)}, bf16[2,1536,512]{2,1,0:T(8,128)(2,1)}, u32[]{:S(2)}, u32[]{:S(2)}) collective-permute-start(bf16[2,1536,512]{2,1,0:T(8,128)(2,1)} %convolution_convert_fusion.2), channel_id=1, source_target_pairs={{0,32},{32,0},{1,33},{33,1},{2,34},{34,2},{3,35},{35,3},{4,36},{36... | collective-permute-start | bytes 9437192 | tf_op jit(solution)/shard_map/ppermute | solution.py:262
  961.9 66.0 %collective-permute-start.58 = (bf16[2,512,1536]{2,1,0:T(8,128)(2,1)}, bf16[2,512,1536]{2,1,0:T(8,128)(2,1)}, u32[]{:S(2)}, u32[]{:S(2)}) collective-permute-start(bf16[2,512,1536]{2,1,0:T(8,128)(2,1)} %convolution_convert_fusion.1), channel_id=1, source_target_pairs={{0,32},{32,0},{1,33},{33,1},{2,34},{34,2},{3,35},{35,3},{4,36},{36... | collective-permute-start | bytes 9437192 | tf_op jit(solution)/shard_map/ppermute | solution.py:262
  974.7 31.2 %all-to-all-start.23 = ((bf16[32,32,768]{2,1,0:T(8,128)(2,1)}), bf16[32,32,768]{2,1,0:T(8,128)(2,1)}, u32[]{:S(2)}, u32[]{:S(2)}) async-start(bf16[32,32,768]{2,1,0:T(8,128)(2,1)} %bitcast.543), calls=%async_computation.23 | async-start | bytes 3145728 | tf_op jit(solution)/shard_map/all_to_all | solution.py:254
  1005.9 38.6 %all-to-all-start.20 = ((bf16[32,48,768]{2,1,0:T(8,128)(2,1)}), bf16[32,48,768]{2,1,0:T(8,128)(2,1)}, u32[]{:S(2)}, u32[]{:S(2)}) async-start(bf16[32,48,768]{2,1,0:T(8,128)(2,1)} %maximum_maximum_fusion), calls=%async_computation.20 | async-start | bytes 4718592 | tf_op jit(solution)/shard_map/all_to_all | solution.py:254
  (340 other events, 3866.5 us)
Sparse Core Ops, SparseCore 0:
  33.3 94.8 all-gather.2

commit v7 on v6

--- a/solution.py
+++ b/solution.py
@@ -268,6 +268,9 @@
         low_half, high_half = mine_of(own, other), mine_of(other, own)
         return jnp.concatenate([low_half, high_half], axis=axis)
 
+    def ordered_by(in_order, own, other):
+        return jnp.stack([jnp.where(in_order, own, other), jnp.where(in_order, other, own)])
+
     def halves(value):
         half = value.shape[-1] // 2
         return value[..., :half], value[..., half:]
@@ -297,29 +300,33 @@
     by_head = jnp.broadcast_to(
         by_head[:, None], (heads, ring, half_rows, part_width + 128)
     ).reshape(shards, half_rows, part_width + 128)
-    down_half = down_rows // 2
-    down_flat = (half_rows, down_half * width // half_rows)
     packed = jnp.concatenate(
-        [
-            my_rows(jnp.concatenate([shared_gate[0], shared_up[0]], axis=1)),
-            mine_of(shared_down[0][:down_half], shared_down[0][down_half:]).reshape(down_flat),
-        ],
-        axis=1,
+        [shared_gate[0], shared_up[0], shared_down[0].reshape(rows_per, shared_width)], axis=1
     )
     by_head, packed = lax.optimization_barrier((by_head, packed))
-    gathered = lax.all_gather(packed, "shard")
+    gathered = lax.all_gather(packed, "shard", axis=0, tiled=True)
+    gate_up_w = gathered[:, : 2 * shared_width]
+    down_w = gathered[:, 2 * shared_width :].reshape(shared_width, width)
     own_part = exchange(by_head)
-    own_part, out_rows = lax.optimization_barrier(
-        (own_part, copies(my_rows(w_output[0]), ring))
-    )
+    out_rows = my_rows(w_output[0])
+    out_rows = ordered_by(
+        position % 2 == 0, out_rows, lax.ppermute(out_rows, "shard", [(p, p ^ 1) for p in range(shards)])
+    )
+    out_parts = [out_rows] + [
+        lax.ppermute(
+            out_rows,
+            "shard",
+            [(p, p // ring * ring + (p % ring - 2 * k) % ring) for p in range(shards)],
+        )
+        for k in range(1, ring // 2)
+    ]
+    own_part, *out_parts = lax.optimization_barrier((own_part, *out_parts))
+    own_out = lax.dynamic_slice_in_dim(
+        jnp.concatenate(out_parts + out_parts), ring - position % ring // 2 * 2, ring, axis=0
+    )
+    output_w = ordered(own_out, twin(own_out), 1).reshape(group_width, width)
     fetched = ordered(own_part, twin(own_part), 1).reshape(width, part_width + 128)
     qkv_w, tail = fetched[:, :part_width], fetched[:, part_width:]
-    own_out = exchange(out_rows, zy_groups)
-    output_w = ordered(own_out, twin(own_out), 1).reshape(group_width, width)
-    own_gate_up = gathered[:, :, : 2 * shared_width]
-    own_down = gathered[:, :, 2 * shared_width :].reshape(shards, down_half, width)
-    gate_up_w = ordered(own_gate_up, twin(own_gate_up), 1).reshape(width, 2 * shared_width)
-    down_w = ordered(own_down, twin(own_down), 1).reshape(shards * down_rows, width)
     router_w = tail[:, :experts]
     gains = tail[:, experts : experts + 2].T.astype(f32)
     gain_one, gain_two = gains[0][None], gains[1][None]
@@ -508,11 +515,11 @@
             kept["cache"],
         )
         carried = results[2] if len(results) > 2 else None
+        query_grad = results[0].reshape(heads * block, group_width)
+        query_part = lax.optimization_barrier(dot_nt(query_grad, qkv_w[:, :group_width]))
         pair_grad = jnp.sum(exchange(results[1], zy_groups).astype(f32), axis=0).astype(bf)
-        qkv_grad = jnp.concatenate(
-            [results[0].reshape(heads * block, group_width), pair_grad], axis=1
-        )
-        normed_one_grad = sum_over_x(dot_nt(qkv_grad, qkv_w))
+        qkv_grad = jnp.concatenate([query_grad, pair_grad], axis=1)
+        normed_one_grad = sum_over_x(query_part + dot_nt(pair_grad, qkv_w[:, group_width:]))
         in_norm_grad, gain_one_grad = norm_back(
             kept["layer_b"].astype(f32), gain_one, normed_one_grad
         )
@@ -577,15 +584,24 @@
 
     def scattered(value, groups=None):
         count = shards if groups is None else len(groups[0])
-        pieces = value.astype(bf).reshape(count, value.shape[0] // count, value.shape[1])
+        pieces = value.reshape(count, value.shape[0] // count, value.shape[1])
         return jnp.sum(exchange(pieces, groups).astype(f32), axis=0)
 
-    share_gate_up, share_down = scattered(grad_gate_up), scattered(grad_down)
 
     grad_out = dot_tn(
         kept_rows("attended").reshape(micros * heads * block, group_width),
         back_rows("ring_hidden"),
     )
+    grad_gate_up, grad_down, grad_out, last_grad = lax.optimization_barrier(
+        (
+            grad_gate_up.astype(bf),
+            grad_down.astype(bf),
+            grad_out.astype(bf),
+            backs[0]["layer_grad"],
+        )
+    )
+    backs[0]["layer_grad"] = last_grad
+    share_gate_up, share_down = scattered(grad_gate_up), scattered(grad_down)
     share_out = scattered(grad_out, zy_groups)
     grad_qkv = dot_tn(kept_rows("ring_one"), back_rows("qkv_grad"))
     grad_router = dot_tn(normed_two, back_rows("logit_grad"))

time: 1070 us -> 1070 us (level)
  waiting for transfers between devices: 358 us -> 326 us
  matrix products: 161 us -> 188 us
  blocking collectives: 54.7 us -> 67.2 us
  other arithmetic: 108 us -> 97.2 us
    ppermute x33, waiting for transfers between devices: 86.6 us -> 59.9 us  [shift_x(): lax.ppermute(value, 'shard', [(p, moved(p, steps)) for p in range(shards)])]
    ppermute x0 -> x4, waiting for transfers between devices: none -> 17.1 us  [the longest x3 17.1 us: body(): lax.ppermute(out_rows, 'shard', [(p, p // ring * ring + (p % ring - 2 * k...]
    all_to_all x2, blocking collectives: 54.7 us -> 67.2 us  [exchange(): lax.all_to_all(value, 'shard', split_axis=0, concat_axis=0, tiled=True, a...]
    dot_general x31, matrix products: 46.2 us -> 58.2 us  [dot(): return jnp.dot(left_side, right_side, preferred_element_type=f32)]
    dot_general x21 -> x24, matrix products: 46.5 us -> 57.3 us  [dot_nt(): lax.dot_general(left_side, right_side, (((1,), (1,)), ((), ())), preferre...]
    ppermute x16 -> x14, starting transfers between devices: 26.6 us -> 17.5 us  [twin(): return lax.ppermute(value, 'dp', [(0, 1), (1, 0)])]
    all_to_all x22 -> x21, waiting for transfers between devices: 230 us -> 223 us  [exchange(): lax.all_to_all(value, 'shard', split_axis=0, concat_axis=0, tiled=True, a...]
    unnamed x567 -> x578, local copies, waits for them, and re-layouts: 31 us -> 34.1 us
  transfers between devices with their start and end apart: 82 -> 83, of which waited for: 52 -> 50; matrix products, arithmetic and copies ran while one was open for 24% -> 26% of each run, Pallas kernels for 2% -> 2%
where the time goes in v7:
time: 1070 us; the launch traced here: 1060 us
  waiting for transfers between devices  326 us (30%)
  starting transfers between devices  229 us (21%)
  matrix products  188 us (18%)
  other arithmetic  97.2 us (9%)
  local copies, waits for them, and re-layouts  83.6 us (8%)
  blocking collectives  67.2 us (6%)
  Pallas kernels  48.4 us (5%)
  between operations  18 us (2%)
    all_to_all x21, waiting for transfers between devices, exchange(): lax.all_to_all(value, 'shard', split_axis=0, concat_axis=0, tiled=True, a...  223 us
    all_to_all x21, starting transfers between devices, exchange(): lax.all_to_all(value, 'shard', split_axis=0, concat_axis=0, tiled=True, a...  144 us
    all_to_all x2, blocking collectives, exchange(): lax.all_to_all(value, 'shard', split_axis=0, concat_axis=0, tiled=True, a...  67.2 us
    ppermute x33, waiting for transfers between devices, shift_x(): lax.ppermute(value, 'shard', [(p, moved(p, steps)) for p in range(shards)])  59.9 us
    dot_general x31, matrix products, dot(): return jnp.dot(left_side, right_side, preferred_element_type=f32)  58.2 us
    dot_general x24, matrix products, dot_nt(): lax.dot_general(left_side, right_side, (((1,), (1,)), ((), ())), preferre...  57.3 us
    dot_general x21, matrix products, wide_einsum(): jnp.einsum(formula, left_side, right_side, preferred_element_type=f32)  48.4 us
    pallas_call x6, Pallas kernels, attention_call(): pl.pallas_call(kernel, out_shape=out_shape, in_specs=[pl.BlockSpec(memory...  48.4 us
  transfers between devices with their start and end apart: 83, of which 50 were waited for; matrix products, arithmetic and copies ran while one was open for 26% of the time, Pallas kernels for 2%

profile of v7, /device:TPU:1, one launch (start us, length us, event | category | flops | bytes accessed | tf_op | source)
XLA Modules:
  0.0 1058.3 jit_solution(13521938540536962633)
XLA Ops:
  43.1 12.9 %collective-permute-done.6 = bf16[2,24,1536]{2,1,0:T(8,128)(2,1)} collective-permute-done((bf16[2,24,1536]{2,1,0:T(8,128)(2,1)S(1)}, bf16[2,24,1536]{2,1,0:T(8,128)(2,1)}, u32[]{:S(2)}, u32[]{:S(2)}) %collective-permute-start.6) | collective-permute-done | bytes 147488 | tf_op jit(solution)/shard_map/ppermute | solution.py:316
  80.6 14.3 %all-to-all-done.1.refs_0_.refs_1_ = bf16[8,256,256]{2,1,0:T(8,128)(2,1)} async-done(((bf16[8,256,256]{2,1,0:T(8,128)(2,1)}), bf16[8,256,256]{2,1,0:T(8,128)(2,1)}, u32[]{:S(2)}, u32[]{:S(2)}) %all-to-all-start.1) | async-done | bytes 1048608 | tf_op jit(solution)/shard_map/all_to_all | solution.py:254
  124.6 36.7 %all_to_all.115 = bf16[32,2,8,1536]{3,2,1,0:T(8,128)(2,1)S(1)} all-to-all(bf16[32,2,8,1536]{3,2,1,0:T(8,128)(2,1)S(1)} %bitcast.523), channel_id=1, replica_groups=mesh['section'=2,'dp'=2,'shard'=32] {'shard'}, dimensions={0} | all-to-all | bytes 3145728 | tf_op jit(solution)/shard_map/all_to_all | solution.py:254
  181.8 12.6 %all-to-all-done.3 = bf16[32,2,8,1536]{3,2,1,0:T(8,128)(2,1)} async-done(((bf16[32,2,8,1536]{3,2,1,0:T(8,128)(2,1)}), bf16[32,2,8,1536]{3,2,1,0:T(8,128)(2,1)}, u32[]{:S(2)}, u32[]{:S(2)}) %all-to-all-start.3) | async-done | bytes 1572896 | tf_op jit(solution)/shard_map/all_to_all | solution.py:254
  235.6 9.2 all-to-all-start.4
  246.0 11.4 %all-to-all-done.4.refs_1_.refs_0_.refs_2_ = bf16[8,256,256]{2,1,0:T(8,128)(2,1)} async-done(((bf16[8,256,256]{2,1,0:T(8,128)(2,1)}), bf16[8,256,256]{2,1,0:T(8,128)(2,1)}, u32[]{:S(2)}, u32[]{:S(2)}) %all-to-all-start.4) | async-done | bytes 1048608 | tf_op jit(solution)/shard_map/all_to_all | solution.py:254
  285.5 30.4 %all_to_all.116 = bf16[32,2,8,1536]{3,2,1,0:T(8,128)(2,1)S(1)} all-to-all(bf16[32,2,8,1536]{3,2,1,0:T(8,128)(2,1)S(1)} %bitcast.524), channel_id=1, replica_groups=mesh['section'=2,'dp'=2,'shard'=32] {'shard'}, dimensions={0} | all-to-all | bytes 3145728 | tf_op jit(solution)/shard_map/all_to_all | solution.py:254
  336.8 12.8 %all-to-all-done.6 = bf16[32,2,8,1536]{3,2,1,0:T(8,128)(2,1)} async-done(((bf16[32,2,8,1536]{3,2,1,0:T(8,128)(2,1)}), bf16[32,2,8,1536]{3,2,1,0:T(8,128)(2,1)}, u32[]{:S(2)}, u32[]{:S(2)}) %all-to-all-start.6) | async-done | bytes 1572896 | tf_op jit(solution)/shard_map/all_to_all | solution.py:254
  368.0 10.1 collective-permute-done.22
  395.1 13.8 %all-to-all-done.7.refs_1_ = bf16[8,256,256]{2,1,0:T(8,128)(2,1)} async-done(((bf16[8,256,256]{2,1,0:T(8,128)(2,1)}), bf16[8,256,256]{2,1,0:T(8,128)(2,1)}, u32[]{:S(2)}, u32[]{:S(2)}) %all-to-all-start.7) | async-done | bytes 1048608 | tf_op jit(solution)/shard_map/all_to_all | solution.py:254
  444.7 17.5 %all-to-all-done.8 = bf16[32,2,8,1536]{3,2,1,0:T(8,128)(2,1)} async-done(((bf16[32,2,8,1536]{3,2,1,0:T(8,128)(2,1)}), bf16[32,2,8,1536]{3,2,1,0:T(8,128)(2,1)}, u32[]{:S(2)}, u32[]{:S(2)}) %all-to-all-start.8) | async-done | bytes 1572896 | tf_op jit(solution)/shard_map/all_to_all | solution.py:254
  481.1 10.0 all-to-all-done.10
  511.3 10.1 all-to-all-done.9
  542.6 9.2 all-to-all-done.11
  565.1 13.4 %shard_map.274 = (bf16[4,64,384]{2,1,0:T(8,128)(2,1)S(1)}, bf16[8,256,256]{2,1,0:T(8,128)(2,1)S(1)}, f32[8,256,256]{2,1,0:T(8,128)S(1)}) custom-call(s32[3]{0:T(128)S(1)} %add_add_fusion.info_ref, bf16[4,64,640]{2,1,0:T(8,128)(2,1)S(1)} %bitcast.495, bf16[4,64,384]{2,1,0:T(8,128)(2,1)S(1)} %bitcast.498, bf16[4,64,384]{2,1,0:T(8,128)(2,1)S(1)} %copy-done.5, ...), custom_call_target="tpu_custom_call" | custom-call | flops 2013265920 | bytes 3112960 | tf_op jit(solution)/shard_map/pallas_call | solution.py:175
  581.5 9.7 all-to-all-start.12
  596.6 11.0 %all-to-all-done.12 = bf16[8,256,256]{2,1,0:T(8,128)(2,1)} async-done(((bf16[8,256,256]{2,1,0:T(8,128)(2,1)}), bf16[8,256,256]{2,1,0:T(8,128)(2,1)}, u32[]{:S(2)}, u32[]{:S(2)}) %all-to-all-start.12) | async-done | bytes 1048608 | tf_op jit(solution)/shard_map/all_to_all | solution.py:254
  710.4 13.4 %shard_map.275 = (bf16[4,64,384]{2,1,0:T(8,128)(2,1)S(1)}, bf16[8,256,256]{2,1,0:T(8,128)(2,1)S(1)}, f32[8,256,256]{2,1,0:T(8,128)S(1)}) custom-call(s32[3]{0:T(128)S(1)} %add_add_fusion.1.info_ref, bf16[4,64,640]{2,1,0:T(8,128)(2,1)S(1)} %bitcast.493, bf16[4,64,384]{2,1,0:T(8,128)(2,1)S(1)} %bitcast.496, bf16[4,64,384]{2,1,0:T(8,128)(2,1)S(1)} %get-tuple-element.48.o_ref, ...), custom_call_target="tpu_custom_call" | custom-call | flops 3019898880 | bytes 4423680 | tf_op jit(solution)/shard_map/pallas_call | solution.py:175
  741.3 9.3 all-to-all-done.15
  776.3 9.0 all-to-all-start.16
  835.6 9.1 all-to-all-done.17
  946.8 9.5 all-to-all-done.22
  976.6 18.4 %all-to-all-done.19 = bf16[32,48,768]{2,1,0:T(8,128)(2,1)} async-done(((bf16[32,48,768]{2,1,0:T(8,128)(2,1)}), bf16[32,48,768]{2,1,0:T(8,128)(2,1)}, u32[]{:S(2)}, u32[]{:S(2)}) %all-to-all-start.19) | async-done | bytes 2359328 | tf_op jit(solution)/shard_map/all_to_all | solution.py:254
  1021.7 21.6 %all-to-all-done.21 = bf16[32,48,1024]{2,1,0:T(8,128)(2,1)} async-done(((bf16[32,48,1024]{2,1,0:T(8,128)(2,1)}), bf16[32,48,1024]{2,1,0:T(8,128)(2,1)}, u32[]{:S(2)}, u32[]{:S(2)}) %all-to-all-start.21) | async-done | bytes 3145760 | tf_op jit(solution)/shard_map/all_to_all | solution.py:254
  (981 shorter events, 704.7 us)
Async XLA Ops:
  7.2 191.7 %all-gather.2.cloned.1.call-start = ((), (), s32[]{:S(2)}) async-start(), calls=%async_computation.23 | async-start | bytes 9732096 | tf_op jit(solution)/shard_map/all_gather | solution.py:307
  26.8 33.5 %all-to-all-start = ((bf16[32,24,768]{2,1,0:T(8,128)(2,1)}), bf16[32,24,768]{2,1,0:T(8,128)(2,1)}, u32[]{:S(2)}, u32[]{:S(2)}) async-start(bf16[32,24,768]{2,1,0:T(8,128)(2,1)} %bitcast.528), calls=%async_computation | async-start | bytes 2359296 | tf_op jit(solution)/shard_map/all_to_all | solution.py:254
  168.2 26.3 %all-to-all-start.3 = ((bf16[32,2,8,1536]{3,2,1,0:T(8,128)(2,1)}), bf16[32,2,8,1536]{3,2,1,0:T(8,128)(2,1)}, u32[]{:S(2)}, u32[]{:S(2)}) async-start(bf16[32,2,8,1536]{3,2,1,0:T(8,128)(2,1)} %bitcast.519), calls=%async_computation.3 | async-start | bytes 3145728 | tf_op jit(solution)/shard_map/all_to_all | solution.py:254
  173.4 45.9 %collective-permute-start.14 = (bf16[64,1536]{1,0:T(8,128)(2,1)}, bf16[64,1536]{1,0:T(8,128)(2,1)}, u32[]{:S(2)}, u32[]{:S(2)}) collective-permute-start(bf16[64,1536]{1,0:T(8,128)(2,1)} %get-tuple-element.163), channel_id=1, source_target_pairs={{0,24},{1,25},{2,26},{3,27},{4,28},{5,29},{6,30},{7,31},{8,0},{9,1... | collective-permute-start | bytes 589832 | tf_op jit(solution)/shard_map/ppermute | solution.py:379
  175.8 44.8 %collective-permute-start.13 = (bf16[64,1536]{1,0:T(8,128)(2,1)}, bf16[64,1536]{1,0:T(8,128)(2,1)}, u32[]{:S(2)}, u32[]{:S(2)}) collective-permute-start(bf16[64,1536]{1,0:T(8,128)(2,1)} %get-tuple-element.163), channel_id=1, source_target_pairs={{0,16},{1,17},{2,18},{3,19},{4,20},{5,21},{6,22},{7,23},{8,24},{9,... | collective-permute-start | bytes 589832 | tf_op jit(solution)/shard_map/ppermute | solution.py:379
  176.4 45.6 %collective-permute-start.12 = (bf16[64,1536]{1,0:T(8,128)(2,1)}, bf16[64,1536]{1,0:T(8,128)(2,1)}, u32[]{:S(2)}, u32[]{:S(2)}) collective-permute-start(bf16[64,1536]{1,0:T(8,128)(2,1)} %get-tuple-element.163), channel_id=1, source_target_pairs={{0,8},{1,9},{2,10},{3,11},{4,12},{5,13},{6,14},{7,15},{8,16},{9,17... | collective-permute-start | bytes 589832 | tf_op jit(solution)/shard_map/ppermute | solution.py:379
  322.7 26.9 %all-to-all-start.6 = ((bf16[32,2,8,1536]{3,2,1,0:T(8,128)(2,1)}), bf16[32,2,8,1536]{3,2,1,0:T(8,128)(2,1)}, u32[]{:S(2)}, u32[]{:S(2)}) async-start(bf16[32,2,8,1536]{3,2,1,0:T(8,128)(2,1)} %bitcast.521), calls=%async_computation.6 | async-start | bytes 3145728 | tf_op jit(solution)/shard_map/all_to_all | solution.py:254
  432.6 29.6 %all-to-all-start.8 = ((bf16[32,2,8,1536]{3,2,1,0:T(8,128)(2,1)}), bf16[32,2,8,1536]{3,2,1,0:T(8,128)(2,1)}, u32[]{:S(2)}, u32[]{:S(2)}) async-start(bf16[32,2,8,1536]{3,2,1,0:T(8,128)(2,1)} %bitcast.522), calls=%async_computation.8 | async-start | bytes 3145728 | tf_op jit(solution)/shard_map/all_to_all | solution.py:254
  462.2 28.9 %all-to-all-start.10 = ((bf16[32,2,8,1536]{3,2,1,0:T(8,128)(2,1)}), bf16[32,2,8,1536]{3,2,1,0:T(8,128)(2,1)}, u32[]{:S(2)}, u32[]{:S(2)}) async-start(bf16[32,2,8,1536]{3,2,1,0:T(8,128)(2,1)} %bitcast.525), calls=%async_computation.10 | async-start | bytes 3145728 | tf_op jit(solution)/shard_map/all_to_all | solution.py:254
  491.1 30.3 %all-to-all-start.9 = ((bf16[32,2,8,1536]{3,2,1,0:T(8,128)(2,1)}), bf16[32,2,8,1536]{3,2,1,0:T(8,128)(2,1)}, u32[]{:S(2)}, u32[]{:S(2)}) async-start(bf16[32,2,8,1536]{3,2,1,0:T(8,128)(2,1)} %bitcast.520), calls=%async_computation.9 | async-start | bytes 3145728 | tf_op jit(solution)/shard_map/all_to_all | solution.py:254
  521.4 30.4 %all-to-all-start.11 = ((bf16[32,2,8,1536]{3,2,1,0:T(8,128)(2,1)}), bf16[32,2,8,1536]{3,2,1,0:T(8,128)(2,1)}, u32[]{:S(2)}, u32[]{:S(2)}) async-start(bf16[32,2,8,1536]{3,2,1,0:T(8,128)(2,1)} %bitcast.517), calls=%async_computation.11 | async-start | bytes 3145728 | tf_op jit(solution)/shard_map/all_to_all | solution.py:254
  581.5 26.2 %all-to-all-start.12 = ((bf16[8,256,256]{2,1,0:T(8,128)(2,1)}), bf16[8,256,256]{2,1,0:T(8,128)(2,1)}, u32[]{:S(2)}, u32[]{:S(2)}) async-start(bf16[8,256,256]{2,1,0:T(8,128)(2,1)} %copy-done.3), calls=%async_computation.12 | async-start | bytes 2097152 | tf_op jit(solution)/shard_map/all_to_all | solution.py:254
  624.6 228.8 %collective-permute-start.29 = (bf16[128,1536]{1,0:T(8,128)(2,1)}, bf16[128,1536]{1,0:T(8,128)(2,1)}, u32[]{:S(2)}, u32[]{:S(2)}) collective-permute-start(bf16[128,1536]{1,0:T(8,128)(2,1)} %pad_maximum_fusion.8), channel_id=1, source_target_pairs={{0,32},{32,0},{1,33},{33,1},{2,34},{34,2},{3,35},{35,3},{4,36},{36... | collective-permute-start | bytes 1179656 | tf_op jit(solution)/shard_map/ppermute | solution.py:262
  631.6 29.6 %all-to-all-start.13 = ((bf16[32,2,8,1536]{3,2,1,0:T(8,128)(2,1)}), bf16[32,2,8,1536]{3,2,1,0:T(8,128)(2,1)}, u32[]{:S(2)}, u32[]{:S(2)}) async-start(bf16[32,2,8,1536]{3,2,1,0:T(8,128)(2,1)} %bitcast.527), calls=%async_computation.13 | async-start | bytes 3145728 | tf_op jit(solution)/shard_map/all_to_all | solution.py:254
  644.9 204.3 %collective-permute-start.45 = (bf16[128,1024]{1,0:T(8,128)(2,1)}, bf16[128,1024]{1,0:T(8,128)(2,1)}, u32[]{:S(2)}, u32[]{:S(2)}) collective-permute-start(bf16[128,1024]{1,0:T(8,128)(2,1)} %pad_maximum_fusion.13), channel_id=1, source_target_pairs={{0,32},{32,0},{1,33},{33,1},{2,34},{34,2},{3,35},{35,3},{4,36},{36... | collective-permute-start | bytes 786440 | tf_op jit(solution)/shard_map/ppermute | solution.py:262
  669.3 27.6 %all-to-all-start.14 = ((bf16[32,2,8,1536]{3,2,1,0:T(8,128)(2,1)}), bf16[32,2,8,1536]{3,2,1,0:T(8,128)(2,1)}, u32[]{:S(2)}, u32[]{:S(2)}) async-start(bf16[32,2,8,1536]{3,2,1,0:T(8,128)(2,1)} %bitcast.518), calls=%async_computation.14 | async-start | bytes 3145728 | tf_op jit(solution)/shard_map/all_to_all | solution.py:254
  776.3 30.6 %all-to-all-start.16 = ((bf16[32,2,8,1536]{3,2,1,0:T(8,128)(2,1)}), bf16[32,2,8,1536]{3,2,1,0:T(8,128)(2,1)}, u32[]{:S(2)}, u32[]{:S(2)}) async-start(bf16[32,2,8,1536]{3,2,1,0:T(8,128)(2,1)} %bitcast.526), calls=%async_computation.16 | async-start | bytes 3145728 | tf_op jit(solution)/shard_map/all_to_all | solution.py:254
  815.8 29.0 %all-to-all-start.17 = ((bf16[32,2,8,1536]{3,2,1,0:T(8,128)(2,1)}), bf16[32,2,8,1536]{3,2,1,0:T(8,128)(2,1)}, u32[]{:S(2)}, u32[]{:S(2)}) async-start(bf16[32,2,8,1536]{3,2,1,0:T(8,128)(2,1)} %bitcast.516), calls=%async_computation.17 | async-start | bytes 3145728 | tf_op jit(solution)/shard_map/all_to_all | solution.py:254
  912.8 50.7 %collective-permute-start.58 = (bf16[2,1536,512]{2,1,0:T(8,128)(2,1)}, bf16[2,1536,512]{2,1,0:T(8,128)(2,1)}, u32[]{:S(2)}, u32[]{:S(2)}) collective-permute-start(bf16[2,1536,512]{2,1,0:T(8,128)(2,1)} %convolution_convert_fusion.3), channel_id=1, source_target_pairs={{0,32},{32,0},{1,33},{33,1},{2,34},{34,2},{3,35},{35,3},{4,36},{36... | collective-permute-start | bytes 9437192 | tf_op jit(solution)/shard_map/ppermute | solution.py:262
  920.4 49.7 %collective-permute-start.59 = (bf16[2,1536,512]{2,1,0:T(8,128)(2,1)}, bf16[2,1536,512]{2,1,0:T(8,128)(2,1)}, u32[]{:S(2)}, u32[]{:S(2)}) collective-permute-start(bf16[2,1536,512]{2,1,0:T(8,128)(2,1)} %convolution_convert_fusion.2), channel_id=1, source_target_pairs={{0,32},{32,0},{1,33},{33,1},{2,34},{34,2},{3,35},{35,3},{4,36},{36... | collective-permute-start | bytes 9437192 | tf_op jit(solution)/shard_map/ppermute | solution.py:262
  923.8 32.5 %all-to-all-start.22 = ((bf16[32,32,768]{2,1,0:T(8,128)(2,1)}), bf16[32,32,768]{2,1,0:T(8,128)(2,1)}, u32[]{:S(2)}, u32[]{:S(2)}) async-start(bf16[32,32,768]{2,1,0:T(8,128)(2,1)} %bitcast.532), calls=%async_computation.22 | async-start | bytes 3145728 | tf_op jit(solution)/shard_map/all_to_all | solution.py:254
  938.4 66.7 %collective-permute-start.60 = (bf16[2,512,1536]{2,1,0:T(8,128)(2,1)}, bf16[2,512,1536]{2,1,0:T(8,128)(2,1)}, u32[]{:S(2)}, u32[]{:S(2)}) collective-permute-start(bf16[2,512,1536]{2,1,0:T(8,128)(2,1)} %convolution_convert_fusion.1), channel_id=1, source_target_pairs={{0,32},{32,0},{1,33},{33,1},{2,34},{34,2},{3,35},{35,3},{4,36},{36... | collective-permute-start | bytes 9437192 | tf_op jit(solution)/shard_map/ppermute | solution.py:262
  956.3 38.7 %all-to-all-start.19 = ((bf16[32,48,768]{2,1,0:T(8,128)(2,1)}), bf16[32,48,768]{2,1,0:T(8,128)(2,1)}, u32[]{:S(2)}, u32[]{:S(2)}) async-start(bf16[32,48,768]{2,1,0:T(8,128)(2,1)} %maximum_maximum_fusion), calls=%async_computation.19 | async-start | bytes 4718592 | tf_op jit(solution)/shard_map/all_to_all | solution.py:254
  995.0 48.2 %all-to-all-start.21 = ((bf16[32,48,1024]{2,1,0:T(8,128)(2,1)}), bf16[32,48,1024]{2,1,0:T(8,128)(2,1)}, u32[]{:S(2)}, u32[]{:S(2)}) async-start(bf16[32,48,1024]{2,1,0:T(8,128)(2,1)} %bitcast.529), calls=%async_computation.21 | async-start | bytes 6291456 | tf_op jit(solution)/shard_map/all_to_all | solution.py:254
  (343 other events, 2563.8 us)
Sparse Core Ops, SparseCore 0:
  17.1 143.1 all-gather.1

commit v8 on v7

--- a/solution.py
+++ b/solution.py
@@ -300,13 +300,17 @@
     by_head = jnp.broadcast_to(
         by_head[:, None], (heads, ring, half_rows, part_width + 128)
     ).reshape(shards, half_rows, part_width + 128)
+    down_half = down_rows // 2
+    down_flat = (half_rows, down_half * width // half_rows)
     packed = jnp.concatenate(
-        [shared_gate[0], shared_up[0], shared_down[0].reshape(rows_per, shared_width)], axis=1
+        [
+            my_rows(jnp.concatenate([shared_gate[0], shared_up[0]], axis=1)),
+            mine_of(shared_down[0][:down_half], shared_down[0][down_half:]).reshape(down_flat),
+        ],
+        axis=1,
     )
     by_head, packed = lax.optimization_barrier((by_head, packed))
-    gathered = lax.all_gather(packed, "shard", axis=0, tiled=True)
-    gate_up_w = gathered[:, : 2 * shared_width]
-    down_w = gathered[:, 2 * shared_width :].reshape(shared_width, width)
+    gathered = lax.all_gather(packed, "shard")
     own_part = exchange(by_head)
     out_rows = my_rows(w_output[0])
     out_rows = ordered_by(
@@ -403,7 +407,15 @@
         for m in range(micros)
     ]
 
-    def forward(moment, received, previous):
+    def shared_weights(gathered):
+        gate_up = gathered[:, :, : 2 * shared_width]
+        down = gathered[:, :, 2 * shared_width :].reshape(shards, down_half, width)
+        return (
+            ordered(gate_up, twin(gate_up), 1).reshape(width, 2 * shared_width),
+            ordered(down, twin(down), 1).reshape(shards * down_rows, width),
+        )
+
+    def forward(moment, received, previous, shared_pair):
         first_micro = min(moment, micros - 1)
         second_micro = max(moment - 1, 0)
         ring_b = jnp.where(is_first, ring_inputs[first_micro], received)
@@ -422,6 +434,10 @@
         attended, logs = attention_forward(attn_info, qkv, previous, cache)
         attended_rows = attended.reshape(heads * block, group_width)
         hidden = layer_in + sum_over_x(dot(attended_rows, output_w))
+        if shared_pair is None:
+            arrived, hidden = lax.optimization_barrier((gathered, hidden))
+            shared_pair = shared_weights(arrived)
+        gate_up_w, down_w = shared_pair
         normed_two = (hidden * inverse_rms(hidden) * gain_two).astype(bf)
         gates = gate_values(normed_two, table)
         expert_in = to_experts(dot_tn(pick, normed_two).astype(bf))
@@ -457,11 +473,13 @@
             shared_up_pre=shared_up_pre,
             shared_act=shared_act,
             output_b=output_b,
+            shared_pair=shared_pair,
         )
 
     def ffn_backward(kept, upstream_b):
         upstream = upstream_b.astype(f32)
         gates, hidden = kept["gates"], kept["hidden"]
+        gate_up_w, down_w = kept["shared_pair"]
         high, low = high_low(gates)
         outgoing = dot_tn(high, upstream_b) + dot_tn(low, upstream_b)
         expert_grad = to_experts(outgoing.astype(bf))
@@ -534,9 +552,10 @@
 
     nothing = jnp.zeros((block, width), bf)
     saved = []
-    received, previous = jnp.zeros((heads, block, width), bf), None
+    received, previous, shared_pair = jnp.zeros((heads, block, width), bf), None, None
     for moment in range(micros + 1):
-        kept = forward(moment, received, previous)
+        kept = forward(moment, received, previous, shared_pair)
+        shared_pair = kept["shared_pair"]
         saved.append(kept)
         previous = kept["cache"]
         if moment < micros:
@@ -582,27 +601,54 @@
     )
     grad_down = dot_tn(both(kept_rows("shared_act")), both_halves(*halves(back_rows("upstream_b"))))
 
-    def scattered(value, groups=None):
-        count = shards if groups is None else len(groups[0])
-        pieces = value.reshape(count, value.shape[0] // count, value.shape[1])
-        return jnp.sum(exchange(pieces, groups).astype(f32), axis=0)
-
+
+    def shift_z(value, steps):
+        pairs = [(p, p // ring * ring + (p % ring + 2 * steps) % ring) for p in range(shards)]
+        return lax.ppermute(value, "shard", pairs)
+
+    def shift_y(value, steps):
+        return lax.ppermute(value, "shard", [(p, p ^ 1) for p in range(shards)])
+
+    along = dict(
+        x=(shift_x, position // ring), z=(shift_z, position % ring // 2), y=(shift_y, position % 2)
+    )
+
+    def reduced(value, name, axis, held_as=bf):
+        shift, here = along[name]
+        count = value.shape[axis]
+
+        def piece(steps):
+            return lax.dynamic_index_in_dim(value, (here + steps) % count, axis, keepdims=False)
+
+        total = piece(0).astype(f32)
+        for steps in range(1, count):
+            total = total + shift(piece(steps), steps).astype(f32)
+        return total.astype(held_as)
+
+    grad_gate_up, grad_down, ring_hidden = lax.optimization_barrier(
+        (grad_gate_up.astype(bf), grad_down.astype(bf), backs[0]["ring_hidden"])
+    )
+    backs[0]["ring_hidden"] = ring_hidden
+    pieces = grad_gate_up.reshape(heads, ring // 2, 2, rows_per, shared_width)
+    share_gate_up = reduced(reduced(reduced(pieces, "x", 0), "z", 0), "y", 0, f32)
+    pieces = grad_down.reshape(heads, ring // 2, 2, down_rows, width // 2)
+    share_down = reduced(reduced(reduced(pieces, "z", 1), "x", 0), "y", 0, f32)
 
     grad_out = dot_tn(
         kept_rows("attended").reshape(micros * heads * block, group_width),
         back_rows("ring_hidden"),
     )
-    grad_gate_up, grad_down, grad_out, last_grad = lax.optimization_barrier(
-        (
-            grad_gate_up.astype(bf),
-            grad_down.astype(bf),
-            grad_out.astype(bf),
-            backs[0]["layer_grad"],
-        )
-    )
+
+    def with_twin(value):
+        value = value.astype(bf)
+        own = my_rows(value)
+        other = mine_of(value[..., half_rows:, :], value[..., :half_rows, :])
+        return (own.astype(f32) + twin(other).astype(f32)).astype(bf)
+
+    grad_out = with_twin(grad_out.reshape(ring, rows_per, width))
+    grad_out, last_grad = lax.optimization_barrier((grad_out, backs[0]["layer_grad"]))
     backs[0]["layer_grad"] = last_grad
-    share_gate_up, share_down = scattered(grad_gate_up), scattered(grad_down)
-    share_out = scattered(grad_out, zy_groups)
+    share_out = jnp.sum(exchange(grad_out, zy_groups).astype(f32), axis=0)
     grad_qkv = dot_tn(kept_rows("ring_one"), back_rows("qkv_grad"))
     grad_router = dot_tn(normed_two, back_rows("logit_grad"))
     gain_sums = jnp.stack(
@@ -611,19 +657,18 @@
     grad_tail = jnp.concatenate(
         [grad_router, gain_sums.T, jnp.zeros((width, 128 - experts - 2), f32)], axis=1
     )
+    grad_qkv = jnp.concatenate([grad_qkv, grad_tail], axis=1)
     pieces = exchange(
-        jnp.concatenate([grad_qkv, grad_tail], axis=1)
-        .astype(bf)
-        .reshape(shards, rows_per, part_width + 128)
+        with_twin(grad_qkv.reshape(shards, rows_per, part_width + 128))
     ).astype(f32)
     share_qkv = jnp.sum(
-        pieces[:, :, :part_width].reshape(heads, ring, rows_per, part_width), axis=1
+        pieces[:, :, :part_width].reshape(heads, ring, half_rows, part_width), axis=1
     )
     share_qkv = share_qkv.transpose(1, 0, 2)
     share_tail = jnp.sum(pieces[:, :, part_width:], axis=0)
 
     def total(share):
-        return share + twin(share)
+        return ordered(share, twin(share), 0)
 
     out_total, qkv_total, tail_total = total(share_out), total(share_qkv), total(share_tail)
     other_gate_up = twin(share_gate_up)

time: 1070 us -> 1090 us (1.019)
  blocking collectives: 67.2 us -> 28.9 us
  starting transfers between devices: 229 us -> 257 us
  other arithmetic: 97.2 us -> 114 us
  waiting for transfers between devices: 326 us -> 341 us
  matrix products: 188 us -> 176 us
    all_to_all x21 -> x20, waiting for transfers between devices: 223 us -> 179 us  [exchange(): lax.all_to_all(value, 'shard', split_axis=0, concat_axis=0, tiled=True, a...]
    all_to_all x2 -> x1, blocking collectives: 67.2 us -> 28.9 us  [exchange(): lax.all_to_all(value, 'shard', split_axis=0, concat_axis=0, tiled=True, a...]
    ppermute x0 -> x8, waiting for transfers between devices: none -> 24.9 us  [the longest x6 23.1 us: shift_z(): return lax.ppermute(value, 'shard', pairs)]
    ppermute x33 -> x39, waiting for transfers between devices: 59.9 us -> 83.2 us  [shift_x(): lax.ppermute(value, 'shard', [(p, moved(p, steps)) for p in range(shards)])]
    ppermute x0 -> x8, starting transfers between devices: none -> 14.8 us  [the longest x6 11.3 us: shift_z(): return lax.ppermute(value, 'shard', pairs)]
    ppermute x14 -> x18, starting transfers between devices: 17.5 us -> 31.2 us  [twin(): return lax.ppermute(value, 'dp', [(0, 1), (1, 0)])]
    all_to_all x21 -> x20, starting transfers between devices: 144 us -> 138 us  [exchange(): lax.all_to_all(value, 'shard', split_axis=0, concat_axis=0, tiled=True, a...]
    unnamed x578 -> x566, local copies, waits for them, and re-layouts: 34.1 us -> 37.3 us
  transfers between devices with their start and end apart: 83 -> 100, of which waited for: 50 -> 58; matrix products, arithmetic and copies ran while one was open for 26% -> 27% of each run, Pallas kernels for 2% -> 2%
where the time goes in v8:
time: 1090 us; the launch traced here: 1080 us
  waiting for transfers between devices  341 us (31%)
  starting transfers between devices  257 us (24%)
  matrix products  176 us (16%)
  other arithmetic  114 us (10%)
  local copies, waits for them, and re-layouts  91.6 us (8%)
  Pallas kernels  48.4 us (4%)
  blocking collectives  28.9 us (3%)
  between operations  18.5 us (2%)
    all_to_all x20, waiting for transfers between devices, exchange(): lax.all_to_all(value, 'shard', split_axis=0, concat_axis=0, tiled=True, a...  179 us
    all_to_all x20, starting transfers between devices, exchange(): lax.all_to_all(value, 'shard', split_axis=0, concat_axis=0, tiled=True, a...  138 us
    ppermute x39, waiting for transfers between devices, shift_x(): lax.ppermute(value, 'shard', [(p, moved(p, steps)) for p in range(shards)])  83.2 us
    dot_general x24, matrix products, dot_nt(): lax.dot_general(left_side, right_side, (((1,), (1,)), ((), ())), preferre...  53.2 us
    dot_general x31, matrix products, dot(): return jnp.dot(left_side, right_side, preferred_element_type=f32)  51.5 us
    pallas_call x6, Pallas kernels, attention_call(): pl.pallas_call(kernel, out_shape=out_shape, in_specs=[pl.BlockSpec(memory...  48.4 us
    dot_general x21, matrix products, wide_einsum(): jnp.einsum(formula, left_side, right_side, preferred_element_type=f32)  48.1 us
    ppermute x39, starting transfers between devices, shift_x(): lax.ppermute(value, 'shard', [(p, moved(p, steps)) for p in range(shards)])  40.9 us
  transfers between devices with their start and end apart: 100, of which 58 were waited for; matrix products, arithmetic and copies ran while one was open for 27% of the time, Pallas kernels for 2%

profile of v8, /device:TPU:1, one launch (start us, length us, event | category | flops | bytes accessed | tf_op | source)
XLA Modules:
  0.0 1075.7 jit_solution(15594590344099553662)
XLA Ops:
  42.9 11.6 %collective-permute-done.6 = bf16[2,24,1536]{2,1,0:T(8,128)(2,1)} collective-permute-done((bf16[2,24,1536]{2,1,0:T(8,128)(2,1)S(1)}, bf16[2,24,1536]{2,1,0:T(8,128)(2,1)}, u32[]{:S(2)}, u32[]{:S(2)}) %collective-permute-start.6) | collective-permute-done | bytes 147488 | tf_op jit(solution)/shard_map/ppermute | solution.py:320
  80.1 17.2 %all-to-all-done.1.refs_0_.refs_1_ = bf16[8,256,256]{2,1,0:T(8,128)(2,1)} async-done(((bf16[8,256,256]{2,1,0:T(8,128)(2,1)}), bf16[8,256,256]{2,1,0:T(8,128)(2,1)}, u32[]{:S(2)}, u32[]{:S(2)}) %all-to-all-start.1) | async-done | bytes 1048608 | tf_op jit(solution)/shard_map/all_to_all | solution.py:254
  179.2 14.2 %all-to-all-done.3 = bf16[32,2,8,1536]{3,2,1,0:T(8,128)(2,1)} async-done(((bf16[32,2,8,1536]{3,2,1,0:T(8,128)(2,1)}), bf16[32,2,8,1536]{3,2,1,0:T(8,128)(2,1)}, u32[]{:S(2)}, u32[]{:S(2)}) %all-to-all-start.3) | async-done | bytes 1572896 | tf_op jit(solution)/shard_map/all_to_all | solution.py:254
  246.9 15.6 %all-to-all-done.4.refs_1_.refs_0_.refs_2_ = bf16[8,256,256]{2,1,0:T(8,128)(2,1)} async-done(((bf16[8,256,256]{2,1,0:T(8,128)(2,1)}), bf16[8,256,256]{2,1,0:T(8,128)(2,1)}, u32[]{:S(2)}, u32[]{:S(2)}) %all-to-all-start.4) | async-done | bytes 1048608 | tf_op jit(solution)/shard_map/all_to_all | solution.py:254
  289.0 28.9 %all_to_all.105 = bf16[32,2,8,1536]{3,2,1,0:T(8,128)(2,1)S(1)} all-to-all(bf16[32,2,8,1536]{3,2,1,0:T(8,128)(2,1)S(1)} %bitcast.600), channel_id=1, replica_groups=mesh['section'=2,'dp'=2,'shard'=32] {'shard'}, dimensions={0} | all-to-all | bytes 3145728 | tf_op jit(solution)/shard_map/all_to_all | solution.py:254
  337.5 14.1 %all-to-all-done.6 = bf16[32,2,8,1536]{3,2,1,0:T(8,128)(2,1)} async-done(((bf16[32,2,8,1536]{3,2,1,0:T(8,128)(2,1)}), bf16[32,2,8,1536]{3,2,1,0:T(8,128)(2,1)}, u32[]{:S(2)}, u32[]{:S(2)}) %all-to-all-start.6) | async-done | bytes 1572896 | tf_op jit(solution)/shard_map/all_to_all | solution.py:254
  370.2 10.3 collective-permute-done.24
  397.5 13.8 %all-to-all-done.7.refs_1_ = bf16[8,256,256]{2,1,0:T(8,128)(2,1)} async-done(((bf16[8,256,256]{2,1,0:T(8,128)(2,1)}), bf16[8,256,256]{2,1,0:T(8,128)(2,1)}, u32[]{:S(2)}, u32[]{:S(2)}) %all-to-all-start.7) | async-done | bytes 1048608 | tf_op jit(solution)/shard_map/all_to_all | solution.py:254
  446.9 17.5 %all-to-all-done.8 = bf16[32,2,8,1536]{3,2,1,0:T(8,128)(2,1)} async-done(((bf16[32,2,8,1536]{3,2,1,0:T(8,128)(2,1)}), bf16[32,2,8,1536]{3,2,1,0:T(8,128)(2,1)}, u32[]{:S(2)}, u32[]{:S(2)}) %all-to-all-start.8) | async-done | bytes 1572896 | tf_op jit(solution)/shard_map/all_to_all | solution.py:254
  483.5 9.8 all-to-all-done.10
  513.4 10.2 all-to-all-done.9
  542.8 11.2 %all-to-all-done.11 = bf16[32,2,8,1536]{3,2,1,0:T(8,128)(2,1)} async-done(((bf16[32,2,8,1536]{3,2,1,0:T(8,128)(2,1)}), bf16[32,2,8,1536]{3,2,1,0:T(8,128)(2,1)}, u32[]{:S(2)}, u32[]{:S(2)}) %all-to-all-start.11) | async-done | bytes 1572896 | tf_op jit(solution)/shard_map/all_to_all | solution.py:254
  567.1 13.4 %shard_map.274 = (bf16[4,64,384]{2,1,0:T(8,128)(2,1)S(1)}, bf16[8,256,256]{2,1,0:T(8,128)(2,1)S(1)}, f32[8,256,256]{2,1,0:T(8,128)S(1)}) custom-call(s32[3]{0:T(128)S(1)} %add_add_fusion.info_ref, bf16[4,64,640]{2,1,0:T(8,128)(2,1)S(1)} %bitcast.554, bf16[4,64,384]{2,1,0:T(8,128)(2,1)S(1)} %bitcast.557, bf16[4,64,384]{2,1,0:T(8,128)(2,1)S(1)} %copy-done.5, ...), custom_call_target="tpu_custom_call" | custom-call | flops 2013265920 | bytes 3112960 | tf_op jit(solution)/shard_map/pallas_call | solution.py:175
  583.5 9.7 all-to-all-start.12
  690.1 8.8 all-to-all-done.14
  711.9 13.4 %shard_map.275 = (bf16[4,64,384]{2,1,0:T(8,128)(2,1)S(1)}, bf16[8,256,256]{2,1,0:T(8,128)(2,1)S(1)}, f32[8,256,256]{2,1,0:T(8,128)S(1)}) custom-call(s32[3]{0:T(128)S(1)} %add_add_fusion.1.info_ref, bf16[4,64,640]{2,1,0:T(8,128)(2,1)S(1)} %bitcast.552, bf16[4,64,384]{2,1,0:T(8,128)(2,1)S(1)} %bitcast.556, bf16[4,64,384]{2,1,0:T(8,128)(2,1)S(1)} %get-tuple-element.53.o_ref, ...), custom_call_target="tpu_custom_call" | custom-call | flops 3019898880 | bytes 4423680 | tf_op jit(solution)/shard_map/pallas_call | solution.py:175
  742.7 9.3 all-to-all-done.15
  782.0 8.4 all-to-all-start.16
  872.7 10.0 all-to-all-start.18
  891.7 13.5 %collective-permute-done.68 = bf16[4,2,32,768]{3,2,1,0:T(8,128)(2,1)S(1)} collective-permute-done((bf16[4,2,32,768]{3,2,1,0:T(8,128)(2,1)S(1)}, bf16[4,2,32,768]{3,2,1,0:T(8,128)(2,1)S(1)}, u32[]{:S(2)}, u32[]{:S(2)}) %collective-permute-start.68) | collective-permute-done | bytes 393248 | tf_op jit(solution)/shard_map/ppermute | solution.py:607
  905.2 8.7 collective-permute-done.69
  943.5 15.6 %collective-permute-done.61 = bf16[4,2,48,1024]{3,2,1,0:T(8,128)(2,1)S(1)} collective-permute-done((bf16[4,2,48,1024]{3,2,1,0:T(8,128)(2,1)S(1)}, bf16[4,2,48,1024]{3,2,1,0:T(8,128)(2,1)S(1)}, u32[]{:S(2)}, u32[]{:S(2)}) %collective-permute-start.61) | collective-permute-done | bytes 786464 | tf_op jit(solution)/shard_map/ppermute | solution.py:383
  1030.0 9.3 all-to-all-start.19
  1046.6 11.7 %all-to-all-done.19 = bf16[32,24,768]{2,1,0:T(8,128)(2,1)} async-done(((bf16[32,24,768]{2,1,0:T(8,128)(2,1)}), bf16[32,24,768]{2,1,0:T(8,128)(2,1)}, u32[]{:S(2)}, u32[]{:S(2)}) %all-to-all-start.19) | async-done | bytes 1179680 | tf_op jit(solution)/shard_map/all_to_all | solution.py:254
  (1024 shorter events, 751.1 us)
Async XLA Ops:
  7.2 115.8 %all-gather.3.cloned.1.call-start = ((), (), s32[]{:S(2)}) async-start(), calls=%async_computation.21 | async-start | bytes 4866048 | tf_op jit(solution)/shard_map/all_gather | solution.py:313
  26.6 32.4 %all-to-all-start = ((bf16[32,24,768]{2,1,0:T(8,128)(2,1)}), bf16[32,24,768]{2,1,0:T(8,128)(2,1)}, u32[]{:S(2)}, u32[]{:S(2)}) async-start(bf16[32,24,768]{2,1,0:T(8,128)(2,1)} %bitcast.604), calls=%async_computation | async-start | bytes 2359296 | tf_op jit(solution)/shard_map/all_to_all | solution.py:254
  132.6 88.2 %collective-permute-start.16 = (bf16[64,1536]{1,0:T(8,128)(2,1)}, bf16[64,1536]{1,0:T(8,128)(2,1)}, u32[]{:S(2)}, u32[]{:S(2)}) collective-permute-start(bf16[64,1536]{1,0:T(8,128)(2,1)} %get-tuple-element.186), channel_id=1, source_target_pairs={{0,24},{1,25},{2,26},{3,27},{4,28},{5,29},{6,30},{7,31},{8,0},{9,1... | collective-permute-start | bytes 589832 | tf_op jit(solution)/shard_map/ppermute | solution.py:383
  135.1 87.0 %collective-permute-start.15 = (bf16[64,1536]{1,0:T(8,128)(2,1)}, bf16[64,1536]{1,0:T(8,128)(2,1)}, u32[]{:S(2)}, u32[]{:S(2)}) collective-permute-start(bf16[64,1536]{1,0:T(8,128)(2,1)} %get-tuple-element.186), channel_id=1, source_target_pairs={{0,16},{1,17},{2,18},{3,19},{4,20},{5,21},{6,22},{7,23},{8,24},{9,... | collective-permute-start | bytes 589832 | tf_op jit(solution)/shard_map/ppermute | solution.py:383
  135.6 87.9 %collective-permute-start.14 = (bf16[64,1536]{1,0:T(8,128)(2,1)}, bf16[64,1536]{1,0:T(8,128)(2,1)}, u32[]{:S(2)}, u32[]{:S(2)}) collective-permute-start(bf16[64,1536]{1,0:T(8,128)(2,1)} %get-tuple-element.186), channel_id=1, source_target_pairs={{0,8},{1,9},{2,10},{3,11},{4,12},{5,13},{6,14},{7,15},{8,16},{9,17... | collective-permute-start | bytes 589832 | tf_op jit(solution)/shard_map/ppermute | solution.py:383
  146.6 29.1 %collective-permute-start.13 = (bf16[32,16,1536]{2,1,0:T(8,128)(2,1)}, bf16[32,16,1536]{2,1,0:T(8,128)(2,1)}, u32[]{:S(2)}, u32[]{:S(2)}) collective-permute-start(bf16[32,16,1536]{2,1,0:T(8,128)(2,1)} %reshape.534), channel_id=1, source_target_pairs={{0,32},{32,0},{1,33},{33,1},{2,34},{34,2},{3,35},{35,3},{4,36},{36... | collective-permute-start | bytes 4718600 | tf_op jit(solution)/shard_map/ppermute | solution.py:262
  149.0 46.9 %collective-permute-start.12 = (bf16[32,24,2048]{2,1,0:T(8,128)(2,1)}, bf16[32,24,2048]{2,1,0:T(8,128)(2,1)}, u32[]{:S(2)}, u32[]{:S(2)}) collective-permute-start(bf16[32,24,2048]{2,1,0:T(8,128)(2,1)} %slice.307), channel_id=1, source_target_pairs={{0,32},{32,0},{1,33},{33,1},{2,34},{34,2},{3,35},{35,3},{4,36},{36... | collective-permute-start | bytes 9437192 | tf_op jit(solution)/shard_map/ppermute | solution.py:262
  164.8 28.6 %all-to-all-start.3 = ((bf16[32,2,8,1536]{3,2,1,0:T(8,128)(2,1)}), bf16[32,2,8,1536]{3,2,1,0:T(8,128)(2,1)}, u32[]{:S(2)}, u32[]{:S(2)}) async-start(bf16[32,2,8,1536]{3,2,1,0:T(8,128)(2,1)} %bitcast.597), calls=%async_computation.3 | async-start | bytes 3145728 | tf_op jit(solution)/shard_map/all_to_all | solution.py:254
  434.8 29.6 %all-to-all-start.8 = ((bf16[32,2,8,1536]{3,2,1,0:T(8,128)(2,1)}), bf16[32,2,8,1536]{3,2,1,0:T(8,128)(2,1)}, u32[]{:S(2)}, u32[]{:S(2)}) async-start(bf16[32,2,8,1536]{3,2,1,0:T(8,128)(2,1)} %bitcast.593), calls=%async_computation.8 | async-start | bytes 3145728 | tf_op jit(solution)/shard_map/all_to_all | solution.py:254
  464.4 28.9 %all-to-all-start.10 = ((bf16[32,2,8,1536]{3,2,1,0:T(8,128)(2,1)}), bf16[32,2,8,1536]{3,2,1,0:T(8,128)(2,1)}, u32[]{:S(2)}, u32[]{:S(2)}) async-start(bf16[32,2,8,1536]{3,2,1,0:T(8,128)(2,1)} %bitcast.601), calls=%async_computation.10 | async-start | bytes 3145728 | tf_op jit(solution)/shard_map/all_to_all | solution.py:254
  493.3 30.3 %all-to-all-start.9 = ((bf16[32,2,8,1536]{3,2,1,0:T(8,128)(2,1)}), bf16[32,2,8,1536]{3,2,1,0:T(8,128)(2,1)}, u32[]{:S(2)}, u32[]{:S(2)}) async-start(bf16[32,2,8,1536]{3,2,1,0:T(8,128)(2,1)} %bitcast.598), calls=%async_computation.9 | async-start | bytes 3145728 | tf_op jit(solution)/shard_map/all_to_all | solution.py:254
  523.6 30.4 %all-to-all-start.11 = ((bf16[32,2,8,1536]{3,2,1,0:T(8,128)(2,1)}), bf16[32,2,8,1536]{3,2,1,0:T(8,128)(2,1)}, u32[]{:S(2)}, u32[]{:S(2)}) async-start(bf16[32,2,8,1536]{3,2,1,0:T(8,128)(2,1)} %bitcast.595), calls=%async_computation.11 | async-start | bytes 3145728 | tf_op jit(solution)/shard_map/all_to_all | solution.py:254
  600.5 227.2 %collective-permute-start.31 = (bf16[128,1536]{1,0:T(8,128)(2,1)}, bf16[128,1536]{1,0:T(8,128)(2,1)}, u32[]{:S(2)}, u32[]{:S(2)}) collective-permute-start(bf16[128,1536]{1,0:T(8,128)(2,1)} %pad_maximum_fusion.11), channel_id=1, source_target_pairs={{0,32},{32,0},{1,33},{33,1},{2,34},{34,2},{3,35},{35,3},{4,36},{36... | collective-permute-start | bytes 1179656 | tf_op jit(solution)/shard_map/ppermute | solution.py:262
  633.5 29.6 %all-to-all-start.13 = ((bf16[32,2,8,1536]{3,2,1,0:T(8,128)(2,1)}), bf16[32,2,8,1536]{3,2,1,0:T(8,128)(2,1)}, u32[]{:S(2)}, u32[]{:S(2)}) async-start(bf16[32,2,8,1536]{3,2,1,0:T(8,128)(2,1)} %bitcast.603), calls=%async_computation.13 | async-start | bytes 3145728 | tf_op jit(solution)/shard_map/all_to_all | solution.py:254
  645.4 158.8 %collective-permute-start.47 = (bf16[128,1024]{1,0:T(8,128)(2,1)}, bf16[128,1024]{1,0:T(8,128)(2,1)}, u32[]{:S(2)}, u32[]{:S(2)}) collective-permute-start(bf16[128,1024]{1,0:T(8,128)(2,1)} %pad_maximum_fusion.14), channel_id=1, source_target_pairs={{0,32},{32,0},{1,33},{33,1},{2,34},{34,2},{3,35},{35,3},{4,36},{36... | collective-permute-start | bytes 786440 | tf_op jit(solution)/shard_map/ppermute | solution.py:262
  782.0 30.0 %all-to-all-start.16 = ((bf16[32,2,8,1536]{3,2,1,0:T(8,128)(2,1)}), bf16[32,2,8,1536]{3,2,1,0:T(8,128)(2,1)}, u32[]{:S(2)}, u32[]{:S(2)}) async-start(bf16[32,2,8,1536]{3,2,1,0:T(8,128)(2,1)} %bitcast.602), calls=%async_computation.16 | async-start | bytes 3145728 | tf_op jit(solution)/shard_map/all_to_all | solution.py:254
  820.8 28.7 %all-to-all-start.17 = ((bf16[32,2,8,1536]{3,2,1,0:T(8,128)(2,1)}), bf16[32,2,8,1536]{3,2,1,0:T(8,128)(2,1)}, u32[]{:S(2)}, u32[]{:S(2)}) async-start(bf16[32,2,8,1536]{3,2,1,0:T(8,128)(2,1)} %bitcast.592), calls=%async_computation.17 | async-start | bytes 3145728 | tf_op jit(solution)/shard_map/all_to_all | solution.py:254
  835.4 176.8 %collective-permute-start.76 = (bf16[2,1536,512]{2,1,0:T(8,128)(2,1)}, bf16[2,1536,512]{2,1,0:T(8,128)(2,1)}, u32[]{:S(2)}, u32[]{:S(2)}) collective-permute-start(bf16[2,1536,512]{2,1,0:T(8,128)(2,1)} %convolution_convert_fusion.3), channel_id=1, source_target_pairs={{0,32},{32,0},{1,33},{33,1},{2,34},{34,2},{3,35},{35,3},{4,36},{36... | collective-permute-start | bytes 9437192 | tf_op jit(solution)/shard_map/ppermute | solution.py:262
  872.7 95.6 %all-to-all-start.18 = ((bf16[8,256,256]{2,1,0:T(8,128)(2,1)}), bf16[8,256,256]{2,1,0:T(8,128)(2,1)}, u32[]{:S(2)}, u32[]{:S(2)}) async-start(bf16[8,256,256]{2,1,0:T(8,128)(2,1)} %copy-done.1), calls=%async_computation.18 | async-start | bytes 2097152 | tf_op jit(solution)/shard_map/all_to_all | solution.py:254
  889.7 39.2 %collective-permute-start.52 = (bf16[8,24,1536]{2,1,0:T(8,128)(2,1)S(1)}, bf16[8,24,1536]{2,1,0:T(8,128)(2,1)S(1)}, u32[]{:S(2)}, u32[]{:S(2)}) collective-permute-start(bf16[8,24,1536]{2,1,0:T(8,128)(2,1)S(1)} %broadcast_select_fusion.8), channel_id=1, source_target_pairs={{0,32},{32,0},{1,33},{33,1},{2,34},{34,2},{3,35},{35,3},{4,36},{36... | collective-permute-start | bytes 1769480 | tf_op jit(solution)/shard_map/ppermute | solution.py:262
  928.9 30.2 %collective-permute-start.61 = (bf16[4,2,48,1024]{3,2,1,0:T(8,128)(2,1)S(1)}, bf16[4,2,48,1024]{3,2,1,0:T(8,128)(2,1)S(1)}, u32[]{:S(2)}, u32[]{:S(2)}) collective-permute-start(bf16[4,2,48,1024]{3,2,1,0:T(8,128)(2,1)S(1)} %get-tuple-element.124), channel_id=1, source_target_pairs={{0,16},{1,17},{2,18},{3,19},{4,20},{5,21},{6,22},{7,23},{8,24},{9,... | collective-permute-start | bytes 2359304 | tf_op jit(solution)/shard_map/ppermute | solution.py:383
  934.1 84.6 %collective-permute-start.77 = (bf16[2,1536,512]{2,1,0:T(8,128)(2,1)}, bf16[2,1536,512]{2,1,0:T(8,128)(2,1)}, u32[]{:S(2)}, u32[]{:S(2)}) collective-permute-start(bf16[2,1536,512]{2,1,0:T(8,128)(2,1)} %convolution_convert_fusion.2), channel_id=1, source_target_pairs={{0,32},{32,0},{1,33},{33,1},{2,34},{34,2},{3,35},{35,3},{4,36},{36... | collective-permute-start | bytes 9437192 | tf_op jit(solution)/shard_map/ppermute | solution.py:262
  982.3 57.0 %collective-permute-start.78 = (bf16[2,512,1536]{2,1,0:T(8,128)(2,1)}, bf16[2,512,1536]{2,1,0:T(8,128)(2,1)}, u32[]{:S(2)}, u32[]{:S(2)}) collective-permute-start(bf16[2,512,1536]{2,1,0:T(8,128)(2,1)} %convolution_convert_fusion.1), channel_id=1, source_target_pairs={{0,32},{32,0},{1,33},{33,1},{2,34},{34,2},{3,35},{35,3},{4,36},{36... | collective-permute-start | bytes 9437192 | tf_op jit(solution)/shard_map/ppermute | solution.py:262
  988.4 36.9 %all-to-all-start.20 = ((bf16[8,24,1536]{2,1,0:T(8,128)(2,1)}), bf16[8,24,1536]{2,1,0:T(8,128)(2,1)}, u32[]{:S(2)}, u32[]{:S(2)}) async-start(bf16[8,24,1536]{2,1,0:T(8,128)(2,1)} %add_convert_fusion.1), calls=%async_computation.20 | async-start | bytes 1179648 | tf_op jit(solution)/shard_map/all_to_all | solution.py:254
  (354 other events, 3006.1 us)
Sparse Core Ops, SparseCore 0:
  16.9 106.0 all-gather.2

commit v9 on v8

--- a/solution.py
+++ b/solution.py
@@ -586,7 +586,7 @@
         wide_einsum("erf,erd->efd", kept_rows("activated", 1), back_rows("expert_grad", 1)),
     ]
     expert_parts = [part.astype(bf) for part in expert_parts]
-    expert_grads = [part.astype(f32) + twin(part).astype(f32) for part in expert_parts]
+    expert_others = [twin(part) for part in expert_parts]
 
     def both(value):
         return jnp.concatenate([value, twin(value)], axis=0)
@@ -625,30 +625,31 @@
             total = total + shift(piece(steps), steps).astype(f32)
         return total.astype(held_as)
 
-    grad_gate_up, grad_down, ring_hidden = lax.optimization_barrier(
-        (grad_gate_up.astype(bf), grad_down.astype(bf), backs[0]["ring_hidden"])
-    )
-    backs[0]["ring_hidden"] = ring_hidden
+    grad_out = dot_tn(
+        kept_rows("attended").reshape(micros * heads * block, group_width),
+        back_rows("ring_hidden"),
+    )
+    grad_gate_up, grad_down, grad_out, last_grad, *expert_others = lax.optimization_barrier(
+        (
+            grad_gate_up.astype(bf),
+            grad_down.astype(bf),
+            grad_out.astype(bf),
+            backs[0]["layer_grad"],
+            *expert_others,
+        )
+    )
+    backs[0]["layer_grad"] = last_grad
+    expert_grads = [
+        part.astype(f32) + other.astype(f32) for part, other in zip(expert_parts, expert_others)
+    ]
     pieces = grad_gate_up.reshape(heads, ring // 2, 2, rows_per, shared_width)
     share_gate_up = reduced(reduced(reduced(pieces, "x", 0), "z", 0), "y", 0, f32)
     pieces = grad_down.reshape(heads, ring // 2, 2, down_rows, width // 2)
     share_down = reduced(reduced(reduced(pieces, "z", 1), "x", 0), "y", 0, f32)
 
-    grad_out = dot_tn(
-        kept_rows("attended").reshape(micros * heads * block, group_width),
-        back_rows("ring_hidden"),
-    )
-
-    def with_twin(value):
-        value = value.astype(bf)
-        own = my_rows(value)
-        other = mine_of(value[..., half_rows:, :], value[..., :half_rows, :])
-        return (own.astype(f32) + twin(other).astype(f32)).astype(bf)
-
-    grad_out = with_twin(grad_out.reshape(ring, rows_per, width))
-    grad_out, last_grad = lax.optimization_barrier((grad_out, backs[0]["layer_grad"]))
-    backs[0]["layer_grad"] = last_grad
-    share_out = jnp.sum(exchange(grad_out, zy_groups).astype(f32), axis=0)
+    share_out = jnp.sum(
+        exchange(grad_out.reshape(ring, rows_per, width), zy_groups).astype(f32), axis=0
+    )
     grad_qkv = dot_tn(kept_rows("ring_one"), back_rows("qkv_grad"))
     grad_router = dot_tn(normed_two, back_rows("logit_grad"))
     gain_sums = jnp.stack(
@@ -659,16 +660,16 @@
     )
     grad_qkv = jnp.concatenate([grad_qkv, grad_tail], axis=1)
     pieces = exchange(
-        with_twin(grad_qkv.reshape(shards, rows_per, part_width + 128))
+        grad_qkv.astype(bf).reshape(shards, rows_per, part_width + 128)
     ).astype(f32)
     share_qkv = jnp.sum(
-        pieces[:, :, :part_width].reshape(heads, ring, half_rows, part_width), axis=1
+        pieces[:, :, :part_width].reshape(heads, ring, rows_per, part_width), axis=1
     )
     share_qkv = share_qkv.transpose(1, 0, 2)
     share_tail = jnp.sum(pieces[:, :, part_width:], axis=0)
 
     def total(share):
-        return ordered(share, twin(share), 0)
+        return share + twin(share)
 
     out_total, qkv_total, tail_total = total(share_out), total(share_qkv), total(share_tail)
     other_gate_up = twin(share_gate_up)

time: 1090 us -> 1070 us (0.982)
  starting transfers between devices: 257 us -> 244 us
    ppermute x2, waiting for transfers between devices: 1.81 us -> 22.8 us  [shift_y(): return lax.ppermute(value, 'shard', [(p, p ^ 1) for p in range(shards)])]
    ppermute x6, waiting for transfers between devices: 23.1 us -> 7.93 us  [shift_z(): return lax.ppermute(value, 'shard', pairs)]
    ppermute x18 -> x16, starting transfers between devices: 31.2 us -> 19.3 us  [twin(): return lax.ppermute(value, 'dp', [(0, 1), (1, 0)])]
    unnamed x566 -> x568, local copies, waits for them, and re-layouts: 37.3 us -> 35.1 us
  transfers between devices with their start and end apart: 100 -> 98, of which waited for: 58 -> 54; matrix products, arithmetic and copies ran while one was open for 27% -> 28% of each run, Pallas kernels for 2% -> 2%
where the time goes in v9:
time: 1070 us; the launch traced here: 1060 us
  waiting for transfers between devices  337 us (31%)
  starting transfers between devices  244 us (23%)
  matrix products  179 us (17%)
  other arithmetic  113 us (11%)
  local copies, waits for them, and re-layouts  91.1 us (9%)
  Pallas kernels  48.4 us (5%)
  blocking collectives  28.9 us (3%)
  between operations  18.2 us (2%)
    all_to_all x20, waiting for transfers between devices, exchange(): lax.all_to_all(value, 'shard', split_axis=0, concat_axis=0, tiled=True, a...  178 us
    all_to_all x20, starting transfers between devices, exchange(): lax.all_to_all(value, 'shard', split_axis=0, concat_axis=0, tiled=True, a...  134 us
    ppermute x39, waiting for transfers between devices, shift_x(): lax.ppermute(value, 'shard', [(p, moved(p, steps)) for p in range(shards)])  76.9 us
    dot_general x24, matrix products, dot_nt(): lax.dot_general(left_side, right_side, (((1,), (1,)), ((), ())), preferre...  54 us
    dot_general x31, matrix products, dot(): return jnp.dot(left_side, right_side, preferred_element_type=f32)  51.6 us
    pallas_call x6, Pallas kernels, attention_call(): pl.pallas_call(kernel, out_shape=out_shape, in_specs=[pl.BlockSpec(memory...  48.4 us
    dot_general x21, matrix products, wide_einsum(): jnp.einsum(formula, left_side, right_side, preferred_element_type=f32)  47.9 us
    ppermute x39, starting transfers between devices, shift_x(): lax.ppermute(value, 'shard', [(p, moved(p, steps)) for p in range(shards)])  43 us
  transfers between devices with their start and end apart: 98, of which 54 were waited for; matrix products, arithmetic and copies ran while one was open for 28% of the time, Pallas kernels for 2%

profile of v9, /device:TPU:1, one launch (start us, length us, event | category | flops | bytes accessed | tf_op | source)
XLA Modules:
  0.0 1060.1 jit_solution(11467566163199700820)
XLA Ops:
  42.9 11.5 %collective-permute-done.6 = bf16[2,24,1536]{2,1,0:T(8,128)(2,1)} collective-permute-done((bf16[2,24,1536]{2,1,0:T(8,128)(2,1)S(1)}, bf16[2,24,1536]{2,1,0:T(8,128)(2,1)}, u32[]{:S(2)}, u32[]{:S(2)}) %collective-permute-start.6) | collective-permute-done | bytes 147488 | tf_op jit(solution)/shard_map/ppermute | solution.py:320
  79.4 16.5 %all-to-all-done.1.refs_0_.refs_1_ = bf16[8,256,256]{2,1,0:T(8,128)(2,1)} async-done(((bf16[8,256,256]{2,1,0:T(8,128)(2,1)}), bf16[8,256,256]{2,1,0:T(8,128)(2,1)}, u32[]{:S(2)}, u32[]{:S(2)}) %all-to-all-start.1) | async-done | bytes 1048608 | tf_op jit(solution)/shard_map/all_to_all | solution.py:254
  177.6 13.0 %all-to-all-done.3 = bf16[32,2,8,1536]{3,2,1,0:T(8,128)(2,1)} async-done(((bf16[32,2,8,1536]{3,2,1,0:T(8,128)(2,1)}), bf16[32,2,8,1536]{3,2,1,0:T(8,128)(2,1)}, u32[]{:S(2)}, u32[]{:S(2)}) %all-to-all-start.3) | async-done | bytes 1572896 | tf_op jit(solution)/shard_map/all_to_all | solution.py:254
  208.5 10.4 collective-permute-start.20
  245.3 15.7 %all-to-all-done.4.refs_1_.refs_0_.refs_2_ = bf16[8,256,256]{2,1,0:T(8,128)(2,1)} async-done(((bf16[8,256,256]{2,1,0:T(8,128)(2,1)}), bf16[8,256,256]{2,1,0:T(8,128)(2,1)}, u32[]{:S(2)}, u32[]{:S(2)}) %all-to-all-start.4) | async-done | bytes 1048608 | tf_op jit(solution)/shard_map/all_to_all | solution.py:254
  288.2 28.9 %all_to_all.105 = bf16[32,2,8,1536]{3,2,1,0:T(8,128)(2,1)S(1)} all-to-all(bf16[32,2,8,1536]{3,2,1,0:T(8,128)(2,1)S(1)} %bitcast.595), channel_id=1, replica_groups=mesh['section'=2,'dp'=2,'shard'=32] {'shard'}, dimensions={0} | all-to-all | bytes 3145728 | tf_op jit(solution)/shard_map/all_to_all | solution.py:254
  336.7 14.1 %all-to-all-done.6 = bf16[32,2,8,1536]{3,2,1,0:T(8,128)(2,1)} async-done(((bf16[32,2,8,1536]{3,2,1,0:T(8,128)(2,1)}), bf16[32,2,8,1536]{3,2,1,0:T(8,128)(2,1)}, u32[]{:S(2)}, u32[]{:S(2)}) %all-to-all-start.6) | async-done | bytes 1572896 | tf_op jit(solution)/shard_map/all_to_all | solution.py:254
  369.3 10.2 collective-permute-done.24
  396.4 13.8 %all-to-all-done.7.refs_1_ = bf16[8,256,256]{2,1,0:T(8,128)(2,1)} async-done(((bf16[8,256,256]{2,1,0:T(8,128)(2,1)}), bf16[8,256,256]{2,1,0:T(8,128)(2,1)}, u32[]{:S(2)}, u32[]{:S(2)}) %all-to-all-start.7) | async-done | bytes 1048608 | tf_op jit(solution)/shard_map/all_to_all | solution.py:254
  446.0 17.5 %all-to-all-done.8 = bf16[32,2,8,1536]{3,2,1,0:T(8,128)(2,1)} async-done(((bf16[32,2,8,1536]{3,2,1,0:T(8,128)(2,1)}), bf16[32,2,8,1536]{3,2,1,0:T(8,128)(2,1)}, u32[]{:S(2)}, u32[]{:S(2)}) %all-to-all-start.8) | async-done | bytes 1572896 | tf_op jit(solution)/shard_map/all_to_all | solution.py:254
  482.5 9.9 all-to-all-done.10
  512.4 10.2 all-to-all-done.9
  541.8 11.2 %all-to-all-done.11 = bf16[32,2,8,1536]{3,2,1,0:T(8,128)(2,1)} async-done(((bf16[32,2,8,1536]{3,2,1,0:T(8,128)(2,1)}), bf16[32,2,8,1536]{3,2,1,0:T(8,128)(2,1)}, u32[]{:S(2)}, u32[]{:S(2)}) %all-to-all-start.11) | async-done | bytes 1572896 | tf_op jit(solution)/shard_map/all_to_all | solution.py:254
  566.2 13.4 %shard_map.274 = (bf16[4,64,384]{2,1,0:T(8,128)(2,1)S(1)}, bf16[8,256,256]{2,1,0:T(8,128)(2,1)S(1)}, f32[8,256,256]{2,1,0:T(8,128)S(1)}) custom-call(s32[3]{0:T(128)S(1)} %add_add_fusion.info_ref, bf16[4,64,640]{2,1,0:T(8,128)(2,1)S(1)} %bitcast.551, bf16[4,64,384]{2,1,0:T(8,128)(2,1)S(1)} %bitcast.554, bf16[4,64,384]{2,1,0:T(8,128)(2,1)S(1)} %copy-done.5, ...), custom_call_target="tpu_custom_call" | custom-call | flops 2013265920 | bytes 3112960 | tf_op jit(solution)/shard_map/pallas_call | solution.py:175
  582.5 9.2 all-to-all-start.12
  599.1 9.2 all-to-all-done.12
  688.7 8.7 all-to-all-done.14
  711.0 13.4 %shard_map.275 = (bf16[4,64,384]{2,1,0:T(8,128)(2,1)S(1)}, bf16[8,256,256]{2,1,0:T(8,128)(2,1)S(1)}, f32[8,256,256]{2,1,0:T(8,128)S(1)}) custom-call(s32[3]{0:T(128)S(1)} %add_add_fusion.1.info_ref, bf16[4,64,640]{2,1,0:T(8,128)(2,1)S(1)} %bitcast.549, bf16[4,64,384]{2,1,0:T(8,128)(2,1)S(1)} %bitcast.552, bf16[4,64,384]{2,1,0:T(8,128)(2,1)S(1)} %get-tuple-element.55.o_ref, ...), custom_call_target="tpu_custom_call" | custom-call | flops 3019898880 | bytes 4423680 | tf_op jit(solution)/shard_map/pallas_call | solution.py:175
  741.8 9.3 all-to-all-done.15
  781.1 8.4 all-to-all-start.16
  819.9 9.2 all-to-all-start.17
  888.5 9.3 all-to-all-done.18
  966.9 18.1 %collective-permute-done.72 = bf16[2,32,768]{2,1,0:T(8,128)(2,1)} collective-permute-done((bf16[2,32,768]{2,1,0:T(8,128)(2,1)S(1)}, bf16[2,32,768]{2,1,0:T(8,128)(2,1)}, u32[]{:S(2)}, u32[]{:S(2)}) %collective-permute-start.72) | collective-permute-done | bytes 98336 | tf_op jit(solution)/shard_map/ppermute | solution.py:383
  1004.7 18.4 %collective-permute-done.75 = bf16[32,768]{1,0:T(8,128)(2,1)S(1)} collective-permute-done((bf16[32,768]{1,0:T(8,128)(2,1)S(1)}, bf16[32,768]{1,0:T(8,128)(2,1)S(1)}, u32[]{:S(2)}, u32[]{:S(2)}) %collective-permute-start.75) | collective-permute-done | bytes 49184 | tf_op jit(solution)/shard_map/ppermute | solution.py:610
  (1016 shorter events, 732.3 us)
Async XLA Ops:
  7.2 114.5 %all-gather.3.cloned.1.call-start = ((), (), s32[]{:S(2)}) async-start(), calls=%async_computation.21 | async-start | bytes 4866048 | tf_op jit(solution)/shard_map/all_gather | solution.py:313
  26.6 32.3 %all-to-all-start = ((bf16[32,24,768]{2,1,0:T(8,128)(2,1)}), bf16[32,24,768]{2,1,0:T(8,128)(2,1)}, u32[]{:S(2)}, u32[]{:S(2)}) async-start(bf16[32,24,768]{2,1,0:T(8,128)(2,1)} %bitcast.599), calls=%async_computation | async-start | bytes 2359296 | tf_op jit(solution)/shard_map/all_to_all | solution.py:254
  131.6 88.7 %collective-permute-start.16 = (bf16[64,1536]{1,0:T(8,128)(2,1)}, bf16[64,1536]{1,0:T(8,128)(2,1)}, u32[]{:S(2)}, u32[]{:S(2)}) collective-permute-start(bf16[64,1536]{1,0:T(8,128)(2,1)} %get-tuple-element.188), channel_id=1, source_target_pairs={{0,24},{1,25},{2,26},{3,27},{4,28},{5,29},{6,30},{7,31},{8,0},{9,1... | collective-permute-start | bytes 589832 | tf_op jit(solution)/shard_map/ppermute | solution.py:383
  134.0 87.5 %collective-permute-start.15 = (bf16[64,1536]{1,0:T(8,128)(2,1)}, bf16[64,1536]{1,0:T(8,128)(2,1)}, u32[]{:S(2)}, u32[]{:S(2)}) collective-permute-start(bf16[64,1536]{1,0:T(8,128)(2,1)} %get-tuple-element.188), channel_id=1, source_target_pairs={{0,16},{1,17},{2,18},{3,19},{4,20},{5,21},{6,22},{7,23},{8,24},{9,... | collective-permute-start | bytes 589832 | tf_op jit(solution)/shard_map/ppermute | solution.py:383
  134.5 88.3 %collective-permute-start.14 = (bf16[64,1536]{1,0:T(8,128)(2,1)}, bf16[64,1536]{1,0:T(8,128)(2,1)}, u32[]{:S(2)}, u32[]{:S(2)}) collective-permute-start(bf16[64,1536]{1,0:T(8,128)(2,1)} %get-tuple-element.188), channel_id=1, source_target_pairs={{0,8},{1,9},{2,10},{3,11},{4,12},{5,13},{6,14},{7,15},{8,16},{9,17... | collective-permute-start | bytes 589832 | tf_op jit(solution)/shard_map/ppermute | solution.py:383
  148.2 45.0 %collective-permute-start.12 = (bf16[32,24,2048]{2,1,0:T(8,128)(2,1)}, bf16[32,24,2048]{2,1,0:T(8,128)(2,1)}, u32[]{:S(2)}, u32[]{:S(2)}) collective-permute-start(bf16[32,24,2048]{2,1,0:T(8,128)(2,1)} %slice.291), channel_id=1, source_target_pairs={{0,32},{32,0},{1,33},{33,1},{2,34},{34,2},{3,35},{35,3},{4,36},{36... | collective-permute-start | bytes 9437192 | tf_op jit(solution)/shard_map/ppermute | solution.py:262
  433.9 29.7 %all-to-all-start.8 = ((bf16[32,2,8,1536]{3,2,1,0:T(8,128)(2,1)}), bf16[32,2,8,1536]{3,2,1,0:T(8,128)(2,1)}, u32[]{:S(2)}, u32[]{:S(2)}) async-start(bf16[32,2,8,1536]{3,2,1,0:T(8,128)(2,1)} %bitcast.588), calls=%async_computation.8 | async-start | bytes 3145728 | tf_op jit(solution)/shard_map/all_to_all | solution.py:254
  492.4 30.3 %all-to-all-start.9 = ((bf16[32,2,8,1536]{3,2,1,0:T(8,128)(2,1)}), bf16[32,2,8,1536]{3,2,1,0:T(8,128)(2,1)}, u32[]{:S(2)}, u32[]{:S(2)}) async-start(bf16[32,2,8,1536]{3,2,1,0:T(8,128)(2,1)} %bitcast.593), calls=%async_computation.9 | async-start | bytes 3145728 | tf_op jit(solution)/shard_map/all_to_all | solution.py:254
  522.6 30.4 %all-to-all-start.11 = ((bf16[32,2,8,1536]{3,2,1,0:T(8,128)(2,1)}), bf16[32,2,8,1536]{3,2,1,0:T(8,128)(2,1)}, u32[]{:S(2)}, u32[]{:S(2)}) async-start(bf16[32,2,8,1536]{3,2,1,0:T(8,128)(2,1)} %bitcast.590), calls=%async_computation.11 | async-start | bytes 3145728 | tf_op jit(solution)/shard_map/all_to_all | solution.py:254
  596.2 232.9 %collective-permute-start.31 = (bf16[128,1536]{1,0:T(8,128)(2,1)}, bf16[128,1536]{1,0:T(8,128)(2,1)}, u32[]{:S(2)}, u32[]{:S(2)}) collective-permute-start(bf16[128,1536]{1,0:T(8,128)(2,1)} %pad_maximum_fusion.10), channel_id=1, source_target_pairs={{0,32},{32,0},{1,33},{33,1},{2,34},{34,2},{3,35},{35,3},{4,36},{36... | collective-permute-start | bytes 1179656 | tf_op jit(solution)/shard_map/ppermute | solution.py:262
  644.1 163.5 %collective-permute-start.47 = (bf16[128,1024]{1,0:T(8,128)(2,1)}, bf16[128,1024]{1,0:T(8,128)(2,1)}, u32[]{:S(2)}, u32[]{:S(2)}) collective-permute-start(bf16[128,1024]{1,0:T(8,128)(2,1)} %pad_maximum_fusion.14), channel_id=1, source_target_pairs={{0,32},{32,0},{1,33},{33,1},{2,34},{34,2},{3,35},{35,3},{4,36},{36... | collective-permute-start | bytes 786440 | tf_op jit(solution)/shard_map/ppermute | solution.py:262
  781.1 30.0 %all-to-all-start.16 = ((bf16[32,2,8,1536]{3,2,1,0:T(8,128)(2,1)}), bf16[32,2,8,1536]{3,2,1,0:T(8,128)(2,1)}, u32[]{:S(2)}, u32[]{:S(2)}) async-start(bf16[32,2,8,1536]{3,2,1,0:T(8,128)(2,1)} %bitcast.597), calls=%async_computation.16 | async-start | bytes 3145728 | tf_op jit(solution)/shard_map/all_to_all | solution.py:254
  819.9 33.0 %all-to-all-start.17 = ((bf16[32,2,8,1536]{3,2,1,0:T(8,128)(2,1)}), bf16[32,2,8,1536]{3,2,1,0:T(8,128)(2,1)}, u32[]{:S(2)}, u32[]{:S(2)}) async-start(bf16[32,2,8,1536]{3,2,1,0:T(8,128)(2,1)} %bitcast.587), calls=%async_computation.17 | async-start | bytes 3145728 | tf_op jit(solution)/shard_map/all_to_all | solution.py:254
  836.8 89.1 %collective-permute-start.55 = (bf16[2,1536,512]{2,1,0:T(8,128)(2,1)}, bf16[2,1536,512]{2,1,0:T(8,128)(2,1)}, u32[]{:S(2)}, u32[]{:S(2)}) collective-permute-start(bf16[2,1536,512]{2,1,0:T(8,128)(2,1)} %convolution_convert_fusion.3), channel_id=1, source_target_pairs={{0,32},{32,0},{1,33},{33,1},{2,34},{34,2},{3,35},{35,3},{4,36},{36... | collective-permute-start | bytes 9437192 | tf_op jit(solution)/shard_map/ppermute | solution.py:262
  841.0 84.9 %collective-permute-start.56 = (bf16[2,1536,512]{2,1,0:T(8,128)(2,1)}, bf16[2,1536,512]{2,1,0:T(8,128)(2,1)}, u32[]{:S(2)}, u32[]{:S(2)}) collective-permute-start(bf16[2,1536,512]{2,1,0:T(8,128)(2,1)} %convolution_convert_fusion.2), channel_id=1, source_target_pairs={{0,32},{32,0},{1,33},{33,1},{2,34},{34,2},{3,35},{35,3},{4,36},{36... | collective-permute-start | bytes 9437192 | tf_op jit(solution)/shard_map/ppermute | solution.py:262
  860.4 65.5 %collective-permute-start.57 = (bf16[2,512,1536]{2,1,0:T(8,128)(2,1)}, bf16[2,512,1536]{2,1,0:T(8,128)(2,1)}, u32[]{:S(2)}, u32[]{:S(2)}) collective-permute-start(bf16[2,512,1536]{2,1,0:T(8,128)(2,1)} %convolution_convert_fusion.1), channel_id=1, source_target_pairs={{0,32},{32,0},{1,33},{33,1},{2,34},{34,2},{3,35},{35,3},{4,36},{36... | collective-permute-start | bytes 9437192 | tf_op jit(solution)/shard_map/ppermute | solution.py:262
  925.9 60.4 %all-to-all-start.20 = ((bf16[8,48,1536]{2,1,0:T(8,128)(2,1)}), bf16[8,48,1536]{2,1,0:T(8,128)(2,1)}, u32[]{:S(2)}, u32[]{:S(2)}) async-start(bf16[8,48,1536]{2,1,0:T(8,128)(2,1)} %bitcast.608), calls=%async_computation.20 | async-start | bytes 2359296 | tf_op jit(solution)/shard_map/all_to_all | solution.py:254
  940.1 57.9 %collective-permute-start.61 = (bf16[4,2,48,1024]{3,2,1,0:T(8,128)(2,1)}, bf16[4,2,48,1024]{3,2,1,0:T(8,128)(2,1)}, u32[]{:S(2)}, u32[]{:S(2)}) collective-permute-start(bf16[4,2,48,1024]{3,2,1,0:T(8,128)(2,1)} %get-tuple-element.126), channel_id=1, source_target_pairs={{0,8},{1,9},{2,10},{3,11},{4,12},{5,13},{6,14},{7,15},{8,16},{9,17... | collective-permute-start | bytes 2359304 | tf_op jit(solution)/shard_map/ppermute | solution.py:383
  940.1 57.9 %collective-permute-start.63 = (bf16[4,2,48,1024]{3,2,1,0:T(8,128)(2,1)}, bf16[4,2,48,1024]{3,2,1,0:T(8,128)(2,1)}, u32[]{:S(2)}, u32[]{:S(2)}) collective-permute-start(bf16[4,2,48,1024]{3,2,1,0:T(8,128)(2,1)} %get-tuple-element.127), channel_id=1, source_target_pairs={{0,24},{1,25},{2,26},{3,27},{4,28},{5,29},{6,30},{7,31},{8,0},{9,1... | collective-permute-start | bytes 2359304 | tf_op jit(solution)/shard_map/ppermute | solution.py:383
  961.5 36.5 %collective-permute-start.62 = (bf16[4,2,48,1024]{3,2,1,0:T(8,128)(2,1)}, bf16[4,2,48,1024]{3,2,1,0:T(8,128)(2,1)}, u32[]{:S(2)}, u32[]{:S(2)}) collective-permute-start(bf16[4,2,48,1024]{3,2,1,0:T(8,128)(2,1)} %get-tuple-element.128), channel_id=1, source_target_pairs={{0,16},{1,17},{2,18},{3,19},{4,20},{5,21},{6,22},{7,23},{8,24},{9,... | collective-permute-start | bytes 2359304 | tf_op jit(solution)/shard_map/ppermute | solution.py:383
  964.1 30.0 %collective-permute-start.74 = (bf16[2,32,768]{2,1,0:T(8,128)(2,1)}, bf16[2,32,768]{2,1,0:T(8,128)(2,1)}, u32[]{:S(2)}, u32[]{:S(2)}) collective-permute-start(bf16[2,32,768]{2,1,0:T(8,128)(2,1)} %get-tuple-element.180), channel_id=1, source_target_pairs={{0,24},{1,25},{2,26},{3,27},{4,28},{5,29},{6,30},{7,31},{8,0},{9,1... | collective-permute-start | bytes 294920 | tf_op jit(solution)/shard_map/ppermute | solution.py:383
  986.3 56.4 %all-to-all-start.19 = ((bf16[32,48,768]{2,1,0:T(8,128)(2,1)}), bf16[32,48,768]{2,1,0:T(8,128)(2,1)}, u32[]{:S(2)}, u32[]{:S(2)}) async-start(bf16[32,48,768]{2,1,0:T(8,128)(2,1)} %maximum_maximum_fusion), calls=%async_computation.19 | async-start | bytes 4718592 | tf_op jit(solution)/shard_map/all_to_all | solution.py:254
  1000.5 32.1 %collective-permute-start.64 = (bf16[2,48,1024]{2,1,0:T(8,128)(2,1)S(1)}, bf16[2,48,1024]{2,1,0:T(8,128)(2,1)S(1)}, u32[]{:S(2)}, u32[]{:S(2)}) collective-permute-start(bf16[2,48,1024]{2,1,0:T(8,128)(2,1)S(1)} %get-tuple-element.144), channel_id=1, source_target_pairs={{0,2},{1,3},{2,4},{3,5},{4,6},{5,7},{6,0},{7,1},{8,10},{9,11},{10,... | collective-permute-start | bytes 589832 | tf_op jit(solution)/shard_map/ppermute | solution.py:607
  1001.8 30.8 %collective-permute-start.66 = (bf16[2,48,1024]{2,1,0:T(8,128)(2,1)S(1)}, bf16[2,48,1024]{2,1,0:T(8,128)(2,1)S(1)}, u32[]{:S(2)}, u32[]{:S(2)}) collective-permute-start(bf16[2,48,1024]{2,1,0:T(8,128)(2,1)S(1)} %get-tuple-element.145), channel_id=1, source_target_pairs={{0,6},{1,7},{2,0},{3,1},{4,2},{5,3},{6,4},{7,5},{8,14},{9,15},{10,... | collective-permute-start | bytes 589832 | tf_op jit(solution)/shard_map/ppermute | solution.py:607
  (353 other events, 3138.2 us)
Sparse Core Ops, SparseCore 0:
  16.9 104.7 all-gather.2

commit v10 on v9

--- a/solution.py
+++ b/solution.py
@@ -21,6 +21,20 @@
 bf = jnp.bfloat16
 f32 = jnp.float32
 VMEM_LIMIT = 32 * 1024 * 1024
+KEPT = ("ring_one", "attended", "normed_two", "shared_act", "expert_in", "activated")
+BACK = (
+    "qkv_grad",
+    "ring_hidden",
+    "gain_one_grad",
+    "gain_two_grad",
+    "logit_grad",
+    "upstream_b",
+    "shared_gate_grad",
+    "shared_up_grad",
+    "expert_grad",
+    "gate_pre_grad",
+    "up_pre_grad",
+)
 
 
 def inverse_rms(rows):
@@ -62,17 +76,19 @@
 
 
 def arrival(info_ref, parts, part):
-    return lax.rem(info_ref[2] + parts - part, parts)
-
-
-def stacked_heads(ref, at):
-    return jnp.concatenate([ref[at, :, g * HD : (g + 1) * HD] for g in range(GROUP)], axis=0)
-
-
-def store_heads(ref, at, rows):
-    block = ref.shape[1]
+    return lax.rem(info_ref[1] + parts - part, parts)
+
+
+def stacked_heads(ref, at, micro):
+    return jnp.concatenate(
+        [ref[at, micro, :, g * HD : (g + 1) * HD] for g in range(GROUP)], axis=0
+    )
+
+
+def store_heads(ref, at, micro, rows):
+    block = ref.shape[2]
     for g in range(GROUP):
-        ref[at, :, g * HD : (g + 1) * HD] = rows[g * block : (g + 1) * block]
+        ref[at, micro, :, g * HD : (g + 1) * HD] = rows[g * block : (g + 1) * block]
 
 
 def cached(ref, span, column):
@@ -80,8 +96,16 @@
     return rows.reshape(rows.shape[0] * rows.shape[1], HD)
 
 
-def block_span(at, block):
-    return pl.ds(pl.multiple_of(at * block, block), block)
+def key_spans(info_ref, parts, micros, block, part, micro):
+    spans = [
+        slice((at * micros + m) * block, (at * micros + m + 1) * block)
+        for m in range(micro)
+        for at in range(parts)
+    ]
+    for p in range(part + 1):
+        start = (arrival(info_ref, parts, p) * micros + micro) * block
+        spans.append(pl.ds(pl.multiple_of(start, block), block))
+    return spans
 
 
 def diagonal_mask(rows, chunk, block, zy):
@@ -90,87 +114,69 @@
     return key_at <= zy * block + lax.rem(row_at, block)
 
 
-def attention_forward_kernel(has_prev, info_ref, q_ref, *refs):
-    prev_ref = refs[0] if has_prev else None
-    cur_ref, o_ref, log_ref = refs[-3:]
-    parts, block, _ = q_ref.shape
+def attention_forward_kernel(info_ref, q_ref, kv_ref, o_ref, log_ref):
+    parts, micros, block, _ = q_ref.shape
     rows = GROUP * block
-    mask = diagonal_mask(rows, cur_ref.shape[0] * block, block, info_ref[0])
-    spans = [block_span(arrival(info_ref, parts, part), block) for part in range(parts)]
+    mask = diagonal_mask(rows, kv_ref.shape[0] * block, block, info_ref[0])
     for part in range(parts):
         at = arrival(info_ref, parts, part)
-        queries = stacked_heads(q_ref, at)
-        pieces = [(prev_ref, slice(None))] if has_prev else []
-        pieces += [(cur_ref, spans[p]) for p in range(part + 1)]
-        scores = [dot_nt(queries, cached(ref, span, 0)) for ref, span in pieces]
-        if has_prev:
-            scores[0] = scores[0] + jnp.where(info_ref[1] > 0, 0.0, masked_score).astype(f32)
-        scores[-1] = jnp.where(mask, scores[-1], masked_score)
-        peak = functools.reduce(
-            jnp.maximum, [jnp.max(s, axis=-1, keepdims=True) for s in scores]
-        )
-        peak = peak * log2_scale
-        total = jnp.zeros((rows, 1), f32)
-        mixed = jnp.zeros((rows, HD), f32)
-        for s, (ref, span) in zip(scores, pieces):
-            probs = jnp.exp2(s * log2_scale - peak)
-            total = total + jnp.sum(probs, axis=-1, keepdims=True)
-            mixed = mixed + dot(probs.astype(bf), cached(ref, span, HD))
-        store_heads(o_ref, at, (mixed / total).astype(bf))
-        log_ref[at] = jnp.broadcast_to(peak + jnp.log2(total), (rows, HD))
-
-
-def attention_backward_kernel(has_prev, has_carry, info_ref, q_ref, do_ref, o_ref, log_ref, *refs):
-    refs = list(refs)
-    sum_ref = refs.pop()
-    carry_ref = refs.pop(0) if has_carry else None
-    prev_ref = refs.pop(0) if has_prev else None
-    cur_ref, dq_ref, dcur_ref = refs[:3]
-    dprev_ref = refs[3] if has_prev else None
-    sum_ref[...] = carry_ref[...] if has_carry else jnp.zeros(sum_ref.shape, f32)
-    if has_prev:
-        dprev_ref[...] = jnp.zeros(dprev_ref.shape, f32)
-    parts, block, _ = q_ref.shape
-    ring = cur_ref.shape[0]
+        for micro in range(micros):
+            queries = stacked_heads(q_ref, at, micro)
+            spans = key_spans(info_ref, parts, micros, block, part, micro)
+            scores = [dot_nt(queries, cached(kv_ref, span, 0)) for span in spans]
+            scores[-1] = jnp.where(mask, scores[-1], masked_score)
+            peak = functools.reduce(
+                jnp.maximum, [jnp.max(s, axis=-1, keepdims=True) for s in scores]
+            )
+            peak = peak * log2_scale
+            total = jnp.zeros((rows, 1), f32)
+            mixed = jnp.zeros((rows, HD), f32)
+            for s, span in zip(scores, spans):
+                probs = jnp.exp2(s * log2_scale - peak)
+                total = total + jnp.sum(probs, axis=-1, keepdims=True)
+                mixed = mixed + dot(probs.astype(bf), cached(kv_ref, span, HD))
+            store_heads(o_ref, at, micro, (mixed / total).astype(bf))
+            log_ref[at, micro] = jnp.broadcast_to(peak + jnp.log2(total), (rows, HD))
+
+
+def attention_backward_kernel(
+    info_ref, q_ref, do_ref, o_ref, log_ref, kv_ref, dq_ref, dkv_ref, sum_ref
+):
+    parts, micros, block, _ = q_ref.shape
+    ring = kv_ref.shape[0]
     rows = GROUP * block
     mask = diagonal_mask(rows, ring * block, block, info_ref[0])
-    spans = [block_span(arrival(info_ref, parts, part), block) for part in range(parts)]
+    sum_ref[...] = jnp.zeros(sum_ref.shape, f32)
     for part in range(parts):
         at = arrival(info_ref, parts, part)
-        queries = stacked_heads(q_ref, at)
-        out_grad = stacked_heads(do_ref, at)
-        out = stacked_heads(o_ref, at)
-        inner = jnp.sum(out_grad.astype(f32) * out.astype(f32), axis=-1, keepdims=True)
-        log_total = log_ref[at][:, :1]
-        query_grad = jnp.zeros((rows, HD), f32)
-        pieces = []
-        if has_prev:
-            log_prev = log_total + jnp.where(info_ref[1] > 0, 0.0, -masked_score).astype(f32)
-            pieces = [
-                (prev_ref, dprev_ref, slice(p * block, (p + 1) * block), log_prev, False)
-                for p in range(parts)
-            ]
-        pieces += [(cur_ref, sum_ref, spans[p], log_total, p == part) for p in range(part + 1)]
-        for ref, grad_ref, span, log_row, on_diagonal in pieces:
-            keys = cached(ref, span, 0)
-            probs = jnp.exp2(dot_nt(queries, keys) * log2_scale - log_row)
-            if on_diagonal:
-                probs = jnp.where(mask, probs, 0.0)
-            probs_grad = dot_nt(out_grad, cached(ref, span, HD))
-            score_grad = (probs * (probs_grad - inner)).astype(bf)
-            query_grad = query_grad + dot(score_grad, keys)
-            key_grad = dot_tn(score_grad, queries) * scaling
-            value_grad = dot_tn(probs.astype(bf), out_grad)
-            grad_ref[:, span, :HD] += key_grad.reshape(ring, block, HD)
-            grad_ref[:, span, HD:] += value_grad.reshape(ring, block, HD)
-        store_heads(dq_ref, at, (query_grad * scaling).astype(bf))
-    dcur_ref[...] = sum_ref[...].astype(bf)
+        for micro in range(micros):
+            queries = stacked_heads(q_ref, at, micro)
+            out_grad = stacked_heads(do_ref, at, micro)
+            out = stacked_heads(o_ref, at, micro)
+            inner = jnp.sum(out_grad.astype(f32) * out.astype(f32), axis=-1, keepdims=True)
+            log_total = log_ref[at, micro][:, :1]
+            query_grad = jnp.zeros((rows, HD), f32)
+            spans = key_spans(info_ref, parts, micros, block, part, micro)
+            for i, span in enumerate(spans):
+                keys = cached(kv_ref, span, 0)
+                probs = jnp.exp2(dot_nt(queries, keys) * log2_scale - log_total)
+                if i == len(spans) - 1:
+                    probs = jnp.where(mask, probs, 0.0)
+                probs_grad = dot_nt(out_grad, cached(kv_ref, span, HD))
+                score_grad = (probs * (probs_grad - inner)).astype(bf)
+                query_grad = query_grad + dot(score_grad, keys)
+                key_grad = dot_tn(score_grad, queries) * scaling
+                value_grad = dot_tn(probs.astype(bf), out_grad)
+                sum_ref[:, span, :HD] += key_grad.reshape(ring, block, HD)
+                sum_ref[:, span, HD:] += value_grad.reshape(ring, block, HD)
+            store_heads(dq_ref, at, micro, (query_grad * scaling).astype(bf))
+    dkv_ref[...] = sum_ref[...].astype(bf)
 
 
 def attention_call(kernel, factor, out_shape, scratch, info, queries, *rest):
-    parts, block, _ = queries.shape
-    rows = parts * GROUP * block
-    keys = sum(ref.shape[0] * ref.shape[1] for ref in rest if ref.shape == rest[-1].shape)
+    parts, micros, block, _ = queries.shape
+    rows = parts * micros * GROUP * block
+    keys = rest[-1].shape[0] * rest[-1].shape[1]
     in_vmem = pl.BlockSpec(memory_space=pltpu.VMEM)
     return pl.pallas_call(
         kernel,
@@ -187,26 +193,20 @@
     )(info, queries, *rest)
 
 
-def attention_forward(info, qkv, prev, cur):
-    parts, block, _ = qkv.shape
+def attention_forward(info, qkv, cache):
+    parts, micros, block, _ = qkv.shape
     shapes = (
-        jax.ShapeDtypeStruct((parts, block, GROUP * HD), bf),
-        jax.ShapeDtypeStruct((parts, GROUP * block, HD), f32),
-    )
-    caches = (cur,) if prev is None else (prev, cur)
-    kernel = functools.partial(attention_forward_kernel, prev is not None)
-    return attention_call(kernel, 2, shapes, [], info, qkv, *caches)
-
-
-def attention_backward(info, qkv, out_grad, out, logs, carry, prev, cur):
-    shapes = (jax.ShapeDtypeStruct(out.shape, bf), jax.ShapeDtypeStruct(cur.shape, bf))
-    if prev is not None:
-        shapes += (jax.ShapeDtypeStruct(cur.shape, f32),)
-    extra = tuple(value for value in (carry, prev) if value is not None)
-    kernel = functools.partial(attention_backward_kernel, prev is not None, carry is not None)
-    scratch = [pltpu.VMEM(cur.shape, f32)]
+        jax.ShapeDtypeStruct((parts, micros, block, GROUP * HD), bf),
+        jax.ShapeDtypeStruct((parts, micros, GROUP * block, HD), f32),
+    )
+    return attention_call(attention_forward_kernel, 2, shapes, [], info, qkv, cache)
+
+
+def attention_backward(info, qkv, out_grad, out, logs, cache):
+    shapes = (jax.ShapeDtypeStruct(out.shape, bf), jax.ShapeDtypeStruct(cache.shape, bf))
+    scratch = [pltpu.VMEM(cache.shape, f32)]
     return attention_call(
-        kernel, 5, shapes, scratch, info, qkv, out_grad, out, logs, *extra, cur
+        attention_backward_kernel, 5, shapes, scratch, info, qkv, out_grad, out, logs, cache
     )
 
 
@@ -229,6 +229,7 @@
     expert_down,
 ):
     micros, block, width = inputs.shape[1:]
+    tokens = micros * block
     shards = lax.axis_size("shard")
     section = lax.axis_index("section")
     core = lax.axis_index("dp")
@@ -237,7 +238,8 @@
     ring = shards // heads
     local_experts = expert_gate.shape[1]
     experts = local_experts * shards
-    slots = experts * CAP
+    room = micros * CAP
+    slots = experts * room
     rows_per = w_query.shape[1]
     half_rows = rows_per // 2
     group_width = GROUP * HD
@@ -338,23 +340,21 @@
     expert_g, expert_u, expert_d = expert_gate[0], expert_up[0], expert_down[0]
     slot_of = jnp.arange(slots, dtype=jnp.int32)
     expert_of = jnp.arange(experts, dtype=jnp.int32)
-    row_of = jnp.arange(block, dtype=jnp.int32)
-    spread = (expert_of[:, None] == slot_of[None, :] // CAP).astype(bf)
+    token_of = jnp.arange(tokens, dtype=jnp.int32)
+    micro_of = token_of // block
+    spread = (expert_of[:, None] == slot_of[None, :] // room).astype(bf)
     router_slots = dot(router_w, spread).astype(bf)
-    earlier = (row_of[:, None] > row_of[None, :]).astype(bf)
-
-    def slot_table(route_rows):
-        named = jnp.any(route_rows[:, :, None] == expert_of[None, None, :], axis=1).astype(bf)
-        slot_ids = dot(earlier, named).astype(bf)
-        return (dot(named, spread) > 0.5) & (
-            dot(slot_ids, spread).astype(jnp.int32) == (slot_of % CAP)[None, :]
-        )
-
-    here = [position % ring, jnp.ones_like(position), position // ring]
-    info_all = jnp.stack(here).astype(jnp.int32)
-    info = jnp.stack([here[0], is_first.astype(here[0].dtype), here[2]]).astype(jnp.int32)
-
-    def gate_values(normed_two, table):
+    local_routes = routes[0, 0].reshape(tokens, TOPK)
+    named = jnp.any(local_routes[:, :, None] == expert_of[None, None, :], axis=1).astype(bf)
+    earlier = (token_of[:, None] > token_of[None, :]) & (micro_of[:, None] == micro_of[None, :])
+    slot_ids = dot(earlier.astype(bf), named) + (CAP * micro_of)[:, None].astype(f32)
+    table = (dot(named, spread) > 0.5) & (
+        dot(slot_ids.astype(bf), spread).astype(jnp.int32) == (slot_of % room)[None, :]
+    )
+    pick = table.astype(bf)
+    info = jnp.stack([position % ring, position // ring]).astype(jnp.int32)
+
+    def gate_values(normed_two):
         logits = jnp.where(table, dot(normed_two, router_slots), masked_score)
         weights = jnp.exp(logits - jnp.max(logits, axis=-1, keepdims=True))
         weights = jnp.where(table, weights, 0.0)
@@ -366,14 +366,14 @@
 
     def to_experts(rows):
         return (
-            exchange(rows.reshape(shards, local_experts, CAP, width))
+            exchange(rows.reshape(shards, local_experts, room, width))
             .transpose(1, 0, 2, 3)
-            .reshape(local_experts, shards * CAP, width)
+            .reshape(local_experts, shards * room, width)
         )
 
     def from_experts(rows):
         return exchange(
-            rows.reshape(local_experts, shards, CAP, width).transpose(1, 0, 2, 3)
+            rows.reshape(local_experts, shards, room, width).transpose(1, 0, 2, 3)
         ).reshape(slots, width)
 
     def moved(p, steps):
@@ -395,17 +395,12 @@
         )
 
     def sum_over_x(rows):
-        parts = rows.reshape(heads, block, width)
+        parts = rows.reshape(heads, tokens, width)
         away = [shift_x(parts[k].astype(bf), -k).astype(f32) for k in range(1, heads)]
         return sum(away, parts[0])
 
     def ring_rows(rows):
         return jnp.concatenate([rows] + [shift_x(rows, k) for k in range(1, heads)], axis=0)
-
-    ring_inputs = [
-        jnp.stack([inputs[0, m]] + [shift_x(inputs[0, m], k) for k in range(1, heads)])
-        for m in range(micros)
-    ]
 
     def shared_weights(gathered):
         gate_up = gathered[:, :, : 2 * shared_width]
@@ -415,31 +410,23 @@
             ordered(down, twin(down), 1).reshape(shards * down_rows, width),
         )
 
-    def forward(moment, received, previous, shared_pair):
-        first_micro = min(moment, micros - 1)
-        second_micro = max(moment - 1, 0)
-        ring_b = jnp.where(is_first, ring_inputs[first_micro], received)
+    def forward(ring_b, shared_pair):
         layer_b = ring_b[0]
-        table = slot_table(
-            jnp.where(is_first, routes[0, 0, first_micro], routes[0, 0, second_micro])
-        )
-        pick = table.astype(bf)
         layer_in = layer_b.astype(f32)
-        ring_in = ring_b.reshape(heads * block, width).astype(f32)
+        ring_in = ring_b.reshape(heads * tokens, width).astype(f32)
         ring_one = (ring_in * inverse_rms(ring_in) * gain_one).astype(bf)
         qkv = dot(ring_one, qkv_w).astype(bf)
         cache = exchange(copies(qkv[:, group_width:], ring), zy_groups)
-        qkv = qkv.reshape(heads, block, part_width)
-        attn_info = info if moment == 1 else info_all
-        attended, logs = attention_forward(attn_info, qkv, previous, cache)
-        attended_rows = attended.reshape(heads * block, group_width)
+        qkv = qkv.reshape(heads, micros, block, part_width)
+        attended, logs = attention_forward(info, qkv, cache)
+        attended_rows = attended.reshape(heads * tokens, group_width)
         hidden = layer_in + sum_over_x(dot(attended_rows, output_w))
         if shared_pair is None:
             arrived, hidden = lax.optimization_barrier((gathered, hidden))
             shared_pair = shared_weights(arrived)
         gate_up_w, down_w = shared_pair
         normed_two = (hidden * inverse_rms(hidden) * gain_two).astype(bf)
-        gates = gate_values(normed_two, table)
+        gates = gate_values(normed_two)
         expert_in = to_experts(dot_tn(pick, normed_two).astype(bf))
         gate_pre = wide_einsum("erd,edf->erf", expert_in, expert_g)
         up_pre = wide_einsum("erd,edf->erf", expert_in, expert_u)
@@ -453,12 +440,9 @@
         output_b = (beside + routed).astype(bf)
         return dict(
             layer_b=layer_b,
-            pick=pick,
             ring_one=ring_one,
             qkv=qkv,
             cache=cache,
-            previous=previous,
-            info=attn_info,
             attended=attended,
             logs=logs,
             hidden=hidden,
@@ -504,7 +488,7 @@
         picked_b = picked_grad.astype(bf)
         normed_two_grad = normed_two_grad + dot_nt(picked_b, router_slots)
         normed_two_grad = lax.optimization_barrier(normed_two_grad)
-        normed_two_grad = normed_two_grad + dot(kept["pick"], returned_grad)
+        normed_two_grad = normed_two_grad + dot(pick, returned_grad)
         logit_grad = dot_nt(picked_b, spread).astype(bf)
         hidden_norm_grad, gain_two_grad = norm_back(hidden, gain_two, normed_two_grad)
         return dict(
@@ -519,21 +503,18 @@
             gain_two_grad=gain_two_grad,
         )
 
-    def attention_back(kept, grads, carried):
+    def attention_back(kept, grads):
         ring_hidden = ring_rows(grads["hidden_grad"].astype(bf))
         out_grad = dot_nt(ring_hidden, output_w).astype(bf)
         results = attention_backward(
-            kept["info"],
+            info,
             kept["qkv"],
-            out_grad.reshape(heads, block, group_width),
+            out_grad.reshape(heads, micros, block, group_width),
             kept["attended"],
             kept["logs"],
-            carried,
-            kept["previous"],
             kept["cache"],
         )
-        carried = results[2] if len(results) > 2 else None
-        query_grad = results[0].reshape(heads * block, group_width)
+        query_grad = results[0].reshape(heads * tokens, group_width)
         query_part = lax.optimization_barrier(dot_nt(query_grad, qkv_w[:, :group_width]))
         pair_grad = jnp.sum(exchange(results[1], zy_groups).astype(f32), axis=0).astype(bf)
         qkv_grad = jnp.concatenate([query_grad, pair_grad], axis=1)
@@ -541,49 +522,33 @@
         in_norm_grad, gain_one_grad = norm_back(
             kept["layer_b"].astype(f32), gain_one, normed_one_grad
         )
-        grads = dict(
+        return dict(
             grads,
             ring_hidden=ring_hidden,
             qkv_grad=qkv_grad,
             gain_one_grad=gain_one_grad,
             layer_grad=(grads["hidden_grad"] + in_norm_grad).astype(bf),
         )
-        return grads, carried
-
-    nothing = jnp.zeros((block, width), bf)
-    saved = []
-    received, previous, shared_pair = jnp.zeros((heads, block, width), bf), None, None
-    for moment in range(micros + 1):
-        kept = forward(moment, received, previous, shared_pair)
-        shared_pair = kept["shared_pair"]
-        saved.append(kept)
-        previous = kept["cache"]
-        if moment < micros:
-            received = next_ring(kept["output_b"])
-    backs = [None] * (micros + 1)
-    received, carried = nothing, None
-    for source in range(micros, -1, -1):
-        own = cotangent[0, source - 1] if source > 0 else nothing
-        upstream_b = jnp.where(is_first, received, own)
-        grads = ffn_backward(saved[source], upstream_b)
-        backs[source], carried = attention_back(saved[source], grads, carried)
-        if source > 0:
-            received = lax.ppermute(backs[source]["layer_grad"], "section", [(1, 0)])
-
-    def live(name, store, axis):
-        ends = jnp.where(is_first, store[0][name], store[micros][name])
-        return jnp.concatenate([ends, store[1][name]], axis=axis)
-
-    def kept_rows(name, axis=0):
-        return live(name, saved, axis)
-
-    def back_rows(name, axis=0):
-        return live(name, backs, axis)
+
+    own_rows = inputs[0].reshape(tokens, width)
+    ring_inputs = jnp.stack([own_rows] + [shift_x(own_rows, k) for k in range(1, heads)])
+    first = forward(ring_inputs, None)
+    second = forward(next_ring(first["output_b"]), first["shared_pair"])
+    second_back = ffn_backward(second, cotangent[0].reshape(tokens, width))
+    second_back = attention_back(second, second_back)
+    received = lax.ppermute(second_back["layer_grad"], "section", [(1, 0)])
+    first_back = attention_back(first, ffn_backward(first, received))
+
+    def live(name, stores):
+        return jnp.where(is_first, stores[0][name], stores[1][name])
+
+    kept = {name: live(name, (first, second)) for name in KEPT}
+    back = {name: live(name, (first_back, second_back)) for name in BACK}
 
     expert_parts = [
-        wide_einsum("erd,erf->edf", kept_rows("expert_in", 1), back_rows("gate_pre_grad", 1)),
-        wide_einsum("erd,erf->edf", kept_rows("expert_in", 1), back_rows("up_pre_grad", 1)),
-        wide_einsum("erf,erd->efd", kept_rows("activated", 1), back_rows("expert_grad", 1)),
+        wide_einsum("erd,erf->edf", kept["expert_in"], back["gate_pre_grad"]),
+        wide_einsum("erd,erf->edf", kept["expert_in"], back["up_pre_grad"]),
+        wide_einsum("erf,erd->efd", kept["activated"], back["expert_grad"]),
     ]
     expert_parts = [part.astype(bf) for part in expert_parts]
     expert_others = [twin(part) for part in expert_parts]
@@ -595,11 +560,11 @@
         own, other = mine_of(low_half, high_half), mine_of(high_half, low_half)
         return jnp.concatenate([own, twin(other)], axis=0)
 
-    normed_two = kept_rows("normed_two")
+    normed_two = kept["normed_two"]
     grad_gate_up = dot_tn(
-        both(normed_two), both_halves(back_rows("shared_gate_grad"), back_rows("shared_up_grad"))
-    )
-    grad_down = dot_tn(both(kept_rows("shared_act")), both_halves(*halves(back_rows("upstream_b"))))
+        both(normed_two), both_halves(back["shared_gate_grad"], back["shared_up_grad"])
+    )
+    grad_down = dot_tn(both(kept["shared_act"]), both_halves(*halves(back["upstream_b"])))
 
 
     def shift_z(value, steps):
@@ -626,19 +591,18 @@
         return total.astype(held_as)
 
     grad_out = dot_tn(
-        kept_rows("attended").reshape(micros * heads * block, group_width),
-        back_rows("ring_hidden"),
+        kept["attended"].reshape(heads * tokens, group_width),
+        back["ring_hidden"],
     )
     grad_gate_up, grad_down, grad_out, last_grad, *expert_others = lax.optimization_barrier(
         (
             grad_gate_up.astype(bf),
             grad_down.astype(bf),
             grad_out.astype(bf),
-            backs[0]["layer_grad"],
+            first_back["layer_grad"],
             *expert_others,
         )
     )
-    backs[0]["layer_grad"] = last_grad
     expert_grads = [
         part.astype(f32) + other.astype(f32) for part, other in zip(expert_parts, expert_others)
     ]
@@ -650,11 +614,9 @@
     share_out = jnp.sum(
         exchange(grad_out.reshape(ring, rows_per, width), zy_groups).astype(f32), axis=0
     )
-    grad_qkv = dot_tn(kept_rows("ring_one"), back_rows("qkv_grad"))
-    grad_router = dot_tn(normed_two, back_rows("logit_grad"))
-    gain_sums = jnp.stack(
-        [sum(grads[name] for grads in backs) for name in ("gain_one_grad", "gain_two_grad")]
-    )
+    grad_qkv = dot_tn(kept["ring_one"], back["qkv_grad"])
+    grad_router = dot_tn(normed_two, back["logit_grad"])
+    gain_sums = jnp.stack([back["gain_one_grad"], back["gain_two_grad"]])
     grad_tail = jnp.concatenate(
         [grad_router, gain_sums.T, jnp.zeros((width, 128 - experts - 2), f32)], axis=1
     )
@@ -675,14 +637,11 @@
     other_gate_up = twin(share_gate_up)
     down_total = ordered(share_down, twin(share_down), 1)
 
-    def by_micro(store, name):
-        return jnp.stack(
-            [jnp.where(is_first, store[m][name], store[m + 1][name]) for m in range(micros)]
-        )[None, None]
-
+    token_shape = (1, 1, micros, block, width)
+    layer_grad = jnp.where(is_first, last_grad, second_back["layer_grad"])
     return (
-        by_micro(saved, "output_b"),
-        by_micro(backs, "layer_grad"),
+        jnp.where(is_first, first["output_b"], second["output_b"]).reshape(token_shape),
+        layer_grad.reshape(token_shape),
         tail_total[:, experts][None],
         qkv_total[:, :, :group_width].reshape(1, rows_per, head_width),
         qkv_total[:, :, group_width : group_width + HD].reshape(1, rows_per, key_width),

time: 1070 us -> 1110 us (1.037)
  waiting for transfers between devices: 337 us -> 463 us
  starting transfers between devices: 244 us -> 187 us
  matrix products: 179 us -> 157 us
    all_to_all x20 -> x14, waiting for transfers between devices: 178 us -> 283 us  [exchange(): lax.all_to_all(value, 'shard', split_axis=0, concat_axis=0, tiled=True, a...]
    ppermute x39 -> x27, waiting for transfers between devices: 76.9 us -> 103 us  [shift_x(): lax.ppermute(value, 'shard', [(p, moved(p, steps)) for p in range(shards)])]
    all_to_all x20 -> x14, starting transfers between devices: 134 us -> 112 us  [exchange(): lax.all_to_all(value, 'shard', split_axis=0, concat_axis=0, tiled=True, a...]
    dot_general x24 -> x15, matrix products: 54 us -> 34.5 us  [dot_nt(): lax.dot_general(left_side, right_side, (((1,), (1,)), ((), ())), preferre...]
    ppermute x39 -> x27, starting transfers between devices: 43 us -> 25.7 us  [shift_x(): lax.ppermute(value, 'shard', [(p, moved(p, steps)) for p in range(shards)])]
    ppermute x3, waiting for transfers between devices: 16 us -> 0.01 us  [body(): lax.ppermute(out_rows, 'shard', [(p, p // ring * ring + (p % ring - 2 * k...]
    ppermute x8 -> x4, starting transfers between devices: 24.5 us -> 14.9 us  [next_ring(): lax.ppermute(value, ('section', 'shard'), [(p, shards + moved(p, steps))...]
    unnamed x568 -> x391, local copies, waits for them, and re-layouts: 35.1 us -> 27.5 us
  transfers between devices with their start and end apart: 98 -> 75, of which waited for: 54 -> 41; matrix products, arithmetic and copies ran while one was open for 28% -> 23% of each run, Pallas kernels for 2% -> 2%
where the time goes in v10:
time: 1110 us; the launch traced here: 1100 us
  waiting for transfers between devices  463 us (42%)
  starting transfers between devices  187 us (17%)
  matrix products  157 us (14%)
  other arithmetic  103 us (9%)
  local copies, waits for them, and re-layouts  91.2 us (8%)
  Pallas kernels  51.1 us (5%)
  blocking collectives  34 us (3%)
  between operations  17.1 us (2%)
    all_to_all x14, waiting for transfers between devices, exchange(): lax.all_to_all(value, 'shard', split_axis=0, concat_axis=0, tiled=True, a...  283 us
    all_to_all x14, starting transfers between devices, exchange(): lax.all_to_all(value, 'shard', split_axis=0, concat_axis=0, tiled=True, a...  112 us
    ppermute x27, waiting for transfers between devices, shift_x(): lax.ppermute(value, 'shard', [(p, moved(p, steps)) for p in range(shards)])  103 us
    pallas_call x4, Pallas kernels, attention_call(): pl.pallas_call(kernel, out_shape=out_shape, in_specs=[pl.BlockSpec(memory...  51.1 us
    dot_general x19, matrix products, dot(): return jnp.dot(left_side, right_side, preferred_element_type=f32)  50.9 us
    dot_general x15, matrix products, wide_einsum(): jnp.einsum(formula, left_side, right_side, preferred_element_type=f32)  43.9 us
    dot_general x15, matrix products, dot_nt(): lax.dot_general(left_side, right_side, (((1,), (1,)), ((), ())), preferre...  34.5 us
    all_to_all x1, blocking collectives, exchange(): lax.all_to_all(value, 'shard', split_axis=0, concat_axis=0, tiled=True, a...  34 us
  transfers between devices with their start and end apart: 75, of which 41 were waited for; matrix products, arithmetic and copies ran while one was open for 23% of the time, Pallas kernels for 2%

profile of v10, /device:TPU:1, one launch (start us, length us, event | category | flops | bytes accessed | tf_op | source)
XLA Modules:
  0.0 1104.5 jit_solution(15999143119649734543)
XLA Ops:
  45.7 9.9 collective-permute-done
  100.1 35.7 %all-to-all-done.1.kv_ref = bf16[8,512,256]{2,1,0:T(8,128)(2,1)} async-done(((bf16[8,512,256]{2,1,0:T(8,128)(2,1)}), bf16[8,512,256]{2,1,0:T(8,128)(2,1)}, u32[]{:S(2)}, u32[]{:S(2)}) %all-to-all-start.1) | async-done | bytes 2097184 | tf_op jit(solution)/shard_map/all_to_all | solution.py:256
  203.3 21.4 %all-to-all-done.2 = bf16[32,2,16,1536]{3,2,1,0:T(8,128)(2,1)} async-done(((bf16[32,2,16,1536]{3,2,1,0:T(8,128)(2,1)}), bf16[32,2,16,1536]{3,2,1,0:T(8,128)(2,1)}, u32[]{:S(2)}, u32[]{:S(2)}) %all-to-all-start.2) | async-done | bytes 3145760 | tf_op jit(solution)/shard_map/all_to_all | solution.py:256
  265.9 20.3 %all-to-all-done.3 = bf16[32,2,16,1536]{3,2,1,0:T(8,128)(2,1)} async-done(((bf16[32,2,16,1536]{3,2,1,0:T(8,128)(2,1)}), bf16[32,2,16,1536]{3,2,1,0:T(8,128)(2,1)}, u32[]{:S(2)}, u32[]{:S(2)}) %all-to-all-start.3) | async-done | bytes 3145760 | tf_op jit(solution)/shard_map/all_to_all | solution.py:256
  314.7 13.3 %collective-permute-done.15 = bf16[128,1536]{1,0:T(8,128)(2,1)} collective-permute-done((bf16[128,1536]{1,0:T(8,128)(2,1)}, bf16[128,1536]{1,0:T(8,128)(2,1)}, u32[]{:S(2)}, u32[]{:S(2)}) %collective-permute-start.15) | collective-permute-done | bytes 393248 | tf_op jit(solution)/shard_map/ppermute | solution.py:388
  339.4 34.0 %all_to_all.75.kv_ref = bf16[8,512,256]{2,1,0:T(8,128)(2,1)S(1)} all-to-all(bf16[8,512,256]{2,1,0:T(8,128)(2,1)S(1)} %broadcast_in_dim.43), channel_id=1, replica_groups={{0,1,2,3,4,5,6,7},{8,9,10,11,12,13,14,15},{16,17,18,19,20,21,22,23},{24..., dimensions={0} | all-to-all | bytes 4194304 | tf_op jit(solution)/shard_map/all_to_all | solution.py:256
  422.3 33.5 %all-to-all-done.5 = bf16[32,2,16,1536]{3,2,1,0:T(8,128)(2,1)} async-done(((bf16[32,2,16,1536]{3,2,1,0:T(8,128)(2,1)}), bf16[32,2,16,1536]{3,2,1,0:T(8,128)(2,1)}, u32[]{:S(2)}, u32[]{:S(2)}) %all-to-all-start.5) | async-done | bytes 3145760 | tf_op jit(solution)/shard_map/all_to_all | solution.py:256
  473.4 31.2 %all-to-all-done.7 = bf16[32,2,16,1536]{3,2,1,0:T(8,128)(2,1)} async-done(((bf16[32,2,16,1536]{3,2,1,0:T(8,128)(2,1)}), bf16[32,2,16,1536]{3,2,1,0:T(8,128)(2,1)}, u32[]{:S(2)}, u32[]{:S(2)}) %all-to-all-start.7) | async-done | bytes 3145760 | tf_op jit(solution)/shard_map/all_to_all | solution.py:256
  532.9 32.5 %all-to-all-done.6 = bf16[32,2,16,1536]{3,2,1,0:T(8,128)(2,1)} async-done(((bf16[32,2,16,1536]{3,2,1,0:T(8,128)(2,1)}), bf16[32,2,16,1536]{3,2,1,0:T(8,128)(2,1)}, u32[]{:S(2)}, u32[]{:S(2)}) %all-to-all-start.6) | async-done | bytes 3145760 | tf_op jit(solution)/shard_map/all_to_all | solution.py:256
  588.0 26.8 %all-to-all-done.8 = bf16[32,2,16,1536]{3,2,1,0:T(8,128)(2,1)} async-done(((bf16[32,2,16,1536]{3,2,1,0:T(8,128)(2,1)}), bf16[32,2,16,1536]{3,2,1,0:T(8,128)(2,1)}, u32[]{:S(2)}, u32[]{:S(2)}) %all-to-all-start.8) | async-done | bytes 3145760 | tf_op jit(solution)/shard_map/all_to_all | solution.py:256
  631.4 10.7 collective-permute-done.22
  643.2 17.7 %shard_map.273 = (bf16[4,2,64,384]{3,2,1,0:T(8,128)(2,1)S(1)}, bf16[8,512,256]{2,1,0:T(8,128)(2,1)S(1)}) custom-call(s32[2]{0:T(128)S(1)} %pad_add_fusion.info_ref, bf16[4,2,64,640]{3,2,1,0:T(8,128)(2,1)S(1)} %bitcast.311, bf16[4,2,64,384]{3,2,1,0:T(8,128)(2,1)S(1)} %bitcast.313, bf16[4,2,64,384]{3,2,1,0:T(8,128)(2,1)S(1)} %copy-done.6, ...), custom_call_target="tpu_custom_call" | custom-call | flops 4026531840 | bytes 3604480 | tf_op jit(solution)/shard_map/pallas_call | solution.py:181
  672.2 23.8 %all-to-all-done.9 = bf16[8,512,256]{2,1,0:T(8,128)(2,1)} async-done(((bf16[8,512,256]{2,1,0:T(8,128)(2,1)}), bf16[8,512,256]{2,1,0:T(8,128)(2,1)}, u32[]{:S(2)}, u32[]{:S(2)}) %all-to-all-start.9) | async-done | bytes 2097184 | tf_op jit(solution)/shard_map/all_to_all | solution.py:256
  704.4 15.8 %collective-permute-done.27 = bf16[128,1536]{1,0:T(8,128)(2,1)S(1)} collective-permute-done((bf16[128,1536]{1,0:T(8,128)(2,1)S(1)}, bf16[128,1536]{1,0:T(8,128)(2,1)S(1)}, u32[]{:S(2)}, u32[]{:S(2)}) %collective-permute-start.27) | collective-permute-done | bytes 393248 | tf_op jit(solution)/shard_map/ppermute | solution.py:383
  726.2 14.5 %collective-permute-done.28 = bf16[128,1536]{1,0:T(8,128)(2,1)S(1)} collective-permute-done((bf16[128,1536]{1,0:T(8,128)(2,1)S(1)}, bf16[128,1536]{1,0:T(8,128)(2,1)S(1)}, u32[]{:S(2)}, u32[]{:S(2)}) %collective-permute-start.28) | collective-permute-done | bytes 393248 | tf_op jit(solution)/shard_map/ppermute | solution.py:539
  744.7 9.6 all-to-all-start.10
  773.9 20.8 %all-to-all-done.10 = bf16[32,2,16,1536]{3,2,1,0:T(8,128)(2,1)} async-done(((bf16[32,2,16,1536]{3,2,1,0:T(8,128)(2,1)}), bf16[32,2,16,1536]{3,2,1,0:T(8,128)(2,1)}, u32[]{:S(2)}, u32[]{:S(2)}) %all-to-all-start.10) | async-done | bytes 3145760 | tf_op jit(solution)/shard_map/all_to_all | solution.py:256
  838.7 18.0 %all-to-all-done.11 = bf16[32,2,16,1536]{3,2,1,0:T(8,128)(2,1)} async-done(((bf16[32,2,16,1536]{3,2,1,0:T(8,128)(2,1)}), bf16[32,2,16,1536]{3,2,1,0:T(8,128)(2,1)}, u32[]{:S(2)}, u32[]{:S(2)}) %all-to-all-start.11) | async-done | bytes 3145760 | tf_op jit(solution)/shard_map/all_to_all | solution.py:256
  872.4 11.5 %collective-permute-done.32 = bf16[128,1536]{1,0:T(8,128)(2,1)S(1)} collective-permute-done((bf16[128,1536]{1,0:T(8,128)(2,1)S(1)}, bf16[128,1536]{1,0:T(8,128)(2,1)S(1)}, u32[]{:S(2)}, u32[]{:S(2)}) %collective-permute-start.32) | collective-permute-done | bytes 393248 | tf_op jit(solution)/shard_map/ppermute | solution.py:383
  884.9 18.5 %shard_map.274 = (bf16[4,2,64,384]{3,2,1,0:T(8,128)(2,1)S(1)}, bf16[8,512,256]{2,1,0:T(8,128)(2,1)S(1)}) custom-call(s32[2]{0:T(128)S(1)} %pad_add_fusion.info_ref, bf16[4,2,64,640]{3,2,1,0:T(8,128)(2,1)S(1)} %bitcast.309, bf16[4,2,64,384]{3,2,1,0:T(8,128)(2,1)S(1)} %bitcast.312, bf16[4,2,64,384]{3,2,1,0:T(8,128)(2,1)S(1)} %get-tuple-element.42.o_ref, ...), custom_call_target="tpu_custom_call" | custom-call | flops 4026531840 | bytes 3604480 | tf_op jit(solution)/shard_map/pallas_call | solution.py:181
  929.1 10.4 all-to-all-done.12
  968.0 11.1 %all-to-all-start.14 = ((bf16[8,48,1536]{2,1,0:T(8,128)(2,1)}), bf16[8,48,1536]{2,1,0:T(8,128)(2,1)}, u32[]{:S(2)}, u32[]{:S(2)}) async-start(bf16[8,48,1536]{2,1,0:T(8,128)(2,1)} %bitcast.383), calls=%async_computation.14 | async-start | bytes 2359296 | tf_op jit(solution)/shard_map/all_to_all | solution.py:256
  1025.1 11.1 %all-to-all-start.13 = ((bf16[32,48,768]{2,1,0:T(8,128)(2,1)}), bf16[32,48,768]{2,1,0:T(8,128)(2,1)}, u32[]{:S(2)}, u32[]{:S(2)}) async-start(bf16[32,48,768]{2,1,0:T(8,128)(2,1)} %maximum_maximum_fusion), calls=%async_computation.13 | async-start | bytes 4718592 | tf_op jit(solution)/shard_map/all_to_all | solution.py:256
  1046.3 17.8 %collective-permute-done.58 = bf16[32,768]{1,0:T(8,128)(2,1)S(1)} collective-permute-done((bf16[32,768]{1,0:T(8,128)(2,1)S(1)}, bf16[32,768]{1,0:T(8,128)(2,1)S(1)}, u32[]{:S(2)}, u32[]{:S(2)}) %collective-permute-start.58) | collective-permute-done | bytes 49184 | tf_op jit(solution)/shard_map/ppermute | solution.py:575
  (728 shorter events, 617.1 us)
Async XLA Ops:
  7.2 164.0 %all-gather.3.cloned.1.call-start = ((), (), s32[]{:S(2)}) async-start(), calls=%async_computation.15 | async-start | bytes 4866048 | tf_op jit(solution)/shard_map/all_gather | solution.py:315
  33.7 36.9 %all-to-all-start = ((bf16[32,24,768]{2,1,0:T(8,128)(2,1)}), bf16[32,24,768]{2,1,0:T(8,128)(2,1)}, u32[]{:S(2)}, u32[]{:S(2)}) async-start(bf16[32,24,768]{2,1,0:T(8,128)(2,1)} %bitcast.360), calls=%async_computation | async-start | bytes 2359296 | tf_op jit(solution)/shard_map/all_to_all | solution.py:256
  86.0 49.8 %all-to-all-start.1 = ((bf16[8,512,256]{2,1,0:T(8,128)(2,1)}), bf16[8,512,256]{2,1,0:T(8,128)(2,1)}, u32[]{:S(2)}, u32[]{:S(2)}) async-start(bf16[8,512,256]{2,1,0:T(8,128)(2,1)} %broadcast_in_dim.40), calls=%async_computation.1 | async-start | bytes 4194304 | tf_op jit(solution)/shard_map/all_to_all | solution.py:256
  178.6 46.1 %all-to-all-start.2 = ((bf16[32,2,16,1536]{3,2,1,0:T(8,128)(2,1)}), bf16[32,2,16,1536]{3,2,1,0:T(8,128)(2,1)}, u32[]{:S(2)}, u32[]{:S(2)}) async-start(bf16[32,2,16,1536]{3,2,1,0:T(8,128)(2,1)} %bitcast.345), calls=%async_computation.2 | async-start | bytes 6291456 | tf_op jit(solution)/shard_map/all_to_all | solution.py:256
  198.4 49.2 %collective-permute-start.13 = (bf16[32,16,1536]{2,1,0:T(8,128)(2,1)}, bf16[32,16,1536]{2,1,0:T(8,128)(2,1)}, u32[]{:S(2)}, u32[]{:S(2)}) collective-permute-start(bf16[32,16,1536]{2,1,0:T(8,128)(2,1)} %reshape.436), channel_id=1, source_target_pairs={{0,32},{32,0},{1,33},{33,1},{2,34},{34,2},{3,35},{35,3},{4,36},{36... | collective-permute-start | bytes 4718600 | tf_op jit(solution)/shard_map/ppermute | solution.py:264
  199.9 51.6 %collective-permute-start.12 = (bf16[32,24,2048]{2,1,0:T(8,128)(2,1)}, bf16[32,24,2048]{2,1,0:T(8,128)(2,1)}, u32[]{:S(2)}, u32[]{:S(2)}) collective-permute-start(bf16[32,24,2048]{2,1,0:T(8,128)(2,1)} %slice.203), channel_id=1, source_target_pairs={{0,32},{32,0},{1,33},{33,1},{2,34},{34,2},{3,35},{35,3},{4,36},{36... | collective-permute-start | bytes 9437192 | tf_op jit(solution)/shard_map/ppermute | solution.py:264
  236.9 49.3 %all-to-all-start.3 = ((bf16[32,2,16,1536]{3,2,1,0:T(8,128)(2,1)}), bf16[32,2,16,1536]{3,2,1,0:T(8,128)(2,1)}, u32[]{:S(2)}, u32[]{:S(2)}) async-start(bf16[32,2,16,1536]{3,2,1,0:T(8,128)(2,1)} %bitcast.343), calls=%async_computation.3 | async-start | bytes 6291456 | tf_op jit(solution)/shard_map/all_to_all | solution.py:256
  408.6 47.3 %all-to-all-start.5 = ((bf16[32,2,16,1536]{3,2,1,0:T(8,128)(2,1)}), bf16[32,2,16,1536]{3,2,1,0:T(8,128)(2,1)}, u32[]{:S(2)}, u32[]{:S(2)}) async-start(bf16[32,2,16,1536]{3,2,1,0:T(8,128)(2,1)} %bitcast.346), calls=%async_computation.5 | async-start | bytes 6291456 | tf_op jit(solution)/shard_map/all_to_all | solution.py:256
  455.8 48.8 %all-to-all-start.7 = ((bf16[32,2,16,1536]{3,2,1,0:T(8,128)(2,1)}), bf16[32,2,16,1536]{3,2,1,0:T(8,128)(2,1)}, u32[]{:S(2)}, u32[]{:S(2)}) async-start(bf16[32,2,16,1536]{3,2,1,0:T(8,128)(2,1)} %bitcast.349), calls=%async_computation.7 | async-start | bytes 6291456 | tf_op jit(solution)/shard_map/all_to_all | solution.py:256
  515.5 50.0 %all-to-all-start.6 = ((bf16[32,2,16,1536]{3,2,1,0:T(8,128)(2,1)}), bf16[32,2,16,1536]{3,2,1,0:T(8,128)(2,1)}, u32[]{:S(2)}, u32[]{:S(2)}) async-start(bf16[32,2,16,1536]{3,2,1,0:T(8,128)(2,1)} %bitcast.347), calls=%async_computation.6 | async-start | bytes 6291456 | tf_op jit(solution)/shard_map/all_to_all | solution.py:256
  565.5 49.3 %all-to-all-start.8 = ((bf16[32,2,16,1536]{3,2,1,0:T(8,128)(2,1)}), bf16[32,2,16,1536]{3,2,1,0:T(8,128)(2,1)}, u32[]{:S(2)}, u32[]{:S(2)}) async-start(bf16[32,2,16,1536]{3,2,1,0:T(8,128)(2,1)} %bitcast.344), calls=%async_computation.8 | async-start | bytes 6291456 | tf_op jit(solution)/shard_map/all_to_all | solution.py:256
  744.7 50.0 %all-to-all-start.10 = ((bf16[32,2,16,1536]{3,2,1,0:T(8,128)(2,1)}), bf16[32,2,16,1536]{3,2,1,0:T(8,128)(2,1)}, u32[]{:S(2)}, u32[]{:S(2)}) async-start(bf16[32,2,16,1536]{3,2,1,0:T(8,128)(2,1)} %bitcast.348), calls=%async_computation.10 | async-start | bytes 6291456 | tf_op jit(solution)/shard_map/all_to_all | solution.py:256
  766.1 98.2 %collective-permute-start.30 = (bf16[128,1024]{1,0:T(8,128)(2,1)}, bf16[128,1024]{1,0:T(8,128)(2,1)}, u32[]{:S(2)}, u32[]{:S(2)}) collective-permute-start(bf16[128,1024]{1,0:T(8,128)(2,1)} %get-tuple-element.78), channel_id=1, source_target_pairs={{0,32},{32,0},{1,33},{33,1},{2,34},{34,2},{3,35},{35,3},{4,36},{36... | collective-permute-start | bytes 786440 | tf_op jit(solution)/shard_map/ppermute | solution.py:264
  806.8 50.0 %all-to-all-start.11 = ((bf16[32,2,16,1536]{3,2,1,0:T(8,128)(2,1)}), bf16[32,2,16,1536]{3,2,1,0:T(8,128)(2,1)}, u32[]{:S(2)}, u32[]{:S(2)}) async-start(bf16[32,2,16,1536]{3,2,1,0:T(8,128)(2,1)} %bitcast.342), calls=%async_computation.11 | async-start | bytes 6291456 | tf_op jit(solution)/shard_map/all_to_all | solution.py:256
  822.4 45.0 %collective-permute-start.31 = (bf16[128,768]{1,0:T(8,128)(2,1)}, bf16[128,768]{1,0:T(8,128)(2,1)}, u32[]{:S(2)}, u32[]{:S(2)}) collective-permute-start(bf16[128,768]{1,0:T(8,128)(2,1)} %get-tuple-element.132), channel_id=1, source_target_pairs={{0,32},{32,0},{1,33},{33,1},{2,34},{34,2},{3,35},{35,3},{4,36},{36... | collective-permute-start | bytes 589832 | tf_op jit(solution)/shard_map/ppermute | solution.py:264
  864.3 80.1 %collective-permute-start.21 = (bf16[128,1536]{1,0:T(8,128)(2,1)}, bf16[128,1536]{1,0:T(8,128)(2,1)}, u32[]{:S(2)}, u32[]{:S(2)}) collective-permute-start(bf16[128,1536]{1,0:T(8,128)(2,1)} %get-tuple-element.84), channel_id=1, source_target_pairs={{0,32},{32,0},{1,33},{33,1},{2,34},{34,2},{3,35},{35,3},{4,36},{36... | collective-permute-start | bytes 1179656 | tf_op jit(solution)/shard_map/ppermute | solution.py:264
  867.3 77.2 %collective-permute-start.29 = (bf16[128,1024]{1,0:T(8,128)(2,1)}, bf16[128,1024]{1,0:T(8,128)(2,1)}, u32[]{:S(2)}, u32[]{:S(2)}) collective-permute-start(bf16[128,1024]{1,0:T(8,128)(2,1)} %broadcast_select_fusion.18), channel_id=1, source_target_pairs={{0,32},{32,0},{1,33},{33,1},{2,34},{34,2},{3,35},{35,3},{4,36},{36... | collective-permute-start | bytes 786440 | tf_op jit(solution)/shard_map/ppermute | solution.py:264
  917.5 49.6 %collective-permute-start.38 = (bf16[2,1536,512]{2,1,0:T(8,128)(2,1)}, bf16[2,1536,512]{2,1,0:T(8,128)(2,1)}, u32[]{:S(2)}, u32[]{:S(2)}) collective-permute-start(bf16[2,1536,512]{2,1,0:T(8,128)(2,1)} %convolution_convert_fusion.3), channel_id=1, source_target_pairs={{0,32},{32,0},{1,33},{33,1},{2,34},{34,2},{3,35},{35,3},{4,36},{36... | collective-permute-start | bytes 9437192 | tf_op jit(solution)/shard_map/ppermute | solution.py:264
  922.0 45.2 %collective-permute-start.39 = (bf16[2,1536,512]{2,1,0:T(8,128)(2,1)}, bf16[2,1536,512]{2,1,0:T(8,128)(2,1)}, u32[]{:S(2)}, u32[]{:S(2)}) collective-permute-start(bf16[2,1536,512]{2,1,0:T(8,128)(2,1)} %convolution_convert_fusion.2), channel_id=1, source_target_pairs={{0,32},{32,0},{1,33},{33,1},{2,34},{34,2},{3,35},{35,3},{4,36},{36... | collective-permute-start | bytes 9437192 | tf_op jit(solution)/shard_map/ppermute | solution.py:264
  925.6 41.6 %collective-permute-start.40 = (bf16[2,512,1536]{2,1,0:T(8,128)(2,1)}, bf16[2,512,1536]{2,1,0:T(8,128)(2,1)}, u32[]{:S(2)}, u32[]{:S(2)}) collective-permute-start(bf16[2,512,1536]{2,1,0:T(8,128)(2,1)} %convolution_convert_fusion.1), channel_id=1, source_target_pairs={{0,32},{32,0},{1,33},{33,1},{2,34},{34,2},{3,35},{35,3},{4,36},{36... | collective-permute-start | bytes 9437192 | tf_op jit(solution)/shard_map/ppermute | solution.py:264
  968.0 57.1 %all-to-all-start.14 = ((bf16[8,48,1536]{2,1,0:T(8,128)(2,1)}), bf16[8,48,1536]{2,1,0:T(8,128)(2,1)}, u32[]{:S(2)}, u32[]{:S(2)}) async-start(bf16[8,48,1536]{2,1,0:T(8,128)(2,1)} %bitcast.383), calls=%async_computation.14 | async-start | bytes 2359296 | tf_op jit(solution)/shard_map/all_to_all | solution.py:256
  982.3 57.8 %collective-permute-start.46 = (bf16[4,2,48,1024]{3,2,1,0:T(8,128)(2,1)}, bf16[4,2,48,1024]{3,2,1,0:T(8,128)(2,1)}, u32[]{:S(2)}, u32[]{:S(2)}) collective-permute-start(bf16[4,2,48,1024]{3,2,1,0:T(8,128)(2,1)} %get-tuple-element.96), channel_id=1, source_target_pairs={{0,24},{1,25},{2,26},{3,27},{4,28},{5,29},{6,30},{7,31},{8,0},{9,1... | collective-permute-start | bytes 2359304 | tf_op jit(solution)/shard_map/ppermute | solution.py:383
  983.8 56.3 %collective-permute-start.45 = (bf16[4,2,48,1024]{3,2,1,0:T(8,128)(2,1)}, bf16[4,2,48,1024]{3,2,1,0:T(8,128)(2,1)}, u32[]{:S(2)}, u32[]{:S(2)}) collective-permute-start(bf16[4,2,48,1024]{3,2,1,0:T(8,128)(2,1)} %get-tuple-element.97), channel_id=1, source_target_pairs={{0,16},{1,17},{2,18},{3,19},{4,20},{5,21},{6,22},{7,23},{8,24},{9,... | collective-permute-start | bytes 2359304 | tf_op jit(solution)/shard_map/ppermute | solution.py:383
  1025.1 60.1 %all-to-all-start.13 = ((bf16[32,48,768]{2,1,0:T(8,128)(2,1)}), bf16[32,48,768]{2,1,0:T(8,128)(2,1)}, u32[]{:S(2)}, u32[]{:S(2)}) async-start(bf16[32,48,768]{2,1,0:T(8,128)(2,1)} %maximum_maximum_fusion), calls=%async_computation.13 | async-start | bytes 4718592 | tf_op jit(solution)/shard_map/all_to_all | solution.py:256
  (243 other events, 3046.4 us)
Sparse Core Ops, SparseCore 0:
  24.9 116.3 all-gather.2

commit v11 on v9

--- a/solution.py
+++ b/solution.py
@@ -424,6 +424,10 @@
             jnp.where(is_first, routes[0, 0, first_micro], routes[0, 0, second_micro])
         )
         pick = table.astype(bf)
+        if moment == micros:
+            last_rows = cotangent[0, micros - 1]
+            last_rows = jnp.where(is_first, jnp.zeros_like(last_rows), last_rows)
+            cotangent_rows = dot_tn(pick, last_rows).astype(bf)
         layer_in = layer_b.astype(f32)
         ring_in = ring_b.reshape(heads * block, width).astype(f32)
         ring_one = (ring_in * inverse_rms(ring_in) * gain_one).astype(bf)
@@ -431,6 +435,10 @@
         cache = exchange(copies(qkv[:, group_width:], ring), zy_groups)
         qkv = qkv.reshape(heads, block, part_width)
         attn_info = info if moment == 1 else info_all
+        early = None
+        if moment == micros:
+            sent, cache = lax.optimization_barrier((cotangent_rows, cache))
+            early = to_experts(sent)
         attended, logs = attention_forward(attn_info, qkv, previous, cache)
         attended_rows = attended.reshape(heads * block, group_width)
         hidden = layer_in + sum_over_x(dot(attended_rows, output_w))
@@ -474,15 +482,16 @@
             shared_act=shared_act,
             output_b=output_b,
             shared_pair=shared_pair,
+            expert_grad=early,
         )
 
     def ffn_backward(kept, upstream_b):
         upstream = upstream_b.astype(f32)
         gates, hidden = kept["gates"], kept["hidden"]
         gate_up_w, down_w = kept["shared_pair"]
-        high, low = high_low(gates)
-        outgoing = dot_tn(high, upstream_b) + dot_tn(low, upstream_b)
-        expert_grad = to_experts(outgoing.astype(bf))
+        expert_grad = kept["expert_grad"]
+        if expert_grad is None:
+            expert_grad = to_experts(dot_tn(kept["pick"], upstream_b).astype(bf))
         act_silu, act_slope = silu_parts(kept["gate_pre"])
         act_grad = wide_einsum("erd,efd->erf", expert_grad, expert_d)
         gate_pre_grad = (act_grad * kept["up_pre"] * act_slope).astype(bf)
@@ -504,7 +513,8 @@
         picked_b = picked_grad.astype(bf)
         normed_two_grad = normed_two_grad + dot_nt(picked_b, router_slots)
         normed_two_grad = lax.optimization_barrier(normed_two_grad)
-        normed_two_grad = normed_two_grad + dot(kept["pick"], returned_grad)
+        high, low = high_low(gates)
+        normed_two_grad = normed_two_grad + (dot(high, returned_grad) + dot(low, returned_grad))
         logit_grad = dot_nt(picked_b, spread).astype(bf)
         hidden_norm_grad, gain_two_grad = norm_back(hidden, gain_two, normed_two_grad)
         return dict(
@@ -521,6 +531,9 @@
 
     def attention_back(kept, grads, carried):
         ring_hidden = ring_rows(grads["hidden_grad"].astype(bf))
+        if not sent_gates:
+            flat, ring_hidden = lax.optimization_barrier((gate_rows, ring_hidden))
+            sent_gates.append(exchange(flat))
         out_grad = dot_nt(ring_hidden, output_w).astype(bf)
         results = attention_backward(
             kept["info"],
@@ -560,6 +573,9 @@
         previous = kept["cache"]
         if moment < micros:
             received = next_ring(kept["output_b"])
+    gate_rows = jnp.stack([jnp.sum(kept["gates"], axis=0) for kept in saved])
+    gate_rows = gate_rows.reshape(micros + 1, shards, local_experts * CAP).transpose(1, 0, 2)
+    sent_gates = []
     backs = [None] * (micros + 1)
     received, carried = nothing, None
     for source in range(micros, -1, -1):
@@ -579,6 +595,14 @@
 
     def back_rows(name, axis=0):
         return live(name, backs, axis)
+
+    expert_gates = sent_gates[0].reshape(shards, micros + 1, local_experts, CAP)
+    expert_gates = expert_gates.transpose(1, 2, 0, 3).reshape(
+        micros + 1, local_experts, shards * CAP, 1
+    )
+    for source, grads in enumerate(backs):
+        for name in ("expert_grad", "gate_pre_grad", "up_pre_grad"):
+            grads[name] = (grads[name].astype(f32) * expert_gates[source]).astype(bf)
 
     expert_parts = [
         wide_einsum("erd,erf->edf", kept_rows("expert_in", 1), back_rows("gate_pre_grad", 1)),

time: 1070 us -> 1100 us (1.028)
  waiting for transfers between devices: 337 us -> 318 us
  matrix products: 179 us -> 193 us
  other arithmetic: 113 us -> 125 us
    all_to_all x20 -> x21, waiting for transfers between devices: 178 us -> 165 us  [exchange(): lax.all_to_all(value, 'shard', split_axis=0, concat_axis=0, tiled=True, a...]
    dot_general x31 -> x34, matrix products: 51.6 us -> 61.9 us  [dot(): return jnp.dot(left_side, right_side, preferred_element_type=f32)]
    all_to_all x20 -> x21, starting transfers between devices: 134 us -> 138 us  [exchange(): lax.all_to_all(value, 'shard', split_axis=0, concat_axis=0, tiled=True, a...]
    unnamed x568 -> x526, local copies, waits for them, and re-layouts: 35.1 us -> 33 us
    dot_general x14 -> x11, matrix products: 25.7 us -> 26.1 us  [dot_tn(): lax.dot_general(left_side, right_side, (((0,), (0,)), ((), ())), preferre...]
  transfers between devices with their start and end apart: 98 -> 99, of which waited for: 54 -> 50; matrix products, arithmetic and copies ran while one was open for 28% -> 31% of each run, Pallas kernels for 2% -> 2%
where the time goes in v11:
time: 1100 us; the launch traced here: 1080 us
  waiting for transfers between devices  318 us (29%)
  starting transfers between devices  249 us (23%)
  matrix products  193 us (18%)
  other arithmetic  125 us (11%)
  local copies, waits for them, and re-layouts  102 us (9%)
  Pallas kernels  48.4 us (4%)
  blocking collectives  28.9 us (3%)
  between operations  17.9 us (2%)
    all_to_all x21, waiting for transfers between devices, exchange(): lax.all_to_all(value, 'shard', split_axis=0, concat_axis=0, tiled=True, a...  165 us
    all_to_all x21, starting transfers between devices, exchange(): lax.all_to_all(value, 'shard', split_axis=0, concat_axis=0, tiled=True, a...  138 us
    ppermute x39, waiting for transfers between devices, shift_x(): lax.ppermute(value, 'shard', [(p, moved(p, steps)) for p in range(shards)])  74.5 us
    dot_general x34, matrix products, dot(): return jnp.dot(left_side, right_side, preferred_element_type=f32)  61.9 us
    dot_general x24, matrix products, dot_nt(): lax.dot_general(left_side, right_side, (((1,), (1,)), ((), ())), preferre...  54.3 us
    dot_general x21, matrix products, wide_einsum(): jnp.einsum(formula, left_side, right_side, preferred_element_type=f32)  50.4 us
    pallas_call x6, Pallas kernels, attention_call(): pl.pallas_call(kernel, out_shape=out_shape, in_specs=[pl.BlockSpec(memory...  48.4 us
    ppermute x39, starting transfers between devices, shift_x(): lax.ppermute(value, 'shard', [(p, moved(p, steps)) for p in range(shards)])  43.7 us
  transfers between devices with their start and end apart: 99, of which 50 were waited for; matrix products, arithmetic and copies ran while one was open for 31% of the time, Pallas kernels for 2%

profile of v11, /device:TPU:1, one launch (start us, length us, event | category | flops | bytes accessed | tf_op | source)
XLA Modules:
  0.0 1082.2 jit_solution(16985505689380096492)
XLA Ops:
  43.0 11.6 %collective-permute-done.6 = bf16[2,24,1536]{2,1,0:T(8,128)(2,1)} collective-permute-done((bf16[2,24,1536]{2,1,0:T(8,128)(2,1)S(1)}, bf16[2,24,1536]{2,1,0:T(8,128)(2,1)}, u32[]{:S(2)}, u32[]{:S(2)}) %collective-permute-start.6) | collective-permute-done | bytes 147488 | tf_op jit(solution)/shard_map/ppermute | solution.py:320
  80.0 15.9 %all-to-all-done.1.refs_0_.refs_1_ = bf16[8,256,256]{2,1,0:T(8,128)(2,1)} async-done(((bf16[8,256,256]{2,1,0:T(8,128)(2,1)}), bf16[8,256,256]{2,1,0:T(8,128)(2,1)}, u32[]{:S(2)}, u32[]{:S(2)}) %all-to-all-start.1) | async-done | bytes 1048608 | tf_op jit(solution)/shard_map/all_to_all | solution.py:254
  176.5 13.6 %all-to-all-done.3 = bf16[32,2,8,1536]{3,2,1,0:T(8,128)(2,1)} async-done(((bf16[32,2,8,1536]{3,2,1,0:T(8,128)(2,1)}), bf16[32,2,8,1536]{3,2,1,0:T(8,128)(2,1)}, u32[]{:S(2)}, u32[]{:S(2)}) %all-to-all-start.3) | async-done | bytes 1572896 | tf_op jit(solution)/shard_map/all_to_all | solution.py:254
  208.0 10.6 collective-permute-start.20
  244.8 15.7 %all-to-all-done.4.refs_1_.refs_0_.refs_2_ = bf16[8,256,256]{2,1,0:T(8,128)(2,1)} async-done(((bf16[8,256,256]{2,1,0:T(8,128)(2,1)}), bf16[8,256,256]{2,1,0:T(8,128)(2,1)}, u32[]{:S(2)}, u32[]{:S(2)}) %all-to-all-start.4) | async-done | bytes 1048608 | tf_op jit(solution)/shard_map/all_to_all | solution.py:254
  287.7 28.9 %all_to_all.110 = bf16[32,2,8,1536]{3,2,1,0:T(8,128)(2,1)S(1)} all-to-all(bf16[32,2,8,1536]{3,2,1,0:T(8,128)(2,1)S(1)} %bitcast.611), channel_id=1, replica_groups=mesh['section'=2,'dp'=2,'shard'=32] {'shard'}, dimensions={0} | all-to-all | bytes 3145728 | tf_op jit(solution)/shard_map/all_to_all | solution.py:254
  336.6 14.0 %all-to-all-done.6 = bf16[32,2,8,1536]{3,2,1,0:T(8,128)(2,1)} async-done(((bf16[32,2,8,1536]{3,2,1,0:T(8,128)(2,1)}), bf16[32,2,8,1536]{3,2,1,0:T(8,128)(2,1)}, u32[]{:S(2)}, u32[]{:S(2)}) %all-to-all-start.6) | async-done | bytes 1572896 | tf_op jit(solution)/shard_map/all_to_all | solution.py:254
  369.0 10.3 collective-permute-done.24
  400.7 9.5 all-to-all-done.7.refs_1_
  449.6 12.9 %all-to-all-done.8 = bf16[32,2,8,1536]{3,2,1,0:T(8,128)(2,1)} async-done(((bf16[32,2,8,1536]{3,2,1,0:T(8,128)(2,1)}), bf16[32,2,8,1536]{3,2,1,0:T(8,128)(2,1)}, u32[]{:S(2)}, u32[]{:S(2)}) %all-to-all-start.8) | async-done | bytes 1572896 | tf_op jit(solution)/shard_map/all_to_all | solution.py:254
  482.5 9.3 all-to-all-done.10
  509.1 12.9 %all-to-all-done.9 = bf16[32,2,8,1536]{3,2,1,0:T(8,128)(2,1)} async-done(((bf16[32,2,8,1536]{3,2,1,0:T(8,128)(2,1)}), bf16[32,2,8,1536]{3,2,1,0:T(8,128)(2,1)}, u32[]{:S(2)}, u32[]{:S(2)}) %all-to-all-start.9) | async-done | bytes 1572896 | tf_op jit(solution)/shard_map/all_to_all | solution.py:254
  541.6 10.8 all-to-all-done.11
  569.9 13.4 %shard_map.274 = (bf16[4,64,384]{2,1,0:T(8,128)(2,1)S(1)}, bf16[8,256,256]{2,1,0:T(8,128)(2,1)S(1)}, f32[8,256,256]{2,1,0:T(8,128)S(1)}) custom-call(s32[3]{0:T(128)S(1)} %add_add_fusion.info_ref, bf16[4,64,640]{2,1,0:T(8,128)(2,1)S(1)} %bitcast.564, bf16[4,64,384]{2,1,0:T(8,128)(2,1)S(1)} %bitcast.567, bf16[4,64,384]{2,1,0:T(8,128)(2,1)S(1)} %copy-done.5, ...), custom_call_target="tpu_custom_call" | custom-call | flops 2013265920 | bytes 3112960 | tf_op jit(solution)/shard_map/pallas_call | solution.py:175
  586.3 9.2 all-to-all-start.12
  602.7 9.4 all-to-all-done.12
  682.0 8.3 all-to-all-start.14
  703.1 11.4 %all-to-all-done.14 = bf16[32,2,8,1536]{3,2,1,0:T(8,128)(2,1)} async-done(((bf16[32,2,8,1536]{3,2,1,0:T(8,128)(2,1)}), bf16[32,2,8,1536]{3,2,1,0:T(8,128)(2,1)}, u32[]{:S(2)}, u32[]{:S(2)}) %all-to-all-start.14) | async-done | bytes 1572896 | tf_op jit(solution)/shard_map/all_to_all | solution.py:254
  731.7 13.4 %shard_map.275 = (bf16[4,64,384]{2,1,0:T(8,128)(2,1)S(1)}, bf16[8,256,256]{2,1,0:T(8,128)(2,1)S(1)}, f32[8,256,256]{2,1,0:T(8,128)S(1)}) custom-call(s32[3]{0:T(128)S(1)} %add_add_fusion.1.info_ref, bf16[4,64,640]{2,1,0:T(8,128)(2,1)S(1)} %bitcast.562, bf16[4,64,384]{2,1,0:T(8,128)(2,1)S(1)} %bitcast.565, bf16[4,64,384]{2,1,0:T(8,128)(2,1)S(1)} %get-tuple-element.59.o_ref, ...), custom_call_target="tpu_custom_call" | custom-call | flops 3019898880 | bytes 4423680 | tf_op jit(solution)/shard_map/pallas_call | solution.py:175
  800.5 8.3 all-to-all-start.16
  839.8 9.2 all-to-all-start.17
  909.9 9.5 all-to-all-done.18
  989.0 18.2 %collective-permute-done.72 = bf16[2,32,768]{2,1,0:T(8,128)(2,1)} collective-permute-done((bf16[2,32,768]{2,1,0:T(8,128)(2,1)S(1)}, bf16[2,32,768]{2,1,0:T(8,128)(2,1)}, u32[]{:S(2)}, u32[]{:S(2)}) %collective-permute-start.72) | collective-permute-done | bytes 98336 | tf_op jit(solution)/shard_map/ppermute | solution.py:383
  1026.9 18.4 %collective-permute-done.75 = bf16[32,768]{1,0:T(8,128)(2,1)S(1)} collective-permute-done((bf16[32,768]{1,0:T(8,128)(2,1)S(1)}, bf16[32,768]{1,0:T(8,128)(2,1)S(1)}, u32[]{:S(2)}, u32[]{:S(2)}) %collective-permute-start.75) | collective-permute-done | bytes 49184 | tf_op jit(solution)/shard_map/ppermute | solution.py:634
  (992 shorter events, 759.8 us)
Async XLA Ops:
  7.2 114.5 %all-gather.3.cloned.1.call-start = ((), (), s32[]{:S(2)}) async-start(), calls=%async_computation.22 | async-start | bytes 4866048 | tf_op jit(solution)/shard_map/all_gather | solution.py:313
  26.7 32.4 %all-to-all-start = ((bf16[32,24,768]{2,1,0:T(8,128)(2,1)}), bf16[32,24,768]{2,1,0:T(8,128)(2,1)}, u32[]{:S(2)}, u32[]{:S(2)}) async-start(bf16[32,24,768]{2,1,0:T(8,128)(2,1)} %bitcast.612), calls=%async_computation | async-start | bytes 2359296 | tf_op jit(solution)/shard_map/all_to_all | solution.py:254
  131.2 88.7 %collective-permute-start.16 = (bf16[64,1536]{1,0:T(8,128)(2,1)}, bf16[64,1536]{1,0:T(8,128)(2,1)}, u32[]{:S(2)}, u32[]{:S(2)}) collective-permute-start(bf16[64,1536]{1,0:T(8,128)(2,1)} %get-tuple-element.207), channel_id=1, source_target_pairs={{0,24},{1,25},{2,26},{3,27},{4,28},{5,29},{6,30},{7,31},{8,0},{9,1... | collective-permute-start | bytes 589832 | tf_op jit(solution)/shard_map/ppermute | solution.py:383
  133.7 87.5 %collective-permute-start.15 = (bf16[64,1536]{1,0:T(8,128)(2,1)}, bf16[64,1536]{1,0:T(8,128)(2,1)}, u32[]{:S(2)}, u32[]{:S(2)}) collective-permute-start(bf16[64,1536]{1,0:T(8,128)(2,1)} %get-tuple-element.207), channel_id=1, source_target_pairs={{0,16},{1,17},{2,18},{3,19},{4,20},{5,21},{6,22},{7,23},{8,24},{9,... | collective-permute-start | bytes 589832 | tf_op jit(solution)/shard_map/ppermute | solution.py:383
  134.2 88.6 %collective-permute-start.14 = (bf16[64,1536]{1,0:T(8,128)(2,1)}, bf16[64,1536]{1,0:T(8,128)(2,1)}, u32[]{:S(2)}, u32[]{:S(2)}) collective-permute-start(bf16[64,1536]{1,0:T(8,128)(2,1)} %get-tuple-element.207), channel_id=1, source_target_pairs={{0,8},{1,9},{2,10},{3,11},{4,12},{5,13},{6,14},{7,15},{8,16},{9,17... | collective-permute-start | bytes 589832 | tf_op jit(solution)/shard_map/ppermute | solution.py:383
  150.6 42.1 %collective-permute-start.12 = (bf16[32,24,2048]{2,1,0:T(8,128)(2,1)}, bf16[32,24,2048]{2,1,0:T(8,128)(2,1)}, u32[]{:S(2)}, u32[]{:S(2)}) collective-permute-start(bf16[32,24,2048]{2,1,0:T(8,128)(2,1)} %slice.310), channel_id=1, source_target_pairs={{0,32},{32,0},{1,33},{33,1},{2,34},{34,2},{3,35},{35,3},{4,36},{36... | collective-permute-start | bytes 9437192 | tf_op jit(solution)/shard_map/ppermute | solution.py:262
  491.8 30.2 %all-to-all-start.9 = ((bf16[32,2,8,1536]{3,2,1,0:T(8,128)(2,1)}), bf16[32,2,8,1536]{3,2,1,0:T(8,128)(2,1)}, u32[]{:S(2)}, u32[]{:S(2)}) async-start(bf16[32,2,8,1536]{3,2,1,0:T(8,128)(2,1)} %bitcast.608), calls=%async_computation.9 | async-start | bytes 3145728 | tf_op jit(solution)/shard_map/all_to_all | solution.py:254
  521.9 30.4 %all-to-all-start.11 = ((bf16[32,2,8,1536]{3,2,1,0:T(8,128)(2,1)}), bf16[32,2,8,1536]{3,2,1,0:T(8,128)(2,1)}, u32[]{:S(2)}, u32[]{:S(2)}) async-start(bf16[32,2,8,1536]{3,2,1,0:T(8,128)(2,1)} %bitcast.606), calls=%async_computation.11 | async-start | bytes 3145728 | tf_op jit(solution)/shard_map/all_to_all | solution.py:254
  600.1 248.8 %collective-permute-start.31 = (bf16[128,1536]{1,0:T(8,128)(2,1)}, bf16[128,1536]{1,0:T(8,128)(2,1)}, u32[]{:S(2)}, u32[]{:S(2)}) collective-permute-start(bf16[128,1536]{1,0:T(8,128)(2,1)} %pad_maximum_fusion.10), channel_id=1, source_target_pairs={{0,32},{32,0},{1,33},{33,1},{2,34},{34,2},{3,35},{35,3},{4,36},{36... | collective-permute-start | bytes 1179656 | tf_op jit(solution)/shard_map/ppermute | solution.py:262
  655.7 171.2 %collective-permute-start.47 = (bf16[128,1024]{1,0:T(8,128)(2,1)}, bf16[128,1024]{1,0:T(8,128)(2,1)}, u32[]{:S(2)}, u32[]{:S(2)}) collective-permute-start(bf16[128,1024]{1,0:T(8,128)(2,1)} %pad_maximum_fusion.14), channel_id=1, source_target_pairs={{0,32},{32,0},{1,33},{33,1},{2,34},{34,2},{3,35},{35,3},{4,36},{36... | collective-permute-start | bytes 786440 | tf_op jit(solution)/shard_map/ppermute | solution.py:262
  682.0 32.5 %all-to-all-start.14 = ((bf16[32,2,8,1536]{3,2,1,0:T(8,128)(2,1)}), bf16[32,2,8,1536]{3,2,1,0:T(8,128)(2,1)}, u32[]{:S(2)}, u32[]{:S(2)}) async-start(bf16[32,2,8,1536]{3,2,1,0:T(8,128)(2,1)} %bitcast.609), calls=%async_computation.14 | async-start | bytes 3145728 | tf_op jit(solution)/shard_map/all_to_all | solution.py:254
  839.8 33.0 %all-to-all-start.17 = ((bf16[32,2,8,1536]{3,2,1,0:T(8,128)(2,1)}), bf16[32,2,8,1536]{3,2,1,0:T(8,128)(2,1)}, u32[]{:S(2)}, u32[]{:S(2)}) async-start(bf16[32,2,8,1536]{3,2,1,0:T(8,128)(2,1)} %bitcast.603), calls=%async_computation.17 | async-start | bytes 3145728 | tf_op jit(solution)/shard_map/all_to_all | solution.py:254
  856.6 90.6 %collective-permute-start.55 = (bf16[2,1536,512]{2,1,0:T(8,128)(2,1)}, bf16[2,1536,512]{2,1,0:T(8,128)(2,1)}, u32[]{:S(2)}, u32[]{:S(2)}) collective-permute-start(bf16[2,1536,512]{2,1,0:T(8,128)(2,1)} %convolution_convert_fusion.3), channel_id=1, source_target_pairs={{0,32},{32,0},{1,33},{33,1},{2,34},{34,2},{3,35},{35,3},{4,36},{36... | collective-permute-start | bytes 9437192 | tf_op jit(solution)/shard_map/ppermute | solution.py:262
  861.0 86.3 %collective-permute-start.56 = (bf16[2,1536,512]{2,1,0:T(8,128)(2,1)}, bf16[2,1536,512]{2,1,0:T(8,128)(2,1)}, u32[]{:S(2)}, u32[]{:S(2)}) collective-permute-start(bf16[2,1536,512]{2,1,0:T(8,128)(2,1)} %convolution_convert_fusion.2), channel_id=1, source_target_pairs={{0,32},{32,0},{1,33},{33,1},{2,34},{34,2},{3,35},{35,3},{4,36},{36... | collective-permute-start | bytes 9437192 | tf_op jit(solution)/shard_map/ppermute | solution.py:262
  881.9 65.3 %collective-permute-start.57 = (bf16[2,512,1536]{2,1,0:T(8,128)(2,1)}, bf16[2,512,1536]{2,1,0:T(8,128)(2,1)}, u32[]{:S(2)}, u32[]{:S(2)}) collective-permute-start(bf16[2,512,1536]{2,1,0:T(8,128)(2,1)} %convolution_convert_fusion.1), channel_id=1, source_target_pairs={{0,32},{32,0},{1,33},{33,1},{2,34},{34,2},{3,35},{35,3},{4,36},{36... | collective-permute-start | bytes 9437192 | tf_op jit(solution)/shard_map/ppermute | solution.py:262
  947.3 61.2 %all-to-all-start.21 = ((bf16[8,48,1536]{2,1,0:T(8,128)(2,1)}), bf16[8,48,1536]{2,1,0:T(8,128)(2,1)}, u32[]{:S(2)}, u32[]{:S(2)}) async-start(bf16[8,48,1536]{2,1,0:T(8,128)(2,1)} %bitcast.621), calls=%async_computation.21 | async-start | bytes 2359296 | tf_op jit(solution)/shard_map/all_to_all | solution.py:254
  953.7 30.1 %collective-permute-start.69 = (bf16[4,2,32,768]{3,2,1,0:T(8,128)(2,1)S(1)}, bf16[4,2,32,768]{3,2,1,0:T(8,128)(2,1)S(1)}, u32[]{:S(2)}, u32[]{:S(2)}) collective-permute-start(bf16[4,2,32,768]{3,2,1,0:T(8,128)(2,1)S(1)} %get-tuple-element.158), channel_id=1, source_target_pairs={{0,2},{1,3},{2,4},{3,5},{4,6},{5,7},{6,0},{7,1},{8,10},{9,11},{10,... | collective-permute-start | bytes 1179656 | tf_op jit(solution)/shard_map/ppermute | solution.py:631
  961.5 58.7 %collective-permute-start.61 = (bf16[4,2,48,1024]{3,2,1,0:T(8,128)(2,1)}, bf16[4,2,48,1024]{3,2,1,0:T(8,128)(2,1)}, u32[]{:S(2)}, u32[]{:S(2)}) collective-permute-start(bf16[4,2,48,1024]{3,2,1,0:T(8,128)(2,1)} %get-tuple-element.145), channel_id=1, source_target_pairs={{0,8},{1,9},{2,10},{3,11},{4,12},{5,13},{6,14},{7,15},{8,16},{9,17... | collective-permute-start | bytes 2359304 | tf_op jit(solution)/shard_map/ppermute | solution.py:383
  961.5 58.7 %collective-permute-start.63 = (bf16[4,2,48,1024]{3,2,1,0:T(8,128)(2,1)}, bf16[4,2,48,1024]{3,2,1,0:T(8,128)(2,1)}, u32[]{:S(2)}, u32[]{:S(2)}) collective-permute-start(bf16[4,2,48,1024]{3,2,1,0:T(8,128)(2,1)} %get-tuple-element.146), channel_id=1, source_target_pairs={{0,24},{1,25},{2,26},{3,27},{4,28},{5,29},{6,30},{7,31},{8,0},{9,1... | collective-permute-start | bytes 2359304 | tf_op jit(solution)/shard_map/ppermute | solution.py:383
  983.7 36.4 %collective-permute-start.62 = (bf16[4,2,48,1024]{3,2,1,0:T(8,128)(2,1)}, bf16[4,2,48,1024]{3,2,1,0:T(8,128)(2,1)}, u32[]{:S(2)}, u32[]{:S(2)}) collective-permute-start(bf16[4,2,48,1024]{3,2,1,0:T(8,128)(2,1)} %get-tuple-element.147), channel_id=1, source_target_pairs={{0,16},{1,17},{2,18},{3,19},{4,20},{5,21},{6,22},{7,23},{8,24},{9,... | collective-permute-start | bytes 2359304 | tf_op jit(solution)/shard_map/ppermute | solution.py:383
  986.3 30.0 %collective-permute-start.74 = (bf16[2,32,768]{2,1,0:T(8,128)(2,1)}, bf16[2,32,768]{2,1,0:T(8,128)(2,1)}, u32[]{:S(2)}, u32[]{:S(2)}) collective-permute-start(bf16[2,32,768]{2,1,0:T(8,128)(2,1)} %get-tuple-element.199), channel_id=1, source_target_pairs={{0,24},{1,25},{2,26},{3,27},{4,28},{5,29},{6,30},{7,31},{8,0},{9,1... | collective-permute-start | bytes 294920 | tf_op jit(solution)/shard_map/ppermute | solution.py:383
  1008.5 56.4 %all-to-all-start.20 = ((bf16[32,48,768]{2,1,0:T(8,128)(2,1)}), bf16[32,48,768]{2,1,0:T(8,128)(2,1)}, u32[]{:S(2)}, u32[]{:S(2)}) async-start(bf16[32,48,768]{2,1,0:T(8,128)(2,1)} %maximum_maximum_fusion), calls=%async_computation.20 | async-start | bytes 4718592 | tf_op jit(solution)/shard_map/all_to_all | solution.py:254
  1022.7 32.1 %collective-permute-start.64 = (bf16[2,48,1024]{2,1,0:T(8,128)(2,1)S(1)}, bf16[2,48,1024]{2,1,0:T(8,128)(2,1)S(1)}, u32[]{:S(2)}, u32[]{:S(2)}) collective-permute-start(bf16[2,48,1024]{2,1,0:T(8,128)(2,1)S(1)} %get-tuple-element.163), channel_id=1, source_target_pairs={{0,2},{1,3},{2,4},{3,5},{4,6},{5,7},{6,0},{7,1},{8,10},{9,11},{10,... | collective-permute-start | bytes 589832 | tf_op jit(solution)/shard_map/ppermute | solution.py:631
  1023.9 30.8 %collective-permute-start.66 = (bf16[2,48,1024]{2,1,0:T(8,128)(2,1)S(1)}, bf16[2,48,1024]{2,1,0:T(8,128)(2,1)S(1)}, u32[]{:S(2)}, u32[]{:S(2)}) collective-permute-start(bf16[2,48,1024]{2,1,0:T(8,128)(2,1)S(1)} %get-tuple-element.164), channel_id=1, source_target_pairs={{0,6},{1,7},{2,0},{3,1},{4,2},{5,3},{6,4},{7,5},{8,14},{9,15},{10,... | collective-permute-start | bytes 589832 | tf_op jit(solution)/shard_map/ppermute | solution.py:631
  (333 other events, 2690.0 us)
Sparse Core Ops, SparseCore 0:
  16.9 104.7 all-gather.2

commit v12 on v9

--- a/solution.py
+++ b/solution.py
@@ -90,84 +90,115 @@
     return key_at <= zy * block + lax.rem(row_at, block)
 
 
+def all_heads(ref, ats):
+    return jnp.concatenate([stacked_heads(ref, at) for at in ats], axis=0)
+
+
+def added_from(total, first, value):
+    if first == 0:
+        return total + value
+    return jnp.concatenate([total[:first], total[first:] + value], axis=0)
+
+
+def masked_first(mask, value, fill):
+    count = mask.shape[0]
+    own = jnp.where(mask, value[:count], fill)
+    return own if value.shape[0] == count else jnp.concatenate([own, value[count:]], axis=0)
+
+
 def attention_forward_kernel(has_prev, info_ref, q_ref, *refs):
     prev_ref = refs[0] if has_prev else None
     cur_ref, o_ref, log_ref = refs[-3:]
     parts, block, _ = q_ref.shape
     rows = GROUP * block
     mask = diagonal_mask(rows, cur_ref.shape[0] * block, block, info_ref[0])
-    spans = [block_span(arrival(info_ref, parts, part), block) for part in range(parts)]
+    ats = [arrival(info_ref, parts, part) for part in range(parts)]
+    queries = all_heads(q_ref, ats)
+    pieces = []
+    if has_prev:
+        bias = jnp.where(info_ref[1] > 0, 0.0, masked_score).astype(f32)
+        everything = slice(None)
+        scores = dot_nt(queries, cached(prev_ref, everything, 0)) + bias
+        pieces.append((scores, prev_ref, everything, 0))
     for part in range(parts):
-        at = arrival(info_ref, parts, part)
-        queries = stacked_heads(q_ref, at)
-        pieces = [(prev_ref, slice(None))] if has_prev else []
-        pieces += [(cur_ref, spans[p]) for p in range(part + 1)]
-        scores = [dot_nt(queries, cached(ref, span, 0)) for ref, span in pieces]
-        if has_prev:
-            scores[0] = scores[0] + jnp.where(info_ref[1] > 0, 0.0, masked_score).astype(f32)
-        scores[-1] = jnp.where(mask, scores[-1], masked_score)
-        peak = functools.reduce(
-            jnp.maximum, [jnp.max(s, axis=-1, keepdims=True) for s in scores]
-        )
-        peak = peak * log2_scale
-        total = jnp.zeros((rows, 1), f32)
-        mixed = jnp.zeros((rows, HD), f32)
-        for s, (ref, span) in zip(scores, pieces):
-            probs = jnp.exp2(s * log2_scale - peak)
-            total = total + jnp.sum(probs, axis=-1, keepdims=True)
-            mixed = mixed + dot(probs.astype(bf), cached(ref, span, HD))
-        store_heads(o_ref, at, (mixed / total).astype(bf))
-        log_ref[at] = jnp.broadcast_to(peak + jnp.log2(total), (rows, HD))
+        span, first = block_span(ats[part], block), part * rows
+        scores = dot_nt(queries[first:], cached(cur_ref, span, 0))
+        pieces.append((masked_first(mask, scores, masked_score), cur_ref, span, first))
+    peaks = []
+    for part in range(parts):
+        at = part * rows
+        tops = [
+            jnp.max(scores[at - first : at - first + rows], axis=-1, keepdims=True)
+            for scores, _, _, first in pieces
+            if first <= at
+        ]
+        peaks.append(functools.reduce(jnp.maximum, tops))
+    peak = jnp.concatenate(peaks, axis=0) * log2_scale
+    total = jnp.zeros((parts * rows, 1), f32)
+    mixed = jnp.zeros((parts * rows, HD), f32)
+    for scores, ref, span, first in pieces:
+        probs = jnp.exp2(scores * log2_scale - peak[first:])
+        total = added_from(total, first, jnp.sum(probs, axis=-1, keepdims=True))
+        mixed = added_from(mixed, first, dot(probs.astype(bf), cached(ref, span, HD)))
+    out = (mixed / total).astype(bf)
+    log_total = peak + jnp.log2(total)
+    for part, at in enumerate(ats):
+        store_heads(o_ref, at, out[part * rows : (part + 1) * rows])
+        log_ref[at] = jnp.broadcast_to(log_total[part * rows : (part + 1) * rows], (rows, HD))
 
 
 def attention_backward_kernel(has_prev, has_carry, info_ref, q_ref, do_ref, o_ref, log_ref, *refs):
     refs = list(refs)
-    sum_ref = refs.pop()
     carry_ref = refs.pop(0) if has_carry else None
     prev_ref = refs.pop(0) if has_prev else None
     cur_ref, dq_ref, dcur_ref = refs[:3]
     dprev_ref = refs[3] if has_prev else None
-    sum_ref[...] = carry_ref[...] if has_carry else jnp.zeros(sum_ref.shape, f32)
-    if has_prev:
-        dprev_ref[...] = jnp.zeros(dprev_ref.shape, f32)
     parts, block, _ = q_ref.shape
     ring = cur_ref.shape[0]
     rows = GROUP * block
     mask = diagonal_mask(rows, ring * block, block, info_ref[0])
-    spans = [block_span(arrival(info_ref, parts, part), block) for part in range(parts)]
+    ats = [arrival(info_ref, parts, part) for part in range(parts)]
+    queries, out_grad = all_heads(q_ref, ats), all_heads(do_ref, ats)
+    out = all_heads(o_ref, ats)
+    inner = jnp.sum(out_grad.astype(f32) * out.astype(f32), axis=-1, keepdims=True)
+    log_total = jnp.concatenate([log_ref[at][:, :1] for at in ats], axis=0)
+
+    def one_block(ref, span, first, log_rows, own_block):
+        keys, values = cached(ref, span, 0), cached(ref, span, HD)
+        some, some_grad = queries[first:], out_grad[first:]
+        probs = jnp.exp2(dot_nt(some, keys) * log2_scale - log_rows[first:])
+        if own_block:
+            probs = masked_first(mask, probs, 0.0)
+        score_grad = (probs * (dot_nt(some_grad, values) - inner[first:])).astype(bf)
+        key_grad = dot_tn(score_grad, some) * scaling
+        value_grad = dot_tn(probs.astype(bf), some_grad)
+        shape = (ring, block, HD)
+        return dot(score_grad, keys), key_grad.reshape(shape), value_grad.reshape(shape)
+
+    query_grad = jnp.zeros((parts * rows, HD), f32)
+    if has_prev:
+        log_prev = log_total + jnp.where(info_ref[1] > 0, 0.0, -masked_score).astype(f32)
+        for part in range(parts):
+            span = slice(part * block, (part + 1) * block)
+            more, key_grad, value_grad = one_block(prev_ref, span, 0, log_prev, False)
+            query_grad = query_grad + more
+            dprev_ref[:, span, :HD] = key_grad
+            dprev_ref[:, span, HD:] = value_grad
     for part in range(parts):
-        at = arrival(info_ref, parts, part)
-        queries = stacked_heads(q_ref, at)
-        out_grad = stacked_heads(do_ref, at)
-        out = stacked_heads(o_ref, at)
-        inner = jnp.sum(out_grad.astype(f32) * out.astype(f32), axis=-1, keepdims=True)
-        log_total = log_ref[at][:, :1]
-        query_grad = jnp.zeros((rows, HD), f32)
-        pieces = []
-        if has_prev:
-            log_prev = log_total + jnp.where(info_ref[1] > 0, 0.0, -masked_score).astype(f32)
-            pieces = [
-                (prev_ref, dprev_ref, slice(p * block, (p + 1) * block), log_prev, False)
-                for p in range(parts)
-            ]
-        pieces += [(cur_ref, sum_ref, spans[p], log_total, p == part) for p in range(part + 1)]
-        for ref, grad_ref, span, log_row, on_diagonal in pieces:
-            keys = cached(ref, span, 0)
-            probs = jnp.exp2(dot_nt(queries, keys) * log2_scale - log_row)
-            if on_diagonal:
-                probs = jnp.where(mask, probs, 0.0)
-            probs_grad = dot_nt(out_grad, cached(ref, span, HD))
-            score_grad = (probs * (probs_grad - inner)).astype(bf)
-            query_grad = query_grad + dot(score_grad, keys)
-            key_grad = dot_tn(score_grad, queries) * scaling
-            value_grad = dot_tn(probs.astype(bf), out_grad)
-            grad_ref[:, span, :HD] += key_grad.reshape(ring, block, HD)
-            grad_ref[:, span, HD:] += value_grad.reshape(ring, block, HD)
-        store_heads(dq_ref, at, (query_grad * scaling).astype(bf))
-    dcur_ref[...] = sum_ref[...].astype(bf)
-
-
-def attention_call(kernel, factor, out_shape, scratch, info, queries, *rest):
+        span = block_span(ats[part], block)
+        more, key_grad, value_grad = one_block(cur_ref, span, part * rows, log_total, True)
+        query_grad = added_from(query_grad, part * rows, more)
+        if has_carry:
+            key_grad = key_grad + carry_ref[:, span, :HD]
+            value_grad = value_grad + carry_ref[:, span, HD:]
+        dcur_ref[:, span, :HD] = key_grad.astype(bf)
+        dcur_ref[:, span, HD:] = value_grad.astype(bf)
+    query_grad = (query_grad * scaling).astype(bf)
+    for part, at in enumerate(ats):
+        store_heads(dq_ref, at, query_grad[part * rows : (part + 1) * rows])
+
+
+def attention_call(kernel, factor, out_shape, info, queries, *rest):
     parts, block, _ = queries.shape
     rows = parts * GROUP * block
     keys = sum(ref.shape[0] * ref.shape[1] for ref in rest if ref.shape == rest[-1].shape)
@@ -177,7 +208,6 @@
         out_shape=out_shape,
         in_specs=[pl.BlockSpec(memory_space=pltpu.SMEM)] + [in_vmem] * (1 + len(rest)),
         out_specs=(in_vmem,) * len(out_shape),
-        scratch_shapes=scratch,
         compiler_params=pltpu.CompilerParams(vmem_limit_bytes=VMEM_LIMIT),
         cost_estimate=pl.CostEstimate(
             flops=factor * rows * keys * HD,
@@ -195,7 +225,7 @@
     )
     caches = (cur,) if prev is None else (prev, cur)
     kernel = functools.partial(attention_forward_kernel, prev is not None)
-    return attention_call(kernel, 2, shapes, [], info, qkv, *caches)
+    return attention_call(kernel, 2, shapes, info, qkv, *caches)
 
 
 def attention_backward(info, qkv, out_grad, out, logs, carry, prev, cur):
@@ -204,10 +234,7 @@
         shapes += (jax.ShapeDtypeStruct(cur.shape, f32),)
     extra = tuple(value for value in (carry, prev) if value is not None)
     kernel = functools.partial(attention_backward_kernel, prev is not None, carry is not None)
-    scratch = [pltpu.VMEM(cur.shape, f32)]
-    return attention_call(
-        kernel, 5, shapes, scratch, info, qkv, out_grad, out, logs, *extra, cur
-    )
+    return attention_call(kernel, 5, shapes, info, qkv, out_grad, out, logs, *extra, cur)
 
 
 def body(

time: 1070 us -> 1070 us (level)
  transfers between devices with their start and end apart: 98 -> 98, of which waited for: 54 -> 53; matrix products, arithmetic and copies ran while one was open for 28% -> 28% of each run, Pallas kernels for 2% -> 2%
where the time goes in v12:
time: 1070 us; the launch traced here: 1050 us
  waiting for transfers between devices  337 us (31%)
  starting transfers between devices  243 us (23%)
  matrix products  179 us (17%)
  other arithmetic  113 us (11%)
  local copies, waits for them, and re-layouts  91.1 us (9%)
  Pallas kernels  42.9 us (4%)
  blocking collectives  29.4 us (3%)
  between operations  18.4 us (2%)
    all_to_all x20, waiting for transfers between devices, exchange(): lax.all_to_all(value, 'shard', split_axis=0, concat_axis=0, tiled=True, a...  178 us
    all_to_all x20, starting transfers between devices, exchange(): lax.all_to_all(value, 'shard', split_axis=0, concat_axis=0, tiled=True, a...  133 us
    ppermute x39, waiting for transfers between devices, shift_x(): lax.ppermute(value, 'shard', [(p, moved(p, steps)) for p in range(shards)])  76.2 us
    dot_general x24, matrix products, dot_nt(): lax.dot_general(left_side, right_side, (((1,), (1,)), ((), ())), preferre...  54 us
    dot_general x31, matrix products, dot(): return jnp.dot(left_side, right_side, preferred_element_type=f32)  51.6 us
    dot_general x21, matrix products, wide_einsum(): jnp.einsum(formula, left_side, right_side, preferred_element_type=f32)  47.9 us
    ppermute x39, starting transfers between devices, shift_x(): lax.ppermute(value, 'shard', [(p, moved(p, steps)) for p in range(shards)])  43.3 us
    pallas_call x6, Pallas kernels, attention_call(): pl.pallas_call(kernel, out_shape=out_shape, in_specs=[pl.BlockSpec(memory...  42.9 us
  transfers between devices with their start and end apart: 98, of which 53 were waited for; matrix products, arithmetic and copies ran while one was open for 28% of the time, Pallas kernels for 2%

profile of v12, /device:TPU:1, one launch (start us, length us, event | category | flops | bytes accessed | tf_op | source)
XLA Modules:
  0.0 1054.3 jit_solution(783765702396481598)
XLA Ops:
  42.9 11.5 %collective-permute-done.6 = bf16[2,24,1536]{2,1,0:T(8,128)(2,1)} collective-permute-done((bf16[2,24,1536]{2,1,0:T(8,128)(2,1)S(1)}, bf16[2,24,1536]{2,1,0:T(8,128)(2,1)}, u32[]{:S(2)}, u32[]{:S(2)}) %collective-permute-start.6) | collective-permute-done | bytes 147488 | tf_op jit(solution)/shard_map/ppermute | solution.py:347
  79.4 16.5 %all-to-all-done.1.refs_0_.refs_1_ = bf16[8,256,256]{2,1,0:T(8,128)(2,1)} async-done(((bf16[8,256,256]{2,1,0:T(8,128)(2,1)}), bf16[8,256,256]{2,1,0:T(8,128)(2,1)}, u32[]{:S(2)}, u32[]{:S(2)}) %all-to-all-start.1) | async-done | bytes 1048608 | tf_op jit(solution)/shard_map/all_to_all | solution.py:281
  177.6 13.0 %all-to-all-done.3 = bf16[32,2,8,1536]{3,2,1,0:T(8,128)(2,1)} async-done(((bf16[32,2,8,1536]{3,2,1,0:T(8,128)(2,1)}), bf16[32,2,8,1536]{3,2,1,0:T(8,128)(2,1)}, u32[]{:S(2)}, u32[]{:S(2)}) %all-to-all-start.3) | async-done | bytes 1572896 | tf_op jit(solution)/shard_map/all_to_all | solution.py:281
  208.6 10.4 collective-permute-start.20
  245.4 15.7 %all-to-all-done.4.refs_1_.refs_0_.refs_2_ = bf16[8,256,256]{2,1,0:T(8,128)(2,1)} async-done(((bf16[8,256,256]{2,1,0:T(8,128)(2,1)}), bf16[8,256,256]{2,1,0:T(8,128)(2,1)}, u32[]{:S(2)}, u32[]{:S(2)}) %all-to-all-start.4) | async-done | bytes 1048608 | tf_op jit(solution)/shard_map/all_to_all | solution.py:281
  289.8 29.4 %all_to_all.105 = bf16[32,2,8,1536]{3,2,1,0:T(8,128)(2,1)S(1)} all-to-all(bf16[32,2,8,1536]{3,2,1,0:T(8,128)(2,1)S(1)} %bitcast.595), channel_id=1, replica_groups=mesh['section'=2,'dp'=2,'shard'=32] {'shard'}, dimensions={0} | all-to-all | bytes 3145728 | tf_op jit(solution)/shard_map/all_to_all | solution.py:281
  338.5 14.1 %all-to-all-done.6 = bf16[32,2,8,1536]{3,2,1,0:T(8,128)(2,1)} async-done(((bf16[32,2,8,1536]{3,2,1,0:T(8,128)(2,1)}), bf16[32,2,8,1536]{3,2,1,0:T(8,128)(2,1)}, u32[]{:S(2)}, u32[]{:S(2)}) %all-to-all-start.6) | async-done | bytes 1572896 | tf_op jit(solution)/shard_map/all_to_all | solution.py:281
  371.2 10.3 collective-permute-done.24
  398.6 13.8 %all-to-all-done.7.refs_1_ = bf16[8,256,256]{2,1,0:T(8,128)(2,1)} async-done(((bf16[8,256,256]{2,1,0:T(8,128)(2,1)}), bf16[8,256,256]{2,1,0:T(8,128)(2,1)}, u32[]{:S(2)}, u32[]{:S(2)}) %all-to-all-start.7) | async-done | bytes 1048608 | tf_op jit(solution)/shard_map/all_to_all | solution.py:281
  449.3 17.5 %all-to-all-done.8 = bf16[32,2,8,1536]{3,2,1,0:T(8,128)(2,1)} async-done(((bf16[32,2,8,1536]{3,2,1,0:T(8,128)(2,1)}), bf16[32,2,8,1536]{3,2,1,0:T(8,128)(2,1)}, u32[]{:S(2)}, u32[]{:S(2)}) %all-to-all-start.8) | async-done | bytes 1572896 | tf_op jit(solution)/shard_map/all_to_all | solution.py:281
  485.9 9.9 all-to-all-done.10
  515.7 10.2 all-to-all-done.9
  544.9 11.2 %all-to-all-done.11 = bf16[32,2,8,1536]{3,2,1,0:T(8,128)(2,1)} async-done(((bf16[32,2,8,1536]{3,2,1,0:T(8,128)(2,1)}), bf16[32,2,8,1536]{3,2,1,0:T(8,128)(2,1)}, u32[]{:S(2)}, u32[]{:S(2)}) %all-to-all-start.11) | async-done | bytes 1572896 | tf_op jit(solution)/shard_map/all_to_all | solution.py:281
  569.3 9.3 shard_map.274
  581.6 9.2 all-to-all-start.12
  597.8 9.6 all-to-all-done.12
  687.8 8.7 all-to-all-done.14
  710.1 9.3 shard_map.275
  722.4 8.1 all-to-all-start.15
  736.5 9.4 all-to-all-done.15
  815.0 9.3 all-to-all-start.17
  882.5 9.3 all-to-all-done.18
  960.8 18.1 %collective-permute-done.72 = bf16[2,32,768]{2,1,0:T(8,128)(2,1)} collective-permute-done((bf16[2,32,768]{2,1,0:T(8,128)(2,1)S(1)}, bf16[2,32,768]{2,1,0:T(8,128)(2,1)}, u32[]{:S(2)}, u32[]{:S(2)}) %collective-permute-start.72) | collective-permute-done | bytes 98336 | tf_op jit(solution)/shard_map/ppermute | solution.py:410
  998.7 18.4 %collective-permute-done.75 = bf16[32,768]{1,0:T(8,128)(2,1)S(1)} collective-permute-done((bf16[32,768]{1,0:T(8,128)(2,1)S(1)}, bf16[32,768]{1,0:T(8,128)(2,1)S(1)}, u32[]{:S(2)}, u32[]{:S(2)}) %collective-permute-start.75) | collective-permute-done | bytes 49184 | tf_op jit(solution)/shard_map/ppermute | solution.py:637
  (1016 shorter events, 733.6 us)
Async XLA Ops:
  7.2 115.0 %all-gather.3.cloned.1.call-start = ((), (), s32[]{:S(2)}) async-start(), calls=%async_computation.21 | async-start | bytes 4866048 | tf_op jit(solution)/shard_map/all_gather | solution.py:340
  26.6 32.3 %all-to-all-start = ((bf16[32,24,768]{2,1,0:T(8,128)(2,1)}), bf16[32,24,768]{2,1,0:T(8,128)(2,1)}, u32[]{:S(2)}, u32[]{:S(2)}) async-start(bf16[32,24,768]{2,1,0:T(8,128)(2,1)} %bitcast.599), calls=%async_computation | async-start | bytes 2359296 | tf_op jit(solution)/shard_map/all_to_all | solution.py:281
  131.6 88.6 %collective-permute-start.16 = (bf16[64,1536]{1,0:T(8,128)(2,1)}, bf16[64,1536]{1,0:T(8,128)(2,1)}, u32[]{:S(2)}, u32[]{:S(2)}) collective-permute-start(bf16[64,1536]{1,0:T(8,128)(2,1)} %get-tuple-element.188), channel_id=1, source_target_pairs={{0,24},{1,25},{2,26},{3,27},{4,28},{5,29},{6,30},{7,31},{8,0},{9,1... | collective-permute-start | bytes 589832 | tf_op jit(solution)/shard_map/ppermute | solution.py:410
  134.1 87.5 %collective-permute-start.15 = (bf16[64,1536]{1,0:T(8,128)(2,1)}, bf16[64,1536]{1,0:T(8,128)(2,1)}, u32[]{:S(2)}, u32[]{:S(2)}) collective-permute-start(bf16[64,1536]{1,0:T(8,128)(2,1)} %get-tuple-element.188), channel_id=1, source_target_pairs={{0,16},{1,17},{2,18},{3,19},{4,20},{5,21},{6,22},{7,23},{8,24},{9,... | collective-permute-start | bytes 589832 | tf_op jit(solution)/shard_map/ppermute | solution.py:410
  134.6 88.5 %collective-permute-start.14 = (bf16[64,1536]{1,0:T(8,128)(2,1)}, bf16[64,1536]{1,0:T(8,128)(2,1)}, u32[]{:S(2)}, u32[]{:S(2)}) collective-permute-start(bf16[64,1536]{1,0:T(8,128)(2,1)} %get-tuple-element.188), channel_id=1, source_target_pairs={{0,8},{1,9},{2,10},{3,11},{4,12},{5,13},{6,14},{7,15},{8,16},{9,17... | collective-permute-start | bytes 589832 | tf_op jit(solution)/shard_map/ppermute | solution.py:410
  148.2 45.0 %collective-permute-start.12 = (bf16[32,24,2048]{2,1,0:T(8,128)(2,1)}, bf16[32,24,2048]{2,1,0:T(8,128)(2,1)}, u32[]{:S(2)}, u32[]{:S(2)}) collective-permute-start(bf16[32,24,2048]{2,1,0:T(8,128)(2,1)} %slice.291), channel_id=1, source_target_pairs={{0,32},{32,0},{1,33},{33,1},{2,34},{34,2},{3,35},{35,3},{4,36},{36... | collective-permute-start | bytes 9437192 | tf_op jit(solution)/shard_map/ppermute | solution.py:289
  495.8 30.1 %all-to-all-start.9 = ((bf16[32,2,8,1536]{3,2,1,0:T(8,128)(2,1)}), bf16[32,2,8,1536]{3,2,1,0:T(8,128)(2,1)}, u32[]{:S(2)}, u32[]{:S(2)}) async-start(bf16[32,2,8,1536]{3,2,1,0:T(8,128)(2,1)} %bitcast.593), calls=%async_computation.9 | async-start | bytes 3145728 | tf_op jit(solution)/shard_map/all_to_all | solution.py:281
  525.9 30.2 %all-to-all-start.11 = ((bf16[32,2,8,1536]{3,2,1,0:T(8,128)(2,1)}), bf16[32,2,8,1536]{3,2,1,0:T(8,128)(2,1)}, u32[]{:S(2)}, u32[]{:S(2)}) async-start(bf16[32,2,8,1536]{3,2,1,0:T(8,128)(2,1)} %bitcast.590), calls=%async_computation.11 | async-start | bytes 3145728 | tf_op jit(solution)/shard_map/all_to_all | solution.py:281
  595.3 229.1 %collective-permute-start.31 = (bf16[128,1536]{1,0:T(8,128)(2,1)}, bf16[128,1536]{1,0:T(8,128)(2,1)}, u32[]{:S(2)}, u32[]{:S(2)}) collective-permute-start(bf16[128,1536]{1,0:T(8,128)(2,1)} %pad_maximum_fusion.10), channel_id=1, source_target_pairs={{0,32},{32,0},{1,33},{33,1},{2,34},{34,2},{3,35},{35,3},{4,36},{36... | collective-permute-start | bytes 1179656 | tf_op jit(solution)/shard_map/ppermute | solution.py:289
  631.2 29.6 %all-to-all-start.13 = ((bf16[32,2,8,1536]{3,2,1,0:T(8,128)(2,1)}), bf16[32,2,8,1536]{3,2,1,0:T(8,128)(2,1)}, u32[]{:S(2)}, u32[]{:S(2)}) async-start(bf16[32,2,8,1536]{3,2,1,0:T(8,128)(2,1)} %bitcast.598), calls=%async_computation.13 | async-start | bytes 3145728 | tf_op jit(solution)/shard_map/all_to_all | solution.py:281
  643.1 159.6 %collective-permute-start.47 = (bf16[128,1024]{1,0:T(8,128)(2,1)}, bf16[128,1024]{1,0:T(8,128)(2,1)}, u32[]{:S(2)}, u32[]{:S(2)}) collective-permute-start(bf16[128,1024]{1,0:T(8,128)(2,1)} %pad_maximum_fusion.14), channel_id=1, source_target_pairs={{0,32},{32,0},{1,33},{33,1},{2,34},{34,2},{3,35},{35,3},{4,36},{36... | collective-permute-start | bytes 786440 | tf_op jit(solution)/shard_map/ppermute | solution.py:289
  776.6 29.6 %all-to-all-start.16 = ((bf16[32,2,8,1536]{3,2,1,0:T(8,128)(2,1)}), bf16[32,2,8,1536]{3,2,1,0:T(8,128)(2,1)}, u32[]{:S(2)}, u32[]{:S(2)}) async-start(bf16[32,2,8,1536]{3,2,1,0:T(8,128)(2,1)} %bitcast.597), calls=%async_computation.16 | async-start | bytes 3145728 | tf_op jit(solution)/shard_map/all_to_all | solution.py:281
  815.0 33.2 %all-to-all-start.17 = ((bf16[32,2,8,1536]{3,2,1,0:T(8,128)(2,1)}), bf16[32,2,8,1536]{3,2,1,0:T(8,128)(2,1)}, u32[]{:S(2)}, u32[]{:S(2)}) async-start(bf16[32,2,8,1536]{3,2,1,0:T(8,128)(2,1)} %bitcast.587), calls=%async_computation.17 | async-start | bytes 3145728 | tf_op jit(solution)/shard_map/all_to_all | solution.py:281
  832.0 87.8 %collective-permute-start.55 = (bf16[2,1536,512]{2,1,0:T(8,128)(2,1)}, bf16[2,1536,512]{2,1,0:T(8,128)(2,1)}, u32[]{:S(2)}, u32[]{:S(2)}) collective-permute-start(bf16[2,1536,512]{2,1,0:T(8,128)(2,1)} %convolution_convert_fusion.3), channel_id=1, source_target_pairs={{0,32},{32,0},{1,33},{33,1},{2,34},{34,2},{3,35},{35,3},{4,36},{36... | collective-permute-start | bytes 9437192 | tf_op jit(solution)/shard_map/ppermute | solution.py:289
  836.3 83.6 %collective-permute-start.56 = (bf16[2,1536,512]{2,1,0:T(8,128)(2,1)}, bf16[2,1536,512]{2,1,0:T(8,128)(2,1)}, u32[]{:S(2)}, u32[]{:S(2)}) collective-permute-start(bf16[2,1536,512]{2,1,0:T(8,128)(2,1)} %convolution_convert_fusion.2), channel_id=1, source_target_pairs={{0,32},{32,0},{1,33},{33,1},{2,34},{34,2},{3,35},{35,3},{4,36},{36... | collective-permute-start | bytes 9437192 | tf_op jit(solution)/shard_map/ppermute | solution.py:289
  855.7 64.2 %collective-permute-start.57 = (bf16[2,512,1536]{2,1,0:T(8,128)(2,1)}, bf16[2,512,1536]{2,1,0:T(8,128)(2,1)}, u32[]{:S(2)}, u32[]{:S(2)}) collective-permute-start(bf16[2,512,1536]{2,1,0:T(8,128)(2,1)} %convolution_convert_fusion.1), channel_id=1, source_target_pairs={{0,32},{32,0},{1,33},{33,1},{2,34},{34,2},{3,35},{35,3},{4,36},{36... | collective-permute-start | bytes 9437192 | tf_op jit(solution)/shard_map/ppermute | solution.py:289
  919.9 60.4 %all-to-all-start.20 = ((bf16[8,48,1536]{2,1,0:T(8,128)(2,1)}), bf16[8,48,1536]{2,1,0:T(8,128)(2,1)}, u32[]{:S(2)}, u32[]{:S(2)}) async-start(bf16[8,48,1536]{2,1,0:T(8,128)(2,1)} %bitcast.608), calls=%async_computation.20 | async-start | bytes 2359296 | tf_op jit(solution)/shard_map/all_to_all | solution.py:281
  933.8 58.2 %collective-permute-start.61 = (bf16[4,2,48,1024]{3,2,1,0:T(8,128)(2,1)}, bf16[4,2,48,1024]{3,2,1,0:T(8,128)(2,1)}, u32[]{:S(2)}, u32[]{:S(2)}) collective-permute-start(bf16[4,2,48,1024]{3,2,1,0:T(8,128)(2,1)} %get-tuple-element.126), channel_id=1, source_target_pairs={{0,8},{1,9},{2,10},{3,11},{4,12},{5,13},{6,14},{7,15},{8,16},{9,17... | collective-permute-start | bytes 2359304 | tf_op jit(solution)/shard_map/ppermute | solution.py:410
  933.8 58.2 %collective-permute-start.63 = (bf16[4,2,48,1024]{3,2,1,0:T(8,128)(2,1)}, bf16[4,2,48,1024]{3,2,1,0:T(8,128)(2,1)}, u32[]{:S(2)}, u32[]{:S(2)}) collective-permute-start(bf16[4,2,48,1024]{3,2,1,0:T(8,128)(2,1)} %get-tuple-element.127), channel_id=1, source_target_pairs={{0,24},{1,25},{2,26},{3,27},{4,28},{5,29},{6,30},{7,31},{8,0},{9,1... | collective-permute-start | bytes 2359304 | tf_op jit(solution)/shard_map/ppermute | solution.py:410
  955.4 36.5 %collective-permute-start.62 = (bf16[4,2,48,1024]{3,2,1,0:T(8,128)(2,1)}, bf16[4,2,48,1024]{3,2,1,0:T(8,128)(2,1)}, u32[]{:S(2)}, u32[]{:S(2)}) collective-permute-start(bf16[4,2,48,1024]{3,2,1,0:T(8,128)(2,1)} %get-tuple-element.128), channel_id=1, source_target_pairs={{0,16},{1,17},{2,18},{3,19},{4,20},{5,21},{6,22},{7,23},{8,24},{9,... | collective-permute-start | bytes 2359304 | tf_op jit(solution)/shard_map/ppermute | solution.py:410
  958.1 30.1 %collective-permute-start.74 = (bf16[2,32,768]{2,1,0:T(8,128)(2,1)}, bf16[2,32,768]{2,1,0:T(8,128)(2,1)}, u32[]{:S(2)}, u32[]{:S(2)}) collective-permute-start(bf16[2,32,768]{2,1,0:T(8,128)(2,1)} %get-tuple-element.180), channel_id=1, source_target_pairs={{0,24},{1,25},{2,26},{3,27},{4,28},{5,29},{6,30},{7,31},{8,0},{9,1... | collective-permute-start | bytes 294920 | tf_op jit(solution)/shard_map/ppermute | solution.py:410
  980.3 56.4 %all-to-all-start.19 = ((bf16[32,48,768]{2,1,0:T(8,128)(2,1)}), bf16[32,48,768]{2,1,0:T(8,128)(2,1)}, u32[]{:S(2)}, u32[]{:S(2)}) async-start(bf16[32,48,768]{2,1,0:T(8,128)(2,1)} %maximum_maximum_fusion), calls=%async_computation.19 | async-start | bytes 4718592 | tf_op jit(solution)/shard_map/all_to_all | solution.py:281
  994.5 32.1 %collective-permute-start.64 = (bf16[2,48,1024]{2,1,0:T(8,128)(2,1)S(1)}, bf16[2,48,1024]{2,1,0:T(8,128)(2,1)S(1)}, u32[]{:S(2)}, u32[]{:S(2)}) collective-permute-start(bf16[2,48,1024]{2,1,0:T(8,128)(2,1)S(1)} %get-tuple-element.144), channel_id=1, source_target_pairs={{0,2},{1,3},{2,4},{3,5},{4,6},{5,7},{6,0},{7,1},{8,10},{9,11},{10,... | collective-permute-start | bytes 589832 | tf_op jit(solution)/shard_map/ppermute | solution.py:634
  995.8 30.8 %collective-permute-start.66 = (bf16[2,48,1024]{2,1,0:T(8,128)(2,1)S(1)}, bf16[2,48,1024]{2,1,0:T(8,128)(2,1)S(1)}, u32[]{:S(2)}, u32[]{:S(2)}) collective-permute-start(bf16[2,48,1024]{2,1,0:T(8,128)(2,1)S(1)} %get-tuple-element.145), channel_id=1, source_target_pairs={{0,6},{1,7},{2,0},{3,1},{4,2},{5,3},{6,4},{7,5},{8,14},{9,15},{10,... | collective-permute-start | bytes 589832 | tf_op jit(solution)/shard_map/ppermute | solution.py:634
  (353 other events, 3143.8 us)
Sparse Core Ops, SparseCore 0:
  16.9 105.2 all-gather.2

commit v13 on v12

--- a/solution.py
+++ b/solution.py
@@ -392,10 +392,11 @@
         return high, (value - high.astype(f32)).astype(bf)
 
     def to_experts(rows):
+        wide = rows.shape[1]
         return (
-            exchange(rows.reshape(shards, local_experts, CAP, width))
+            exchange(rows.reshape(shards, local_experts, CAP, wide))
             .transpose(1, 0, 2, 3)
-            .reshape(local_experts, shards * CAP, width)
+            .reshape(local_experts, shards * CAP, wide)
         )
 
     def from_experts(rows):
@@ -458,6 +459,13 @@
         cache = exchange(copies(qkv[:, group_width:], ring), zy_groups)
         qkv = qkv.reshape(heads, block, part_width)
         attn_info = info if moment == 1 else info_all
+        early = None
+        if moment == micros:
+            last_rows = cotangent[0, micros - 1]
+            last_rows = jnp.where(is_first, jnp.zeros_like(last_rows), last_rows)
+            last_rows = dot_tn(pick, last_rows).astype(bf)
+            last_rows, cache = lax.optimization_barrier((last_rows, cache))
+            early = to_experts(last_rows)
         attended, logs = attention_forward(attn_info, qkv, previous, cache)
         attended_rows = attended.reshape(heads * block, group_width)
         hidden = layer_in + sum_over_x(dot(attended_rows, output_w))
@@ -465,6 +473,8 @@
             arrived, hidden = lax.optimization_barrier((gathered, hidden))
             shared_pair = shared_weights(arrived)
         gate_up_w, down_w = shared_pair
+        if early is not None:
+            early, hidden = lax.optimization_barrier((early, hidden))
         normed_two = (hidden * inverse_rms(hidden) * gain_two).astype(bf)
         gates = gate_values(normed_two, table)
         expert_in = to_experts(dot_tn(pick, normed_two).astype(bf))
@@ -501,15 +511,23 @@
             shared_act=shared_act,
             output_b=output_b,
             shared_pair=shared_pair,
-        )
-
-    def ffn_backward(kept, upstream_b):
+            expert_grad=early,
+        )
+
+    def ffn_backward(kept, upstream_b, riders=None):
         upstream = upstream_b.astype(f32)
         gates, hidden = kept["gates"], kept["hidden"]
         gate_up_w, down_w = kept["shared_pair"]
         high, low = high_low(gates)
-        outgoing = dot_tn(high, upstream_b) + dot_tn(low, upstream_b)
-        expert_grad = to_experts(outgoing.astype(bf))
+        expert_grad, arrived = kept["expert_grad"], None
+        unscaled = expert_grad is not None
+        if not unscaled:
+            outgoing = (dot_tn(high, upstream_b) + dot_tn(low, upstream_b)).astype(bf)
+            if riders is not None:
+                outgoing = jnp.concatenate([outgoing, riders], axis=1)
+            expert_grad = to_experts(outgoing)
+            if riders is not None:
+                expert_grad, arrived = expert_grad[..., :width], expert_grad[..., width:]
         act_silu, act_slope = silu_parts(kept["gate_pre"])
         act_grad = wide_einsum("erd,efd->erf", expert_grad, expert_d)
         gate_pre_grad = (act_grad * kept["up_pre"] * act_slope).astype(bf)
@@ -531,7 +549,11 @@
         picked_b = picked_grad.astype(bf)
         normed_two_grad = normed_two_grad + dot_nt(picked_b, router_slots)
         normed_two_grad = lax.optimization_barrier(normed_two_grad)
-        normed_two_grad = normed_two_grad + dot(kept["pick"], returned_grad)
+        if unscaled:
+            routed_grad = dot(high, returned_grad) + dot(low, returned_grad)
+        else:
+            routed_grad = dot(kept["pick"], returned_grad)
+        normed_two_grad = normed_two_grad + routed_grad
         logit_grad = dot_nt(picked_b, spread).astype(bf)
         hidden_norm_grad, gain_two_grad = norm_back(hidden, gain_two, normed_two_grad)
         return dict(
@@ -544,6 +566,7 @@
             shared_up_grad=shared_up_grad,
             logit_grad=logit_grad,
             gain_two_grad=gain_two_grad,
+            arrived=arrived,
         )
 
     def attention_back(kept, grads, carried):
@@ -592,7 +615,11 @@
     for source in range(micros, -1, -1):
         own = cotangent[0, source - 1] if source > 0 else nothing
         upstream_b = jnp.where(is_first, received, own)
-        grads = ffn_backward(saved[source], upstream_b)
+        riders = None
+        if source == micros - 1:
+            slot_gates = jnp.stack(high_low(jnp.sum(saved[micros]["gates"], axis=0)), axis=1)
+            riders = jnp.pad(slot_gates, ((0, 0), (0, 126)))
+        grads = ffn_backward(saved[source], upstream_b, riders)
         backs[source], carried = attention_back(saved[source], grads, carried)
         if source > 0:
             received = lax.ppermute(backs[source]["layer_grad"], "section", [(1, 0)])
@@ -606,6 +633,12 @@
 
     def back_rows(name, axis=0):
         return live(name, backs, axis)
+
+    late_gates = backs[micros - 1]["arrived"][..., :2].astype(f32)
+    late_gates = jnp.sum(late_gates, axis=-1, keepdims=True)
+    for name in ("expert_grad", "gate_pre_grad", "up_pre_grad"):
+        rows = backs[micros][name].astype(f32) * late_gates
+        backs[micros][name] = rows.astype(bf)
 
     expert_parts = [
         wide_einsum("erd,erf->edf", kept_rows("expert_in", 1), back_rows("gate_pre_grad", 1)),

time: 1070 us -> 1070 us (level)
    all_to_all x20, waiting for transfers between devices: 178 us -> 167 us  [exchange(): lax.all_to_all(value, 'shard', split_axis=0, concat_axis=0, tiled=True, a...]
    unnamed x568 -> x584, local copies, waits for them, and re-layouts: 35.1 us -> 39.7 us
    dot_general x31 -> x32, matrix products: 51.6 us -> 52.4 us  [dot(): return jnp.dot(left_side, right_side, preferred_element_type=f32)]
    dot_general x14 -> x13, matrix products: 25.7 us -> 25.9 us  [dot_tn(): lax.dot_general(left_side, right_side, (((0,), (0,)), ((), ())), preferre...]
  transfers between devices with their start and end apart: 98 -> 98, of which waited for: 53 -> 52; matrix products, arithmetic and copies ran while one was open for 28% -> 27% of each run, Pallas kernels for 2% -> 2%
where the time goes in v13:
time: 1070 us; the launch traced here: 1060 us
  waiting for transfers between devices  331 us (31%)
  starting transfers between devices  244 us (23%)
  matrix products  180 us (17%)
  other arithmetic  115 us (11%)
  local copies, waits for them, and re-layouts  98.7 us (9%)
  Pallas kernels  42.9 us (4%)
  blocking collectives  29.4 us (3%)
  between operations  18.4 us (2%)
    all_to_all x20, waiting for transfers between devices, exchange(): lax.all_to_all(value, 'shard', split_axis=0, concat_axis=0, tiled=True, a...  167 us
    all_to_all x20, starting transfers between devices, exchange(): lax.all_to_all(value, 'shard', split_axis=0, concat_axis=0, tiled=True, a...  127 us
    ppermute x39, waiting for transfers between devices, shift_x(): lax.ppermute(value, 'shard', [(p, moved(p, steps)) for p in range(shards)])  84.3 us
    dot_general x24, matrix products, dot_nt(): lax.dot_general(left_side, right_side, (((1,), (1,)), ((), ())), preferre...  54.6 us
    dot_general x32, matrix products, dot(): return jnp.dot(left_side, right_side, preferred_element_type=f32)  52.4 us
    ppermute x39, starting transfers between devices, shift_x(): lax.ppermute(value, 'shard', [(p, moved(p, steps)) for p in range(shards)])  47.8 us
    dot_general x21, matrix products, wide_einsum(): jnp.einsum(formula, left_side, right_side, preferred_element_type=f32)  47 us
    pallas_call x6, Pallas kernels, attention_call(): pl.pallas_call(kernel, out_shape=out_shape, in_specs=[pl.BlockSpec(memory...  42.9 us
  transfers between devices with their start and end apart: 98, of which 52 were waited for; matrix products, arithmetic and copies ran while one was open for 27% of the time, Pallas kernels for 2%

profile of v13, /device:TPU:1, one launch (start us, length us, event | category | flops | bytes accessed | tf_op | source)
XLA Modules:
  0.0 1060.4 jit_solution(12953364493792340695)
XLA Ops:
  42.9 11.6 %collective-permute-done.6 = bf16[2,24,1536]{2,1,0:T(8,128)(2,1)} collective-permute-done((bf16[2,24,1536]{2,1,0:T(8,128)(2,1)S(1)}, bf16[2,24,1536]{2,1,0:T(8,128)(2,1)}, u32[]{:S(2)}, u32[]{:S(2)}) %collective-permute-start.6) | collective-permute-done | bytes 147488 | tf_op jit(solution)/shard_map/ppermute | solution.py:347
  80.2 17.1 %all-to-all-done.1.refs_0_.refs_1_ = bf16[8,256,256]{2,1,0:T(8,128)(2,1)} async-done(((bf16[8,256,256]{2,1,0:T(8,128)(2,1)}), bf16[8,256,256]{2,1,0:T(8,128)(2,1)}, u32[]{:S(2)}, u32[]{:S(2)}) %all-to-all-start.1) | async-done | bytes 1048608 | tf_op jit(solution)/shard_map/all_to_all | solution.py:281
  177.7 10.9 %all-to-all-done.3 = bf16[32,2,8,1536]{3,2,1,0:T(8,128)(2,1)} async-done(((bf16[32,2,8,1536]{3,2,1,0:T(8,128)(2,1)}), bf16[32,2,8,1536]{3,2,1,0:T(8,128)(2,1)}, u32[]{:S(2)}, u32[]{:S(2)}) %all-to-all-start.3) | async-done | bytes 1572896 | tf_op jit(solution)/shard_map/all_to_all | solution.py:281
  206.5 13.3 %collective-permute-start.20 = (bf16[64,1536]{1,0:T(8,128)(2,1)S(1)}, bf16[64,1536]{1,0:T(8,128)(2,1)S(1)}, u32[]{:S(2)}, u32[]{:S(2)}) collective-permute-start(bf16[64,1536]{1,0:T(8,128)(2,1)S(1)} %add_convert_fusion.2), channel_id=1, source_target_pairs={{0,88},{1,89},{2,90},{3,91},{4,92},{5,93},{6,94},{7,95},{8,64},{9,... | collective-permute-start | bytes 589832 | tf_op jit(solution)/shard_map/ppermute | solution.py:416
  246.8 15.7 %all-to-all-done.4.refs_1_.refs_0_.refs_2_ = bf16[8,256,256]{2,1,0:T(8,128)(2,1)} async-done(((bf16[8,256,256]{2,1,0:T(8,128)(2,1)}), bf16[8,256,256]{2,1,0:T(8,128)(2,1)}, u32[]{:S(2)}, u32[]{:S(2)}) %all-to-all-start.4) | async-done | bytes 1048608 | tf_op jit(solution)/shard_map/all_to_all | solution.py:281
  290.7 29.4 %all_to_all.105 = bf16[32,2,8,1536]{3,2,1,0:T(8,128)(2,1)S(1)} all-to-all(bf16[32,2,8,1536]{3,2,1,0:T(8,128)(2,1)S(1)} %bitcast.584), channel_id=1, replica_groups=mesh['section'=2,'dp'=2,'shard'=32] {'shard'}, dimensions={0} | all-to-all | bytes 3145728 | tf_op jit(solution)/shard_map/all_to_all | solution.py:281
  339.4 14.1 %all-to-all-done.6 = bf16[32,2,8,1536]{3,2,1,0:T(8,128)(2,1)} async-done(((bf16[32,2,8,1536]{3,2,1,0:T(8,128)(2,1)}), bf16[32,2,8,1536]{3,2,1,0:T(8,128)(2,1)}, u32[]{:S(2)}, u32[]{:S(2)}) %all-to-all-start.6) | async-done | bytes 1572896 | tf_op jit(solution)/shard_map/all_to_all | solution.py:281
  372.1 10.3 collective-permute-done.24
  403.6 9.5 all-to-all-done.7.refs_1_
  433.0 8.8 collective-permute-done.28
  471.2 14.2 %all-to-all-done.9 = bf16[32,2,8,1536]{3,2,1,0:T(8,128)(2,1)} async-done(((bf16[32,2,8,1536]{3,2,1,0:T(8,128)(2,1)}), bf16[32,2,8,1536]{3,2,1,0:T(8,128)(2,1)}, u32[]{:S(2)}, u32[]{:S(2)}) %all-to-all-start.9) | async-done | bytes 1572896 | tf_op jit(solution)/shard_map/all_to_all | solution.py:281
  511.7 12.6 %all-to-all-done.10 = bf16[32,2,8,1536]{3,2,1,0:T(8,128)(2,1)} async-done(((bf16[32,2,8,1536]{3,2,1,0:T(8,128)(2,1)}), bf16[32,2,8,1536]{3,2,1,0:T(8,128)(2,1)}, u32[]{:S(2)}, u32[]{:S(2)}) %all-to-all-start.10) | async-done | bytes 1572896 | tf_op jit(solution)/shard_map/all_to_all | solution.py:281
  544.3 10.4 all-to-all-done.11
  571.7 9.3 shard_map.274
  598.4 9.7 all-to-all-done.12
  653.8 13.4 %all-to-all-done.13 = bf16[32,2,8,1664]{3,2,1,0:T(8,128)(2,1)} async-done(((bf16[32,2,8,1664]{3,2,1,0:T(8,128)(2,1)}), bf16[32,2,8,1664]{3,2,1,0:T(8,128)(2,1)}, u32[]{:S(2)}, u32[]{:S(2)}) %all-to-all-start.13) | async-done | bytes 1703968 | tf_op jit(solution)/shard_map/all_to_all | solution.py:281
  696.0 9.3 all-to-all-done.14
  721.5 9.3 shard_map.275
  745.5 8.8 all-to-all-done.15
  784.3 8.1 all-to-all-start.16
  823.2 9.4 all-to-all-start.17
  890.7 9.3 all-to-all-done.18
  966.7 17.4 %collective-permute-done.72 = bf16[2,32,768]{2,1,0:T(8,128)(2,1)} collective-permute-done((bf16[2,32,768]{2,1,0:T(8,128)(2,1)S(1)}, bf16[2,32,768]{2,1,0:T(8,128)(2,1)}, u32[]{:S(2)}, u32[]{:S(2)}) %collective-permute-start.72) | collective-permute-done | bytes 98336 | tf_op jit(solution)/shard_map/ppermute | solution.py:411
  1003.9 18.4 %collective-permute-done.75 = bf16[32,768]{1,0:T(8,128)(2,1)S(1)} collective-permute-done((bf16[32,768]{1,0:T(8,128)(2,1)S(1)}, bf16[32,768]{1,0:T(8,128)(2,1)S(1)}, u32[]{:S(2)}, u32[]{:S(2)}) %collective-permute-start.75) | collective-permute-done | bytes 49184 | tf_op jit(solution)/shard_map/ppermute | solution.py:670
  (1041 shorter events, 741.7 us)
Async XLA Ops:
  7.2 116.4 %all-gather.3.cloned.1.call-start = ((), (), s32[]{:S(2)}) async-start(), calls=%async_computation.21 | async-start | bytes 4866048 | tf_op jit(solution)/shard_map/all_gather | solution.py:340
  26.6 32.4 %all-to-all-start = ((bf16[32,24,768]{2,1,0:T(8,128)(2,1)}), bf16[32,24,768]{2,1,0:T(8,128)(2,1)}, u32[]{:S(2)}, u32[]{:S(2)}) async-start(bf16[32,24,768]{2,1,0:T(8,128)(2,1)} %bitcast.586), calls=%async_computation | async-start | bytes 2359296 | tf_op jit(solution)/shard_map/all_to_all | solution.py:281
  133.0 88.1 %collective-permute-start.16 = (bf16[64,1536]{1,0:T(8,128)(2,1)}, bf16[64,1536]{1,0:T(8,128)(2,1)}, u32[]{:S(2)}, u32[]{:S(2)}) collective-permute-start(bf16[64,1536]{1,0:T(8,128)(2,1)} %get-tuple-element.198), channel_id=1, source_target_pairs={{0,24},{1,25},{2,26},{3,27},{4,28},{5,29},{6,30},{7,31},{8,0},{9,1... | collective-permute-start | bytes 589832 | tf_op jit(solution)/shard_map/ppermute | solution.py:411
  135.5 87.0 %collective-permute-start.15 = (bf16[64,1536]{1,0:T(8,128)(2,1)}, bf16[64,1536]{1,0:T(8,128)(2,1)}, u32[]{:S(2)}, u32[]{:S(2)}) collective-permute-start(bf16[64,1536]{1,0:T(8,128)(2,1)} %get-tuple-element.198), channel_id=1, source_target_pairs={{0,16},{1,17},{2,18},{3,19},{4,20},{5,21},{6,22},{7,23},{8,24},{9,... | collective-permute-start | bytes 589832 | tf_op jit(solution)/shard_map/ppermute | solution.py:411
  135.9 88.0 %collective-permute-start.14 = (bf16[64,1536]{1,0:T(8,128)(2,1)}, bf16[64,1536]{1,0:T(8,128)(2,1)}, u32[]{:S(2)}, u32[]{:S(2)}) collective-permute-start(bf16[64,1536]{1,0:T(8,128)(2,1)} %get-tuple-element.198), channel_id=1, source_target_pairs={{0,8},{1,9},{2,10},{3,11},{4,12},{5,13},{6,14},{7,15},{8,16},{9,17... | collective-permute-start | bytes 589832 | tf_op jit(solution)/shard_map/ppermute | solution.py:411
  149.8 41.3 %collective-permute-start.12 = (bf16[32,24,2048]{2,1,0:T(8,128)(2,1)}, bf16[32,24,2048]{2,1,0:T(8,128)(2,1)}, u32[]{:S(2)}, u32[]{:S(2)}) collective-permute-start(bf16[32,24,2048]{2,1,0:T(8,128)(2,1)} %slice.300), channel_id=1, source_target_pairs={{0,32},{32,0},{1,33},{33,1},{2,34},{34,2},{3,35},{35,3},{4,36},{36... | collective-permute-start | bytes 9437192 | tf_op jit(solution)/shard_map/ppermute | solution.py:289
  413.1 36.9 %all-to-all-start.8 = ((bf16[32,2,8,1536]{3,2,1,0:T(8,128)(2,1)}), bf16[32,2,8,1536]{3,2,1,0:T(8,128)(2,1)}, u32[]{:S(2)}, u32[]{:S(2)}) async-start(bf16[32,2,8,1536]{3,2,1,0:T(8,128)(2,1)} %bitcast.575), calls=%async_computation.8 | async-start | bytes 3145728 | tf_op jit(solution)/shard_map/all_to_all | solution.py:281
  524.3 30.3 %all-to-all-start.11 = ((bf16[32,2,8,1536]{3,2,1,0:T(8,128)(2,1)}), bf16[32,2,8,1536]{3,2,1,0:T(8,128)(2,1)}, u32[]{:S(2)}, u32[]{:S(2)}) async-start(bf16[32,2,8,1536]{3,2,1,0:T(8,128)(2,1)} %bitcast.577), calls=%async_computation.11 | async-start | bytes 3145728 | tf_op jit(solution)/shard_map/all_to_all | solution.py:281
  636.1 31.1 %all-to-all-start.13 = ((bf16[32,2,8,1664]{3,2,1,0:T(8,128)(2,1)}), bf16[32,2,8,1664]{3,2,1,0:T(8,128)(2,1)}, u32[]{:S(2)}, u32[]{:S(2)}) async-start(bf16[32,2,8,1664]{3,2,1,0:T(8,128)(2,1)} %bitcast.574), calls=%async_computation.13 | async-start | bytes 3407872 | tf_op jit(solution)/shard_map/all_to_all | solution.py:281
  648.6 184.0 %collective-permute-start.31 = (bf16[128,1536]{1,0:T(8,128)(2,1)}, bf16[128,1536]{1,0:T(8,128)(2,1)}, u32[]{:S(2)}, u32[]{:S(2)}) collective-permute-start(bf16[128,1536]{1,0:T(8,128)(2,1)} %pad_maximum_fusion.10), channel_id=1, source_target_pairs={{0,32},{32,0},{1,33},{33,1},{2,34},{34,2},{3,35},{35,3},{4,36},{36... | collective-permute-start | bytes 1179656 | tf_op jit(solution)/shard_map/ppermute | solution.py:289
  653.5 157.0 %collective-permute-start.47 = (bf16[128,1024]{1,0:T(8,128)(2,1)}, bf16[128,1024]{1,0:T(8,128)(2,1)}, u32[]{:S(2)}, u32[]{:S(2)}) collective-permute-start(bf16[128,1024]{1,0:T(8,128)(2,1)} %pad_maximum_fusion.14), channel_id=1, source_target_pairs={{0,32},{32,0},{1,33},{33,1},{2,34},{34,2},{3,35},{35,3},{4,36},{36... | collective-permute-start | bytes 786440 | tf_op jit(solution)/shard_map/ppermute | solution.py:289
  675.8 29.5 %all-to-all-start.14 = ((bf16[32,2,8,1536]{3,2,1,0:T(8,128)(2,1)}), bf16[32,2,8,1536]{3,2,1,0:T(8,128)(2,1)}, u32[]{:S(2)}, u32[]{:S(2)}) async-start(bf16[32,2,8,1536]{3,2,1,0:T(8,128)(2,1)} %bitcast.579), calls=%async_computation.14 | async-start | bytes 3145728 | tf_op jit(solution)/shard_map/all_to_all | solution.py:281
  784.3 29.7 %all-to-all-start.16 = ((bf16[32,2,8,1536]{3,2,1,0:T(8,128)(2,1)}), bf16[32,2,8,1536]{3,2,1,0:T(8,128)(2,1)}, u32[]{:S(2)}, u32[]{:S(2)}) async-start(bf16[32,2,8,1536]{3,2,1,0:T(8,128)(2,1)} %bitcast.585), calls=%async_computation.16 | async-start | bytes 3145728 | tf_op jit(solution)/shard_map/all_to_all | solution.py:281
  823.2 33.3 %all-to-all-start.17 = ((bf16[32,2,8,1536]{3,2,1,0:T(8,128)(2,1)}), bf16[32,2,8,1536]{3,2,1,0:T(8,128)(2,1)}, u32[]{:S(2)}, u32[]{:S(2)}) async-start(bf16[32,2,8,1536]{3,2,1,0:T(8,128)(2,1)} %bitcast.576), calls=%async_computation.17 | async-start | bytes 3145728 | tf_op jit(solution)/shard_map/all_to_all | solution.py:281
  840.4 84.7 %collective-permute-start.55 = (bf16[2,1536,512]{2,1,0:T(8,128)(2,1)}, bf16[2,1536,512]{2,1,0:T(8,128)(2,1)}, u32[]{:S(2)}, u32[]{:S(2)}) collective-permute-start(bf16[2,1536,512]{2,1,0:T(8,128)(2,1)} %convolution_convert_fusion.3), channel_id=1, source_target_pairs={{0,32},{32,0},{1,33},{33,1},{2,34},{34,2},{3,35},{35,3},{4,36},{36... | collective-permute-start | bytes 9437192 | tf_op jit(solution)/shard_map/ppermute | solution.py:289
  844.7 80.4 %collective-permute-start.56 = (bf16[2,1536,512]{2,1,0:T(8,128)(2,1)}, bf16[2,1536,512]{2,1,0:T(8,128)(2,1)}, u32[]{:S(2)}, u32[]{:S(2)}) collective-permute-start(bf16[2,1536,512]{2,1,0:T(8,128)(2,1)} %convolution_convert_fusion.2), channel_id=1, source_target_pairs={{0,32},{32,0},{1,33},{33,1},{2,34},{34,2},{3,35},{35,3},{4,36},{36... | collective-permute-start | bytes 9437192 | tf_op jit(solution)/shard_map/ppermute | solution.py:289
  864.0 61.1 %collective-permute-start.57 = (bf16[2,512,1536]{2,1,0:T(8,128)(2,1)}, bf16[2,512,1536]{2,1,0:T(8,128)(2,1)}, u32[]{:S(2)}, u32[]{:S(2)}) collective-permute-start(bf16[2,512,1536]{2,1,0:T(8,128)(2,1)} %convolution_convert_fusion.1), channel_id=1, source_target_pairs={{0,32},{32,0},{1,33},{33,1},{2,34},{34,2},{3,35},{35,3},{4,36},{36... | collective-permute-start | bytes 9437192 | tf_op jit(solution)/shard_map/ppermute | solution.py:289
  925.1 60.4 %all-to-all-start.20 = ((bf16[8,48,1536]{2,1,0:T(8,128)(2,1)}), bf16[8,48,1536]{2,1,0:T(8,128)(2,1)}, u32[]{:S(2)}, u32[]{:S(2)}) async-start(bf16[8,48,1536]{2,1,0:T(8,128)(2,1)} %bitcast.595), calls=%async_computation.20 | async-start | bytes 2359296 | tf_op jit(solution)/shard_map/all_to_all | solution.py:281
  939.0 58.1 %collective-permute-start.61 = (bf16[4,2,48,1024]{3,2,1,0:T(8,128)(2,1)}, bf16[4,2,48,1024]{3,2,1,0:T(8,128)(2,1)}, u32[]{:S(2)}, u32[]{:S(2)}) collective-permute-start(bf16[4,2,48,1024]{3,2,1,0:T(8,128)(2,1)} %get-tuple-element.135), channel_id=1, source_target_pairs={{0,8},{1,9},{2,10},{3,11},{4,12},{5,13},{6,14},{7,15},{8,16},{9,17... | collective-permute-start | bytes 2359304 | tf_op jit(solution)/shard_map/ppermute | solution.py:411
  939.0 58.1 %collective-permute-start.63 = (bf16[4,2,48,1024]{3,2,1,0:T(8,128)(2,1)}, bf16[4,2,48,1024]{3,2,1,0:T(8,128)(2,1)}, u32[]{:S(2)}, u32[]{:S(2)}) collective-permute-start(bf16[4,2,48,1024]{3,2,1,0:T(8,128)(2,1)} %get-tuple-element.136), channel_id=1, source_target_pairs={{0,24},{1,25},{2,26},{3,27},{4,28},{5,29},{6,30},{7,31},{8,0},{9,1... | collective-permute-start | bytes 2359304 | tf_op jit(solution)/shard_map/ppermute | solution.py:411
  960.7 36.5 %collective-permute-start.62 = (bf16[4,2,48,1024]{3,2,1,0:T(8,128)(2,1)}, bf16[4,2,48,1024]{3,2,1,0:T(8,128)(2,1)}, u32[]{:S(2)}, u32[]{:S(2)}) collective-permute-start(bf16[4,2,48,1024]{3,2,1,0:T(8,128)(2,1)} %get-tuple-element.137), channel_id=1, source_target_pairs={{0,16},{1,17},{2,18},{3,19},{4,20},{5,21},{6,22},{7,23},{8,24},{9,... | collective-permute-start | bytes 2359304 | tf_op jit(solution)/shard_map/ppermute | solution.py:411
  985.5 57.1 %all-to-all-start.19 = ((bf16[32,48,768]{2,1,0:T(8,128)(2,1)}), bf16[32,48,768]{2,1,0:T(8,128)(2,1)}, u32[]{:S(2)}, u32[]{:S(2)}) async-start(bf16[32,48,768]{2,1,0:T(8,128)(2,1)} %maximum_maximum_fusion), calls=%async_computation.19 | async-start | bytes 4718592 | tf_op jit(solution)/shard_map/all_to_all | solution.py:281
  999.7 32.1 %collective-permute-start.64 = (bf16[2,48,1024]{2,1,0:T(8,128)(2,1)S(1)}, bf16[2,48,1024]{2,1,0:T(8,128)(2,1)S(1)}, u32[]{:S(2)}, u32[]{:S(2)}) collective-permute-start(bf16[2,48,1024]{2,1,0:T(8,128)(2,1)S(1)} %get-tuple-element.153), channel_id=1, source_target_pairs={{0,2},{1,3},{2,4},{3,5},{4,6},{5,7},{6,0},{7,1},{8,10},{9,11},{10,... | collective-permute-start | bytes 589832 | tf_op jit(solution)/shard_map/ppermute | solution.py:667
  1000.9 30.9 %collective-permute-start.66 = (bf16[2,48,1024]{2,1,0:T(8,128)(2,1)S(1)}, bf16[2,48,1024]{2,1,0:T(8,128)(2,1)S(1)}, u32[]{:S(2)}, u32[]{:S(2)}) collective-permute-start(bf16[2,48,1024]{2,1,0:T(8,128)(2,1)S(1)} %get-tuple-element.154), channel_id=1, source_target_pairs={{0,6},{1,7},{2,0},{3,1},{4,2},{5,3},{6,4},{7,5},{8,14},{9,15},{10,... | collective-permute-start | bytes 589832 | tf_op jit(solution)/shard_map/ppermute | solution.py:667
  (362 other events, 3078.1 us)
Sparse Core Ops, SparseCore 0:
  16.9 106.6 all-gather.2

commit v14 on v12

--- a/solution.py
+++ b/solution.py
@@ -656,8 +656,26 @@
         kept_rows("attended").reshape(micros * heads * block, group_width),
         back_rows("ring_hidden"),
     )
-    grad_gate_up, grad_down, grad_out, last_grad, *expert_others = lax.optimization_barrier(
+    grad_qkv = dot_tn(kept_rows("ring_one"), back_rows("qkv_grad"))
+    grad_router = dot_tn(normed_two, back_rows("logit_grad"))
+    gain_sums = jnp.stack(
+        [sum(grads[name] for grads in backs) for name in ("gain_one_grad", "gain_two_grad")]
+    )
+    grad_tail = jnp.concatenate(
+        [grad_router, gain_sums.T, jnp.zeros((width, 128 - experts - 2), f32)], axis=1
+    )
+    grad_qkv = jnp.concatenate([grad_qkv, grad_tail], axis=1)
+    grad_qkv = grad_qkv.astype(bf).reshape(shards, rows_per, part_width + 128)
+    (
+        grad_qkv,
+        grad_gate_up,
+        grad_down,
+        grad_out,
+        last_grad,
+        *expert_others,
+    ) = lax.optimization_barrier(
         (
+            grad_qkv,
             grad_gate_up.astype(bf),
             grad_down.astype(bf),
             grad_out.astype(bf),
@@ -666,6 +684,8 @@
         )
     )
     backs[0]["layer_grad"] = last_grad
+    pieces = exchange(grad_qkv)
+    attention_pieces, grad_out = lax.optimization_barrier((pieces, grad_out))
     expert_grads = [
         part.astype(f32) + other.astype(f32) for part, other in zip(expert_parts, expert_others)
     ]
@@ -677,23 +697,12 @@
     share_out = jnp.sum(
         exchange(grad_out.reshape(ring, rows_per, width), zy_groups).astype(f32), axis=0
     )
-    grad_qkv = dot_tn(kept_rows("ring_one"), back_rows("qkv_grad"))
-    grad_router = dot_tn(normed_two, back_rows("logit_grad"))
-    gain_sums = jnp.stack(
-        [sum(grads[name] for grads in backs) for name in ("gain_one_grad", "gain_two_grad")]
-    )
-    grad_tail = jnp.concatenate(
-        [grad_router, gain_sums.T, jnp.zeros((width, 128 - experts - 2), f32)], axis=1
-    )
-    grad_qkv = jnp.concatenate([grad_qkv, grad_tail], axis=1)
-    pieces = exchange(
-        grad_qkv.astype(bf).reshape(shards, rows_per, part_width + 128)
-    ).astype(f32)
+    attention_pieces = attention_pieces.astype(f32)
     share_qkv = jnp.sum(
-        pieces[:, :, :part_width].reshape(heads, ring, rows_per, part_width), axis=1
+        attention_pieces[:, :, :part_width].reshape(heads, ring, rows_per, part_width), axis=1
     )
     share_qkv = share_qkv.transpose(1, 0, 2)
-    share_tail = jnp.sum(pieces[:, :, part_width:], axis=0)
+    share_tail = jnp.sum(attention_pieces[:, :, part_width:], axis=0)
 
     def total(share):
         return share + twin(share)

time: 1070 us -> 1080 us (level)
    ppermute x2, waiting for transfers between devices: 22.8 us -> 3.78 us  [shift_y(): return lax.ppermute(value, 'shard', [(p, p ^ 1) for p in range(shards)])]
    all_to_all x20, waiting for transfers between devices: 178 us -> 189 us  [exchange(): lax.all_to_all(value, 'shard', split_axis=0, concat_axis=0, tiled=True, a...]
  transfers between devices with their start and end apart: 98 -> 98, of which waited for: 53 -> 56; matrix products, arithmetic and copies ran while one was open for 28% -> 28% of each run, Pallas kernels for 2% -> 2%
where the time goes in v14:
time: 1080 us; the launch traced here: 1060 us
  waiting for transfers between devices  343 us (32%)
  starting transfers between devices  246 us (23%)
  matrix products  179 us (17%)
  other arithmetic  113 us (10%)
  local copies, waits for them, and re-layouts  92.6 us (9%)
  Pallas kernels  42.9 us (4%)
  blocking collectives  29.3 us (3%)
  between operations  18.4 us (2%)
    all_to_all x20, waiting for transfers between devices, exchange(): lax.all_to_all(value, 'shard', split_axis=0, concat_axis=0, tiled=True, a...  189 us
    all_to_all x20, starting transfers between devices, exchange(): lax.all_to_all(value, 'shard', split_axis=0, concat_axis=0, tiled=True, a...  131 us
    ppermute x39, waiting for transfers between devices, shift_x(): lax.ppermute(value, 'shard', [(p, moved(p, steps)) for p in range(shards)])  79.8 us
    dot_general x24, matrix products, dot_nt(): lax.dot_general(left_side, right_side, (((1,), (1,)), ((), ())), preferre...  54 us
    dot_general x31, matrix products, dot(): return jnp.dot(left_side, right_side, preferred_element_type=f32)  51.6 us
    dot_general x21, matrix products, wide_einsum(): jnp.einsum(formula, left_side, right_side, preferred_element_type=f32)  47.9 us
    ppermute x39, starting transfers between devices, shift_x(): lax.ppermute(value, 'shard', [(p, moved(p, steps)) for p in range(shards)])  44.9 us
    pallas_call x6, Pallas kernels, attention_call(): pl.pallas_call(kernel, out_shape=out_shape, in_specs=[pl.BlockSpec(memory...  42.9 us
  transfers between devices with their start and end apart: 98, of which 56 were waited for; matrix products, arithmetic and copies ran while one was open for 28% of the time, Pallas kernels for 2%

profile of v14, /device:TPU:1, one launch (start us, length us, event | category | flops | bytes accessed | tf_op | source)
XLA Modules:
  0.0 1064.9 jit_solution(16729505107584964191)
XLA Ops:
  42.9 11.5 %collective-permute-done.6 = bf16[2,24,1536]{2,1,0:T(8,128)(2,1)} collective-permute-done((bf16[2,24,1536]{2,1,0:T(8,128)(2,1)S(1)}, bf16[2,24,1536]{2,1,0:T(8,128)(2,1)}, u32[]{:S(2)}, u32[]{:S(2)}) %collective-permute-start.6) | collective-permute-done | bytes 147488 | tf_op jit(solution)/shard_map/ppermute | solution.py:347
  79.4 16.5 %all-to-all-done.1.refs_0_.refs_1_ = bf16[8,256,256]{2,1,0:T(8,128)(2,1)} async-done(((bf16[8,256,256]{2,1,0:T(8,128)(2,1)}), bf16[8,256,256]{2,1,0:T(8,128)(2,1)}, u32[]{:S(2)}, u32[]{:S(2)}) %all-to-all-start.1) | async-done | bytes 1048608 | tf_op jit(solution)/shard_map/all_to_all | solution.py:281
  177.6 13.0 %all-to-all-done.3 = bf16[32,2,8,1536]{3,2,1,0:T(8,128)(2,1)} async-done(((bf16[32,2,8,1536]{3,2,1,0:T(8,128)(2,1)}), bf16[32,2,8,1536]{3,2,1,0:T(8,128)(2,1)}, u32[]{:S(2)}, u32[]{:S(2)}) %all-to-all-start.3) | async-done | bytes 1572896 | tf_op jit(solution)/shard_map/all_to_all | solution.py:281
  208.6 10.4 collective-permute-start.20
  245.4 15.7 %all-to-all-done.4.refs_1_.refs_0_.refs_2_ = bf16[8,256,256]{2,1,0:T(8,128)(2,1)} async-done(((bf16[8,256,256]{2,1,0:T(8,128)(2,1)}), bf16[8,256,256]{2,1,0:T(8,128)(2,1)}, u32[]{:S(2)}, u32[]{:S(2)}) %all-to-all-start.4) | async-done | bytes 1048608 | tf_op jit(solution)/shard_map/all_to_all | solution.py:281
  289.8 29.3 %all_to_all.105 = bf16[32,2,8,1536]{3,2,1,0:T(8,128)(2,1)S(1)} all-to-all(bf16[32,2,8,1536]{3,2,1,0:T(8,128)(2,1)S(1)} %bitcast.595), channel_id=1, replica_groups=mesh['section'=2,'dp'=2,'shard'=32] {'shard'}, dimensions={0} | all-to-all | bytes 3145728 | tf_op jit(solution)/shard_map/all_to_all | solution.py:281
  338.5 14.1 %all-to-all-done.6 = bf16[32,2,8,1536]{3,2,1,0:T(8,128)(2,1)} async-done(((bf16[32,2,8,1536]{3,2,1,0:T(8,128)(2,1)}), bf16[32,2,8,1536]{3,2,1,0:T(8,128)(2,1)}, u32[]{:S(2)}, u32[]{:S(2)}) %all-to-all-start.6) | async-done | bytes 1572896 | tf_op jit(solution)/shard_map/all_to_all | solution.py:281
  371.2 10.3 collective-permute-done.24
  398.6 13.8 %all-to-all-done.7.refs_1_ = bf16[8,256,256]{2,1,0:T(8,128)(2,1)} async-done(((bf16[8,256,256]{2,1,0:T(8,128)(2,1)}), bf16[8,256,256]{2,1,0:T(8,128)(2,1)}, u32[]{:S(2)}, u32[]{:S(2)}) %all-to-all-start.7) | async-done | bytes 1048608 | tf_op jit(solution)/shard_map/all_to_all | solution.py:281
  449.3 17.5 %all-to-all-done.8 = bf16[32,2,8,1536]{3,2,1,0:T(8,128)(2,1)} async-done(((bf16[32,2,8,1536]{3,2,1,0:T(8,128)(2,1)}), bf16[32,2,8,1536]{3,2,1,0:T(8,128)(2,1)}, u32[]{:S(2)}, u32[]{:S(2)}) %all-to-all-start.8) | async-done | bytes 1572896 | tf_op jit(solution)/shard_map/all_to_all | solution.py:281
  485.9 9.9 all-to-all-done.10
  515.6 10.2 all-to-all-done.9
  544.9 11.2 %all-to-all-done.11 = bf16[32,2,8,1536]{3,2,1,0:T(8,128)(2,1)} async-done(((bf16[32,2,8,1536]{3,2,1,0:T(8,128)(2,1)}), bf16[32,2,8,1536]{3,2,1,0:T(8,128)(2,1)}, u32[]{:S(2)}, u32[]{:S(2)}) %all-to-all-start.11) | async-done | bytes 1572896 | tf_op jit(solution)/shard_map/all_to_all | solution.py:281
  569.2 9.3 shard_map.274
  581.6 9.2 all-to-all-start.12
  597.8 9.6 all-to-all-done.12
  687.8 8.7 all-to-all-done.14
  710.0 9.3 shard_map.275
  736.5 9.4 all-to-all-done.15
  776.3 8.3 all-to-all-start.16
  815.0 9.3 all-to-all-start.17
  882.4 9.3 all-to-all-done.18
  975.7 17.5 %collective-permute-done.72 = bf16[2,32,768]{2,1,0:T(8,128)(2,1)S(1)} collective-permute-done((bf16[2,32,768]{2,1,0:T(8,128)(2,1)S(1)}, bf16[2,32,768]{2,1,0:T(8,128)(2,1)S(1)}, u32[]{:S(2)}, u32[]{:S(2)}) %collective-permute-start.72) | collective-permute-done | bytes 98336 | tf_op jit(solution)/shard_map/ppermute | solution.py:410
  1033.7 10.9 %all-to-all-done.20 = bf16[8,48,1536]{2,1,0:T(8,128)(2,1)} async-done(((bf16[8,48,1536]{2,1,0:T(8,128)(2,1)}), bf16[8,48,1536]{2,1,0:T(8,128)(2,1)}, u32[]{:S(2)}, u32[]{:S(2)}) %all-to-all-start.20) | async-done | bytes 1179680 | tf_op jit(solution)/shard_map/all_to_all | solution.py:281
  (1016 shorter events, 752.3 us)
Async XLA Ops:
  7.2 115.0 %all-gather.3.cloned.1.call-start = ((), (), s32[]{:S(2)}) async-start(), calls=%async_computation.21 | async-start | bytes 4866048 | tf_op jit(solution)/shard_map/all_gather | solution.py:340
  26.6 32.3 %all-to-all-start = ((bf16[32,24,768]{2,1,0:T(8,128)(2,1)}), bf16[32,24,768]{2,1,0:T(8,128)(2,1)}, u32[]{:S(2)}, u32[]{:S(2)}) async-start(bf16[32,24,768]{2,1,0:T(8,128)(2,1)} %bitcast.599), calls=%async_computation | async-start | bytes 2359296 | tf_op jit(solution)/shard_map/all_to_all | solution.py:281
  131.6 88.6 %collective-permute-start.16 = (bf16[64,1536]{1,0:T(8,128)(2,1)}, bf16[64,1536]{1,0:T(8,128)(2,1)}, u32[]{:S(2)}, u32[]{:S(2)}) collective-permute-start(bf16[64,1536]{1,0:T(8,128)(2,1)} %get-tuple-element.194), channel_id=1, source_target_pairs={{0,24},{1,25},{2,26},{3,27},{4,28},{5,29},{6,30},{7,31},{8,0},{9,1... | collective-permute-start | bytes 589832 | tf_op jit(solution)/shard_map/ppermute | solution.py:410
  134.1 87.5 %collective-permute-start.15 = (bf16[64,1536]{1,0:T(8,128)(2,1)}, bf16[64,1536]{1,0:T(8,128)(2,1)}, u32[]{:S(2)}, u32[]{:S(2)}) collective-permute-start(bf16[64,1536]{1,0:T(8,128)(2,1)} %get-tuple-element.194), channel_id=1, source_target_pairs={{0,16},{1,17},{2,18},{3,19},{4,20},{5,21},{6,22},{7,23},{8,24},{9,... | collective-permute-start | bytes 589832 | tf_op jit(solution)/shard_map/ppermute | solution.py:410
  134.6 88.5 %collective-permute-start.14 = (bf16[64,1536]{1,0:T(8,128)(2,1)}, bf16[64,1536]{1,0:T(8,128)(2,1)}, u32[]{:S(2)}, u32[]{:S(2)}) collective-permute-start(bf16[64,1536]{1,0:T(8,128)(2,1)} %get-tuple-element.194), channel_id=1, source_target_pairs={{0,8},{1,9},{2,10},{3,11},{4,12},{5,13},{6,14},{7,15},{8,16},{9,17... | collective-permute-start | bytes 589832 | tf_op jit(solution)/shard_map/ppermute | solution.py:410
  148.2 45.0 %collective-permute-start.12 = (bf16[32,24,2048]{2,1,0:T(8,128)(2,1)}, bf16[32,24,2048]{2,1,0:T(8,128)(2,1)}, u32[]{:S(2)}, u32[]{:S(2)}) collective-permute-start(bf16[32,24,2048]{2,1,0:T(8,128)(2,1)} %slice.291), channel_id=1, source_target_pairs={{0,32},{32,0},{1,33},{33,1},{2,34},{34,2},{3,35},{35,3},{4,36},{36... | collective-permute-start | bytes 9437192 | tf_op jit(solution)/shard_map/ppermute | solution.py:289
  437.6 29.2 %all-to-all-start.8 = ((bf16[32,2,8,1536]{3,2,1,0:T(8,128)(2,1)}), bf16[32,2,8,1536]{3,2,1,0:T(8,128)(2,1)}, u32[]{:S(2)}, u32[]{:S(2)}) async-start(bf16[32,2,8,1536]{3,2,1,0:T(8,128)(2,1)} %bitcast.588), calls=%async_computation.8 | async-start | bytes 3145728 | tf_op jit(solution)/shard_map/all_to_all | solution.py:281
  495.8 30.1 %all-to-all-start.9 = ((bf16[32,2,8,1536]{3,2,1,0:T(8,128)(2,1)}), bf16[32,2,8,1536]{3,2,1,0:T(8,128)(2,1)}, u32[]{:S(2)}, u32[]{:S(2)}) async-start(bf16[32,2,8,1536]{3,2,1,0:T(8,128)(2,1)} %bitcast.593), calls=%async_computation.9 | async-start | bytes 3145728 | tf_op jit(solution)/shard_map/all_to_all | solution.py:281
  525.9 30.2 %all-to-all-start.11 = ((bf16[32,2,8,1536]{3,2,1,0:T(8,128)(2,1)}), bf16[32,2,8,1536]{3,2,1,0:T(8,128)(2,1)}, u32[]{:S(2)}, u32[]{:S(2)}) async-start(bf16[32,2,8,1536]{3,2,1,0:T(8,128)(2,1)} %bitcast.590), calls=%async_computation.11 | async-start | bytes 3145728 | tf_op jit(solution)/shard_map/all_to_all | solution.py:281
  595.2 229.1 %collective-permute-start.51 = (bf16[128,1536]{1,0:T(8,128)(2,1)}, bf16[128,1536]{1,0:T(8,128)(2,1)}, u32[]{:S(2)}, u32[]{:S(2)}) collective-permute-start(bf16[128,1536]{1,0:T(8,128)(2,1)} %pad_maximum_fusion.10), channel_id=1, source_target_pairs={{0,32},{32,0},{1,33},{33,1},{2,34},{34,2},{3,35},{35,3},{4,36},{36... | collective-permute-start | bytes 1179656 | tf_op jit(solution)/shard_map/ppermute | solution.py:289
  631.2 29.6 %all-to-all-start.13 = ((bf16[32,2,8,1536]{3,2,1,0:T(8,128)(2,1)}), bf16[32,2,8,1536]{3,2,1,0:T(8,128)(2,1)}, u32[]{:S(2)}, u32[]{:S(2)}) async-start(bf16[32,2,8,1536]{3,2,1,0:T(8,128)(2,1)} %bitcast.598), calls=%async_computation.13 | async-start | bytes 3145728 | tf_op jit(solution)/shard_map/all_to_all | solution.py:281
  643.1 159.5 %collective-permute-start.53 = (bf16[128,1024]{1,0:T(8,128)(2,1)}, bf16[128,1024]{1,0:T(8,128)(2,1)}, u32[]{:S(2)}, u32[]{:S(2)}) collective-permute-start(bf16[128,1024]{1,0:T(8,128)(2,1)} %pad_maximum_fusion.14), channel_id=1, source_target_pairs={{0,32},{32,0},{1,33},{33,1},{2,34},{34,2},{3,35},{35,3},{4,36},{36... | collective-permute-start | bytes 786440 | tf_op jit(solution)/shard_map/ppermute | solution.py:289
  776.3 29.9 %all-to-all-start.16 = ((bf16[32,2,8,1536]{3,2,1,0:T(8,128)(2,1)}), bf16[32,2,8,1536]{3,2,1,0:T(8,128)(2,1)}, u32[]{:S(2)}, u32[]{:S(2)}) async-start(bf16[32,2,8,1536]{3,2,1,0:T(8,128)(2,1)} %bitcast.597), calls=%async_computation.16 | async-start | bytes 3145728 | tf_op jit(solution)/shard_map/all_to_all | solution.py:281
  815.0 33.2 %all-to-all-start.17 = ((bf16[32,2,8,1536]{3,2,1,0:T(8,128)(2,1)}), bf16[32,2,8,1536]{3,2,1,0:T(8,128)(2,1)}, u32[]{:S(2)}, u32[]{:S(2)}) async-start(bf16[32,2,8,1536]{3,2,1,0:T(8,128)(2,1)} %bitcast.587), calls=%async_computation.17 | async-start | bytes 3145728 | tf_op jit(solution)/shard_map/all_to_all | solution.py:281
  832.0 87.2 %collective-permute-start.55 = (bf16[2,1536,512]{2,1,0:T(8,128)(2,1)}, bf16[2,1536,512]{2,1,0:T(8,128)(2,1)}, u32[]{:S(2)}, u32[]{:S(2)}) collective-permute-start(bf16[2,1536,512]{2,1,0:T(8,128)(2,1)} %convolution_convert_fusion.3), channel_id=1, source_target_pairs={{0,32},{32,0},{1,33},{33,1},{2,34},{34,2},{3,35},{35,3},{4,36},{36... | collective-permute-start | bytes 9437192 | tf_op jit(solution)/shard_map/ppermute | solution.py:289
  836.2 82.9 %collective-permute-start.56 = (bf16[2,1536,512]{2,1,0:T(8,128)(2,1)}, bf16[2,1536,512]{2,1,0:T(8,128)(2,1)}, u32[]{:S(2)}, u32[]{:S(2)}) collective-permute-start(bf16[2,1536,512]{2,1,0:T(8,128)(2,1)} %convolution_convert_fusion.2), channel_id=1, source_target_pairs={{0,32},{32,0},{1,33},{33,1},{2,34},{34,2},{3,35},{35,3},{4,36},{36... | collective-permute-start | bytes 9437192 | tf_op jit(solution)/shard_map/ppermute | solution.py:289
  855.6 63.5 %collective-permute-start.57 = (bf16[2,512,1536]{2,1,0:T(8,128)(2,1)}, bf16[2,512,1536]{2,1,0:T(8,128)(2,1)}, u32[]{:S(2)}, u32[]{:S(2)}) collective-permute-start(bf16[2,512,1536]{2,1,0:T(8,128)(2,1)} %convolution_convert_fusion.1), channel_id=1, source_target_pairs={{0,32},{32,0},{1,33},{33,1},{2,34},{34,2},{3,35},{35,3},{4,36},{36... | collective-permute-start | bytes 9437192 | tf_op jit(solution)/shard_map/ppermute | solution.py:289
  919.2 102.4 %all-to-all-start.19 = ((bf16[32,48,768]{2,1,0:T(8,128)(2,1)}), bf16[32,48,768]{2,1,0:T(8,128)(2,1)}, u32[]{:S(2)}, u32[]{:S(2)}) async-start(bf16[32,48,768]{2,1,0:T(8,128)(2,1)} %maximum_maximum_fusion), calls=%async_computation.19 | async-start | bytes 4718592 | tf_op jit(solution)/shard_map/all_to_all | solution.py:281
  927.5 34.9 %collective-permute-start.69 = (bf16[4,2,32,768]{3,2,1,0:T(8,128)(2,1)S(1)}, bf16[4,2,32,768]{3,2,1,0:T(8,128)(2,1)S(1)}, u32[]{:S(2)}, u32[]{:S(2)}) collective-permute-start(bf16[4,2,32,768]{3,2,1,0:T(8,128)(2,1)S(1)} %get-tuple-element.145), channel_id=1, source_target_pairs={{0,2},{1,3},{2,4},{3,5},{4,6},{5,7},{6,0},{7,1},{8,10},{9,11},{10,... | collective-permute-start | bytes 1179656 | tf_op jit(solution)/shard_map/ppermute | solution.py:634
  928.8 36.4 %collective-permute-start.71 = (bf16[4,2,32,768]{3,2,1,0:T(8,128)(2,1)S(1)}, bf16[4,2,32,768]{3,2,1,0:T(8,128)(2,1)S(1)}, u32[]{:S(2)}, u32[]{:S(2)}) collective-permute-start(bf16[4,2,32,768]{3,2,1,0:T(8,128)(2,1)S(1)} %get-tuple-element.146), channel_id=1, source_target_pairs={{0,6},{1,7},{2,0},{3,1},{4,2},{5,3},{6,4},{7,5},{8,14},{9,15},{10,... | collective-permute-start | bytes 1179656 | tf_op jit(solution)/shard_map/ppermute | solution.py:634
  930.3 41.3 %collective-permute-start.70 = (bf16[4,2,32,768]{3,2,1,0:T(8,128)(2,1)S(1)}, bf16[4,2,32,768]{3,2,1,0:T(8,128)(2,1)S(1)}, u32[]{:S(2)}, u32[]{:S(2)}) collective-permute-start(bf16[4,2,32,768]{3,2,1,0:T(8,128)(2,1)S(1)} %get-tuple-element.147), channel_id=1, source_target_pairs={{0,4},{1,5},{2,6},{3,7},{4,0},{5,1},{6,2},{7,3},{8,12},{9,13},{10,... | collective-permute-start | bytes 1179656 | tf_op jit(solution)/shard_map/ppermute | solution.py:634
  933.6 66.6 %collective-permute-start.61 = (bf16[4,2,48,1024]{3,2,1,0:T(8,128)(2,1)S(1)}, bf16[4,2,48,1024]{3,2,1,0:T(8,128)(2,1)S(1)}, u32[]{:S(2)}, u32[]{:S(2)}) collective-permute-start(bf16[4,2,48,1024]{3,2,1,0:T(8,128)(2,1)S(1)} %get-tuple-element.132), channel_id=1, source_target_pairs={{0,8},{1,9},{2,10},{3,11},{4,12},{5,13},{6,14},{7,15},{8,16},{9,17... | collective-permute-start | bytes 2359304 | tf_op jit(solution)/shard_map/ppermute | solution.py:410
  935.1 65.1 %collective-permute-start.63 = (bf16[4,2,48,1024]{3,2,1,0:T(8,128)(2,1)S(1)}, bf16[4,2,48,1024]{3,2,1,0:T(8,128)(2,1)S(1)}, u32[]{:S(2)}, u32[]{:S(2)}) collective-permute-start(bf16[4,2,48,1024]{3,2,1,0:T(8,128)(2,1)S(1)} %get-tuple-element.133), channel_id=1, source_target_pairs={{0,24},{1,25},{2,26},{3,27},{4,28},{5,29},{6,30},{7,31},{8,0},{9,1... | collective-permute-start | bytes 2359304 | tf_op jit(solution)/shard_map/ppermute | solution.py:410
  962.5 37.7 %collective-permute-start.62 = (bf16[4,2,48,1024]{3,2,1,0:T(8,128)(2,1)S(1)}, bf16[4,2,48,1024]{3,2,1,0:T(8,128)(2,1)S(1)}, u32[]{:S(2)}, u32[]{:S(2)}) collective-permute-start(bf16[4,2,48,1024]{3,2,1,0:T(8,128)(2,1)S(1)} %get-tuple-element.134), channel_id=1, source_target_pairs={{0,16},{1,17},{2,18},{3,19},{4,20},{5,21},{6,22},{7,23},{8,24},{9,... | collective-permute-start | bytes 2359304 | tf_op jit(solution)/shard_map/ppermute | solution.py:410
  (353 other events, 3076.3 us)
Sparse Core Ops, SparseCore 0:
  16.9 105.2 all-gather.2

commit v15 on v14

--- a/solution.py
+++ b/solution.py
@@ -690,13 +690,14 @@
         part.astype(f32) + other.astype(f32) for part, other in zip(expert_parts, expert_others)
     ]
     pieces = grad_gate_up.reshape(heads, ring // 2, 2, rows_per, shared_width)
-    share_gate_up = reduced(reduced(reduced(pieces, "x", 0), "z", 0), "y", 0, f32)
+    pieces, out_pieces = lax.optimization_barrier(
+        (reduced(pieces, "x", 0), exchange(grad_out.reshape(ring, rows_per, width), zy_groups))
+    )
+    share_gate_up = reduced(reduced(pieces, "z", 0), "y", 0, f32)
     pieces = grad_down.reshape(heads, ring // 2, 2, down_rows, width // 2)
     share_down = reduced(reduced(reduced(pieces, "z", 1), "x", 0), "y", 0, f32)
 
-    share_out = jnp.sum(
-        exchange(grad_out.reshape(ring, rows_per, width), zy_groups).astype(f32), axis=0
-    )
+    share_out = jnp.sum(out_pieces.astype(f32), axis=0)
     attention_pieces = attention_pieces.astype(f32)
     share_qkv = jnp.sum(
         attention_pieces[:, :, :part_width].reshape(heads, ring, rows_per, part_width), axis=1

time: 1080 us -> 1070 us (level)
  waiting for transfers between devices: 343 us -> 326 us
    ppermute x39, waiting for transfers between devices: 79.8 us -> 58.2 us  [shift_x(): lax.ppermute(value, 'shard', [(p, moved(p, steps)) for p in range(shards)])]
    ppermute x6, waiting for transfers between devices: 18.5 us -> 29.6 us  [shift_z(): return lax.ppermute(value, 'shard', pairs)]
  transfers between devices with their start and end apart: 98 -> 98, of which waited for: 56 -> 54; matrix products, arithmetic and copies ran while one was open for 28% -> 29% of each run, Pallas kernels for 2% -> 2%
where the time goes in v15:
time: 1070 us; the launch traced here: 1050 us
  waiting for transfers between devices  326 us (30%)
  starting transfers between devices  248 us (23%)
  matrix products  179 us (17%)
  other arithmetic  116 us (11%)
  local copies, waits for them, and re-layouts  94.7 us (9%)
  Pallas kernels  42.9 us (4%)
  blocking collectives  29.3 us (3%)
  between operations  18.4 us (2%)
    all_to_all x20, waiting for transfers between devices, exchange(): lax.all_to_all(value, 'shard', split_axis=0, concat_axis=0, tiled=True, a...  186 us
    all_to_all x20, starting transfers between devices, exchange(): lax.all_to_all(value, 'shard', split_axis=0, concat_axis=0, tiled=True, a...  131 us
    ppermute x39, waiting for transfers between devices, shift_x(): lax.ppermute(value, 'shard', [(p, moved(p, steps)) for p in range(shards)])  58.2 us
    dot_general x24, matrix products, dot_nt(): lax.dot_general(left_side, right_side, (((1,), (1,)), ((), ())), preferre...  53.9 us
    dot_general x31, matrix products, dot(): return jnp.dot(left_side, right_side, preferred_element_type=f32)  51.6 us
    dot_general x21, matrix products, wide_einsum(): jnp.einsum(formula, left_side, right_side, preferred_element_type=f32)  47.9 us
    ppermute x39, starting transfers between devices, shift_x(): lax.ppermute(value, 'shard', [(p, moved(p, steps)) for p in range(shards)])  45 us
    pallas_call x6, Pallas kernels, attention_call(): pl.pallas_call(kernel, out_shape=out_shape, in_specs=[pl.BlockSpec(memory...  42.9 us
  transfers between devices with their start and end apart: 98, of which 54 were waited for; matrix products, arithmetic and copies ran while one was open for 29% of the time, Pallas kernels for 2%

profile of v15, /device:TPU:1, one launch (start us, length us, event | category | flops | bytes accessed | tf_op | source)
XLA Modules:
  0.0 1054.8 jit_solution(13006458141830269743)
XLA Ops:
  42.9 11.5 %collective-permute-done.6 = bf16[2,24,1536]{2,1,0:T(8,128)(2,1)} collective-permute-done((bf16[2,24,1536]{2,1,0:T(8,128)(2,1)S(1)}, bf16[2,24,1536]{2,1,0:T(8,128)(2,1)}, u32[]{:S(2)}, u32[]{:S(2)}) %collective-permute-start.6) | collective-permute-done | bytes 147488 | tf_op jit(solution)/shard_map/ppermute | solution.py:347
  79.4 16.4 %all-to-all-done.1.refs_0_.refs_1_ = bf16[8,256,256]{2,1,0:T(8,128)(2,1)} async-done(((bf16[8,256,256]{2,1,0:T(8,128)(2,1)}), bf16[8,256,256]{2,1,0:T(8,128)(2,1)}, u32[]{:S(2)}, u32[]{:S(2)}) %all-to-all-start.1) | async-done | bytes 1048608 | tf_op jit(solution)/shard_map/all_to_all | solution.py:281
  176.7 12.1 %all-to-all-done.3 = bf16[32,2,8,1536]{3,2,1,0:T(8,128)(2,1)} async-done(((bf16[32,2,8,1536]{3,2,1,0:T(8,128)(2,1)}), bf16[32,2,8,1536]{3,2,1,0:T(8,128)(2,1)}, u32[]{:S(2)}, u32[]{:S(2)}) %all-to-all-start.3) | async-done | bytes 1572896 | tf_op jit(solution)/shard_map/all_to_all | solution.py:281
  206.7 12.1 %collective-permute-start.20 = (bf16[64,1536]{1,0:T(8,128)(2,1)S(1)}, bf16[64,1536]{1,0:T(8,128)(2,1)S(1)}, u32[]{:S(2)}, u32[]{:S(2)}) collective-permute-start(bf16[64,1536]{1,0:T(8,128)(2,1)S(1)} %add_convert_fusion.2), channel_id=1, source_target_pairs={{0,88},{1,89},{2,90},{3,91},{4,92},{5,93},{6,94},{7,95},{8,64},{9,... | collective-permute-start | bytes 589832 | tf_op jit(solution)/shard_map/ppermute | solution.py:415
  245.2 15.7 %all-to-all-done.4.refs_1_.refs_0_.refs_2_ = bf16[8,256,256]{2,1,0:T(8,128)(2,1)} async-done(((bf16[8,256,256]{2,1,0:T(8,128)(2,1)}), bf16[8,256,256]{2,1,0:T(8,128)(2,1)}, u32[]{:S(2)}, u32[]{:S(2)}) %all-to-all-start.4) | async-done | bytes 1048608 | tf_op jit(solution)/shard_map/all_to_all | solution.py:281
  289.6 29.3 %all_to_all.105 = bf16[32,2,8,1536]{3,2,1,0:T(8,128)(2,1)S(1)} all-to-all(bf16[32,2,8,1536]{3,2,1,0:T(8,128)(2,1)S(1)} %bitcast.595), channel_id=1, replica_groups=mesh['section'=2,'dp'=2,'shard'=32] {'shard'}, dimensions={0} | all-to-all | bytes 3145728 | tf_op jit(solution)/shard_map/all_to_all | solution.py:281
  338.3 14.0 %all-to-all-done.6 = bf16[32,2,8,1536]{3,2,1,0:T(8,128)(2,1)} async-done(((bf16[32,2,8,1536]{3,2,1,0:T(8,128)(2,1)}), bf16[32,2,8,1536]{3,2,1,0:T(8,128)(2,1)}, u32[]{:S(2)}, u32[]{:S(2)}) %all-to-all-start.6) | async-done | bytes 1572896 | tf_op jit(solution)/shard_map/all_to_all | solution.py:281
  370.9 10.2 collective-permute-done.24
  398.3 13.8 %all-to-all-done.7.refs_1_ = bf16[8,256,256]{2,1,0:T(8,128)(2,1)} async-done(((bf16[8,256,256]{2,1,0:T(8,128)(2,1)}), bf16[8,256,256]{2,1,0:T(8,128)(2,1)}, u32[]{:S(2)}, u32[]{:S(2)}) %all-to-all-start.7) | async-done | bytes 1048608 | tf_op jit(solution)/shard_map/all_to_all | solution.py:281
  448.9 17.5 %all-to-all-done.8 = bf16[32,2,8,1536]{3,2,1,0:T(8,128)(2,1)} async-done(((bf16[32,2,8,1536]{3,2,1,0:T(8,128)(2,1)}), bf16[32,2,8,1536]{3,2,1,0:T(8,128)(2,1)}, u32[]{:S(2)}, u32[]{:S(2)}) %all-to-all-start.8) | async-done | bytes 1572896 | tf_op jit(solution)/shard_map/all_to_all | solution.py:281
  485.6 9.8 all-to-all-done.10
  515.4 10.2 all-to-all-done.9
  544.6 11.2 %all-to-all-done.11 = bf16[32,2,8,1536]{3,2,1,0:T(8,128)(2,1)} async-done(((bf16[32,2,8,1536]{3,2,1,0:T(8,128)(2,1)}), bf16[32,2,8,1536]{3,2,1,0:T(8,128)(2,1)}, u32[]{:S(2)}, u32[]{:S(2)}) %all-to-all-start.11) | async-done | bytes 1572896 | tf_op jit(solution)/shard_map/all_to_all | solution.py:281
  568.9 9.3 shard_map.274
  581.2 9.2 all-to-all-start.12
  597.6 9.5 all-to-all-done.12
  687.5 8.8 all-to-all-done.14
  709.8 9.4 shard_map.275
  736.4 9.4 all-to-all-done.15
  814.8 9.3 all-to-all-start.17
  882.1 9.4 all-to-all-done.18
  943.9 18.4 %collective-permute-done.69 = bf16[4,2,32,768]{3,2,1,0:T(8,128)(2,1)S(1)} collective-permute-done((bf16[4,2,32,768]{3,2,1,0:T(8,128)(2,1)S(1)}, bf16[4,2,32,768]{3,2,1,0:T(8,128)(2,1)S(1)}, u32[]{:S(2)}, u32[]{:S(2)}) %collective-permute-start.69) | collective-permute-done | bytes 393248 | tf_op jit(solution)/shard_map/ppermute | solution.py:634
  962.2 9.0 collective-permute-done.70
  1011.0 9.7 all-to-all-done.20
  (1016 shorter events, 741.2 us)
Async XLA Ops:
  7.2 115.0 %all-gather.3.cloned.1.call-start = ((), (), s32[]{:S(2)}) async-start(), calls=%async_computation.21 | async-start | bytes 4866048 | tf_op jit(solution)/shard_map/all_gather | solution.py:340
  26.6 32.3 %all-to-all-start = ((bf16[32,24,768]{2,1,0:T(8,128)(2,1)}), bf16[32,24,768]{2,1,0:T(8,128)(2,1)}, u32[]{:S(2)}, u32[]{:S(2)}) async-start(bf16[32,24,768]{2,1,0:T(8,128)(2,1)} %bitcast.599), calls=%async_computation | async-start | bytes 2359296 | tf_op jit(solution)/shard_map/all_to_all | solution.py:281
  131.6 88.6 %collective-permute-start.16 = (bf16[64,1536]{1,0:T(8,128)(2,1)}, bf16[64,1536]{1,0:T(8,128)(2,1)}, u32[]{:S(2)}, u32[]{:S(2)}) collective-permute-start(bf16[64,1536]{1,0:T(8,128)(2,1)} %get-tuple-element.198), channel_id=1, source_target_pairs={{0,24},{1,25},{2,26},{3,27},{4,28},{5,29},{6,30},{7,31},{8,0},{9,1... | collective-permute-start | bytes 589832 | tf_op jit(solution)/shard_map/ppermute | solution.py:410
  134.1 87.4 %collective-permute-start.15 = (bf16[64,1536]{1,0:T(8,128)(2,1)}, bf16[64,1536]{1,0:T(8,128)(2,1)}, u32[]{:S(2)}, u32[]{:S(2)}) collective-permute-start(bf16[64,1536]{1,0:T(8,128)(2,1)} %get-tuple-element.198), channel_id=1, source_target_pairs={{0,16},{1,17},{2,18},{3,19},{4,20},{5,21},{6,22},{7,23},{8,24},{9,... | collective-permute-start | bytes 589832 | tf_op jit(solution)/shard_map/ppermute | solution.py:410
  134.5 88.5 %collective-permute-start.14 = (bf16[64,1536]{1,0:T(8,128)(2,1)}, bf16[64,1536]{1,0:T(8,128)(2,1)}, u32[]{:S(2)}, u32[]{:S(2)}) collective-permute-start(bf16[64,1536]{1,0:T(8,128)(2,1)} %get-tuple-element.198), channel_id=1, source_target_pairs={{0,8},{1,9},{2,10},{3,11},{4,12},{5,13},{6,14},{7,15},{8,16},{9,17... | collective-permute-start | bytes 589832 | tf_op jit(solution)/shard_map/ppermute | solution.py:410
  148.3 43.1 %collective-permute-start.12 = (bf16[32,24,2048]{2,1,0:T(8,128)(2,1)}, bf16[32,24,2048]{2,1,0:T(8,128)(2,1)}, u32[]{:S(2)}, u32[]{:S(2)}) collective-permute-start(bf16[32,24,2048]{2,1,0:T(8,128)(2,1)} %slice.291), channel_id=1, source_target_pairs={{0,32},{32,0},{1,33},{33,1},{2,34},{34,2},{3,35},{35,3},{4,36},{36... | collective-permute-start | bytes 9437192 | tf_op jit(solution)/shard_map/ppermute | solution.py:289
  437.2 29.2 %all-to-all-start.8 = ((bf16[32,2,8,1536]{3,2,1,0:T(8,128)(2,1)}), bf16[32,2,8,1536]{3,2,1,0:T(8,128)(2,1)}, u32[]{:S(2)}, u32[]{:S(2)}) async-start(bf16[32,2,8,1536]{3,2,1,0:T(8,128)(2,1)} %bitcast.588), calls=%async_computation.8 | async-start | bytes 3145728 | tf_op jit(solution)/shard_map/all_to_all | solution.py:281
  466.4 29.1 %all-to-all-start.10 = ((bf16[32,2,8,1536]{3,2,1,0:T(8,128)(2,1)}), bf16[32,2,8,1536]{3,2,1,0:T(8,128)(2,1)}, u32[]{:S(2)}, u32[]{:S(2)}) async-start(bf16[32,2,8,1536]{3,2,1,0:T(8,128)(2,1)} %bitcast.596), calls=%async_computation.10 | async-start | bytes 3145728 | tf_op jit(solution)/shard_map/all_to_all | solution.py:281
  495.5 30.1 %all-to-all-start.9 = ((bf16[32,2,8,1536]{3,2,1,0:T(8,128)(2,1)}), bf16[32,2,8,1536]{3,2,1,0:T(8,128)(2,1)}, u32[]{:S(2)}, u32[]{:S(2)}) async-start(bf16[32,2,8,1536]{3,2,1,0:T(8,128)(2,1)} %bitcast.593), calls=%async_computation.9 | async-start | bytes 3145728 | tf_op jit(solution)/shard_map/all_to_all | solution.py:281
  525.6 30.2 %all-to-all-start.11 = ((bf16[32,2,8,1536]{3,2,1,0:T(8,128)(2,1)}), bf16[32,2,8,1536]{3,2,1,0:T(8,128)(2,1)}, u32[]{:S(2)}, u32[]{:S(2)}) async-start(bf16[32,2,8,1536]{3,2,1,0:T(8,128)(2,1)} %bitcast.590), calls=%async_computation.11 | async-start | bytes 3145728 | tf_op jit(solution)/shard_map/all_to_all | solution.py:281
  594.9 229.1 %collective-permute-start.51 = (bf16[128,1536]{1,0:T(8,128)(2,1)}, bf16[128,1536]{1,0:T(8,128)(2,1)}, u32[]{:S(2)}, u32[]{:S(2)}) collective-permute-start(bf16[128,1536]{1,0:T(8,128)(2,1)} %pad_maximum_fusion.10), channel_id=1, source_target_pairs={{0,32},{32,0},{1,33},{33,1},{2,34},{34,2},{3,35},{35,3},{4,36},{36... | collective-permute-start | bytes 1179656 | tf_op jit(solution)/shard_map/ppermute | solution.py:289
  630.9 29.6 %all-to-all-start.13 = ((bf16[32,2,8,1536]{3,2,1,0:T(8,128)(2,1)}), bf16[32,2,8,1536]{3,2,1,0:T(8,128)(2,1)}, u32[]{:S(2)}, u32[]{:S(2)}) async-start(bf16[32,2,8,1536]{3,2,1,0:T(8,128)(2,1)} %bitcast.598), calls=%async_computation.13 | async-start | bytes 3145728 | tf_op jit(solution)/shard_map/all_to_all | solution.py:281
  642.8 159.6 %collective-permute-start.53 = (bf16[128,1024]{1,0:T(8,128)(2,1)}, bf16[128,1024]{1,0:T(8,128)(2,1)}, u32[]{:S(2)}, u32[]{:S(2)}) collective-permute-start(bf16[128,1024]{1,0:T(8,128)(2,1)} %pad_maximum_fusion.14), channel_id=1, source_target_pairs={{0,32},{32,0},{1,33},{33,1},{2,34},{34,2},{3,35},{35,3},{4,36},{36... | collective-permute-start | bytes 786440 | tf_op jit(solution)/shard_map/ppermute | solution.py:289
  775.9 30.1 %all-to-all-start.16 = ((bf16[32,2,8,1536]{3,2,1,0:T(8,128)(2,1)}), bf16[32,2,8,1536]{3,2,1,0:T(8,128)(2,1)}, u32[]{:S(2)}, u32[]{:S(2)}) async-start(bf16[32,2,8,1536]{3,2,1,0:T(8,128)(2,1)} %bitcast.597), calls=%async_computation.16 | async-start | bytes 3145728 | tf_op jit(solution)/shard_map/all_to_all | solution.py:281
  814.8 33.2 %all-to-all-start.17 = ((bf16[32,2,8,1536]{3,2,1,0:T(8,128)(2,1)}), bf16[32,2,8,1536]{3,2,1,0:T(8,128)(2,1)}, u32[]{:S(2)}, u32[]{:S(2)}) async-start(bf16[32,2,8,1536]{3,2,1,0:T(8,128)(2,1)} %bitcast.587), calls=%async_computation.17 | async-start | bytes 3145728 | tf_op jit(solution)/shard_map/all_to_all | solution.py:281
  831.8 86.9 %collective-permute-start.55 = (bf16[2,1536,512]{2,1,0:T(8,128)(2,1)}, bf16[2,1536,512]{2,1,0:T(8,128)(2,1)}, u32[]{:S(2)}, u32[]{:S(2)}) collective-permute-start(bf16[2,1536,512]{2,1,0:T(8,128)(2,1)} %convolution_convert_fusion.3), channel_id=1, source_target_pairs={{0,32},{32,0},{1,33},{33,1},{2,34},{34,2},{3,35},{35,3},{4,36},{36... | collective-permute-start | bytes 9437192 | tf_op jit(solution)/shard_map/ppermute | solution.py:289
  836.1 82.7 %collective-permute-start.56 = (bf16[2,1536,512]{2,1,0:T(8,128)(2,1)}, bf16[2,1536,512]{2,1,0:T(8,128)(2,1)}, u32[]{:S(2)}, u32[]{:S(2)}) collective-permute-start(bf16[2,1536,512]{2,1,0:T(8,128)(2,1)} %convolution_convert_fusion.2), channel_id=1, source_target_pairs={{0,32},{32,0},{1,33},{33,1},{2,34},{34,2},{3,35},{35,3},{4,36},{36... | collective-permute-start | bytes 9437192 | tf_op jit(solution)/shard_map/ppermute | solution.py:289
  855.4 63.4 %collective-permute-start.57 = (bf16[2,512,1536]{2,1,0:T(8,128)(2,1)}, bf16[2,512,1536]{2,1,0:T(8,128)(2,1)}, u32[]{:S(2)}, u32[]{:S(2)}) collective-permute-start(bf16[2,512,1536]{2,1,0:T(8,128)(2,1)} %convolution_convert_fusion.1), channel_id=1, source_target_pairs={{0,32},{32,0},{1,33},{33,1},{2,34},{34,2},{3,35},{35,3},{4,36},{36... | collective-permute-start | bytes 9437192 | tf_op jit(solution)/shard_map/ppermute | solution.py:289
  918.8 79.4 %all-to-all-start.19 = ((bf16[32,48,768]{2,1,0:T(8,128)(2,1)}), bf16[32,48,768]{2,1,0:T(8,128)(2,1)}, u32[]{:S(2)}, u32[]{:S(2)}) async-start(bf16[32,48,768]{2,1,0:T(8,128)(2,1)} %maximum_maximum_fusion), calls=%async_computation.19 | async-start | bytes 4718592 | tf_op jit(solution)/shard_map/all_to_all | solution.py:281
  927.2 35.1 %collective-permute-start.69 = (bf16[4,2,32,768]{3,2,1,0:T(8,128)(2,1)S(1)}, bf16[4,2,32,768]{3,2,1,0:T(8,128)(2,1)S(1)}, u32[]{:S(2)}, u32[]{:S(2)}) collective-permute-start(bf16[4,2,32,768]{3,2,1,0:T(8,128)(2,1)S(1)} %get-tuple-element.149), channel_id=1, source_target_pairs={{0,2},{1,3},{2,4},{3,5},{4,6},{5,7},{6,0},{7,1},{8,10},{9,11},{10,... | collective-permute-start | bytes 1179656 | tf_op jit(solution)/shard_map/ppermute | solution.py:634
  928.4 33.8 %collective-permute-start.71 = (bf16[4,2,32,768]{3,2,1,0:T(8,128)(2,1)S(1)}, bf16[4,2,32,768]{3,2,1,0:T(8,128)(2,1)S(1)}, u32[]{:S(2)}, u32[]{:S(2)}) collective-permute-start(bf16[4,2,32,768]{3,2,1,0:T(8,128)(2,1)S(1)} %get-tuple-element.150), channel_id=1, source_target_pairs={{0,6},{1,7},{2,0},{3,1},{4,2},{5,3},{6,4},{7,5},{8,14},{9,15},{10,... | collective-permute-start | bytes 1179656 | tf_op jit(solution)/shard_map/ppermute | solution.py:634
  929.9 41.3 %collective-permute-start.70 = (bf16[4,2,32,768]{3,2,1,0:T(8,128)(2,1)S(1)}, bf16[4,2,32,768]{3,2,1,0:T(8,128)(2,1)S(1)}, u32[]{:S(2)}, u32[]{:S(2)}) collective-permute-start(bf16[4,2,32,768]{3,2,1,0:T(8,128)(2,1)S(1)} %get-tuple-element.151), channel_id=1, source_target_pairs={{0,4},{1,5},{2,6},{3,7},{4,0},{5,1},{6,2},{7,3},{8,12},{9,13},{10,... | collective-permute-start | bytes 1179656 | tf_op jit(solution)/shard_map/ppermute | solution.py:634
  934.4 71.9 %collective-permute-start.60 = (bf16[4,2,48,1024]{3,2,1,0:T(8,128)(2,1)}, bf16[4,2,48,1024]{3,2,1,0:T(8,128)(2,1)}, u32[]{:S(2)}, u32[]{:S(2)}) collective-permute-start(bf16[4,2,48,1024]{3,2,1,0:T(8,128)(2,1)} %get-tuple-element.136), channel_id=1, source_target_pairs={{0,8},{1,9},{2,10},{3,11},{4,12},{5,13},{6,14},{7,15},{8,16},{9,17... | collective-permute-start | bytes 2359304 | tf_op jit(solution)/shard_map/ppermute | solution.py:410
  935.8 70.5 %collective-permute-start.62 = (bf16[4,2,48,1024]{3,2,1,0:T(8,128)(2,1)}, bf16[4,2,48,1024]{3,2,1,0:T(8,128)(2,1)}, u32[]{:S(2)}, u32[]{:S(2)}) collective-permute-start(bf16[4,2,48,1024]{3,2,1,0:T(8,128)(2,1)} %get-tuple-element.137), channel_id=1, source_target_pairs={{0,24},{1,25},{2,26},{3,27},{4,28},{5,29},{6,30},{7,31},{8,0},{9,1... | collective-permute-start | bytes 2359304 | tf_op jit(solution)/shard_map/ppermute | solution.py:410
  (353 other events, 3041.5 us)
Sparse Core Ops, SparseCore 0:
  16.9 105.2 all-gather.2
